TPU v7x, 512 devices: a whole 4x8x8 slice. The times are simulated.
512 devices in a mesh: ctx: 32 (over x, y), tp: 16 (over z, core).
Axes of the slice: x: 4, y: 8, z: 8, core: 2. Of those that a mesh axis runs over, the one named last changes fastest.
Arguments:
- hidden: bfloat16 [6144, 16384], P(('ctx', 'tp')), may hold values from -32 to 32
- query_weight: bfloat16 [16384, 2048], P('ctx', 'tp'), may hold values from -0.046875 to 0.046875
- kv_weight: bfloat16 [16384, 256], P('tp'), may hold values from -0.046875 to 0.046875
Outputs:
- context_out: bfloat16 [6144, 2048], P('ctx', 'tp')
All inputs are finite; a program needn't handle non-finite values.
Results may differ from a plain program's by a relative error of at most 0.0315.
The roundings to bfloat16 on the way count: a program that leaves them out, or rounds other values in their place, can miss the bound.
Values may be sent and summed in bfloat16 or wider, within the bound.
No kernel may reach another device: no remote copies, remote signals or barrier semaphores. Data moves between devices by JAX's collectives and lax.ppermute only.
A program may use at most 64 MiB of HBM per device.

v0:
```python
import jax
import jax.numpy as jnp
from jax import lax
from jax.sharding import PartitionSpec as P

HD = 128
KEY_TILE = 512


def rotate(field, positions):
    half_width = field.shape[1] // 2
    exponent = jnp.arange(half_width, dtype=jnp.float32) * (2.0 / field.shape[1])
    frequency = jnp.power(jnp.float32(500000.0), -exponent)
    angles = positions.astype(jnp.float32)[:, None] * frequency[None, :]
    cosine = jnp.cos(angles)
    sine = jnp.sin(angles)
    first_half = field[:, :half_width]
    second_half = field[:, half_width:]
    return jnp.concatenate(
        [first_half * cosine - second_half * sine, second_half * cosine + first_half * sine], axis=1
    )


def attend(queries, positions, key_rows, value_rows):
    row_count = queries.shape[0]
    width = value_rows.shape[1]
    scale = HD ** (-0.5)
    tile_count = positions[row_count - 1] // KEY_TILE + 1
    key_offsets = jnp.arange(KEY_TILE, dtype=jnp.int32)

    def advance(tile_index, state_now):
        running, totals, accum = state_now
        first_key = tile_index * KEY_TILE
        key_tile = lax.dynamic_slice_in_dim(key_rows, first_key, KEY_TILE, 0)
        value_tile = lax.dynamic_slice_in_dim(value_rows, first_key, KEY_TILE, 0)
        scores = (
            lax.dot_general(
                queries, key_tile, (((1,), (1,)), ((), ())), preferred_element_type=jnp.float32
            )
            * scale
        )
        scores = jnp.where(
            positions[:, None] >= (first_key + key_offsets)[None, :], scores, -jnp.inf
        )
        updated = jnp.maximum(running, jnp.max(scores, axis=1))
        shrink = jnp.exp(running - updated)
        expo = jnp.exp(scores - updated[:, None])
        totals = totals * shrink + jnp.sum(expo, axis=1)
        accum = accum * shrink[:, None] + jnp.dot(
            expo.astype(jnp.bfloat16), value_tile, preferred_element_type=jnp.float32
        )
        return (updated, totals, accum)

    start_state = (
        jnp.full((row_count,), -1e30, jnp.float32),
        jnp.zeros((row_count,), jnp.float32),
        jnp.zeros((row_count, width), jnp.float32),
    )
    running, totals, accum = lax.fori_loop(0, tile_count, advance, start_state)
    return (accum / totals[:, None]).astype(jnp.bfloat16)


def body(hidden, query_weight, kv_weight):
    ctx_index = lax.axis_index("ctx")
    tp_index = lax.axis_index("tp")
    tp_count = lax.axis_size("tp")
    tok_rows = hidden.shape[0] * tp_count
    slab_width = kv_weight.shape[0]
    base = ctx_index * tok_rows
    query_pos = base + jnp.arange(tok_rows, dtype=jnp.int32)
    gathered = lax.all_gather(hidden, "tp", axis=0, tiled=True)
    query_sums = jnp.dot(
        gathered,
        lax.all_gather(query_weight, "ctx", axis=0, tiled=True),
        preferred_element_type=jnp.float32,
    )
    own_columns = lax.dynamic_slice_in_dim(gathered, tp_index * slab_width, slab_width, 1)
    queries = rotate(query_sums, query_pos).astype(jnp.bfloat16)
    summed = lax.psum(jnp.dot(own_columns, kv_weight, preferred_element_type=jnp.float32), "tp")
    key_part = rotate(summed[:, :HD], query_pos).astype(jnp.bfloat16)
    value_part = summed[:, HD:].astype(jnp.bfloat16)
    key_rows, value_rows = (
        lax.all_gather(key_part, "ctx", axis=0, tiled=True),
        lax.all_gather(value_part, "ctx", axis=0, tiled=True),
    )
    return attend(queries, query_pos, key_rows, value_rows)


def solution(mesh):
    in_specs = (P(("ctx", "tp"), None), P("ctx", "tp"), P("tp", None))
    out_specs = P("ctx", "tp")
    return jax.shard_map(body, mesh=mesh, in_specs=in_specs, out_specs=out_specs, check_vma=False)
```

profile of v0, /device:TPU:6, one launch (start us, length us, event | category | flops | bytes accessed | tf_op | source)
XLA Modules:
  0.0 396.8 jit_solution(13686248922859410238)
XLA Ops:
  8.1 66.1 %all-gather.12.cloned.1.call-done = bf16[16,12,16384]{2,1,0:T(8,128)(2,1)} async-done(((bf16[1,12,16384]{2,1,0:T(8,128)(2,1)}), bf16[16,12,16384]{2,1,0:T(8,128)(2,1)}) %all-gather.12.cloned.1.call-update) | async-done | bytes 6291472 | tf_op jit(solution)/shard_map/all_gather | solution.py:71
  74.3 8.8 %reshape.19 = bf16[192,16384]{1,0:T(8,128)(2,1)} reshape(bf16[16,12,16384]{2,1,0:T(8,128)(2,1)} %all-gather.12.cloned.1.call-done) | data formatting | bytes 12582912
  83.0 1.9 fusion.14
  85.6 108.7 %all-reduce.2.cloned.1.call-done = f32[192,256]{1,0:T(8,128)} async-done(((f32[192,256]{1,0:T(8,128)}), f32[192,256]{1,0:T(8,128)}) %all-reduce.2.cloned.1.call-update) | async-done | bytes 196624 | tf_op jit(solution)/shard_map/psum | solution.py:79
  194.4 1.5 slice.42
  196.1 5.9 %fusion.35 = f32[192,128]{1,0:T(8,128)S(1)} fusion(bf16[192,16384]{1,0:T(8,128)(2,1)} %reshape.19, bf16[16384,128]{1,0:T(8,128)(2,1)} %all-gather.8.cloned.1.call-done), kind=kOutput, calls=%fused_computation.47 | convolution fusion | flops 805306368 | bytes 10584064 | tf_op jit(solution)/shard_map/dot_general | solution.py:72
  206.2 71.2 %all-gather.10.cloned.1.call-done = bf16[6144,128]{1,0:T(8,128)(2,1)} async-done(((bf16[192,128]{1,0:T(8,128)(2,1)}), bf16[6144,128]{1,0:T(8,128)(2,1)}) %all-gather.10.cloned.1.call-update) | async-done | bytes 1572880 | tf_op jit(solution)/shard_map/all_gather | solution.py:84
  277.4 83.8 %all-gather.6.cloned.1.call-done = bf16[6144,128]{1,0:T(8,128)(2,1)} async-done(((bf16[192,128]{1,0:T(8,128)(2,1)}), bf16[6144,128]{1,0:T(8,128)(2,1)}) %all-gather.6.cloned.1.call-update) | async-done | bytes 1572880 | tf_op jit(solution)/shard_map/all_gather | solution.py:83
  361.3 27.2 %while.15 = (s32[]{:T(128)}, f32[192]{0:T(256)S(1)}, f32[192]{0:T(256)S(1)}, f32[192,128]{1,0:T(8,128)S(1)}, s32[]{:T(128)}, /*index=5*/bf16[6144,128]{1,0:T(8,1...) while((s32[]{:T(128)}, f32[192]{0:T(256)S(1)}, ...), condition=%wide.region_4.5_spmd.clone, body=%wide.region_1.4_spmd.clone.sunk | while | flops 51168324 | bytes 1705659 | solution.py:59
  361.3 1.2 fusion.48
  362.8 1.2 convolution_add_fusion.2
  364.0 1.2 fusion.48
  365.5 1.2 convolution_add_fusion.2
  366.7 1.2 fusion.48
  368.2 1.2 convolution_add_fusion.2
  369.5 1.2 fusion.48
  370.9 1.2 convolution_add_fusion.2
  372.2 1.2 fusion.48
  373.6 1.2 convolution_add_fusion.2
  374.9 1.2 fusion.48
  377.6 1.2 fusion.48
  380.3 1.2 fusion.48
  383.1 1.2 fusion.48
  385.8 1.2 fusion.48
  (91 shorter events, 12.6 us)
Async XLA Ops:
  7.4 75.7 %copy-start = (bf16[1024,256]{1,0:T(8,128)(2,1)S(1)}, bf16[1024,256]{1,0:T(8,128)(2,1)}, u32[]{:S(2)}) copy-start(bf16[1024,256]{1,0:T(8,128)(2,1)} %param.7) | copy-start | bytes 1572868
  7.4 66.9 %all-gather.12.cloned.1.call-start = ((), (), s32[]{:S(2)}) async-start(), calls=%async_computation.4 | async-start | bytes 8912896 | tf_op jit(solution)/shard_map/all_gather | solution.py:71
  8.1 186.3 %all-reduce.2.cloned.1.call-start = ((), (), s32[]{:S(2)}) async-start(), calls=%async_computation | async-start | bytes 393216 | tf_op jit(solution)/shard_map/psum | solution.py:79
  85.0 111.0 %all-gather.8.cloned.1.call-start = ((), (), s32[]{:S(2)}) async-start(), calls=%async_computation.2 | async-start | bytes 4325376 | tf_op jit(solution)/shard_map/all_gather | solution.py:74
  85.6 191.8 %all-gather.10.cloned.1.call-start = ((), (), s32[]{:S(2)}) async-start(), calls=%async_computation.3 | async-start | bytes 1622016 | tf_op jit(solution)/shard_map/all_gather | solution.py:84
  195.9 165.3 %all-gather.6.cloned.1.call-start = ((), (), s32[]{:S(2)}) async-start(), calls=%async_computation.1 | async-start | bytes 1622016 | tf_op jit(solution)/shard_map/all_gather | solution.py:83
  196.0 6.0 %copy-start.1 = (f32[192,256]{1,0:T(8,128)S(1)}, f32[192,256]{1,0:T(8,128)}, u32[]{:S(2)}) copy-start(f32[192,256]{1,0:T(8,128)} %all-reduce.2.cloned.1.call-done) | copy-start | bytes 589828
Sparse Core Ops, SparseCore 0:
  10.3 63.9 all-gather.11
  85.1 109.2 all-reduce.1
Sparse Core Ops, SparseCore 1:
  88.7 83.5 all-gather.7
  196.0 81.4 all-gather.9
  281.0 80.2 all-gather.5
where the time goes:
time: 401 us; the launch traced here: 397 us
  waiting for transfers between devices  331 us (83%)
  matrix products  32 us (8%)
  between operations  17.4 us (4%)
  local copies, waits for them, and re-layouts  10.9 us (3%)
  other arithmetic  4.47 us (1%)
    psum x1, waiting for transfers between devices, body(): lax.psum(jnp.dot(own_columns, kv_weight, preferred_element_type=jnp.float...  109 us
    all_gather x1, waiting for transfers between devices, body(): lax.all_gather(key_part, 'ctx', axis=0, tiled=True)  83.8 us
    all_gather x1, waiting for transfers between devices, body(): lax.all_gather(value_part, 'ctx', axis=0, tiled=True)  71.2 us
    all_gather x1, waiting for transfers between devices, body(): gathered = lax.all_gather(hidden, 'tp', axis=0, tiled=True)  66.1 us
    dot_general x10, matrix products, advance(): lax.dot_general(queries, key_tile, (((1,), (1,)), ((), ())), preferred_el...  12.2 us
    dot_general x10, matrix products, advance(): jnp.dot(expo.astype(jnp.bfloat16), value_tile, preferred_element_type=jnp...  12 us
    unnamed x5, local copies, waits for them, and re-layouts  8.77 us
  transfers between devices with their start and end apart: 5, of which 4 were waited for; matrix products, arithmetic and copies ran while one was open for 2% of the time, Pallas kernels for 0%

commit v1 on v0

v1 whole, which is shorter than its diff:
```python
import math

import jax
import jax.numpy as jnp
from jax import lax
from jax.experimental import pallas as pl
from jax.experimental.pallas import tpu as pltpu
from jax.sharding import Mesh
from jax.sharding import PartitionSpec as P

HD = 128
CTX = ("x", "yh", "yl")
TP = ("z", "core")
AXES = CTX + TP
KEY_TILE = 768


def fine_mesh(mesh):
    return Mesh(mesh.devices.reshape(4, 2, 4, 8, 2), AXES)


def angles_of(positions):
    half = HD // 2
    exponent = jnp.arange(half, dtype=jnp.float32) * (2.0 / HD)
    frequency = jnp.power(jnp.float32(500000.0), -exponent)
    angles = positions.astype(jnp.float32)[:, None] * frequency[None, :]
    return jnp.cos(angles), jnp.sin(angles)


def rotate(field, cosine, sine):
    half = HD // 2
    first, second = field[:, :half], field[:, half:]
    return jnp.concatenate(
        [first * cosine - second * sine, second * cosine + first * sine], axis=1
    )


def broadcast_gather(x, axis):
    n = lax.axis_size(axis)
    return lax.all_to_all(
        jnp.broadcast_to(x[None], (n,) + x.shape), axis, 0, 0, tiled=True
    )


def project_kernel(info_ref, h_ref, *refs):
    w_refs, o_ref, h_buf, w_buf, sems = refs[:4], *refs[4:]
    x = info_ref[0]
    copies = []
    for n in range(4):
        at = pl.multiple_of(lax.rem(x + 4 - n, 4) * 2048, 2048)
        copies.append(
            (
                pltpu.make_async_copy(h_ref.at[:, pl.ds(at, 2048)], h_buf.at[n], sems.at[n, 0]),
                pltpu.make_async_copy(w_refs[n], w_buf.at[n], sems.at[n, 1]),
            )
        )
        for copy in copies[n]:
            copy.start()
    total = None
    for n in range(4):
        for copy in copies[n]:
            copy.wait()
        term = jnp.dot(h_buf[n], w_buf[n], preferred_element_type=jnp.float32)
        total = term if total is None else total + term
    for part in range(16):
        for sel in range(2):
            at = part * 24 + sel * 12
            o_ref[sel, part * 12 : part * 12 + 12, :] = total[at : at + 12]


def attend_kernel(info_ref, q_ref, cos_ref, sin_ref, *refs):
    mine, near_ref, far_ref, o_ref, buf, s_ref, sems = refs[:4], *refs[4:]
    rows = q_ref.shape[0]
    x, y, core = info_ref[0], info_ref[1], info_ref[2]
    size = near_ref.shape[0]
    own = (y * rows) // KEY_TILE
    full = own + x * (size // KEY_TILE)

    def copies(i):
        other = near_ref if i == 0 else far_ref.at[pl.ds((i - 1) * size, size)]
        return [
            pltpu.make_async_copy(mine[i], buf.at[i, core], sems.at[i, 0]),
            pltpu.make_async_copy(other, buf.at[i, 1 - core], sems.at[i, 1]),
        ]

    for i in range(4):

        @pl.when(x >= i)
        def _(i=i):
            for copy in copies(i):
                copy.start()

    sums = q_ref[...]
    q = sums * cos_ref[...] + pltpu.roll(sums, HD // 2, 1) * sin_ref[...]
    q = q.astype(jnp.bfloat16)

    def where(j):
        back = jnp.where(j < own, 0, (j - own) // (size // KEY_TILE) + 1)
        first = jnp.where(j < own, 0, lax.rem(j - own, size // KEY_TILE)) * KEY_TILE
        return back, pl.ds(pl.multiple_of(first, KEY_TILE), KEY_TILE)

    def lanes(v, op):
        out = v[:, :HD]
        for i in range(1, v.shape[1] // HD):
            out = op(out, v[:, i * HD : (i + 1) * HD])
        return out

    def scores(k):
        return lax.dot_general(
            q, k, (((1,), (1,)), ((), ())), preferred_element_type=jnp.float32
        )

    for copy in copies(0):
        copy.wait()
    at = pl.multiple_of(own * KEY_TILE, KEY_TILE)
    s = scores(buf[0, 0, pl.ds(at, KEY_TILE), :])
    qp = y * rows + lax.broadcasted_iota(jnp.int32, s.shape, 0)
    kp = at + lax.broadcasted_iota(jnp.int32, s.shape, 1)
    s = jnp.where(qp >= kp, s, -jnp.inf)
    s_ref[full] = s
    top = lanes(s, jnp.maximum)
    for i in range(1, 4):

        @pl.when(x >= i)
        def _(i=i):
            for copy in copies(i):
                copy.wait()

    def first_pass(j, top):
        back, at = where(j)
        s = scores(buf[back, 0, at, :])
        s_ref[j] = s
        return jnp.maximum(top, lanes(s, jnp.maximum))

    top = jnp.max(lax.fori_loop(0, full, first_pass, top), axis=1, keepdims=True)
    scale = HD**-0.5 * math.log2(math.e)

    def weigh(s, v, state):
        tot, acc = state
        e = jnp.exp2((s - top) * scale)
        return tot + lanes(e, jnp.add), acc + jnp.dot(
            e.astype(jnp.bfloat16), v, preferred_element_type=jnp.float32
        )

    def second_pass(j, state):
        back, at = where(j)
        return weigh(s_ref[j], buf[back, 1, at, :], state)

    zero = jnp.zeros((rows, HD), jnp.float32)
    state = weigh(s_ref[full], buf[0, 1, pl.ds(at, KEY_TILE), :], (zero, zero))
    tot, acc = lax.fori_loop(0, full, second_pass, state)
    o_ref[...] = (acc / jnp.sum(tot, axis=1, keepdims=True)).astype(o_ref.dtype)


def project(info, h, pieces):
    m, depth = h.shape
    hbm = pl.BlockSpec(memory_space=pl.ANY)
    return pl.pallas_call(
        project_kernel,
        in_specs=[pl.BlockSpec(memory_space=pltpu.SMEM)] + [hbm] * 5,
        out_specs=pl.BlockSpec(memory_space=pltpu.VMEM),
        out_shape=jax.ShapeDtypeStruct((2, m // 2, HD), jnp.float32),
        scratch_shapes=[
            pltpu.VMEM((4, m, depth // 4), jnp.bfloat16),
            pltpu.VMEM((4, depth // 4, HD), jnp.bfloat16),
            pltpu.SemaphoreType.DMA((4, 2)),
        ],
        compiler_params=pltpu.CompilerParams(vmem_limit_bytes=48 * 2**20),
        cost_estimate=pl.CostEstimate(
            flops=2 * m * depth * HD, bytes_accessed=2 * depth * (m + HD), transcendentals=0
        ),
        name="project",
    )(info, h, *pieces)


def attend(info, sums, cosine, sine, mine, other):
    vm = pl.BlockSpec(memory_space=pltpu.VMEM)
    return pl.pallas_call(
        attend_kernel,
        in_specs=[pl.BlockSpec(memory_space=pltpu.SMEM), vm, vm, vm]
        + [pl.BlockSpec(memory_space=pl.ANY)] * 6,
        out_specs=vm,
        out_shape=jax.ShapeDtypeStruct(sums.shape, jnp.bfloat16),
        scratch_shapes=[
            pltpu.VMEM((4, 2, 1536, HD), jnp.bfloat16),
            pltpu.VMEM((6144 // KEY_TILE, 192, KEY_TILE), jnp.float32),
            pltpu.SemaphoreType.DMA((4, 2)),
        ],
        compiler_params=pltpu.CompilerParams(vmem_limit_bytes=40 * 2**20),
        cost_estimate=pl.CostEstimate(
            flops=4 * 192 * 6144 * HD,
            bytes_accessed=4 * 6144 * HD,
            transcendentals=192 * 6144,
        ),
        name="attend",
    )(info, sums, cosine, sine, *mine, *other)


def shift(v, axis, by):
    n = lax.axis_size(axis)
    return lax.ppermute(v, axis, [(i, (i + by) % n) for i in range(n)])


def shift_up(v, axis, by):
    n = lax.axis_size(axis)
    return lax.ppermute(v, axis, [(i, i + by) for i in range(n - by)])


def swap(v, axis):
    return lax.ppermute(v, axis, [(0, 1), (1, 0)])


def body(hidden, query_weight, kv_weight):
    x, yh, yl, z, core = (lax.axis_index(a) for a in AXES)
    y = yh * 4 + yl
    base = (x * 8 + y) * 192
    info = jnp.stack([x, y, core])
    tie = lax.optimization_barrier

    w = lax.all_gather(query_weight, "yl", axis=0, tiled=True)

    hs = hidden.reshape(12, 16, 1024).transpose(1, 0, 2)
    hs, hidden = tie((hs, hidden))
    hs = lax.all_to_all(hs, TP, 0, 0, tiled=True).reshape(192, 1024)

    parts = [hidden[:, i * 2048 : (i + 1) * 2048] for i in range(8)]
    halves = [jnp.concatenate(parts[i::2], axis=1) for i in range(2)]
    keep = jnp.where(yh == 0, halves[0], halves[1])
    come = swap(jnp.where(yh == 0, halves[1], halves[0]), "yh")
    h = jnp.where(
        yh == 0, jnp.concatenate([keep, come], 0), jnp.concatenate([come, keep], 0)
    )
    part = jnp.dot(hs, kv_weight, preferred_element_type=jnp.float32)
    part = part.reshape(8, 24, 2, HD).transpose(0, 2, 1, 3).reshape(16, 24, HD)
    h, w, part = tie((h, w, part))
    h = lax.all_gather(h, TP, axis=0, tiled=True)

    part = lax.all_to_all(part, TP, 0, 0, tiled=True)
    up, down = shift(w, "x", 1), shift(w, "x", -1)
    rows = jnp.sum(part, axis=0)
    cosine, sine = angles_of(base + z * 24 + jnp.arange(24, dtype=jnp.int32))
    rows = jnp.where(core == 0, rotate(rows, cosine, sine), rows).astype(jnp.bfloat16)
    rows, up, down = tie((rows, up, down))
    rows = broadcast_gather(rows, ("yh", "yl", "z")).reshape(1536, HD)
    cross = [shift(up[:1024], "x", 1), shift(down[1024:], "x", -1)]
    rows, cross = tie((rows, cross))
    mine = [rows] + [shift_up(rows, "x", d) for d in (1, 2, 3)]

    sums = project(info, h, (w, up, jnp.concatenate(cross, axis=0), down))
    come, sums = tie((mine[1:], sums))
    other = [swap(rows, "core"), swap(jnp.concatenate(come, axis=0), "core")]
    keep = jnp.where(yh == 0, sums[0], sums[1])
    come = swap(jnp.where(yh == 0, sums[1], sums[0]), "yh")
    cosine, sine = angles_of(base + jnp.arange(192, dtype=jnp.int32))
    cosine = jnp.concatenate([cosine, cosine], axis=1)
    sine = jnp.concatenate([-sine, sine], axis=1)
    return attend(info, keep + come, cosine, sine, mine, other)


def solution(mesh):
    in_specs = (P(AXES, None), P(CTX, TP), P(TP, None))
    out_specs = P(CTX, TP)
    return jax.shard_map(
        body, mesh=fine_mesh(mesh), in_specs=in_specs, out_specs=out_specs, check_vma=False
    )
```

time: 401 us -> 152 us (0.38)
  waiting for transfers between devices: 331 us -> 36.6 us
  starting transfers between devices: 0.17 us -> 61.5 us
  matrix products: 32 us -> 1.01 us
  blocking collectives: 0 us -> 16.2 us
  Pallas kernels: 0 us -> 12.7 us
  local copies, waits for them, and re-layouts: 10.9 us -> 4.75 us
    all_gather x4 -> x1, waiting for transfers between devices: 221 us -> 0.02 us  [body(): h = lax.all_gather(h, TP, axis=0, tiled=True)]
    psum x1 -> x0, waiting for transfers between devices: 109 us -> none  [body(): lax.psum(jnp.dot(own_columns, kv_weight, preferred_element_type=jnp.float...]
    ppermute x0 -> x11, starting transfers between devices: none -> 33.6 us  [the longest x4 18.1 us: swap(): return lax.ppermute(v, axis, [(0, 1), (1, 0)])]
    dot_general x22 -> x1, matrix products: 32 us -> 1.01 us  [body(): part = jnp.dot(hs, kv_weight, preferred_element_type=jnp.float32)]
    ppermute x0 -> x11, waiting for transfers between devices: none -> 28.3 us  [the longest x4 15.6 us: shift(): return lax.ppermute(v, axis, [(i, (i + by) % n) for i in range(n)])]
    all_to_all x0 -> x3, starting transfers between devices: none -> 27.8 us  [the longest x1 10.8 us: broadcast_gather(): lax.all_to_all(jnp.broadcast_to(x[None], (n,) + x.shape), axis, 0, 0, til...]
    all_gather x0 -> x1, blocking collectives: none -> 16.2 us  [body(): w = lax.all_gather(query_weight, 'yl', axis=0, tiled=True)]
    pallas_call x0 -> x2, Pallas kernels: none -> 12.7 us  [the longest x1 6.58 us: attend(): pl.pallas_call(attend_kernel, in_specs=[pl.BlockSpec(memory_space=pltpu.S...]
  transfers between devices with their start and end apart: 5 -> 15, of which waited for: 4 -> 9; matrix products, arithmetic and copies ran while one was open for 2% -> 3% of each run, Pallas kernels for 0% -> 4%
where the time goes in v1:
time: 152 us; the launch traced here: 149 us
  starting transfers between devices  61.5 us (40%)
  waiting for transfers between devices  36.6 us (24%)
  blocking collectives  16.2 us (11%)
  between operations  13.8 us (9%)
  Pallas kernels  12.7 us (8%)
  local copies, waits for them, and re-layouts  4.75 us (3%)
  other arithmetic  3.03 us (2%)
    ppermute x4, starting transfers between devices, swap(): return lax.ppermute(v, axis, [(0, 1), (1, 0)])  18.1 us
    all_gather x1, blocking collectives, body(): w = lax.all_gather(query_weight, 'yl', axis=0, tiled=True)  16.2 us
    ppermute x4, waiting for transfers between devices, shift(): return lax.ppermute(v, axis, [(i, (i + by) % n) for i in range(n)])  15.6 us
    ppermute x4, starting transfers between devices, shift(): return lax.ppermute(v, axis, [(i, (i + by) % n) for i in range(n)])  11.7 us
    all_to_all x1, starting transfers between devices, broadcast_gather(): lax.all_to_all(jnp.broadcast_to(x[None], (n,) + x.shape), axis, 0, 0, til...  10.8 us
    all_to_all x1, starting transfers between devices, body(): hs = lax.all_to_all(hs, TP, 0, 0, tiled=True).reshape(192, 1024)  10.4 us
    ppermute x3, waiting for transfers between devices, shift_up(): return lax.ppermute(v, axis, [(i, i + by) for i in range(n - by)])  8.21 us
    all_to_all x1, starting transfers between devices, body(): part = lax.all_to_all(part, TP, 0, 0, tiled=True)  6.58 us
  transfers between devices with their start and end apart: 15, of which 9 were waited for; matrix products, arithmetic and copies ran while one was open for 3% of the time, Pallas kernels for 4%

profile of v1, /device:TPU:6, one launch (start us, length us, event | category | flops | bytes accessed | tf_op | source)
XLA Modules:
  0.0 149.5 jit_solution(2470848341985627844)
XLA Ops:
  6.5 1.4 copy.10
  9.2 7.7 %collective-permute-start = (bf16[12,8192]{1,0:T(8,128)(2,1)S(1)}, bf16[12,8192]{1,0:T(8,128)(2,1)S(1)}, u32[]{:S(2)}, u32[]{:S(2)}) collective-permute-start(bf16[12,8192]{1,0:T(8,128)(2,1)S(1)} %get-tuple-element.36), channel_id=1, source_target_pairs={{0,64},{64,0},{1,65},{65,1},{2,66},{66,2},{3,67},{67,3},{4,68},{68... | collective-permute-start | bytes 589832 | tf_op jit(solution)/shard_map/ppermute | solution.py:210
  17.0 10.4 %all-to-all-start = ((bf16[16,12,1024]{2,1,0:T(8,128)(2,1)}), bf16[16,12,1024]{2,1,0:T(8,128)(2,1)S(1)}, u32[]{:S(2)}, u32[]{:S(2)}) async-start(bf16[16,12,1024]{2,1,0:T(8,128)(2,1)} %bitcast.24), calls=%async_computation | async-start | bytes 1048576 | tf_op jit(solution)/shard_map/all_to_all | solution.py:224
  27.7 16.2 %all_gather.6.refs_0_ = bf16[2048,128]{1,0:T(8,128)(2,1)S(1)} all-gather(bf16[512,128]{1,0:T(8,128)(2,1)S(1)} %copy-done.4), channel_id=1, replica_groups=mesh['x'=4,'yh'=2,'yl'=4,'z'=8,'core'=2] {'yl'}, dimensions={0}, use_global_device_ids=true | all-gather | bytes 655360 | tf_op jit(solution)/shard_map/all_gather | solution.py:220
  45.9 6.6 %all-to-all-start.1 = ((f32[16,24,128]{2,1,0:T(8,128)}), f32[16,24,128]{2,1,0:T(8,128)S(1)}, u32[]{:S(2)}, u32[]{:S(2)}) async-start(f32[16,24,128]{2,1,0:T(8,128)} %bitcast.9), calls=%async_computation.1 | async-start | bytes 393216 | tf_op jit(solution)/shard_map/all_to_all | solution.py:238
  52.6 2.4 %collective-permute-start.1 = (bf16[2048,128]{1,0:T(8,128)(2,1)S(1)}, bf16[2048,128]{1,0:T(8,128)(2,1)S(1)}, u32[]{:S(2)}, u32[]{:S(2)}) collective-permute-start(bf16[2048,128]{1,0:T(8,128)(2,1)S(1)} %all_gather.6.refs_0_), channel_id=1, source_target_pairs={{0,128},{128,256},{256,384},{384,0},{1,129},{129,257},{257,385},{3... | collective-permute-start | bytes 1572872 | tf_op jit(solution)/shard_map/ppermute | solution.py:201
  55.0 3.5 %collective-permute-start.2 = (bf16[2048,128]{1,0:T(8,128)(2,1)S(1)}, bf16[2048,128]{1,0:T(8,128)(2,1)S(1)}, u32[]{:S(2)}, u32[]{:S(2)}) collective-permute-start(bf16[2048,128]{1,0:T(8,128)(2,1)S(1)} %all_gather.6.refs_0_), channel_id=1, source_target_pairs={{0,384},{128,0},{256,128},{384,256},{1,385},{129,1},{257,129},{385... | collective-permute-start | bytes 1572872 | tf_op jit(solution)/shard_map/ppermute | solution.py:201
  58.4 4.0 %all-to-all-done.1 = f32[16,24,128]{2,1,0:T(8,128)S(1)} async-done(((f32[16,24,128]{2,1,0:T(8,128)}), f32[16,24,128]{2,1,0:T(8,128)S(1)}, u32[]{:S(2)}, u32[]{:S(2)}) %all-to-all-start.1) | async-done | bytes 196640 | tf_op jit(solution)/shard_map/all_to_all | solution.py:238
  62.7 5.9 %collective-permute-done.1.refs_1_ = bf16[2048,128]{1,0:T(8,128)(2,1)S(1)} collective-permute-done((bf16[2048,128]{1,0:T(8,128)(2,1)S(1)}, bf16[2048,128]{1,0:T(8,128)(2,1)S(1)}, u32[]{:S(2)}, u32[]{:S(2)}) %collective-permute-start.1) | collective-permute-done | bytes 524320 | tf_op jit(solution)/shard_map/ppermute | solution.py:201
  68.7 3.3 %collective-permute-done.2.refs_3_ = bf16[2048,128]{1,0:T(8,128)(2,1)S(1)} collective-permute-done((bf16[2048,128]{1,0:T(8,128)(2,1)S(1)}, bf16[2048,128]{1,0:T(8,128)(2,1)S(1)}, u32[]{:S(2)}, u32[]{:S(2)}) %collective-permute-start.2) | collective-permute-done | bytes 524320 | tf_op jit(solution)/shard_map/ppermute | solution.py:201
  72.8 10.8 %all-to-all-start.2 = ((bf16[64,24,128]{2,1,0:T(8,128)(2,1)}), bf16[64,24,128]{2,1,0:T(8,128)(2,1)S(1)}, u32[]{:S(2)}, u32[]{:S(2)}) async-start(bf16[64,24,128]{2,1,0:T(8,128)(2,1)} %broadcast_in_dim.2), calls=%async_computation.2 | async-start | bytes 786432 | tf_op jit(solution)/shard_map/all_to_all | solution.py:40
  83.7 2.2 %collective-permute-start.3 = (bf16[1024,128]{1,0:T(8,128)(2,1)S(1)}, bf16[1024,128]{1,0:T(8,128)(2,1)S(1)}, u32[]{:S(2)}, u32[]{:S(2)}) collective-permute-start(bf16[1024,128]{1,0:T(8,128)(2,1)S(1)} %slice.54), channel_id=1, source_target_pairs={{0,128},{128,256},{256,384},{384,0},{1,129},{129,257},{257,385},{3... | collective-permute-start | bytes 786440 | tf_op jit(solution)/shard_map/ppermute | solution.py:201
  85.9 3.7 %collective-permute-start.4 = (bf16[1024,128]{1,0:T(8,128)(2,1)S(1)}, bf16[1024,128]{1,0:T(8,128)(2,1)}, u32[]{:S(2)}, u32[]{:S(2)}) collective-permute-start(bf16[1024,128]{1,0:T(8,128)(2,1)S(1)} %slice.55), channel_id=1, source_target_pairs={{0,384},{128,0},{256,128},{384,256},{1,385},{129,1},{257,129},{385... | collective-permute-start | bytes 786440 | tf_op jit(solution)/shard_map/ppermute | solution.py:201
  89.6 3.0 %collective-permute-done.3 = bf16[1024,128]{1,0:T(8,128)(2,1)S(1)} collective-permute-done((bf16[1024,128]{1,0:T(8,128)(2,1)S(1)}, bf16[1024,128]{1,0:T(8,128)(2,1)S(1)}, u32[]{:S(2)}, u32[]{:S(2)}) %collective-permute-start.3) | collective-permute-done | bytes 262176 | tf_op jit(solution)/shard_map/ppermute | solution.py:201
  92.6 3.3 %collective-permute-done.4 = bf16[1024,128]{1,0:T(8,128)(2,1)} collective-permute-done((bf16[1024,128]{1,0:T(8,128)(2,1)S(1)}, bf16[1024,128]{1,0:T(8,128)(2,1)}, u32[]{:S(2)}, u32[]{:S(2)}) %collective-permute-start.4) | collective-permute-done | bytes 262176 | tf_op jit(solution)/shard_map/ppermute | solution.py:201
  95.9 4.2 %all-to-all-done.2 = bf16[64,24,128]{2,1,0:T(8,128)(2,1)S(1)} async-done(((bf16[64,24,128]{2,1,0:T(8,128)(2,1)}), bf16[64,24,128]{2,1,0:T(8,128)(2,1)S(1)}, u32[]{:S(2)}, u32[]{:S(2)}) %all-to-all-start.2) | async-done | bytes 393248 | tf_op jit(solution)/shard_map/all_to_all | solution.py:40
  101.4 1.3 collective-permute-start.6
  106.2 6.1 %project.1 = f32[2,192,128]{2,1,0:T(8,128)S(1)} custom-call(s32[3]{0:T(128)S(1)} %pad_add_fusion.info_ref, bf16[384,8192]{1,0:T(8,128)(2,1)} %all-gather.2.cloned.1.call-done.h_ref, bf16[2048,128]{1,0:T(8,128)(2,1)S(1)} %all_gather.6.refs_0_, bf16[2048,128]{1,0:T(8,128)(2,1)S(1)} %collective-permute-done.1.refs_1_, ...), custom_call_target="tpu_custom_call" | custom-call | flops 805306368 | bytes 8388608 | tf_op jit(solution)/shard_map/project/pallas_call | solution.py:158
  112.7 7.8 %collective-permute-done.7.refs_3_ = bf16[1536,128]{1,0:T(8,128)(2,1)S(1)} collective-permute-done((bf16[1536,128]{1,0:T(8,128)(2,1)S(1)}, bf16[1536,128]{1,0:T(8,128)(2,1)S(1)}, u32[]{:S(2)}, u32[]{:S(2)}) %collective-permute-start.7) | collective-permute-done | bytes 393248 | tf_op jit(solution)/shard_map/ppermute | solution.py:206
  120.6 1.9 %collective-permute-start.10 = (bf16[4608,128]{1,0:T(8,128)(2,1)S(1)}, bf16[4608,128]{1,0:T(8,128)(2,1)S(1)}, u32[]{:S(2)}, u32[]{:S(2)}) collective-permute-start(bf16[4608,128]{1,0:T(8,128)(2,1)S(1)} %pad_maximum_fusion), channel_id=1, source_target_pairs={{0,1},{1,0},{2,3},{3,2},{4,5},{5,4},{6,7},{7,6},{8,9},{9,8},{10,11... | collective-permute-start | bytes 3538952 | tf_op jit(solution)/shard_map/ppermute | solution.py:210
  122.9 2.4 %collective-permute-start.9 = (bf16[1536,128]{1,0:T(8,128)(2,1)S(1)}, bf16[1536,128]{1,0:T(8,128)(2,1)S(1)}, u32[]{:S(2)}, u32[]{:S(2)}) collective-permute-start(bf16[1536,128]{1,0:T(8,128)(2,1)S(1)} %bitcast.28), channel_id=1, source_target_pairs={{0,1},{1,0},{2,3},{3,2},{4,5},{5,4},{6,7},{7,6},{8,9},{9,8},{10,11... | collective-permute-start | bytes 1179656 | tf_op jit(solution)/shard_map/ppermute | solution.py:210
  125.4 6.0 %collective-permute-start.8 = (f32[192,128]{1,0:T(8,128)S(1)}, f32[192,128]{1,0:T(8,128)S(1)}, u32[]{:S(2)}, u32[]{:S(2)}) collective-permute-start(f32[192,128]{1,0:T(8,128)S(1)} %select_bitcast_fusion), channel_id=1, source_target_pairs={{0,64},{64,0},{1,65},{65,1},{2,66},{66,2},{3,67},{67,3},{4,68},{68... | collective-permute-start | bytes 294920 | tf_op jit(solution)/shard_map/ppermute | solution.py:210
  131.5 4.5 %collective-permute-done.8 = f32[192,128]{1,0:T(8,128)S(1)} collective-permute-done((f32[192,128]{1,0:T(8,128)S(1)}, f32[192,128]{1,0:T(8,128)S(1)}, u32[]{:S(2)}, u32[]{:S(2)}) %collective-permute-start.8) | collective-permute-done | bytes 98336 | tf_op jit(solution)/shard_map/ppermute | solution.py:210
  136.0 6.6 %attend.1 = bf16[192,128]{1,0:T(8,128)(2,1)} custom-call(s32[3]{0:T(128)S(1)} %pad_add_fusion.info_ref, f32[192,128]{1,0:T(8,128)S(1)} %bitcast_add_fusion.q_ref, f32[192,128]{1,0:T(8,128)S(1)} %get-tuple-element.50.cos_ref, f32[192,128]{1,0:T(8,128)S(1)} %get-tuple-element.51.sin_ref, bf16[1536,128]{1,0:T(8,128)(2,1)S(1)} %bitcast.29, ...), custom_call_target="tpu_custom_call" | custom-call | flops 603979776 | bytes 3145728 | tf_op jit(solution)/shard_map/attend/pallas_call | solution.py:178
  (45 shorter events, 10.4 us)
Async XLA Ops:
  6.5 2.5 %copy-start.2 = (bf16[12,16384]{1,0:T(8,128)(2,1)S(1)}, bf16[12,16384]{1,0:T(8,128)(2,1)}, u32[]{:S(2)}) copy-start(bf16[12,16384]{1,0:T(8,128)(2,1)} %param.3) | copy-start | bytes 1179652
  7.9 19.5 %copy-start.3 = (bf16[1024,256]{1,0:T(8,128)(2,1)S(1)}, bf16[1024,256]{1,0:T(8,128)(2,1)}, u32[]{:S(2)}) copy-start(bf16[1024,256]{1,0:T(8,128)(2,1)} %param.5) | copy-start | bytes 1572868
  8.0 19.7 %copy-start.4 = (bf16[512,128]{1,0:T(8,128)(2,1)S(1)}, bf16[512,128]{1,0:T(8,128)(2,1)}, u32[]{:S(2)}) copy-start(bf16[512,128]{1,0:T(8,128)(2,1)} %param.4) | copy-start | bytes 393220
  9.2 34.6 %collective-permute-start = (bf16[12,8192]{1,0:T(8,128)(2,1)S(1)}, bf16[12,8192]{1,0:T(8,128)(2,1)S(1)}, u32[]{:S(2)}, u32[]{:S(2)}) collective-permute-start(bf16[12,8192]{1,0:T(8,128)(2,1)S(1)} %get-tuple-element.36), channel_id=1, source_target_pairs={{0,64},{64,0},{1,65},{65,1},{2,66},{66,2},{3,67},{67,3},{4,68},{68... | collective-permute-start | bytes 589832 | tf_op jit(solution)/shard_map/ppermute | solution.py:210
  17.0 27.8 %all-to-all-start = ((bf16[16,12,1024]{2,1,0:T(8,128)(2,1)}), bf16[16,12,1024]{2,1,0:T(8,128)(2,1)S(1)}, u32[]{:S(2)}, u32[]{:S(2)}) async-start(bf16[16,12,1024]{2,1,0:T(8,128)(2,1)} %bitcast.24), calls=%async_computation | async-start | bytes 1048576 | tf_op jit(solution)/shard_map/all_to_all | solution.py:224
  27.4 77.7 %all-gather.2.cloned.1.call-start = ((), (), s32[]{:S(2)}) async-start(), calls=%async_computation.3 | async-start | bytes 6684672 | tf_op jit(solution)/shard_map/all_gather | solution.py:236
  45.9 16.5 %all-to-all-start.1 = ((f32[16,24,128]{2,1,0:T(8,128)}), f32[16,24,128]{2,1,0:T(8,128)S(1)}, u32[]{:S(2)}, u32[]{:S(2)}) async-start(f32[16,24,128]{2,1,0:T(8,128)} %bitcast.9), calls=%async_computation.1 | async-start | bytes 393216 | tf_op jit(solution)/shard_map/all_to_all | solution.py:238
  52.6 16.1 %collective-permute-start.1 = (bf16[2048,128]{1,0:T(8,128)(2,1)S(1)}, bf16[2048,128]{1,0:T(8,128)(2,1)S(1)}, u32[]{:S(2)}, u32[]{:S(2)}) collective-permute-start(bf16[2048,128]{1,0:T(8,128)(2,1)S(1)} %all_gather.6.refs_0_), channel_id=1, source_target_pairs={{0,128},{128,256},{256,384},{384,0},{1,129},{129,257},{257,385},{3... | collective-permute-start | bytes 1572872 | tf_op jit(solution)/shard_map/ppermute | solution.py:201
  55.0 17.0 %collective-permute-start.2 = (bf16[2048,128]{1,0:T(8,128)(2,1)S(1)}, bf16[2048,128]{1,0:T(8,128)(2,1)S(1)}, u32[]{:S(2)}, u32[]{:S(2)}) collective-permute-start(bf16[2048,128]{1,0:T(8,128)(2,1)S(1)} %all_gather.6.refs_0_), channel_id=1, source_target_pairs={{0,384},{128,0},{256,128},{384,256},{1,385},{129,1},{257,129},{385... | collective-permute-start | bytes 1572872 | tf_op jit(solution)/shard_map/ppermute | solution.py:201
  72.0 32.1 %copy-start = (bf16[2048,128]{1,0:T(8,128)(2,1)}, bf16[2048,128]{1,0:T(8,128)(2,1)S(1)}, u32[]{:S(2)}) copy-start(bf16[2048,128]{1,0:T(8,128)(2,1)S(1)} %collective-permute-done.2.refs_3_) | copy-start | bytes 1572868
  72.8 27.3 %all-to-all-start.2 = ((bf16[64,24,128]{2,1,0:T(8,128)(2,1)}), bf16[64,24,128]{2,1,0:T(8,128)(2,1)S(1)}, u32[]{:S(2)}, u32[]{:S(2)}) async-start(bf16[64,24,128]{2,1,0:T(8,128)(2,1)} %broadcast_in_dim.2), calls=%async_computation.2 | async-start | bytes 786432 | tf_op jit(solution)/shard_map/all_to_all | solution.py:40
  83.7 8.9 %collective-permute-start.3 = (bf16[1024,128]{1,0:T(8,128)(2,1)S(1)}, bf16[1024,128]{1,0:T(8,128)(2,1)S(1)}, u32[]{:S(2)}, u32[]{:S(2)}) collective-permute-start(bf16[1024,128]{1,0:T(8,128)(2,1)S(1)} %slice.54), channel_id=1, source_target_pairs={{0,128},{128,256},{256,384},{384,0},{1,129},{129,257},{257,385},{3... | collective-permute-start | bytes 786440 | tf_op jit(solution)/shard_map/ppermute | solution.py:201
  85.9 10.0 %collective-permute-start.4 = (bf16[1024,128]{1,0:T(8,128)(2,1)S(1)}, bf16[1024,128]{1,0:T(8,128)(2,1)}, u32[]{:S(2)}, u32[]{:S(2)}) collective-permute-start(bf16[1024,128]{1,0:T(8,128)(2,1)S(1)} %slice.55), channel_id=1, source_target_pairs={{0,384},{128,0},{256,128},{384,256},{1,385},{129,1},{257,129},{385... | collective-permute-start | bytes 786440 | tf_op jit(solution)/shard_map/ppermute | solution.py:201
  100.2 12.1 %collective-permute-start.5 = (bf16[1536,128]{1,0:T(8,128)(2,1)S(1)}, bf16[1536,128]{1,0:T(8,128)(2,1)S(1)}, u32[]{:S(2)}, u32[]{:S(2)}) collective-permute-start(bf16[1536,128]{1,0:T(8,128)(2,1)S(1)} %bitcast.25), channel_id=1, source_target_pairs={{0,128},{128,256},{256,384},{1,129},{129,257},{257,385},{2,130},{1... | collective-permute-start | bytes 1179656 | tf_op jit(solution)/shard_map/ppermute | solution.py:206
  101.4 11.2 %collective-permute-start.6 = (bf16[1536,128]{1,0:T(8,128)(2,1)S(1)}, bf16[1536,128]{1,0:T(8,128)(2,1)S(1)}, u32[]{:S(2)}, u32[]{:S(2)}) collective-permute-start(bf16[1536,128]{1,0:T(8,128)(2,1)S(1)} %bitcast.26), channel_id=1, source_target_pairs={{0,256},{128,384},{1,257},{129,385},{2,258},{130,386},{3,259},{131... | collective-permute-start | bytes 1179656 | tf_op jit(solution)/shard_map/ppermute | solution.py:206
  102.7 17.8 %collective-permute-start.7 = (bf16[1536,128]{1,0:T(8,128)(2,1)S(1)}, bf16[1536,128]{1,0:T(8,128)(2,1)S(1)}, u32[]{:S(2)}, u32[]{:S(2)}) collective-permute-start(bf16[1536,128]{1,0:T(8,128)(2,1)S(1)} %bitcast.27), channel_id=1, source_target_pairs={{0,384},{1,385},{2,386},{3,387},{4,388},{5,389},{6,390},{7,391},{8... | collective-permute-start | bytes 1179656 | tf_op jit(solution)/shard_map/ppermute | solution.py:206
  105.1 1.0 copy-start.1
  120.6 15.5 %collective-permute-start.10 = (bf16[4608,128]{1,0:T(8,128)(2,1)S(1)}, bf16[4608,128]{1,0:T(8,128)(2,1)S(1)}, u32[]{:S(2)}, u32[]{:S(2)}) collective-permute-start(bf16[4608,128]{1,0:T(8,128)(2,1)S(1)} %pad_maximum_fusion), channel_id=1, source_target_pairs={{0,1},{1,0},{2,3},{3,2},{4,5},{5,4},{6,7},{7,6},{8,9},{9,8},{10,11... | collective-permute-start | bytes 3538952 | tf_op jit(solution)/shard_map/ppermute | solution.py:210
  122.9 13.1 %collective-permute-start.9 = (bf16[1536,128]{1,0:T(8,128)(2,1)S(1)}, bf16[1536,128]{1,0:T(8,128)(2,1)S(1)}, u32[]{:S(2)}, u32[]{:S(2)}) collective-permute-start(bf16[1536,128]{1,0:T(8,128)(2,1)S(1)} %bitcast.28), channel_id=1, source_target_pairs={{0,1},{1,0},{2,3},{3,2},{4,5},{5,4},{6,7},{7,6},{8,9},{9,8},{10,11... | collective-permute-start | bytes 1179656 | tf_op jit(solution)/shard_map/ppermute | solution.py:210
  125.4 10.6 %collective-permute-start.8 = (f32[192,128]{1,0:T(8,128)S(1)}, f32[192,128]{1,0:T(8,128)S(1)}, u32[]{:S(2)}, u32[]{:S(2)}) collective-permute-start(f32[192,128]{1,0:T(8,128)S(1)} %select_bitcast_fusion), channel_id=1, source_target_pairs={{0,64},{64,0},{1,65},{65,1},{2,66},{66,2},{3,67},{67,3},{4,68},{68... | collective-permute-start | bytes 294920 | tf_op jit(solution)/shard_map/ppermute | solution.py:210
Sparse Core Ops, SparseCore 0:
  46.1 56.4 all-gather.1

commit v2 on v1

--- a/solution.py
+++ b/solution.py
@@ -12,7 +12,6 @@
 CTX = ("x", "yh", "yl")
 TP = ("z", "core")
 AXES = CTX + TP
-KEY_TILE = 768
 
 
 def fine_mesh(mesh):
@@ -73,8 +72,6 @@
     rows = q_ref.shape[0]
     x, y, core = info_ref[0], info_ref[1], info_ref[2]
     size = near_ref.shape[0]
-    own = (y * rows) // KEY_TILE
-    full = own + x * (size // KEY_TILE)
 
     def copies(i):
         other = near_ref if i == 0 else far_ref.at[pl.ds((i - 1) * size, size)]
@@ -94,11 +91,6 @@
     q = sums * cos_ref[...] + pltpu.roll(sums, HD // 2, 1) * sin_ref[...]
     q = q.astype(jnp.bfloat16)
 
-    def where(j):
-        back = jnp.where(j < own, 0, (j - own) // (size // KEY_TILE) + 1)
-        first = jnp.where(j < own, 0, lax.rem(j - own, size // KEY_TILE)) * KEY_TILE
-        return back, pl.ds(pl.multiple_of(first, KEY_TILE), KEY_TILE)
-
     def lanes(v, op):
         out = v[:, :HD]
         for i in range(1, v.shape[1] // HD):
@@ -112,12 +104,11 @@
 
     for copy in copies(0):
         copy.wait()
-    at = pl.multiple_of(own * KEY_TILE, KEY_TILE)
-    s = scores(buf[0, 0, pl.ds(at, KEY_TILE), :])
+    s = scores(buf[0, 0])
     qp = y * rows + lax.broadcasted_iota(jnp.int32, s.shape, 0)
-    kp = at + lax.broadcasted_iota(jnp.int32, s.shape, 1)
+    kp = lax.broadcasted_iota(jnp.int32, s.shape, 1)
     s = jnp.where(qp >= kp, s, -jnp.inf)
-    s_ref[full] = s
+    s_ref[0] = s
     top = lanes(s, jnp.maximum)
     for i in range(1, 4):
 
@@ -126,29 +117,24 @@
             for copy in copies(i):
                 copy.wait()
 
-    def first_pass(j, top):
-        back, at = where(j)
-        s = scores(buf[back, 0, at, :])
-        s_ref[j] = s
+    def first_pass(i, top):
+        s = scores(buf[i, 0])
+        s_ref[i] = s
         return jnp.maximum(top, lanes(s, jnp.maximum))
 
-    top = jnp.max(lax.fori_loop(0, full, first_pass, top), axis=1, keepdims=True)
+    top = lax.fori_loop(1, x + 1, first_pass, top)
+    top = jnp.max(top, axis=1, keepdims=True)
     scale = HD**-0.5 * math.log2(math.e)
 
-    def weigh(s, v, state):
+    def second_pass(i, state):
         tot, acc = state
-        e = jnp.exp2((s - top) * scale)
+        e = jnp.exp2((s_ref[i] - top) * scale)
         return tot + lanes(e, jnp.add), acc + jnp.dot(
-            e.astype(jnp.bfloat16), v, preferred_element_type=jnp.float32
+            e.astype(jnp.bfloat16), buf[i, 1], preferred_element_type=jnp.float32
         )
 
-    def second_pass(j, state):
-        back, at = where(j)
-        return weigh(s_ref[j], buf[back, 1, at, :], state)
-
     zero = jnp.zeros((rows, HD), jnp.float32)
-    state = weigh(s_ref[full], buf[0, 1, pl.ds(at, KEY_TILE), :], (zero, zero))
-    tot, acc = lax.fori_loop(0, full, second_pass, state)
+    tot, acc = lax.fori_loop(0, x + 1, second_pass, (zero, zero))
     o_ref[...] = (acc / jnp.sum(tot, axis=1, keepdims=True)).astype(o_ref.dtype)
 
 
@@ -183,7 +169,7 @@
         out_shape=jax.ShapeDtypeStruct(sums.shape, jnp.bfloat16),
         scratch_shapes=[
             pltpu.VMEM((4, 2, 1536, HD), jnp.bfloat16),
-            pltpu.VMEM((6144 // KEY_TILE, 192, KEY_TILE), jnp.float32),
+            pltpu.VMEM((4, 192, 1536), jnp.float32),
             pltpu.SemaphoreType.DMA((4, 2)),
         ],
         compiler_params=pltpu.CompilerParams(vmem_limit_bytes=40 * 2**20),
@@ -232,7 +218,7 @@
     )
     part = jnp.dot(hs, kv_weight, preferred_element_type=jnp.float32)
     part = part.reshape(8, 24, 2, HD).transpose(0, 2, 1, 3).reshape(16, 24, HD)
-    h, w, part = tie((h, w, part))
+    h, w, _ = tie((h, w, part))
     h = lax.all_gather(h, TP, axis=0, tiled=True)
 
     part = lax.all_to_all(part, TP, 0, 0, tiled=True)
@@ -240,17 +226,16 @@
     rows = jnp.sum(part, axis=0)
     cosine, sine = angles_of(base + z * 24 + jnp.arange(24, dtype=jnp.int32))
     rows = jnp.where(core == 0, rotate(rows, cosine, sine), rows).astype(jnp.bfloat16)
+    rows = broadcast_gather(rows, ("yh", "yl", "z")).reshape(1536, HD)
     rows, up, down = tie((rows, up, down))
-    rows = broadcast_gather(rows, ("yh", "yl", "z")).reshape(1536, HD)
     cross = [shift(up[:1024], "x", 1), shift(down[1024:], "x", -1)]
-    rows, cross = tie((rows, cross))
     mine = [rows] + [shift_up(rows, "x", d) for d in (1, 2, 3)]
 
     sums = project(info, h, (w, up, jnp.concatenate(cross, axis=0), down))
-    come, sums = tie((mine[1:], sums))
-    other = [swap(rows, "core"), swap(jnp.concatenate(come, axis=0), "core")]
     keep = jnp.where(yh == 0, sums[0], sums[1])
     come = swap(jnp.where(yh == 0, sums[1], sums[0]), "yh")
+    away, come = tie((mine[1:], come))
+    other = [swap(rows, "core"), swap(jnp.concatenate(away, axis=0), "core")]
     cosine, sine = angles_of(base + jnp.arange(192, dtype=jnp.int32))
     cosine = jnp.concatenate([cosine, cosine], axis=1)
     sine = jnp.concatenate([-sine, sine], axis=1)

time: 152 us -> 148 us (0.974)
  starting transfers between devices: 61.5 us -> 58.7 us
    ppermute x3, waiting for transfers between devices: 8.21 us -> 0.01 us  [shift_up(): return lax.ppermute(v, axis, [(i, i + by) for i in range(n - by)])]
    ppermute x4, waiting for transfers between devices: 15.6 us -> 23.7 us  [shift(): return lax.ppermute(v, axis, [(i, (i + by) % n) for i in range(n)])]
    all_to_all x1, waiting for transfers between devices: 4.03 us -> 9.91 us  [body(): part = lax.all_to_all(part, TP, 0, 0, tiled=True)]
    all_to_all x1, waiting for transfers between devices: 4.24 us -> 0.01 us  [broadcast_gather(): lax.all_to_all(jnp.broadcast_to(x[None], (n,) + x.shape), axis, 0, 0, til...]
    all_to_all x1, starting transfers between devices: 10.8 us -> 7.11 us  [broadcast_gather(): lax.all_to_all(jnp.broadcast_to(x[None], (n,) + x.shape), axis, 0, 0, til...]
  transfers between devices with their start and end apart: 15 -> 15, of which waited for: 9 -> 6; matrix products, arithmetic and copies ran while one was open for 3% -> 2% of each run, Pallas kernels for 4% -> 4%
where the time goes in v2:
time: 148 us; the launch traced here: 146 us
  starting transfers between devices  58.7 us (40%)
  waiting for transfers between devices  38 us (26%)
  blocking collectives  16.2 us (11%)
  between operations  13.8 us (9%)
  Pallas kernels  11.8 us (8%)
  local copies, waits for them, and re-layouts  4.71 us (3%)
  other arithmetic  2.08 us (1%)
    ppermute x4, waiting for transfers between devices, shift(): return lax.ppermute(v, axis, [(i, (i + by) % n) for i in range(n)])  23.7 us
    ppermute x4, starting transfers between devices, swap(): return lax.ppermute(v, axis, [(0, 1), (1, 0)])  19 us
    all_gather x1, blocking collectives, body(): w = lax.all_gather(query_weight, 'yl', axis=0, tiled=True)  16.2 us
    ppermute x4, starting transfers between devices, shift(): return lax.ppermute(v, axis, [(i, (i + by) % n) for i in range(n)])  11.7 us
    all_to_all x1, starting transfers between devices, body(): hs = lax.all_to_all(hs, TP, 0, 0, tiled=True).reshape(192, 1024)  10.4 us
    all_to_all x1, waiting for transfers between devices, body(): part = lax.all_to_all(part, TP, 0, 0, tiled=True)  9.91 us
    all_to_all x1, starting transfers between devices, broadcast_gather(): lax.all_to_all(jnp.broadcast_to(x[None], (n,) + x.shape), axis, 0, 0, til...  7.11 us
    all_to_all x1, starting transfers between devices, body(): part = lax.all_to_all(part, TP, 0, 0, tiled=True)  6.58 us
  transfers between devices with their start and end apart: 15, of which 6 were waited for; matrix products, arithmetic and copies ran while one was open for 2% of the time, Pallas kernels for 4%

profile of v2, /device:TPU:6, one launch (start us, length us, event | category | flops | bytes accessed | tf_op | source)
XLA Modules:
  0.0 146.3 jit_solution(12051065082246452600)
XLA Ops:
  6.5 1.4 copy.10
  8.0 1.0 copy.12
  9.2 7.7 %collective-permute-start = (bf16[12,8192]{1,0:T(8,128)(2,1)S(1)}, bf16[12,8192]{1,0:T(8,128)(2,1)S(1)}, u32[]{:S(2)}, u32[]{:S(2)}) collective-permute-start(bf16[12,8192]{1,0:T(8,128)(2,1)S(1)} %get-tuple-element.28), channel_id=1, source_target_pairs={{0,64},{64,0},{1,65},{65,1},{2,66},{66,2},{3,67},{67,3},{4,68},{68... | collective-permute-start | bytes 589832 | tf_op jit(solution)/shard_map/ppermute | solution.py:196
  17.0 10.4 %all-to-all-start = ((bf16[16,12,1024]{2,1,0:T(8,128)(2,1)}), bf16[16,12,1024]{2,1,0:T(8,128)(2,1)S(1)}, u32[]{:S(2)}, u32[]{:S(2)}) async-start(bf16[16,12,1024]{2,1,0:T(8,128)(2,1)} %bitcast.24), calls=%async_computation | async-start | bytes 1048576 | tf_op jit(solution)/shard_map/all_to_all | solution.py:210
  27.7 16.2 %all_gather.6.refs_0_ = bf16[2048,128]{1,0:T(8,128)(2,1)S(1)} all-gather(bf16[512,128]{1,0:T(8,128)(2,1)S(1)} %copy-done.4), channel_id=1, replica_groups=mesh['x'=4,'yh'=2,'yl'=4,'z'=8,'core'=2] {'yl'}, dimensions={0}, use_global_device_ids=true | all-gather | bytes 655360 | tf_op jit(solution)/shard_map/all_gather | solution.py:206
  45.9 6.6 %all-to-all-start.1 = ((f32[16,24,128]{2,1,0:T(8,128)}), f32[16,24,128]{2,1,0:T(8,128)S(1)}, u32[]{:S(2)}, u32[]{:S(2)}) async-start(f32[16,24,128]{2,1,0:T(8,128)} %bitcast.9), calls=%async_computation.1 | async-start | bytes 393216 | tf_op jit(solution)/shard_map/all_to_all | solution.py:224
  52.6 9.9 %all-to-all-done.1 = f32[16,24,128]{2,1,0:T(8,128)S(1)} async-done(((f32[16,24,128]{2,1,0:T(8,128)}), f32[16,24,128]{2,1,0:T(8,128)S(1)}, u32[]{:S(2)}, u32[]{:S(2)}) %all-to-all-start.1) | async-done | bytes 196640 | tf_op jit(solution)/shard_map/all_to_all | solution.py:224
  63.5 7.1 %all-to-all-start.2 = ((bf16[64,24,128]{2,1,0:T(8,128)(2,1)}), bf16[64,24,128]{2,1,0:T(8,128)(2,1)S(1)}, u32[]{:S(2)}, u32[]{:S(2)}) async-start(bf16[64,24,128]{2,1,0:T(8,128)(2,1)} %broadcast_in_dim.2), calls=%async_computation.2 | async-start | bytes 786432 | tf_op jit(solution)/shard_map/all_to_all | solution.py:39
  70.6 2.4 %collective-permute-start.1 = (bf16[2048,128]{1,0:T(8,128)(2,1)S(1)}, bf16[2048,128]{1,0:T(8,128)(2,1)S(1)}, u32[]{:S(2)}, u32[]{:S(2)}) collective-permute-start(bf16[2048,128]{1,0:T(8,128)(2,1)S(1)} %all_gather.6.refs_0_), channel_id=1, source_target_pairs={{0,128},{128,256},{256,384},{384,0},{1,129},{129,257},{257,385},{3... | collective-permute-start | bytes 1572872 | tf_op jit(solution)/shard_map/ppermute | solution.py:187
  73.0 3.5 %collective-permute-start.2 = (bf16[2048,128]{1,0:T(8,128)(2,1)S(1)}, bf16[2048,128]{1,0:T(8,128)(2,1)S(1)}, u32[]{:S(2)}, u32[]{:S(2)}) collective-permute-start(bf16[2048,128]{1,0:T(8,128)(2,1)S(1)} %all_gather.6.refs_0_), channel_id=1, source_target_pairs={{0,384},{128,0},{256,128},{384,256},{1,385},{129,1},{257,129},{385... | collective-permute-start | bytes 1572872 | tf_op jit(solution)/shard_map/ppermute | solution.py:187
  76.5 9.7 %collective-permute-done.1.refs_1_ = bf16[2048,128]{1,0:T(8,128)(2,1)S(1)} collective-permute-done((bf16[2048,128]{1,0:T(8,128)(2,1)S(1)}, bf16[2048,128]{1,0:T(8,128)(2,1)S(1)}, u32[]{:S(2)}, u32[]{:S(2)}) %collective-permute-start.1) | collective-permute-done | bytes 524320 | tf_op jit(solution)/shard_map/ppermute | solution.py:187
  86.2 3.3 %collective-permute-done.2.refs_3_ = bf16[2048,128]{1,0:T(8,128)(2,1)S(1)} collective-permute-done((bf16[2048,128]{1,0:T(8,128)(2,1)S(1)}, bf16[2048,128]{1,0:T(8,128)(2,1)S(1)}, u32[]{:S(2)}, u32[]{:S(2)}) %collective-permute-start.2) | collective-permute-done | bytes 524320 | tf_op jit(solution)/shard_map/ppermute | solution.py:187
  89.6 2.2 %collective-permute-start.3 = (bf16[1024,128]{1,0:T(8,128)(2,1)S(1)}, bf16[1024,128]{1,0:T(8,128)(2,1)S(1)}, u32[]{:S(2)}, u32[]{:S(2)}) collective-permute-start(bf16[1024,128]{1,0:T(8,128)(2,1)S(1)} %slice.54), channel_id=1, source_target_pairs={{0,128},{128,256},{256,384},{384,0},{1,129},{129,257},{257,385},{3... | collective-permute-start | bytes 786440 | tf_op jit(solution)/shard_map/ppermute | solution.py:187
  91.8 3.7 %collective-permute-start.4 = (bf16[1024,128]{1,0:T(8,128)(2,1)S(1)}, bf16[1024,128]{1,0:T(8,128)(2,1)S(1)}, u32[]{:S(2)}, u32[]{:S(2)}) collective-permute-start(bf16[1024,128]{1,0:T(8,128)(2,1)S(1)} %slice.55), channel_id=1, source_target_pairs={{0,384},{128,0},{256,128},{384,256},{1,385},{129,1},{257,129},{385... | collective-permute-start | bytes 786440 | tf_op jit(solution)/shard_map/ppermute | solution.py:187
  95.5 1.3 collective-permute-start.5
  96.8 1.3 collective-permute-start.6
  98.1 1.3 collective-permute-start.7
  99.4 10.7 %collective-permute-done.4 = bf16[1024,128]{1,0:T(8,128)(2,1)S(1)} collective-permute-done((bf16[1024,128]{1,0:T(8,128)(2,1)S(1)}, bf16[1024,128]{1,0:T(8,128)(2,1)S(1)}, u32[]{:S(2)}, u32[]{:S(2)}) %collective-permute-start.4) | collective-permute-done | bytes 262176 | tf_op jit(solution)/shard_map/ppermute | solution.py:187
  111.2 6.1 %project.1 = f32[2,192,128]{2,1,0:T(8,128)S(1)} custom-call(s32[3]{0:T(128)S(1)} %pad_add_fusion.info_ref, bf16[384,8192]{1,0:T(8,128)(2,1)} %all-gather.2.cloned.1.call-done.h_ref, bf16[2048,128]{1,0:T(8,128)(2,1)S(1)} %all_gather.6.refs_0_, bf16[2048,128]{1,0:T(8,128)(2,1)S(1)} %collective-permute-done.1.refs_1_, ...), custom_call_target="tpu_custom_call" | custom-call | flops 805306368 | bytes 8388608 | tf_op jit(solution)/shard_map/project/pallas_call | solution.py:144
  117.3 6.9 %collective-permute-start.8 = (f32[192,128]{1,0:T(8,128)S(1)}, f32[192,128]{1,0:T(8,128)S(1)}, u32[]{:S(2)}, u32[]{:S(2)}) collective-permute-start(f32[192,128]{1,0:T(8,128)S(1)} %select_bitcast_fusion), channel_id=1, source_target_pairs={{0,64},{64,0},{1,65},{65,1},{2,66},{66,2},{3,67},{67,3},{4,68},{68... | collective-permute-start | bytes 294920 | tf_op jit(solution)/shard_map/ppermute | solution.py:196
  124.3 3.6 %collective-permute-done.8 = f32[192,128]{1,0:T(8,128)S(1)} collective-permute-done((f32[192,128]{1,0:T(8,128)S(1)}, f32[192,128]{1,0:T(8,128)S(1)}, u32[]{:S(2)}, u32[]{:S(2)}) %collective-permute-start.8) | collective-permute-done | bytes 98336 | tf_op jit(solution)/shard_map/ppermute | solution.py:196
  127.9 1.9 %collective-permute-start.10 = (bf16[4608,128]{1,0:T(8,128)(2,1)S(1)}, bf16[4608,128]{1,0:T(8,128)(2,1)S(1)}, u32[]{:S(2)}, u32[]{:S(2)}) collective-permute-start(bf16[4608,128]{1,0:T(8,128)(2,1)S(1)} %pad_maximum_fusion), channel_id=1, source_target_pairs={{0,1},{1,0},{2,3},{3,2},{4,5},{5,4},{6,7},{7,6},{8,9},{9,8},{10,11... | collective-permute-start | bytes 3538952 | tf_op jit(solution)/shard_map/ppermute | solution.py:196
  129.9 2.4 %collective-permute-start.9 = (bf16[1536,128]{1,0:T(8,128)(2,1)S(1)}, bf16[1536,128]{1,0:T(8,128)(2,1)S(1)}, u32[]{:S(2)}, u32[]{:S(2)}) collective-permute-start(bf16[1536,128]{1,0:T(8,128)(2,1)S(1)} %bitcast.28), channel_id=1, source_target_pairs={{0,1},{1,0},{2,3},{3,2},{4,5},{5,4},{6,7},{7,6},{8,9},{9,8},{10,11... | collective-permute-start | bytes 1179656 | tf_op jit(solution)/shard_map/ppermute | solution.py:196
  133.6 5.8 %attend.1 = bf16[192,128]{1,0:T(8,128)(2,1)} custom-call(s32[3]{0:T(128)S(1)} %pad_add_fusion.info_ref, f32[192,128]{1,0:T(8,128)S(1)} %bitcast_add_fusion.q_ref, f32[192,128]{1,0:T(8,128)S(1)} %get-tuple-element.42.cos_ref, f32[192,128]{1,0:T(8,128)S(1)} %get-tuple-element.43.sin_ref, bf16[1536,128]{1,0:T(8,128)(2,1)S(1)} %bitcast.29, ...), custom_call_target="tpu_custom_call" | custom-call | flops 603979776 | bytes 3145728 | tf_op jit(solution)/shard_map/attend/pallas_call | solution.py:164
  (45 shorter events, 6.2 us)
Async XLA Ops:
  6.5 2.5 %copy-start.2 = (bf16[12,16384]{1,0:T(8,128)(2,1)S(1)}, bf16[12,16384]{1,0:T(8,128)(2,1)}, u32[]{:S(2)}) copy-start(bf16[12,16384]{1,0:T(8,128)(2,1)} %param.3) | copy-start | bytes 1179652
  7.9 19.5 %copy-start.3 = (bf16[1024,256]{1,0:T(8,128)(2,1)S(1)}, bf16[1024,256]{1,0:T(8,128)(2,1)}, u32[]{:S(2)}) copy-start(bf16[1024,256]{1,0:T(8,128)(2,1)} %param.5) | copy-start | bytes 1572868
  8.0 19.7 %copy-start.4 = (bf16[512,128]{1,0:T(8,128)(2,1)S(1)}, bf16[512,128]{1,0:T(8,128)(2,1)}, u32[]{:S(2)}) copy-start(bf16[512,128]{1,0:T(8,128)(2,1)} %param.4) | copy-start | bytes 393220
  9.2 34.6 %collective-permute-start = (bf16[12,8192]{1,0:T(8,128)(2,1)S(1)}, bf16[12,8192]{1,0:T(8,128)(2,1)S(1)}, u32[]{:S(2)}, u32[]{:S(2)}) collective-permute-start(bf16[12,8192]{1,0:T(8,128)(2,1)S(1)} %get-tuple-element.28), channel_id=1, source_target_pairs={{0,64},{64,0},{1,65},{65,1},{2,66},{66,2},{3,67},{67,3},{4,68},{68... | collective-permute-start | bytes 589832 | tf_op jit(solution)/shard_map/ppermute | solution.py:196
  17.0 27.8 %all-to-all-start = ((bf16[16,12,1024]{2,1,0:T(8,128)(2,1)}), bf16[16,12,1024]{2,1,0:T(8,128)(2,1)S(1)}, u32[]{:S(2)}, u32[]{:S(2)}) async-start(bf16[16,12,1024]{2,1,0:T(8,128)(2,1)} %bitcast.24), calls=%async_computation | async-start | bytes 1048576 | tf_op jit(solution)/shard_map/all_to_all | solution.py:210
  27.4 82.8 %all-gather.2.cloned.1.call-start = ((), (), s32[]{:S(2)}) async-start(), calls=%async_computation.3 | async-start | bytes 6684672 | tf_op jit(solution)/shard_map/all_gather | solution.py:222
  45.9 16.5 %all-to-all-start.1 = ((f32[16,24,128]{2,1,0:T(8,128)}), f32[16,24,128]{2,1,0:T(8,128)S(1)}, u32[]{:S(2)}, u32[]{:S(2)}) async-start(f32[16,24,128]{2,1,0:T(8,128)} %bitcast.9), calls=%async_computation.1 | async-start | bytes 393216 | tf_op jit(solution)/shard_map/all_to_all | solution.py:224
  63.5 26.0 %all-to-all-start.2 = ((bf16[64,24,128]{2,1,0:T(8,128)(2,1)}), bf16[64,24,128]{2,1,0:T(8,128)(2,1)S(1)}, u32[]{:S(2)}, u32[]{:S(2)}) async-start(bf16[64,24,128]{2,1,0:T(8,128)(2,1)} %broadcast_in_dim.2), calls=%async_computation.2 | async-start | bytes 786432 | tf_op jit(solution)/shard_map/all_to_all | solution.py:39
  70.6 15.6 %collective-permute-start.1 = (bf16[2048,128]{1,0:T(8,128)(2,1)S(1)}, bf16[2048,128]{1,0:T(8,128)(2,1)S(1)}, u32[]{:S(2)}, u32[]{:S(2)}) collective-permute-start(bf16[2048,128]{1,0:T(8,128)(2,1)S(1)} %all_gather.6.refs_0_), channel_id=1, source_target_pairs={{0,128},{128,256},{256,384},{384,0},{1,129},{129,257},{257,385},{3... | collective-permute-start | bytes 1572872 | tf_op jit(solution)/shard_map/ppermute | solution.py:187
  73.0 16.5 %collective-permute-start.2 = (bf16[2048,128]{1,0:T(8,128)(2,1)S(1)}, bf16[2048,128]{1,0:T(8,128)(2,1)S(1)}, u32[]{:S(2)}, u32[]{:S(2)}) collective-permute-start(bf16[2048,128]{1,0:T(8,128)(2,1)S(1)} %all_gather.6.refs_0_), channel_id=1, source_target_pairs={{0,384},{128,0},{256,128},{384,256},{1,385},{129,1},{257,129},{385... | collective-permute-start | bytes 1572872 | tf_op jit(solution)/shard_map/ppermute | solution.py:187
  89.5 9.9 %copy-start = (bf16[2048,128]{1,0:T(8,128)(2,1)}, bf16[2048,128]{1,0:T(8,128)(2,1)S(1)}, u32[]{:S(2)}) copy-start(bf16[2048,128]{1,0:T(8,128)(2,1)S(1)} %collective-permute-done.2.refs_3_) | copy-start | bytes 1572868
  89.6 9.9 %collective-permute-start.3 = (bf16[1024,128]{1,0:T(8,128)(2,1)S(1)}, bf16[1024,128]{1,0:T(8,128)(2,1)S(1)}, u32[]{:S(2)}, u32[]{:S(2)}) collective-permute-start(bf16[1024,128]{1,0:T(8,128)(2,1)S(1)} %slice.54), channel_id=1, source_target_pairs={{0,128},{128,256},{256,384},{384,0},{1,129},{129,257},{257,385},{3... | collective-permute-start | bytes 786440 | tf_op jit(solution)/shard_map/ppermute | solution.py:187
  91.8 18.4 %collective-permute-start.4 = (bf16[1024,128]{1,0:T(8,128)(2,1)S(1)}, bf16[1024,128]{1,0:T(8,128)(2,1)S(1)}, u32[]{:S(2)}, u32[]{:S(2)}) collective-permute-start(bf16[1024,128]{1,0:T(8,128)(2,1)S(1)} %slice.55), channel_id=1, source_target_pairs={{0,384},{128,0},{256,128},{384,256},{1,385},{129,1},{257,129},{385... | collective-permute-start | bytes 786440 | tf_op jit(solution)/shard_map/ppermute | solution.py:187
  95.5 28.8 %collective-permute-start.5 = (bf16[1536,128]{1,0:T(8,128)(2,1)S(1)}, bf16[1536,128]{1,0:T(8,128)(2,1)S(1)}, u32[]{:S(2)}, u32[]{:S(2)}) collective-permute-start(bf16[1536,128]{1,0:T(8,128)(2,1)S(1)} %bitcast.25), channel_id=1, source_target_pairs={{0,128},{128,256},{256,384},{1,129},{129,257},{257,385},{2,130},{1... | collective-permute-start | bytes 1179656 | tf_op jit(solution)/shard_map/ppermute | solution.py:192
  96.8 27.5 %collective-permute-start.6 = (bf16[1536,128]{1,0:T(8,128)(2,1)S(1)}, bf16[1536,128]{1,0:T(8,128)(2,1)S(1)}, u32[]{:S(2)}, u32[]{:S(2)}) collective-permute-start(bf16[1536,128]{1,0:T(8,128)(2,1)S(1)} %bitcast.26), channel_id=1, source_target_pairs={{0,256},{128,384},{1,257},{129,385},{2,258},{130,386},{3,259},{131... | collective-permute-start | bytes 1179656 | tf_op jit(solution)/shard_map/ppermute | solution.py:192
  98.1 26.2 %collective-permute-start.7 = (bf16[1536,128]{1,0:T(8,128)(2,1)S(1)}, bf16[1536,128]{1,0:T(8,128)(2,1)S(1)}, u32[]{:S(2)}, u32[]{:S(2)}) collective-permute-start(bf16[1536,128]{1,0:T(8,128)(2,1)S(1)} %bitcast.27), channel_id=1, source_target_pairs={{0,384},{1,385},{2,386},{3,387},{4,388},{5,389},{6,390},{7,391},{8... | collective-permute-start | bytes 1179656 | tf_op jit(solution)/shard_map/ppermute | solution.py:192
  110.2 1.0 copy-start.1
  117.3 10.5 %collective-permute-start.8 = (f32[192,128]{1,0:T(8,128)S(1)}, f32[192,128]{1,0:T(8,128)S(1)}, u32[]{:S(2)}, u32[]{:S(2)}) collective-permute-start(f32[192,128]{1,0:T(8,128)S(1)} %select_bitcast_fusion), channel_id=1, source_target_pairs={{0,64},{64,0},{1,65},{65,1},{2,66},{66,2},{3,67},{67,3},{4,68},{68... | collective-permute-start | bytes 294920 | tf_op jit(solution)/shard_map/ppermute | solution.py:196
  127.9 5.7 %collective-permute-start.10 = (bf16[4608,128]{1,0:T(8,128)(2,1)S(1)}, bf16[4608,128]{1,0:T(8,128)(2,1)S(1)}, u32[]{:S(2)}, u32[]{:S(2)}) collective-permute-start(bf16[4608,128]{1,0:T(8,128)(2,1)S(1)} %pad_maximum_fusion), channel_id=1, source_target_pairs={{0,1},{1,0},{2,3},{3,2},{4,5},{5,4},{6,7},{7,6},{8,9},{9,8},{10,11... | collective-permute-start | bytes 3538952 | tf_op jit(solution)/shard_map/ppermute | solution.py:196
  129.9 3.7 %collective-permute-start.9 = (bf16[1536,128]{1,0:T(8,128)(2,1)S(1)}, bf16[1536,128]{1,0:T(8,128)(2,1)S(1)}, u32[]{:S(2)}, u32[]{:S(2)}) collective-permute-start(bf16[1536,128]{1,0:T(8,128)(2,1)S(1)} %bitcast.28), channel_id=1, source_target_pairs={{0,1},{1,0},{2,3},{3,2},{4,5},{5,4},{6,7},{7,6},{8,9},{9,8},{10,11... | collective-permute-start | bytes 1179656 | tf_op jit(solution)/shard_map/ppermute | solution.py:196
Sparse Core Ops, SparseCore 0:
  46.1 56.4 all-gather.1

commit v3 on v2

--- a/solution.py
+++ b/solution.py
@@ -41,22 +41,58 @@
     )
 
 
+def slabs_kernel(h_ref, o_ref):
+    width = o_ref.shape[2]
+    for i in range(o_ref.shape[0]):
+        o_ref[i] = h_ref[:, i * width : (i + 1) * width]
+
+
+def halves_kernel(info_ref, h_ref, keep_ref, send_ref):
+    yh = info_ref[1] // 4
+    for i in range(4):
+        low = h_ref[:, i * 4096 : i * 4096 + 2048]
+        high = h_ref[:, i * 4096 + 2048 : (i + 1) * 4096]
+        keep_ref[:, i * 2048 : (i + 1) * 2048] = jnp.where(yh == 0, low, high)
+        send_ref[:, i * 2048 : (i + 1) * 2048] = jnp.where(yh == 0, high, low)
+
+
+def ends_kernel(up_ref, down_ref, first_ref, last_ref):
+    part = first_ref.shape[0]
+    first_ref[...] = up_ref[:part]
+    last_ref[...] = down_ref[part:]
+
+
+def small_kernel(kernel, name, outs, args, cost=0):
+    vm = pl.BlockSpec(memory_space=pltpu.VMEM)
+    smem = pl.BlockSpec(memory_space=pltpu.SMEM)
+    return pl.pallas_call(
+        kernel,
+        in_specs=[smem if a.ndim == 1 else vm for a in args],
+        out_specs=[vm] * len(outs),
+        out_shape=[jax.ShapeDtypeStruct(o, jnp.bfloat16) for o in outs],
+        compiler_params=pltpu.CompilerParams(vmem_limit_bytes=24 * 2**20),
+        cost_estimate=pl.CostEstimate(flops=0, bytes_accessed=cost, transcendentals=0),
+        name=name,
+    )(*args)
+
+
 def project_kernel(info_ref, h_ref, *refs):
     w_refs, o_ref, h_buf, w_buf, sems = refs[:4], *refs[4:]
     x = info_ref[0]
     copies = []
-    for n in range(4):
-        at = pl.multiple_of(lax.rem(x + 4 - n, 4) * 2048, 2048)
+    for n in range(8):
+        at = pl.multiple_of(lax.rem(x + 4 - n // 2, 4) * 2048 + n % 2 * 1024, 1024)
+        tile = w_refs[n // 2].at[pl.ds(n % 2 * 1024, 1024)]
         copies.append(
             (
-                pltpu.make_async_copy(h_ref.at[:, pl.ds(at, 2048)], h_buf.at[n], sems.at[n, 0]),
-                pltpu.make_async_copy(w_refs[n], w_buf.at[n], sems.at[n, 1]),
+                pltpu.make_async_copy(h_ref.at[:, pl.ds(at, 1024)], h_buf.at[n], sems.at[n, 0]),
+                pltpu.make_async_copy(tile, w_buf.at[n], sems.at[n, 1]),
             )
         )
         for copy in copies[n]:
             copy.start()
     total = None
-    for n in range(4):
+    for n in range(8):
         for copy in copies[n]:
             copy.wait()
         term = jnp.dot(h_buf[n], w_buf[n], preferred_element_type=jnp.float32)
@@ -68,13 +104,13 @@
 
 
 def attend_kernel(info_ref, q_ref, cos_ref, sin_ref, *refs):
-    mine, near_ref, far_ref, o_ref, buf, s_ref, sems = refs[:4], *refs[4:]
+    mine, other_ref, o_ref, buf, s_ref, sems = refs[:4], *refs[4:]
     rows = q_ref.shape[0]
     x, y, core = info_ref[0], info_ref[1], info_ref[2]
-    size = near_ref.shape[0]
+    size = mine[0].shape[0]
 
     def copies(i):
-        other = near_ref if i == 0 else far_ref.at[pl.ds((i - 1) * size, size)]
+        other = other_ref.at[pl.ds(i * size, size)]
         return [
             pltpu.make_async_copy(mine[i], buf.at[i, core], sems.at[i, 0]),
             pltpu.make_async_copy(other, buf.at[i, 1 - core], sems.at[i, 1]),
@@ -147,9 +183,9 @@
         out_specs=pl.BlockSpec(memory_space=pltpu.VMEM),
         out_shape=jax.ShapeDtypeStruct((2, m // 2, HD), jnp.float32),
         scratch_shapes=[
-            pltpu.VMEM((4, m, depth // 4), jnp.bfloat16),
-            pltpu.VMEM((4, depth // 4, HD), jnp.bfloat16),
-            pltpu.SemaphoreType.DMA((4, 2)),
+            pltpu.VMEM((8, m, depth // 8), jnp.bfloat16),
+            pltpu.VMEM((8, depth // 8, HD), jnp.bfloat16),
+            pltpu.SemaphoreType.DMA((8, 2)),
         ],
         compiler_params=pltpu.CompilerParams(vmem_limit_bytes=48 * 2**20),
         cost_estimate=pl.CostEstimate(
@@ -164,7 +200,7 @@
     return pl.pallas_call(
         attend_kernel,
         in_specs=[pl.BlockSpec(memory_space=pltpu.SMEM), vm, vm, vm]
-        + [pl.BlockSpec(memory_space=pl.ANY)] * 6,
+        + [pl.BlockSpec(memory_space=pl.ANY)] * 5,
         out_specs=vm,
         out_shape=jax.ShapeDtypeStruct(sums.shape, jnp.bfloat16),
         scratch_shapes=[
@@ -179,7 +215,7 @@
             transcendentals=192 * 6144,
         ),
         name="attend",
-    )(info, sums, cosine, sine, *mine, *other)
+    )(info, sums, cosine, sine, *mine, other)
 
 
 def shift(v, axis, by):
@@ -205,14 +241,13 @@
 
     w = lax.all_gather(query_weight, "yl", axis=0, tiled=True)
 
-    hs = hidden.reshape(12, 16, 1024).transpose(1, 0, 2)
-    hs, hidden = tie((hs, hidden))
+    (hs,) = small_kernel(slabs_kernel, "slabs", [(16, 12, 1024)], (hidden,), 2**20)
     hs = lax.all_to_all(hs, TP, 0, 0, tiled=True).reshape(192, 1024)
 
-    parts = [hidden[:, i * 2048 : (i + 1) * 2048] for i in range(8)]
-    halves = [jnp.concatenate(parts[i::2], axis=1) for i in range(2)]
-    keep = jnp.where(yh == 0, halves[0], halves[1])
-    come = swap(jnp.where(yh == 0, halves[1], halves[0]), "yh")
+    keep, send = small_kernel(
+        halves_kernel, "halves", [(12, 8192)] * 2, (info, hidden), 100 * 2**20
+    )
+    come = swap(send, "yh")
     h = jnp.where(
         yh == 0, jnp.concatenate([keep, come], 0), jnp.concatenate([come, keep], 0)
     )
@@ -227,15 +262,18 @@
     cosine, sine = angles_of(base + z * 24 + jnp.arange(24, dtype=jnp.int32))
     rows = jnp.where(core == 0, rotate(rows, cosine, sine), rows).astype(jnp.bfloat16)
     rows = broadcast_gather(rows, ("yh", "yl", "z")).reshape(1536, HD)
-    rows, up, down = tie((rows, up, down))
-    cross = [shift(up[:1024], "x", 1), shift(down[1024:], "x", -1)]
+    first, last = small_kernel(
+        ends_kernel, "ends", [(1024, HD)] * 2, (up, down), 60 * 2**20
+    )
+    cross = [shift(first, "x", 1), shift(last, "x", -1)]
+    rows, cross = tie((rows, cross))
     mine = [rows] + [shift_up(rows, "x", d) for d in (1, 2, 3)]
 
     sums = project(info, h, (w, up, jnp.concatenate(cross, axis=0), down))
     keep = jnp.where(yh == 0, sums[0], sums[1])
     come = swap(jnp.where(yh == 0, sums[1], sums[0]), "yh")
     away, come = tie((mine[1:], come))
-    other = [swap(rows, "core"), swap(jnp.concatenate(away, axis=0), "core")]
+    other = swap(jnp.concatenate([rows] + away, axis=0), "core")
     cosine, sine = angles_of(base + jnp.arange(192, dtype=jnp.int32))
     cosine = jnp.concatenate([cosine, cosine], axis=1)
     sine = jnp.concatenate([-sine, sine], axis=1)

time: 148 us -> 141 us (0.953)
  waiting for transfers between devices: 38 us -> 32.8 us
  starting transfers between devices: 58.7 us -> 54.3 us
  other arithmetic: 2.08 us -> 3.95 us
    ppermute x4, waiting for transfers between devices: 23.7 us -> 10.2 us  [shift(): return lax.ppermute(v, axis, [(i, (i + by) % n) for i in range(n)])]
    all_gather x1, waiting for transfers between devices: 0.02 us -> 9.89 us  [body(): h = lax.all_gather(h, TP, axis=0, tiled=True)]
    all_to_all x1, waiting for transfers between devices: 9.91 us -> 4.09 us  [body(): part = lax.all_to_all(part, TP, 0, 0, tiled=True)]
    ppermute x4 -> x3, starting transfers between devices: 19 us -> 16 us  [swap(): return lax.ppermute(v, axis, [(0, 1), (1, 0)])]
    ppermute x4 -> x3, waiting for transfers between devices: 4.32 us -> 7.29 us  [swap(): return lax.ppermute(v, axis, [(0, 1), (1, 0)])]
    all_to_all x1, starting transfers between devices: 7.11 us -> 4.94 us  [broadcast_gather(): lax.all_to_all(jnp.broadcast_to(x[None], (n,) + x.shape), axis, 0, 0, til...]
  transfers between devices with their start and end apart: 15 -> 14, of which waited for: 6 -> 9; matrix products, arithmetic and copies ran while one was open for 2% -> 3% of each run, Pallas kernels for 4% -> 5%
where the time goes in v3:
time: 141 us; the launch traced here: 139 us
  starting transfers between devices  54.3 us (39%)
  waiting for transfers between devices  32.8 us (23%)
  blocking collectives  16.2 us (11%)
  between operations  13.7 us (10%)
  Pallas kernels  13.2 us (9%)
  local copies, waits for them, and re-layouts  4.24 us (3%)
  other arithmetic  3.95 us (3%)
    all_gather x1, blocking collectives, body(): w = lax.all_gather(query_weight, 'yl', axis=0, tiled=True)  16.2 us
    ppermute x3, starting transfers between devices, swap(): return lax.ppermute(v, axis, [(0, 1), (1, 0)])  16 us
    ppermute x4, starting transfers between devices, shift(): return lax.ppermute(v, axis, [(i, (i + by) % n) for i in range(n)])  11.7 us
    all_to_all x1, starting transfers between devices, body(): hs = lax.all_to_all(hs, TP, 0, 0, tiled=True).reshape(192, 1024)  10.4 us
    ppermute x4, waiting for transfers between devices, shift(): return lax.ppermute(v, axis, [(i, (i + by) % n) for i in range(n)])  10.2 us
    all_gather x1, waiting for transfers between devices, body(): h = lax.all_gather(h, TP, axis=0, tiled=True)  9.89 us
    all_to_all x1, starting transfers between devices, body(): part = lax.all_to_all(part, TP, 0, 0, tiled=True)  7.31 us
    ppermute x3, waiting for transfers between devices, swap(): return lax.ppermute(v, axis, [(0, 1), (1, 0)])  7.29 us
  transfers between devices with their start and end apart: 14, of which 9 were waited for; matrix products, arithmetic and copies ran while one was open for 3% of the time, Pallas kernels for 5%

profile of v3, /device:TPU:6, one launch (start us, length us, event | category | flops | bytes accessed | tf_op | source)
XLA Modules:
  0.0 139.3 jit_solution(6724625229400254328)
XLA Ops:
  8.3 7.7 %collective-permute-start = (bf16[12,8192]{1,0:T(8,128)(2,1)S(1)}, bf16[12,8192]{1,0:T(8,128)(2,1)S(1)}, u32[]{:S(2)}, u32[]{:S(2)}) collective-permute-start(bf16[12,8192]{1,0:T(8,128)(2,1)S(1)} %get-tuple-element.19), channel_id=1, source_target_pairs={{0,64},{64,0},{1,65},{65,1},{2,66},{66,2},{3,67},{67,3},{4,68},{68... | collective-permute-start | bytes 589832 | tf_op jit(solution)/shard_map/ppermute | solution.py:232
  17.9 10.4 %all-to-all-start = ((bf16[16,12,1024]{2,1,0:T(8,128)(2,1)}), bf16[16,12,1024]{2,1,0:T(8,128)(2,1)S(1)}, u32[]{:S(2)}, u32[]{:S(2)}) async-start(bf16[16,12,1024]{2,1,0:T(8,128)(2,1)} %slabs.1), calls=%async_computation | async-start | bytes 1048576 | tf_op jit(solution)/shard_map/all_to_all | solution.py:245
  29.6 16.2 %all_gather.6.refs_0_ = bf16[2048,128]{1,0:T(8,128)(2,1)S(1)} all-gather(bf16[512,128]{1,0:T(8,128)(2,1)S(1)} %copy-done.3), channel_id=1, replica_groups=mesh['x'=4,'yh'=2,'yl'=4,'z'=8,'core'=2] {'yl'}, dimensions={0}, use_global_device_ids=true | all-gather | bytes 655360 | tf_op jit(solution)/shard_map/all_gather | solution.py:242
  47.9 7.3 %all-to-all-start.1 = ((f32[16,24,128]{2,1,0:T(8,128)}), f32[16,24,128]{2,1,0:T(8,128)S(1)}, u32[]{:S(2)}, u32[]{:S(2)}) async-start(f32[16,24,128]{2,1,0:T(8,128)} %bitcast.8), calls=%async_computation.1 | async-start | bytes 393216 | tf_op jit(solution)/shard_map/all_to_all | solution.py:259
  55.3 2.4 %collective-permute-start.1 = (bf16[2048,128]{1,0:T(8,128)(2,1)S(1)}, bf16[2048,128]{1,0:T(8,128)(2,1)S(1)}, u32[]{:S(2)}, u32[]{:S(2)}) collective-permute-start(bf16[2048,128]{1,0:T(8,128)(2,1)S(1)} %all_gather.6.refs_0_), channel_id=1, source_target_pairs={{0,128},{128,256},{256,384},{384,0},{1,129},{129,257},{257,385},{3... | collective-permute-start | bytes 1572872 | tf_op jit(solution)/shard_map/ppermute | solution.py:223
  57.7 3.5 %collective-permute-start.2 = (bf16[2048,128]{1,0:T(8,128)(2,1)S(1)}, bf16[2048,128]{1,0:T(8,128)(2,1)S(1)}, u32[]{:S(2)}, u32[]{:S(2)}) collective-permute-start(bf16[2048,128]{1,0:T(8,128)(2,1)S(1)} %all_gather.6.refs_0_), channel_id=1, source_target_pairs={{0,384},{128,0},{256,128},{384,256},{1,385},{129,1},{257,129},{385... | collective-permute-start | bytes 1572872 | tf_op jit(solution)/shard_map/ppermute | solution.py:223
  61.1 4.1 %all-to-all-done.1 = f32[16,24,128]{2,1,0:T(8,128)S(1)} async-done(((f32[16,24,128]{2,1,0:T(8,128)}), f32[16,24,128]{2,1,0:T(8,128)S(1)}, u32[]{:S(2)}, u32[]{:S(2)}) %all-to-all-start.1) | async-done | bytes 196640 | tf_op jit(solution)/shard_map/all_to_all | solution.py:259
  66.3 4.9 %all-to-all-start.2 = ((bf16[64,24,128]{2,1,0:T(8,128)(2,1)}), bf16[64,24,128]{2,1,0:T(8,128)(2,1)S(1)}, u32[]{:S(2)}, u32[]{:S(2)}) async-start(bf16[64,24,128]{2,1,0:T(8,128)(2,1)} %broadcast_in_dim.2), calls=%async_computation.2 | async-start | bytes 786432 | tf_op jit(solution)/shard_map/all_to_all | solution.py:39
  71.4 3.3 %collective-permute-done.2.down_ref.refs_3_ = bf16[2048,128]{1,0:T(8,128)(2,1)S(1)} collective-permute-done((bf16[2048,128]{1,0:T(8,128)(2,1)S(1)}, bf16[2048,128]{1,0:T(8,128)(2,1)S(1)}, u32[]{:S(2)}, u32[]{:S(2)}) %collective-permute-start.2) | collective-permute-done | bytes 524320 | tf_op jit(solution)/shard_map/ppermute | solution.py:223
  74.7 2.2 %collective-permute-start.3 = (bf16[1024,128]{1,0:T(8,128)(2,1)S(1)}, bf16[1024,128]{1,0:T(8,128)(2,1)S(1)}, u32[]{:S(2)}, u32[]{:S(2)}) collective-permute-start(bf16[1024,128]{1,0:T(8,128)(2,1)S(1)} %get-tuple-element.22), channel_id=1, source_target_pairs={{0,128},{128,256},{256,384},{384,0},{1,129},{129,257},{257,385},{3... | collective-permute-start | bytes 786440 | tf_op jit(solution)/shard_map/ppermute | solution.py:223
  76.9 3.7 %collective-permute-start.4 = (bf16[1024,128]{1,0:T(8,128)(2,1)S(1)}, bf16[1024,128]{1,0:T(8,128)(2,1)S(1)}, u32[]{:S(2)}, u32[]{:S(2)}) collective-permute-start(bf16[1024,128]{1,0:T(8,128)(2,1)S(1)} %get-tuple-element.23), channel_id=1, source_target_pairs={{0,384},{128,0},{256,128},{384,256},{1,385},{129,1},{257,129},{385... | collective-permute-start | bytes 786440 | tf_op jit(solution)/shard_map/ppermute | solution.py:223
  80.6 3.6 %collective-permute-done.3 = bf16[1024,128]{1,0:T(8,128)(2,1)S(1)} collective-permute-done((bf16[1024,128]{1,0:T(8,128)(2,1)S(1)}, bf16[1024,128]{1,0:T(8,128)(2,1)S(1)}, u32[]{:S(2)}, u32[]{:S(2)}) %collective-permute-start.3) | collective-permute-done | bytes 262176 | tf_op jit(solution)/shard_map/ppermute | solution.py:223
  84.2 3.1 %collective-permute-done.4 = bf16[1024,128]{1,0:T(8,128)(2,1)S(1)} collective-permute-done((bf16[1024,128]{1,0:T(8,128)(2,1)S(1)}, bf16[1024,128]{1,0:T(8,128)(2,1)S(1)}, u32[]{:S(2)}, u32[]{:S(2)}) %collective-permute-start.4) | collective-permute-done | bytes 262176 | tf_op jit(solution)/shard_map/ppermute | solution.py:223
  87.3 1.3 all-to-all-done.2
  88.6 1.3 collective-permute-start.5
  89.9 1.3 collective-permute-start.6
  91.2 1.3 collective-permute-start.7
  93.5 9.9 %all-gather.2.cloned.1.call-done.h_ref = bf16[384,8192]{1,0:T(8,128)(2,1)} async-done(((bf16[24,8192]{1,0:T(8,128)(2,1)}), bf16[384,8192]{1,0:T(8,128)(2,1)}) %all-gather.2.cloned.1.call-update) | async-done | bytes 6291472 | tf_op jit(solution)/shard_map/all_gather | solution.py:257
  103.4 5.8 %project.1 = f32[2,192,128]{2,1,0:T(8,128)S(1)} custom-call(s32[3]{0:T(128)S(1)} %pad_add_fusion.info_ref, bf16[384,8192]{1,0:T(8,128)(2,1)} %all-gather.2.cloned.1.call-done.h_ref, bf16[2048,128]{1,0:T(8,128)(2,1)S(1)} %all_gather.6.refs_0_, bf16[2048,128]{1,0:T(8,128)(2,1)S(1)} %collective-permute-done.1.up_ref.refs_1_, ...), custom_call_target="tpu_custom_call" | custom-call | flops 805306368 | bytes 8388608 | tf_op jit(solution)/shard_map/project/pallas_call | solution.py:180
  109.2 6.3 %collective-permute-start.8 = (f32[192,128]{1,0:T(8,128)S(1)}, f32[192,128]{1,0:T(8,128)S(1)}, u32[]{:S(2)}, u32[]{:S(2)}) collective-permute-start(f32[192,128]{1,0:T(8,128)S(1)} %select_bitcast_fusion), channel_id=1, source_target_pairs={{0,64},{64,0},{1,65},{65,1},{2,66},{66,2},{3,67},{67,3},{4,68},{68... | collective-permute-start | bytes 294920 | tf_op jit(solution)/shard_map/ppermute | solution.py:232
  115.6 4.5 %collective-permute-done.8 = f32[192,128]{1,0:T(8,128)S(1)} collective-permute-done((f32[192,128]{1,0:T(8,128)S(1)}, f32[192,128]{1,0:T(8,128)S(1)}, u32[]{:S(2)}, u32[]{:S(2)}) %collective-permute-start.8) | collective-permute-done | bytes 98336 | tf_op jit(solution)/shard_map/ppermute | solution.py:232
  121.2 1.9 %collective-permute-start.9 = (bf16[6144,128]{1,0:T(8,128)(2,1)S(1)}, bf16[6144,128]{1,0:T(8,128)(2,1)S(1)}, u32[]{:S(2)}, u32[]{:S(2)}) collective-permute-start(bf16[6144,128]{1,0:T(8,128)(2,1)S(1)} %pad_maximum_fusion), channel_id=1, source_target_pairs={{0,1},{1,0},{2,3},{3,2},{4,5},{5,4},{6,7},{7,6},{8,9},{9,8},{10,11... | collective-permute-start | bytes 4718600 | tf_op jit(solution)/shard_map/ppermute | solution.py:232
  123.7 2.8 %collective-permute-done.9.refs_4_ = bf16[6144,128]{1,0:T(8,128)(2,1)S(1)} collective-permute-done((bf16[6144,128]{1,0:T(8,128)(2,1)S(1)}, bf16[6144,128]{1,0:T(8,128)(2,1)S(1)}, u32[]{:S(2)}, u32[]{:S(2)}) %collective-permute-start.9) | collective-permute-done | bytes 1572896 | tf_op jit(solution)/shard_map/ppermute | solution.py:232
  126.5 6.0 %attend.1 = bf16[192,128]{1,0:T(8,128)(2,1)} custom-call(s32[3]{0:T(128)S(1)} %pad_add_fusion.info_ref, f32[192,128]{1,0:T(8,128)S(1)} %bitcast_add_fusion.q_ref, f32[192,128]{1,0:T(8,128)S(1)} %get-tuple-element.36.cos_ref, f32[192,128]{1,0:T(8,128)S(1)} %get-tuple-element.37.sin_ref, bf16[1536,128]{1,0:T(8,128)(2,1)S(1)} %bitcast.23, ...), custom_call_target="tpu_custom_call" | custom-call | flops 603979776 | bytes 3145728 | tf_op jit(solution)/shard_map/attend/pallas_call | solution.py:200
  (37 shorter events, 10.9 us)
Async XLA Ops:
  6.6 1.0 copy-start
  7.7 22.0 %copy-start.3 = (bf16[512,128]{1,0:T(8,128)(2,1)S(1)}, bf16[512,128]{1,0:T(8,128)(2,1)}, u32[]{:S(2)}) copy-start(bf16[512,128]{1,0:T(8,128)(2,1)} %param.4) | copy-start | bytes 393220
  8.3 37.5 %collective-permute-start = (bf16[12,8192]{1,0:T(8,128)(2,1)S(1)}, bf16[12,8192]{1,0:T(8,128)(2,1)S(1)}, u32[]{:S(2)}, u32[]{:S(2)}) collective-permute-start(bf16[12,8192]{1,0:T(8,128)(2,1)S(1)} %get-tuple-element.19), channel_id=1, source_target_pairs={{0,64},{64,0},{1,65},{65,1},{2,66},{66,2},{3,67},{67,3},{4,68},{68... | collective-permute-start | bytes 589832 | tf_op jit(solution)/shard_map/ppermute | solution.py:232
  16.0 1.0 copy-start.1
  17.9 28.9 %all-to-all-start = ((bf16[16,12,1024]{2,1,0:T(8,128)(2,1)}), bf16[16,12,1024]{2,1,0:T(8,128)(2,1)S(1)}, u32[]{:S(2)}, u32[]{:S(2)}) async-start(bf16[16,12,1024]{2,1,0:T(8,128)(2,1)} %slabs.1), calls=%async_computation | async-start | bytes 1048576 | tf_op jit(solution)/shard_map/all_to_all | solution.py:245
  28.3 75.1 %all-gather.2.cloned.1.call-start = ((), (), s32[]{:S(2)}) async-start(), calls=%async_computation.3 | async-start | bytes 6684672 | tf_op jit(solution)/shard_map/all_gather | solution.py:257
  47.9 17.3 %all-to-all-start.1 = ((f32[16,24,128]{2,1,0:T(8,128)}), f32[16,24,128]{2,1,0:T(8,128)S(1)}, u32[]{:S(2)}, u32[]{:S(2)}) async-start(f32[16,24,128]{2,1,0:T(8,128)} %bitcast.8), calls=%async_computation.1 | async-start | bytes 393216 | tf_op jit(solution)/shard_map/all_to_all | solution.py:259
  55.3 16.1 %collective-permute-start.1 = (bf16[2048,128]{1,0:T(8,128)(2,1)S(1)}, bf16[2048,128]{1,0:T(8,128)(2,1)S(1)}, u32[]{:S(2)}, u32[]{:S(2)}) collective-permute-start(bf16[2048,128]{1,0:T(8,128)(2,1)S(1)} %all_gather.6.refs_0_), channel_id=1, source_target_pairs={{0,128},{128,256},{256,384},{384,0},{1,129},{129,257},{257,385},{3... | collective-permute-start | bytes 1572872 | tf_op jit(solution)/shard_map/ppermute | solution.py:223
  57.7 17.0 %collective-permute-start.2 = (bf16[2048,128]{1,0:T(8,128)(2,1)S(1)}, bf16[2048,128]{1,0:T(8,128)(2,1)S(1)}, u32[]{:S(2)}, u32[]{:S(2)}) collective-permute-start(bf16[2048,128]{1,0:T(8,128)(2,1)S(1)} %all_gather.6.refs_0_), channel_id=1, source_target_pairs={{0,384},{128,0},{256,128},{384,256},{1,385},{129,1},{257,129},{385... | collective-permute-start | bytes 1572872 | tf_op jit(solution)/shard_map/ppermute | solution.py:223
  66.3 22.3 %all-to-all-start.2 = ((bf16[64,24,128]{2,1,0:T(8,128)(2,1)}), bf16[64,24,128]{2,1,0:T(8,128)(2,1)S(1)}, u32[]{:S(2)}, u32[]{:S(2)}) async-start(bf16[64,24,128]{2,1,0:T(8,128)(2,1)} %broadcast_in_dim.2), calls=%async_computation.2 | async-start | bytes 786432 | tf_op jit(solution)/shard_map/all_to_all | solution.py:39
  74.7 9.5 %collective-permute-start.3 = (bf16[1024,128]{1,0:T(8,128)(2,1)S(1)}, bf16[1024,128]{1,0:T(8,128)(2,1)S(1)}, u32[]{:S(2)}, u32[]{:S(2)}) collective-permute-start(bf16[1024,128]{1,0:T(8,128)(2,1)S(1)} %get-tuple-element.22), channel_id=1, source_target_pairs={{0,128},{128,256},{256,384},{384,0},{1,129},{129,257},{257,385},{3... | collective-permute-start | bytes 786440 | tf_op jit(solution)/shard_map/ppermute | solution.py:223
  76.9 10.4 %collective-permute-start.4 = (bf16[1024,128]{1,0:T(8,128)(2,1)S(1)}, bf16[1024,128]{1,0:T(8,128)(2,1)S(1)}, u32[]{:S(2)}, u32[]{:S(2)}) collective-permute-start(bf16[1024,128]{1,0:T(8,128)(2,1)S(1)} %get-tuple-element.23), channel_id=1, source_target_pairs={{0,384},{128,0},{256,128},{384,256},{1,385},{129,1},{257,129},{385... | collective-permute-start | bytes 786440 | tf_op jit(solution)/shard_map/ppermute | solution.py:223
  87.3 1.3 copy-start.2
  88.6 26.9 %collective-permute-start.5 = (bf16[1536,128]{1,0:T(8,128)(2,1)S(1)}, bf16[1536,128]{1,0:T(8,128)(2,1)S(1)}, u32[]{:S(2)}, u32[]{:S(2)}) collective-permute-start(bf16[1536,128]{1,0:T(8,128)(2,1)S(1)} %bitcast.19), channel_id=1, source_target_pairs={{0,128},{128,256},{256,384},{1,129},{129,257},{257,385},{2,130},{1... | collective-permute-start | bytes 1179656 | tf_op jit(solution)/shard_map/ppermute | solution.py:228
  89.9 25.6 %collective-permute-start.6 = (bf16[1536,128]{1,0:T(8,128)(2,1)S(1)}, bf16[1536,128]{1,0:T(8,128)(2,1)S(1)}, u32[]{:S(2)}, u32[]{:S(2)}) collective-permute-start(bf16[1536,128]{1,0:T(8,128)(2,1)S(1)} %bitcast.20), channel_id=1, source_target_pairs={{0,256},{128,384},{1,257},{129,385},{2,258},{130,386},{3,259},{131... | collective-permute-start | bytes 1179656 | tf_op jit(solution)/shard_map/ppermute | solution.py:228
  91.2 24.3 %collective-permute-start.7 = (bf16[1536,128]{1,0:T(8,128)(2,1)S(1)}, bf16[1536,128]{1,0:T(8,128)(2,1)}, u32[]{:S(2)}, u32[]{:S(2)}) collective-permute-start(bf16[1536,128]{1,0:T(8,128)(2,1)S(1)} %bitcast.21), channel_id=1, source_target_pairs={{0,384},{1,385},{2,386},{3,387},{4,388},{5,389},{6,390},{7,391},{8... | collective-permute-start | bytes 1179656 | tf_op jit(solution)/shard_map/ppermute | solution.py:228
  109.2 10.9 %collective-permute-start.8 = (f32[192,128]{1,0:T(8,128)S(1)}, f32[192,128]{1,0:T(8,128)S(1)}, u32[]{:S(2)}, u32[]{:S(2)}) collective-permute-start(f32[192,128]{1,0:T(8,128)S(1)} %select_bitcast_fusion), channel_id=1, source_target_pairs={{0,64},{64,0},{1,65},{65,1},{2,66},{66,2},{3,67},{67,3},{4,68},{68... | collective-permute-start | bytes 294920 | tf_op jit(solution)/shard_map/ppermute | solution.py:232
  121.2 5.3 %collective-permute-start.9 = (bf16[6144,128]{1,0:T(8,128)(2,1)S(1)}, bf16[6144,128]{1,0:T(8,128)(2,1)S(1)}, u32[]{:S(2)}, u32[]{:S(2)}) collective-permute-start(bf16[6144,128]{1,0:T(8,128)(2,1)S(1)} %pad_maximum_fusion), channel_id=1, source_target_pairs={{0,1},{1,0},{2,3},{3,2},{4,5},{5,4},{6,7},{7,6},{8,9},{9,8},{10,11... | collective-permute-start | bytes 4718600 | tf_op jit(solution)/shard_map/ppermute | solution.py:232
Sparse Core Ops, SparseCore 0:
  48.0 55.3 all-gather.1

commit v4 on v3

--- a/solution.py
+++ b/solution.py
@@ -9,13 +9,14 @@
 from jax.sharding import PartitionSpec as P
 
 HD = 128
-CTX = ("x", "yh", "yl")
+CTX = ("x", "yq", "yp")
 TP = ("z", "core")
+PAIR = ("yp", "z", "core")
 AXES = CTX + TP
 
 
 def fine_mesh(mesh):
-    return Mesh(mesh.devices.reshape(4, 2, 4, 8, 2), AXES)
+    return Mesh(mesh.devices.reshape(4, 4, 2, 8, 2), AXES)
 
 
 def angles_of(positions):
@@ -42,18 +43,42 @@
 
 
 def slabs_kernel(h_ref, o_ref):
-    width = o_ref.shape[2]
-    for i in range(o_ref.shape[0]):
-        o_ref[i] = h_ref[:, i * width : (i + 1) * width]
-
-
-def halves_kernel(info_ref, h_ref, keep_ref, send_ref):
-    yh = info_ref[1] // 4
-    for i in range(4):
-        low = h_ref[:, i * 4096 : i * 4096 + 2048]
-        high = h_ref[:, i * 4096 + 2048 : (i + 1) * 4096]
-        keep_ref[:, i * 2048 : (i + 1) * 2048] = jnp.where(yh == 0, low, high)
-        send_ref[:, i * 2048 : (i + 1) * 2048] = jnp.where(yh == 0, high, low)
+    for yp in range(2):
+        for t in range(16):
+            at = (2 * t + yp) * 512
+            o_ref[yp * 16 + t] = h_ref[:, at : at + 512]
+
+
+def mix_kernel(info_ref, x_ref, w_ref, rows_ref, o_ref, buf):
+    yp = lax.rem(info_ref[1], 2)
+    for i in range(32):
+        buf[i * 12 : (i + 1) * 12, :] = x_ref[i].astype(jnp.float32)
+    rows = buf[...].astype(jnp.bfloat16)
+    rows_ref[...] = rows
+    w = w_ref[pl.ds(pl.multiple_of(yp * 512, 512), 512), :]
+    sums = jnp.dot(rows, w, preferred_element_type=jnp.float32)
+    for i in range(16):
+        for k in range(2):
+            o_ref[2 * i + k] = sums[i * 24 : (i + 1) * 24, k * HD : (k + 1) * HD]
+
+
+def mix(info, x, w):
+    vm = pl.BlockSpec(memory_space=pltpu.VMEM)
+    return pl.pallas_call(
+        mix_kernel,
+        in_specs=[pl.BlockSpec(memory_space=pltpu.SMEM), vm, vm],
+        out_specs=[vm, vm],
+        out_shape=[
+            jax.ShapeDtypeStruct((384, 512), jnp.bfloat16),
+            jax.ShapeDtypeStruct((32, 24, HD), jnp.float32),
+        ],
+        scratch_shapes=[pltpu.VMEM((384, 512), jnp.float32)],
+        compiler_params=pltpu.CompilerParams(vmem_limit_bytes=24 * 2**20),
+        cost_estimate=pl.CostEstimate(
+            flops=2 * 384 * 512 * 256, bytes_accessed=2**20, transcendentals=0
+        ),
+        name="mix",
+    )(info, x, w)
 
 
 def ends_kernel(up_ref, down_ref, first_ref, last_ref):
@@ -62,7 +87,13 @@
     last_ref[...] = down_ref[part:]
 
 
-def small_kernel(kernel, name, outs, args, cost=0):
+def join_kernel(*refs):
+    size = refs[0].shape[0]
+    for i, ref in enumerate(refs[:-1]):
+        refs[-1][i * size : (i + 1) * size] = ref[...]
+
+
+def small_kernel(kernel, name, outs, args):
     vm = pl.BlockSpec(memory_space=pltpu.VMEM)
     smem = pl.BlockSpec(memory_space=pltpu.SMEM)
     return pl.pallas_call(
@@ -71,7 +102,7 @@
         out_specs=[vm] * len(outs),
         out_shape=[jax.ShapeDtypeStruct(o, jnp.bfloat16) for o in outs],
         compiler_params=pltpu.CompilerParams(vmem_limit_bytes=24 * 2**20),
-        cost_estimate=pl.CostEstimate(flops=0, bytes_accessed=cost, transcendentals=0),
+        cost_estimate=pl.CostEstimate(flops=0, bytes_accessed=2**20, transcendentals=0),
         name=name,
     )(*args)
 
@@ -80,27 +111,25 @@
     w_refs, o_ref, h_buf, w_buf, sems = refs[:4], *refs[4:]
     x = info_ref[0]
     copies = []
-    for n in range(8):
-        at = pl.multiple_of(lax.rem(x + 4 - n // 2, 4) * 2048 + n % 2 * 1024, 1024)
-        tile = w_refs[n // 2].at[pl.ds(n % 2 * 1024, 1024)]
+    for n in range(4):
+        at = lax.rem(x + 4 - n, 4) * 4
         copies.append(
             (
-                pltpu.make_async_copy(h_ref.at[:, pl.ds(at, 1024)], h_buf.at[n], sems.at[n, 0]),
-                pltpu.make_async_copy(tile, w_buf.at[n], sems.at[n, 1]),
+                pltpu.make_async_copy(h_ref.at[pl.ds(at, 4)], h_buf.at[n], sems.at[n, 0]),
+                pltpu.make_async_copy(w_refs[n], w_buf.at[n], sems.at[n, 1]),
             )
         )
         for copy in copies[n]:
             copy.start()
     total = None
-    for n in range(8):
+    for n in range(4):
         for copy in copies[n]:
             copy.wait()
-        term = jnp.dot(h_buf[n], w_buf[n], preferred_element_type=jnp.float32)
+        a = jnp.concatenate([h_buf[n, i] for i in range(4)], axis=1)
+        term = jnp.dot(a, w_buf[n], preferred_element_type=jnp.float32)
         total = term if total is None else total + term
-    for part in range(16):
-        for sel in range(2):
-            at = part * 24 + sel * 12
-            o_ref[sel, part * 12 : part * 12 + 12, :] = total[at : at + 12]
+    for sel in range(2):
+        o_ref[sel] = total[sel * 192 : (sel + 1) * 192]
 
 
 def attend_kernel(info_ref, q_ref, cos_ref, sin_ref, *refs):
@@ -175,7 +204,7 @@
 
 
 def project(info, h, pieces):
-    m, depth = h.shape
+    count, m, part = h.shape
     hbm = pl.BlockSpec(memory_space=pl.ANY)
     return pl.pallas_call(
         project_kernel,
@@ -183,13 +212,15 @@
         out_specs=pl.BlockSpec(memory_space=pltpu.VMEM),
         out_shape=jax.ShapeDtypeStruct((2, m // 2, HD), jnp.float32),
         scratch_shapes=[
-            pltpu.VMEM((8, m, depth // 8), jnp.bfloat16),
-            pltpu.VMEM((8, depth // 8, HD), jnp.bfloat16),
-            pltpu.SemaphoreType.DMA((8, 2)),
+            pltpu.VMEM((4, count // 4, m, part), jnp.bfloat16),
+            pltpu.VMEM((4, count // 4 * part, HD), jnp.bfloat16),
+            pltpu.SemaphoreType.DMA((4, 2)),
         ],
         compiler_params=pltpu.CompilerParams(vmem_limit_bytes=48 * 2**20),
         cost_estimate=pl.CostEstimate(
-            flops=2 * m * depth * HD, bytes_accessed=2 * depth * (m + HD), transcendentals=0
+            flops=2 * m * count * part * HD,
+            bytes_accessed=2 * count * part * (m + HD),
+            transcendentals=0,
         ),
         name="project",
     )(info, h, *pieces)
@@ -233,47 +264,37 @@
 
 
 def body(hidden, query_weight, kv_weight):
-    x, yh, yl, z, core = (lax.axis_index(a) for a in AXES)
-    y = yh * 4 + yl
+    x, yq, yp, z, core = (lax.axis_index(a) for a in AXES)
+    y = yq * 2 + yp
     base = (x * 8 + y) * 192
     info = jnp.stack([x, y, core])
     tie = lax.optimization_barrier
 
-    w = lax.all_gather(query_weight, "yl", axis=0, tiled=True)
-
-    (hs,) = small_kernel(slabs_kernel, "slabs", [(16, 12, 1024)], (hidden,), 2**20)
-    hs = lax.all_to_all(hs, TP, 0, 0, tiled=True).reshape(192, 1024)
-
-    keep, send = small_kernel(
-        halves_kernel, "halves", [(12, 8192)] * 2, (info, hidden), 100 * 2**20
-    )
-    come = swap(send, "yh")
-    h = jnp.where(
-        yh == 0, jnp.concatenate([keep, come], 0), jnp.concatenate([come, keep], 0)
-    )
-    part = jnp.dot(hs, kv_weight, preferred_element_type=jnp.float32)
-    part = part.reshape(8, 24, 2, HD).transpose(0, 2, 1, 3).reshape(16, 24, HD)
-    h, w, _ = tie((h, w, part))
-    h = lax.all_gather(h, TP, axis=0, tiled=True)
-
-    part = lax.all_to_all(part, TP, 0, 0, tiled=True)
+    w = lax.all_gather(query_weight, "yq", axis=0, tiled=True)
+
+    (hs,) = small_kernel(slabs_kernel, "slabs", [(32, 12, 512)], (hidden,))
+    hs = lax.all_to_all(hs, PAIR, 0, 0, tiled=True)
+    h, part = mix(info, hs, kv_weight)
+    h, w, part = tie((h, w, part))
+    h = lax.all_gather(h, TP, axis=0, tiled=False)
+
+    part = lax.all_to_all(part, PAIR, 0, 0, tiled=True)
     up, down = shift(w, "x", 1), shift(w, "x", -1)
     rows = jnp.sum(part, axis=0)
     cosine, sine = angles_of(base + z * 24 + jnp.arange(24, dtype=jnp.int32))
     rows = jnp.where(core == 0, rotate(rows, cosine, sine), rows).astype(jnp.bfloat16)
-    rows = broadcast_gather(rows, ("yh", "yl", "z")).reshape(1536, HD)
-    first, last = small_kernel(
-        ends_kernel, "ends", [(1024, HD)] * 2, (up, down), 60 * 2**20
-    )
+    rows = broadcast_gather(rows, ("yq", "yp", "z")).reshape(1536, HD)
+    first, last = small_kernel(ends_kernel, "ends", [(1024, HD)] * 2, (up, down))
     cross = [shift(first, "x", 1), shift(last, "x", -1)]
     rows, cross = tie((rows, cross))
     mine = [rows] + [shift_up(rows, "x", d) for d in (1, 2, 3)]
 
     sums = project(info, h, (w, up, jnp.concatenate(cross, axis=0), down))
-    keep = jnp.where(yh == 0, sums[0], sums[1])
-    come = swap(jnp.where(yh == 0, sums[1], sums[0]), "yh")
+    keep = jnp.where(yp == 0, sums[0], sums[1])
+    come = swap(jnp.where(yp == 0, sums[1], sums[0]), "yp")
     away, come = tie((mine[1:], come))
-    other = swap(jnp.concatenate([rows] + away, axis=0), "core")
+    (other,) = small_kernel(join_kernel, "join", [(6144, HD)], (rows, *away))
+    other = swap(other, "core")
     cosine, sine = angles_of(base + jnp.arange(192, dtype=jnp.int32))
     cosine = jnp.concatenate([cosine, cosine], axis=1)
     sine = jnp.concatenate([-sine, sine], axis=1)

time: 141 us -> 137 us (0.972)
  blocking collectives: 16.2 us -> 22 us
  starting transfers between devices: 54.3 us -> 48.5 us
  Pallas kernels: 13.2 us -> 15.7 us
  local copies, waits for them, and re-layouts: 4.24 us -> 1.88 us
  other arithmetic: 3.95 us -> 1.91 us
    ppermute x3 -> x2, starting transfers between devices: 16 us -> 5.37 us  [swap(): return lax.ppermute(v, axis, [(0, 1), (1, 0)])]
    all_gather x1, blocking collectives: 16.2 us -> 22 us  [body(): w = lax.all_gather(query_weight, 'yq', axis=0, tiled=True)]
    all_to_all x2, waiting for transfers between devices: 4.09 us -> 8.4 us  [the longest x1 8.4 us: body(): part = lax.all_to_all(part, PAIR, 0, 0, tiled=True)]
    all_gather x1, waiting for transfers between devices: 9.89 us -> 6.22 us  [body(): h = lax.all_gather(h, TP, axis=0, tiled=False)]
    all_to_all x1, starting transfers between devices: 4.94 us -> 8.29 us  [broadcast_gather(): lax.all_to_all(jnp.broadcast_to(x[None], (n,) + x.shape), axis, 0, 0, til...]
    ppermute x4, waiting for transfers between devices: 10.2 us -> 7.61 us  [shift(): return lax.ppermute(v, axis, [(i, (i + by) % n) for i in range(n)])]
    ppermute x3 -> x2, waiting for transfers between devices: 7.29 us -> 4.77 us  [swap(): return lax.ppermute(v, axis, [(0, 1), (1, 0)])]
    all_to_all x1, waiting for transfers between devices: 1.3 us -> 3.81 us  [broadcast_gather(): lax.all_to_all(jnp.broadcast_to(x[None], (n,) + x.shape), axis, 0, 0, til...]
  transfers between devices with their start and end apart: 14 -> 13, of which waited for: 9 -> 8; matrix products, arithmetic and copies ran while one was open for 3% -> 2% of each run, Pallas kernels for 5% -> 4%
where the time goes in v4:
time: 137 us; the launch traced here: 136 us
  starting transfers between devices  48.5 us (35%)
  waiting for transfers between devices  32.2 us (24%)
  blocking collectives  22 us (16%)
  Pallas kernels  15.7 us (11%)
  between operations  13.7 us (10%)
  other arithmetic  1.91 us (1%)
  local copies, waits for them, and re-layouts  1.88 us (1%)
    all_gather x1, blocking collectives, body(): w = lax.all_gather(query_weight, 'yq', axis=0, tiled=True)  22 us
    all_to_all x1, starting transfers between devices, body(): hs = lax.all_to_all(hs, PAIR, 0, 0, tiled=True)  11.7 us
    ppermute x4, starting transfers between devices, shift(): return lax.ppermute(v, axis, [(i, (i + by) % n) for i in range(n)])  11.7 us
    all_to_all x1, waiting for transfers between devices, body(): part = lax.all_to_all(part, PAIR, 0, 0, tiled=True)  8.4 us
    all_to_all x1, starting transfers between devices, broadcast_gather(): lax.all_to_all(jnp.broadcast_to(x[None], (n,) + x.shape), axis, 0, 0, til...  8.29 us
    ppermute x4, waiting for transfers between devices, shift(): return lax.ppermute(v, axis, [(i, (i + by) % n) for i in range(n)])  7.61 us
    all_to_all x1, starting transfers between devices, body(): part = lax.all_to_all(part, PAIR, 0, 0, tiled=True)  7.54 us
    all_gather x1, waiting for transfers between devices, body(): h = lax.all_gather(h, TP, axis=0, tiled=False)  6.22 us
  transfers between devices with their start and end apart: 13, of which 8 were waited for; matrix products, arithmetic and copies ran while one was open for 2% of the time, Pallas kernels for 4%

profile of v4, /device:TPU:6, one launch (start us, length us, event | category | flops | bytes accessed | tf_op | source)
XLA Modules:
  0.0 135.9 jit_solution(3221842424421758259)
XLA Ops:
  8.4 11.7 %all-to-all-start = ((bf16[32,12,512]{2,1,0:T(8,128)(2,1)}), bf16[32,12,512]{2,1,0:T(8,128)(2,1)S(1)}, u32[]{:S(2)}, u32[]{:S(2)}) async-start(bf16[32,12,512]{2,1,0:T(8,128)(2,1)} %slabs.1), calls=%async_computation | async-start | bytes 1048576 | tf_op jit(solution)/shard_map/all_to_all | solution.py:276
  20.3 22.0 %all_gather.9.refs_0_ = bf16[2048,128]{1,0:T(8,128)(2,1)S(1)} all-gather(bf16[512,128]{1,0:T(8,128)(2,1)S(1)} %copy-done.3), channel_id=1, replica_groups=mesh['x'=4,'yq'=4,'yp'=2,'z'=8,'core'=2] {'yq'}, dimensions={0}, use_global_device_ids=true | all-gather | bytes 655360 | tf_op jit(solution)/shard_map/all_gather | solution.py:273
  42.3 1.6 %mix.1 = (bf16[384,512]{1,0:T(8,128)(2,1)}, f32[32,24,128]{2,1,0:T(8,128)}) custom-call(s32[3]{0:T(128)S(1)} %pad_add_fusion.info_ref, bf16[32,12,512]{2,1,0:T(8,128)(2,1)S(1)} %all-to-all-done.x_ref, bf16[1024,256]{1,0:T(8,128)(2,1)S(1)} %copy-done.1), custom_call_target="tpu_custom_call" | custom-call | flops 100663296 | bytes 1048576 | tf_op jit(solution)/shard_map/mix/pallas_call | solution.py:67
  44.0 7.5 %all-to-all-start.1 = ((f32[32,24,128]{2,1,0:T(8,128)}), f32[32,24,128]{2,1,0:T(8,128)S(1)}, u32[]{:S(2)}, u32[]{:S(2)}) async-start(f32[32,24,128]{2,1,0:T(8,128)} %get-tuple-element.23), calls=%async_computation.1 | async-start | bytes 786432 | tf_op jit(solution)/shard_map/all_to_all | solution.py:281
  51.6 2.4 %collective-permute-start = (bf16[2048,128]{1,0:T(8,128)(2,1)S(1)}, bf16[2048,128]{1,0:T(8,128)(2,1)S(1)}, u32[]{:S(2)}, u32[]{:S(2)}) collective-permute-start(bf16[2048,128]{1,0:T(8,128)(2,1)S(1)} %all_gather.9.refs_0_), channel_id=1, source_target_pairs={{0,128},{128,256},{256,384},{384,0},{1,129},{129,257},{257,385},{3... | collective-permute-start | bytes 1572872 | tf_op jit(solution)/shard_map/ppermute | solution.py:254
  54.0 3.5 %collective-permute-start.1 = (bf16[2048,128]{1,0:T(8,128)(2,1)S(1)}, bf16[2048,128]{1,0:T(8,128)(2,1)S(1)}, u32[]{:S(2)}, u32[]{:S(2)}) collective-permute-start(bf16[2048,128]{1,0:T(8,128)(2,1)S(1)} %all_gather.9.refs_0_), channel_id=1, source_target_pairs={{0,384},{128,0},{256,128},{384,256},{1,385},{129,1},{257,129},{385... | collective-permute-start | bytes 1572872 | tf_op jit(solution)/shard_map/ppermute | solution.py:254
  57.4 8.4 %all-to-all-done.1 = f32[32,24,128]{2,1,0:T(8,128)S(1)} async-done(((f32[32,24,128]{2,1,0:T(8,128)}), f32[32,24,128]{2,1,0:T(8,128)S(1)}, u32[]{:S(2)}, u32[]{:S(2)}) %all-to-all-start.1) | async-done | bytes 393248 | tf_op jit(solution)/shard_map/all_to_all | solution.py:281
  66.9 8.3 %all-to-all-start.2 = ((bf16[64,24,128]{2,1,0:T(8,128)(2,1)}), bf16[64,24,128]{2,1,0:T(8,128)(2,1)S(1)}, u32[]{:S(2)}, u32[]{:S(2)}) async-start(bf16[64,24,128]{2,1,0:T(8,128)(2,1)} %broadcast_in_dim.2), calls=%async_computation.2 | async-start | bytes 786432 | tf_op jit(solution)/shard_map/all_to_all | solution.py:40
  75.3 2.4 %collective-permute-start.2 = (bf16[1024,128]{1,0:T(8,128)(2,1)S(1)}, bf16[1024,128]{1,0:T(8,128)(2,1)S(1)}, u32[]{:S(2)}, u32[]{:S(2)}) collective-permute-start(bf16[1024,128]{1,0:T(8,128)(2,1)S(1)} %get-tuple-element.24), channel_id=1, source_target_pairs={{0,128},{128,256},{256,384},{384,0},{1,129},{129,257},{257,385},{3... | collective-permute-start | bytes 786440 | tf_op jit(solution)/shard_map/ppermute | solution.py:254
  77.7 3.5 %collective-permute-start.3 = (bf16[1024,128]{1,0:T(8,128)(2,1)S(1)}, bf16[1024,128]{1,0:T(8,128)(2,1)S(1)}, u32[]{:S(2)}, u32[]{:S(2)}) collective-permute-start(bf16[1024,128]{1,0:T(8,128)(2,1)S(1)} %get-tuple-element.25), channel_id=1, source_target_pairs={{0,384},{128,0},{256,128},{384,256},{1,385},{129,1},{257,129},{385... | collective-permute-start | bytes 786440 | tf_op jit(solution)/shard_map/ppermute | solution.py:254
  81.1 4.3 %collective-permute-done.2 = bf16[1024,128]{1,0:T(8,128)(2,1)S(1)} collective-permute-done((bf16[1024,128]{1,0:T(8,128)(2,1)S(1)}, bf16[1024,128]{1,0:T(8,128)(2,1)S(1)}, u32[]{:S(2)}, u32[]{:S(2)}) %collective-permute-start.2) | collective-permute-done | bytes 262176 | tf_op jit(solution)/shard_map/ppermute | solution.py:254
  85.4 3.3 %collective-permute-done.3 = bf16[1024,128]{1,0:T(8,128)(2,1)S(1)} collective-permute-done((bf16[1024,128]{1,0:T(8,128)(2,1)S(1)}, bf16[1024,128]{1,0:T(8,128)(2,1)S(1)}, u32[]{:S(2)}, u32[]{:S(2)}) %collective-permute-start.3) | collective-permute-done | bytes 262176 | tf_op jit(solution)/shard_map/ppermute | solution.py:254
  88.7 3.8 %all-to-all-done.2 = bf16[64,24,128]{2,1,0:T(8,128)(2,1)S(1)} async-done(((bf16[64,24,128]{2,1,0:T(8,128)(2,1)}), bf16[64,24,128]{2,1,0:T(8,128)(2,1)S(1)}, u32[]{:S(2)}, u32[]{:S(2)}) %all-to-all-start.2) | async-done | bytes 393248 | tf_op jit(solution)/shard_map/all_to_all | solution.py:40
  92.5 1.3 collective-permute-start.4
  93.8 1.3 collective-permute-start.5
  95.1 1.3 collective-permute-start.6
  97.4 6.2 %all-gather.3.cloned.1.call-done = bf16[6144,512]{1,0:T(8,128)(2,1)} async-done(((bf16[384,512]{1,0:T(8,128)(2,1)}), bf16[6144,512]{1,0:T(8,128)(2,1)}) %all-gather.3.cloned.1.call-update) | async-done | bytes 6291472 | tf_op jit(solution)/shard_map/all_gather | solution.py:279
  103.6 6.1 %project.1 = f32[2,192,128]{2,1,0:T(8,128)S(1)} custom-call(s32[3]{0:T(128)S(1)} %pad_add_fusion.info_ref, bf16[16,384,512]{2,1,0:T(8,128)(2,1)} %bitcast.14, bf16[2048,128]{1,0:T(8,128)(2,1)S(1)} %all_gather.9.refs_0_, bf16[2048,128]{1,0:T(8,128)(2,1)S(1)} %collective-permute-done.up_ref.refs_1_, bf16[2048,128]{1,0:T(8,128)(2,1)S(1)} %pad_maximum_fusion.refs_2_, ...), custom_call_target="tpu_custom_call" | custom-call | flops 805306368 | bytes 8388608 | tf_op jit(solution)/shard_map/project/pallas_call | solution.py:209
  109.7 3.4 %collective-permute-start.7 = (f32[192,128]{1,0:T(8,128)S(1)}, f32[192,128]{1,0:T(8,128)S(1)}, u32[]{:S(2)}, u32[]{:S(2)}) collective-permute-start(f32[192,128]{1,0:T(8,128)S(1)} %select_bitcast_fusion), channel_id=1, source_target_pairs={{0,16},{16,0},{1,17},{17,1},{2,18},{18,2},{3,19},{19,3},{4,20},{20... | collective-permute-start | bytes 294920 | tf_op jit(solution)/shard_map/ppermute | solution.py:263
  113.2 1.4 %collective-permute-done.6.refs_3_ = bf16[1536,128]{1,0:T(8,128)(2,1)} collective-permute-done((bf16[1536,128]{1,0:T(8,128)(2,1)S(1)}, bf16[1536,128]{1,0:T(8,128)(2,1)}, u32[]{:S(2)}, u32[]{:S(2)}) %collective-permute-start.6) | collective-permute-done | bytes 393248 | tf_op jit(solution)/shard_map/ppermute | solution.py:259
  114.6 2.0 %collective-permute-done.7 = f32[192,128]{1,0:T(8,128)S(1)} collective-permute-done((f32[192,128]{1,0:T(8,128)S(1)}, f32[192,128]{1,0:T(8,128)S(1)}, u32[]{:S(2)}, u32[]{:S(2)}) %collective-permute-start.7) | collective-permute-done | bytes 98336 | tf_op jit(solution)/shard_map/ppermute | solution.py:263
  117.7 1.9 %collective-permute-start.8 = (bf16[6144,128]{1,0:T(8,128)(2,1)S(1)}, bf16[6144,128]{1,0:T(8,128)(2,1)S(1)}, u32[]{:S(2)}, u32[]{:S(2)}) collective-permute-start(bf16[6144,128]{1,0:T(8,128)(2,1)S(1)} %join.1), channel_id=1, source_target_pairs={{0,1},{1,0},{2,3},{3,2},{4,5},{5,4},{6,7},{7,6},{8,9},{9,8},{10,11... | collective-permute-start | bytes 4718600 | tf_op jit(solution)/shard_map/ppermute | solution.py:263
  120.2 2.8 %collective-permute-done.8.refs_4_ = bf16[6144,128]{1,0:T(8,128)(2,1)S(1)} collective-permute-done((bf16[6144,128]{1,0:T(8,128)(2,1)S(1)}, bf16[6144,128]{1,0:T(8,128)(2,1)S(1)}, u32[]{:S(2)}, u32[]{:S(2)}) %collective-permute-start.8) | collective-permute-done | bytes 1572896 | tf_op jit(solution)/shard_map/ppermute | solution.py:263
  123.0 6.0 %attend.1 = bf16[192,128]{1,0:T(8,128)(2,1)} custom-call(s32[3]{0:T(128)S(1)} %pad_add_fusion.info_ref, f32[192,128]{1,0:T(8,128)S(1)} %bitcast_add_fusion.q_ref, f32[192,128]{1,0:T(8,128)S(1)} %get-tuple-element.38.cos_ref, f32[192,128]{1,0:T(8,128)S(1)} %get-tuple-element.39.sin_ref, bf16[1536,128]{1,0:T(8,128)(2,1)S(1)} %bitcast.13, ...), custom_call_target="tpu_custom_call" | custom-call | flops 603979776 | bytes 3145728 | tf_op jit(solution)/shard_map/attend/pallas_call | solution.py:231
  (31 shorter events, 5.8 us)
Async XLA Ops:
  6.5 1.0 copy-start
  7.6 12.7 %copy-start.3 = (bf16[512,128]{1,0:T(8,128)(2,1)S(1)}, bf16[512,128]{1,0:T(8,128)(2,1)}, u32[]{:S(2)}) copy-start(bf16[512,128]{1,0:T(8,128)(2,1)} %param.4) | copy-start | bytes 393220
  7.6 34.7 %copy-start.1 = (bf16[1024,256]{1,0:T(8,128)(2,1)S(1)}, bf16[1024,256]{1,0:T(8,128)(2,1)}, u32[]{:S(2)}) copy-start(bf16[1024,256]{1,0:T(8,128)(2,1)} %w_ref.1) | copy-start | bytes 1572868
  8.4 33.9 %all-to-all-start = ((bf16[32,12,512]{2,1,0:T(8,128)(2,1)}), bf16[32,12,512]{2,1,0:T(8,128)(2,1)S(1)}, u32[]{:S(2)}, u32[]{:S(2)}) async-start(bf16[32,12,512]{2,1,0:T(8,128)(2,1)} %slabs.1), calls=%async_computation | async-start | bytes 1048576 | tf_op jit(solution)/shard_map/all_to_all | solution.py:276
  20.1 83.5 %all-gather.3.cloned.1.call-start = ((), (), s32[]{:S(2)}) async-start(), calls=%async_computation.3 | async-start | bytes 6684672 | tf_op jit(solution)/shard_map/all_gather | solution.py:279
  44.0 21.9 %all-to-all-start.1 = ((f32[32,24,128]{2,1,0:T(8,128)}), f32[32,24,128]{2,1,0:T(8,128)S(1)}, u32[]{:S(2)}, u32[]{:S(2)}) async-start(f32[32,24,128]{2,1,0:T(8,128)} %get-tuple-element.23), calls=%async_computation.1 | async-start | bytes 786432 | tf_op jit(solution)/shard_map/all_to_all | solution.py:281
  51.6 23.6 %collective-permute-start = (bf16[2048,128]{1,0:T(8,128)(2,1)S(1)}, bf16[2048,128]{1,0:T(8,128)(2,1)S(1)}, u32[]{:S(2)}, u32[]{:S(2)}) collective-permute-start(bf16[2048,128]{1,0:T(8,128)(2,1)S(1)} %all_gather.9.refs_0_), channel_id=1, source_target_pairs={{0,128},{128,256},{256,384},{384,0},{1,129},{129,257},{257,385},{3... | collective-permute-start | bytes 1572872 | tf_op jit(solution)/shard_map/ppermute | solution.py:254
  54.0 21.3 %collective-permute-start.1 = (bf16[2048,128]{1,0:T(8,128)(2,1)S(1)}, bf16[2048,128]{1,0:T(8,128)(2,1)S(1)}, u32[]{:S(2)}, u32[]{:S(2)}) collective-permute-start(bf16[2048,128]{1,0:T(8,128)(2,1)S(1)} %all_gather.9.refs_0_), channel_id=1, source_target_pairs={{0,384},{128,0},{256,128},{384,256},{1,385},{129,1},{257,129},{385... | collective-permute-start | bytes 1572872 | tf_op jit(solution)/shard_map/ppermute | solution.py:254
  66.9 25.6 %all-to-all-start.2 = ((bf16[64,24,128]{2,1,0:T(8,128)(2,1)}), bf16[64,24,128]{2,1,0:T(8,128)(2,1)S(1)}, u32[]{:S(2)}, u32[]{:S(2)}) async-start(bf16[64,24,128]{2,1,0:T(8,128)(2,1)} %broadcast_in_dim.2), calls=%async_computation.2 | async-start | bytes 786432 | tf_op jit(solution)/shard_map/all_to_all | solution.py:40
  75.3 10.1 %collective-permute-start.2 = (bf16[1024,128]{1,0:T(8,128)(2,1)S(1)}, bf16[1024,128]{1,0:T(8,128)(2,1)S(1)}, u32[]{:S(2)}, u32[]{:S(2)}) collective-permute-start(bf16[1024,128]{1,0:T(8,128)(2,1)S(1)} %get-tuple-element.24), channel_id=1, source_target_pairs={{0,128},{128,256},{256,384},{384,0},{1,129},{129,257},{257,385},{3... | collective-permute-start | bytes 786440 | tf_op jit(solution)/shard_map/ppermute | solution.py:254
  77.7 11.1 %collective-permute-start.3 = (bf16[1024,128]{1,0:T(8,128)(2,1)S(1)}, bf16[1024,128]{1,0:T(8,128)(2,1)S(1)}, u32[]{:S(2)}, u32[]{:S(2)}) collective-permute-start(bf16[1024,128]{1,0:T(8,128)(2,1)S(1)} %get-tuple-element.25), channel_id=1, source_target_pairs={{0,384},{128,0},{256,128},{384,256},{1,385},{129,1},{257,129},{385... | collective-permute-start | bytes 786440 | tf_op jit(solution)/shard_map/ppermute | solution.py:254
  88.7 3.8 %copy-start.2 = (bf16[1024,128]{1,0:T(8,128)(2,1)}, bf16[1024,128]{1,0:T(8,128)(2,1)S(1)}, u32[]{:S(2)}) copy-start(bf16[1024,128]{1,0:T(8,128)(2,1)S(1)} %collective-permute-done.3) | copy-start | bytes 786436
  92.5 20.7 %collective-permute-start.4 = (bf16[1536,128]{1,0:T(8,128)(2,1)S(1)}, bf16[1536,128]{1,0:T(8,128)(2,1)S(1)}, u32[]{:S(2)}, u32[]{:S(2)}) collective-permute-start(bf16[1536,128]{1,0:T(8,128)(2,1)S(1)} %bitcast.9), channel_id=1, source_target_pairs={{0,128},{128,256},{256,384},{1,129},{129,257},{257,385},{2,130},{1... | collective-permute-start | bytes 1179656 | tf_op jit(solution)/shard_map/ppermute | solution.py:259
  93.8 19.4 %collective-permute-start.5 = (bf16[1536,128]{1,0:T(8,128)(2,1)S(1)}, bf16[1536,128]{1,0:T(8,128)(2,1)S(1)}, u32[]{:S(2)}, u32[]{:S(2)}) collective-permute-start(bf16[1536,128]{1,0:T(8,128)(2,1)S(1)} %bitcast.10), channel_id=1, source_target_pairs={{0,256},{128,384},{1,257},{129,385},{2,258},{130,386},{3,259},{131... | collective-permute-start | bytes 1179656 | tf_op jit(solution)/shard_map/ppermute | solution.py:259
  95.1 19.5 %collective-permute-start.6 = (bf16[1536,128]{1,0:T(8,128)(2,1)S(1)}, bf16[1536,128]{1,0:T(8,128)(2,1)}, u32[]{:S(2)}, u32[]{:S(2)}) collective-permute-start(bf16[1536,128]{1,0:T(8,128)(2,1)S(1)} %bitcast.11), channel_id=1, source_target_pairs={{0,384},{1,385},{2,386},{3,387},{4,388},{5,389},{6,390},{7,391},{8... | collective-permute-start | bytes 1179656 | tf_op jit(solution)/shard_map/ppermute | solution.py:259
  109.7 6.8 %collective-permute-start.7 = (f32[192,128]{1,0:T(8,128)S(1)}, f32[192,128]{1,0:T(8,128)S(1)}, u32[]{:S(2)}, u32[]{:S(2)}) collective-permute-start(f32[192,128]{1,0:T(8,128)S(1)} %select_bitcast_fusion), channel_id=1, source_target_pairs={{0,16},{16,0},{1,17},{17,1},{2,18},{18,2},{3,19},{19,3},{4,20},{20... | collective-permute-start | bytes 294920 | tf_op jit(solution)/shard_map/ppermute | solution.py:263
  117.7 5.3 %collective-permute-start.8 = (bf16[6144,128]{1,0:T(8,128)(2,1)S(1)}, bf16[6144,128]{1,0:T(8,128)(2,1)S(1)}, u32[]{:S(2)}, u32[]{:S(2)}) collective-permute-start(bf16[6144,128]{1,0:T(8,128)(2,1)S(1)} %join.1), channel_id=1, source_target_pairs={{0,1},{1,0},{2,3},{3,2},{4,5},{5,4},{6,7},{7,6},{8,9},{9,8},{10,11... | collective-permute-start | bytes 4718600 | tf_op jit(solution)/shard_map/ppermute | solution.py:263
Sparse Core Ops, SparseCore 0:
  44.1 59.5 all-gather.2

commit v5 on v4

--- a/solution.py
+++ b/solution.py
@@ -108,26 +108,24 @@
 
 
 def project_kernel(info_ref, h_ref, *refs):
-    w_refs, o_ref, h_buf, w_buf, sems = refs[:4], *refs[4:]
-    x = info_ref[0]
+    w_refs, o_ref, buf, sems = refs[:4], *refs[4:]
+    x, yq = info_ref[0], info_ref[1] // 2
     copies = []
     for n in range(4):
-        at = lax.rem(x + 4 - n, 4) * 4
-        copies.append(
-            (
-                pltpu.make_async_copy(h_ref.at[pl.ds(at, 4)], h_buf.at[n], sems.at[n, 0]),
-                pltpu.make_async_copy(w_refs[n], w_buf.at[n], sems.at[n, 1]),
-            )
-        )
-        for copy in copies[n]:
-            copy.start()
+        for back in range(4):
+            block = lax.rem(x + 4 - n, 4) * 4 + lax.rem(yq + 4 - back, 4)
+            i = 4 * n + back
+            copies.append(pltpu.make_async_copy(h_ref.at[block], buf.at[i], sems.at[i]))
+            copies[-1].start()
     total = None
     for n in range(4):
-        for copy in copies[n]:
-            copy.wait()
-        a = jnp.concatenate([h_buf[n, i] for i in range(4)], axis=1)
-        term = jnp.dot(a, w_buf[n], preferred_element_type=jnp.float32)
-        total = term if total is None else total + term
+        for half in range(2):
+            for i in range(2):
+                copies[4 * n + 2 * half + i].wait()
+            a = jnp.concatenate([buf[4 * n + 2 * half + i] for i in range(2)], axis=1)
+            w = w_refs[n][half * 1024 : (half + 1) * 1024]
+            term = jnp.dot(a, w, preferred_element_type=jnp.float32)
+            total = term if total is None else total + term
     for sel in range(2):
         o_ref[sel] = total[sel * 192 : (sel + 1) * 192]
 
@@ -205,18 +203,21 @@
 
 def project(info, h, pieces):
     count, m, part = h.shape
-    hbm = pl.BlockSpec(memory_space=pl.ANY)
+    vm = pl.BlockSpec(memory_space=pltpu.VMEM)
     return pl.pallas_call(
         project_kernel,
-        in_specs=[pl.BlockSpec(memory_space=pltpu.SMEM)] + [hbm] * 5,
-        out_specs=pl.BlockSpec(memory_space=pltpu.VMEM),
+        in_specs=[
+            pl.BlockSpec(memory_space=pltpu.SMEM),
+            pl.BlockSpec(memory_space=pl.ANY),
+        ]
+        + [vm] * 4,
+        out_specs=vm,
         out_shape=jax.ShapeDtypeStruct((2, m // 2, HD), jnp.float32),
         scratch_shapes=[
-            pltpu.VMEM((4, count // 4, m, part), jnp.bfloat16),
-            pltpu.VMEM((4, count // 4 * part, HD), jnp.bfloat16),
-            pltpu.SemaphoreType.DMA((4, 2)),
+            pltpu.VMEM(h.shape, jnp.bfloat16),
+            pltpu.SemaphoreType.DMA((count,)),
         ],
-        compiler_params=pltpu.CompilerParams(vmem_limit_bytes=48 * 2**20),
+        compiler_params=pltpu.CompilerParams(vmem_limit_bytes=32 * 2**20),
         cost_estimate=pl.CostEstimate(
             flops=2 * m * count * part * HD,
             bytes_accessed=2 * count * part * (m + HD),
@@ -270,12 +271,13 @@
     info = jnp.stack([x, y, core])
     tie = lax.optimization_barrier
 
-    w = lax.all_gather(query_weight, "yq", axis=0, tiled=True)
-
     (hs,) = small_kernel(slabs_kernel, "slabs", [(32, 12, 512)], (hidden,))
+    hs, w = tie((hs, query_weight))
     hs = lax.all_to_all(hs, PAIR, 0, 0, tiled=True)
+
+    w = jnp.concatenate([w] + [shift(w, "yq", d) for d in (1, 2, 3)], axis=0)
     h, part = mix(info, hs, kv_weight)
-    h, w, part = tie((h, w, part))
+    w, part = tie((w, part))
     h = lax.all_gather(h, TP, axis=0, tiled=False)
 
     part = lax.all_to_all(part, PAIR, 0, 0, tiled=True)
@@ -292,7 +294,7 @@
     sums = project(info, h, (w, up, jnp.concatenate(cross, axis=0), down))
     keep = jnp.where(yp == 0, sums[0], sums[1])
     come = swap(jnp.where(yp == 0, sums[1], sums[0]), "yp")
-    away, come = tie((mine[1:], come))
+    away, sums = tie((mine[1:], sums))
     (other,) = small_kernel(join_kernel, "join", [(6144, HD)], (rows, *away))
     other = swap(other, "core")
     cosine, sine = angles_of(base + jnp.arange(192, dtype=jnp.int32))

time: 137 us -> 155 us (1.13)
  waiting for transfers between devices: 32.2 us -> 54.6 us
  blocking collectives: 22 us -> 0 us
  starting transfers between devices: 48.5 us -> 59.9 us
  local copies, waits for them, and re-layouts: 1.88 us -> 4.63 us
  Pallas kernels: 15.7 us -> 17.8 us
    all_gather x1 -> x0, blocking collectives: 22 us -> none  [body(): w = lax.all_gather(query_weight, 'yq', axis=0, tiled=True)]
    all_to_all x1, waiting for transfers between devices: 0.01 us -> 15.7 us  [body(): hs = lax.all_to_all(hs, PAIR, 0, 0, tiled=True)]
    ppermute x4 -> x7, starting transfers between devices: 11.7 us -> 26.5 us  [shift(): return lax.ppermute(v, axis, [(i, (i + by) % n) for i in range(n)])]
    ppermute x4 -> x7, waiting for transfers between devices: 7.61 us -> 16 us  [shift(): return lax.ppermute(v, axis, [(i, (i + by) % n) for i in range(n)])]
    all_gather x1, waiting for transfers between devices: 6.22 us -> 0.02 us  [body(): h = lax.all_gather(h, TP, axis=0, tiled=False)]
    ppermute x3, waiting for transfers between devices: 1.39 us -> 5.34 us  [shift_up(): return lax.ppermute(v, axis, [(i, i + by) for i in range(n - by)])]
    all_to_all x1, starting transfers between devices: 7.54 us -> 4.31 us  [body(): part = lax.all_to_all(part, PAIR, 0, 0, tiled=True)]
    unnamed x8, local copies, waits for them, and re-layouts: 1.05 us -> 3.83 us
  transfers between devices with their start and end apart: 13 -> 16, of which waited for: 8 -> 9; matrix products, arithmetic and copies ran while one was open for 2% -> 2% of each run, Pallas kernels for 4% -> 5%
where the time goes in v5:
time: 155 us; the launch traced here: 153 us
  starting transfers between devices  59.9 us (39%)
  waiting for transfers between devices  54.6 us (35%)
  Pallas kernels  17.8 us (11%)
  between operations  13.7 us (9%)
  local copies, waits for them, and re-layouts  4.63 us (3%)
  other arithmetic  2.02 us (1%)
    ppermute x7, starting transfers between devices, shift(): return lax.ppermute(v, axis, [(i, (i + by) % n) for i in range(n)])  26.5 us
    ppermute x7, waiting for transfers between devices, shift(): return lax.ppermute(v, axis, [(i, (i + by) % n) for i in range(n)])  16 us
    all_to_all x1, waiting for transfers between devices, body(): hs = lax.all_to_all(hs, PAIR, 0, 0, tiled=True)  15.7 us
    all_to_all x1, starting transfers between devices, body(): hs = lax.all_to_all(hs, PAIR, 0, 0, tiled=True)  11.7 us
    all_to_all x1, waiting for transfers between devices, body(): part = lax.all_to_all(part, PAIR, 0, 0, tiled=True)  9.89 us
    all_to_all x1, starting transfers between devices, broadcast_gather(): lax.all_to_all(jnp.broadcast_to(x[None], (n,) + x.shape), axis, 0, 0, til...  8.68 us
    pallas_call x1, Pallas kernels, project(): pl.pallas_call(project_kernel, in_specs=[pl.BlockSpec(memory_space=pltpu....  7.52 us
    pallas_call x1, Pallas kernels, attend(): pl.pallas_call(attend_kernel, in_specs=[pl.BlockSpec(memory_space=pltpu.S...  5.58 us
  transfers between devices with their start and end apart: 16, of which 9 were waited for; matrix products, arithmetic and copies ran while one was open for 2% of the time, Pallas kernels for 5%

profile of v5, /device:TPU:6, one launch (start us, length us, event | category | flops | bytes accessed | tf_op | source)
XLA Modules:
  0.0 152.7 jit_solution(15170132313196474292)
XLA Ops:
  8.4 11.7 %all-to-all-start = ((bf16[32,12,512]{2,1,0:T(8,128)(2,1)}), bf16[32,12,512]{2,1,0:T(8,128)(2,1)S(1)}, u32[]{:S(2)}, u32[]{:S(2)}) async-start(bf16[32,12,512]{2,1,0:T(8,128)(2,1)} %slabs.1), calls=%async_computation | async-start | bytes 1048576 | tf_op jit(solution)/shard_map/all_to_all | solution.py:276
  20.3 15.7 %all-to-all-done.x_ref = bf16[32,12,512]{2,1,0:T(8,128)(2,1)S(1)} async-done(((bf16[32,12,512]{2,1,0:T(8,128)(2,1)}), bf16[32,12,512]{2,1,0:T(8,128)(2,1)S(1)}, u32[]{:S(2)}, u32[]{:S(2)}) %all-to-all-start) | async-done | bytes 393248 | tf_op jit(solution)/shard_map/all_to_all | solution.py:276
  37.7 4.5 %collective-permute-start = (bf16[512,128]{1,0:T(8,128)(2,1)S(1)}, bf16[512,128]{1,0:T(8,128)(2,1)S(1)}, u32[]{:S(2)}, u32[]{:S(2)}) collective-permute-start(bf16[512,128]{1,0:T(8,128)(2,1)S(1)} %copy-done.3), channel_id=1, source_target_pairs={{0,32},{32,64},{64,96},{96,0},{1,33},{33,65},{65,97},{97,1},{2,34}... | collective-permute-start | bytes 393224 | tf_op jit(solution)/shard_map/ppermute | solution.py:255
  42.2 5.0 %collective-permute-start.1 = (bf16[512,128]{1,0:T(8,128)(2,1)S(1)}, bf16[512,128]{1,0:T(8,128)(2,1)S(1)}, u32[]{:S(2)}, u32[]{:S(2)}) collective-permute-start(bf16[512,128]{1,0:T(8,128)(2,1)S(1)} %copy-done.3), channel_id=1, source_target_pairs={{0,64},{32,96},{64,0},{96,32},{1,65},{33,97},{65,1},{97,33},{2,66}... | collective-permute-start | bytes 393224 | tf_op jit(solution)/shard_map/ppermute | solution.py:255
  47.2 5.3 %collective-permute-start.2 = (bf16[512,128]{1,0:T(8,128)(2,1)S(1)}, bf16[512,128]{1,0:T(8,128)(2,1)S(1)}, u32[]{:S(2)}, u32[]{:S(2)}) collective-permute-start(bf16[512,128]{1,0:T(8,128)(2,1)S(1)} %copy-done.3), channel_id=1, source_target_pairs={{0,96},{32,0},{64,32},{96,64},{1,97},{33,1},{65,33},{97,65},{2,98}... | collective-permute-start | bytes 393224 | tf_op jit(solution)/shard_map/ppermute | solution.py:255
  52.5 4.0 %collective-permute-done.1 = bf16[512,128]{1,0:T(8,128)(2,1)S(1)} collective-permute-done((bf16[512,128]{1,0:T(8,128)(2,1)S(1)}, bf16[512,128]{1,0:T(8,128)(2,1)S(1)}, u32[]{:S(2)}, u32[]{:S(2)}) %collective-permute-start.1) | collective-permute-done | bytes 131104 | tf_op jit(solution)/shard_map/ppermute | solution.py:255
  56.5 4.1 %collective-permute-done.2 = bf16[512,128]{1,0:T(8,128)(2,1)S(1)} collective-permute-done((bf16[512,128]{1,0:T(8,128)(2,1)S(1)}, bf16[512,128]{1,0:T(8,128)(2,1)S(1)}, u32[]{:S(2)}, u32[]{:S(2)}) %collective-permute-start.2) | collective-permute-done | bytes 131104 | tf_op jit(solution)/shard_map/ppermute | solution.py:255
  60.7 4.3 %all-to-all-start.1 = ((f32[32,24,128]{2,1,0:T(8,128)}), f32[32,24,128]{2,1,0:T(8,128)S(1)}, u32[]{:S(2)}, u32[]{:S(2)}) async-start(f32[32,24,128]{2,1,0:T(8,128)} %get-tuple-element.24), calls=%async_computation.1 | async-start | bytes 786432 | tf_op jit(solution)/shard_map/all_to_all | solution.py:283
  65.0 2.4 %collective-permute-start.3 = (bf16[2048,128]{1,0:T(8,128)(2,1)S(1)}, bf16[2048,128]{1,0:T(8,128)(2,1)S(1)}, u32[]{:S(2)}, u32[]{:S(2)}) collective-permute-start(bf16[2048,128]{1,0:T(8,128)(2,1)S(1)} %pad_maximum_fusion.refs_0_), channel_id=1, source_target_pairs={{0,128},{128,256},{256,384},{384,0},{1,129},{129,257},{257,385},{3... | collective-permute-start | bytes 1572872 | tf_op jit(solution)/shard_map/ppermute | solution.py:255
  67.4 3.5 %collective-permute-start.4 = (bf16[2048,128]{1,0:T(8,128)(2,1)S(1)}, bf16[2048,128]{1,0:T(8,128)(2,1)S(1)}, u32[]{:S(2)}, u32[]{:S(2)}) collective-permute-start(bf16[2048,128]{1,0:T(8,128)(2,1)S(1)} %pad_maximum_fusion.refs_0_), channel_id=1, source_target_pairs={{0,384},{128,0},{256,128},{384,256},{1,385},{129,1},{257,129},{385... | collective-permute-start | bytes 1572872 | tf_op jit(solution)/shard_map/ppermute | solution.py:255
  70.9 9.9 %all-to-all-done.1 = f32[32,24,128]{2,1,0:T(8,128)S(1)} async-done(((f32[32,24,128]{2,1,0:T(8,128)}), f32[32,24,128]{2,1,0:T(8,128)S(1)}, u32[]{:S(2)}, u32[]{:S(2)}) %all-to-all-start.1) | async-done | bytes 393248 | tf_op jit(solution)/shard_map/all_to_all | solution.py:283
  81.8 8.7 %all-to-all-start.2 = ((bf16[64,24,128]{2,1,0:T(8,128)(2,1)}), bf16[64,24,128]{2,1,0:T(8,128)(2,1)S(1)}, u32[]{:S(2)}, u32[]{:S(2)}) async-start(bf16[64,24,128]{2,1,0:T(8,128)(2,1)} %broadcast_in_dim.2), calls=%async_computation.2 | async-start | bytes 786432 | tf_op jit(solution)/shard_map/all_to_all | solution.py:40
  90.6 2.4 %collective-permute-start.5 = (bf16[1024,128]{1,0:T(8,128)(2,1)S(1)}, bf16[1024,128]{1,0:T(8,128)(2,1)}, u32[]{:S(2)}, u32[]{:S(2)}) collective-permute-start(bf16[1024,128]{1,0:T(8,128)(2,1)S(1)} %get-tuple-element.25), channel_id=1, source_target_pairs={{0,128},{128,256},{256,384},{384,0},{1,129},{129,257},{257,385},{3... | collective-permute-start | bytes 786440 | tf_op jit(solution)/shard_map/ppermute | solution.py:255
  93.0 3.5 %collective-permute-start.6 = (bf16[1024,128]{1,0:T(8,128)(2,1)S(1)}, bf16[1024,128]{1,0:T(8,128)(2,1)}, u32[]{:S(2)}, u32[]{:S(2)}) collective-permute-start(bf16[1024,128]{1,0:T(8,128)(2,1)S(1)} %get-tuple-element.26), channel_id=1, source_target_pairs={{0,384},{128,0},{256,128},{384,256},{1,385},{129,1},{257,129},{385... | collective-permute-start | bytes 786440 | tf_op jit(solution)/shard_map/ppermute | solution.py:255
  96.5 4.5 %collective-permute-done.5 = bf16[1024,128]{1,0:T(8,128)(2,1)} collective-permute-done((bf16[1024,128]{1,0:T(8,128)(2,1)S(1)}, bf16[1024,128]{1,0:T(8,128)(2,1)}, u32[]{:S(2)}, u32[]{:S(2)}) %collective-permute-start.5) | collective-permute-done | bytes 262176 | tf_op jit(solution)/shard_map/ppermute | solution.py:255
  100.9 3.3 %collective-permute-done.6 = bf16[1024,128]{1,0:T(8,128)(2,1)} collective-permute-done((bf16[1024,128]{1,0:T(8,128)(2,1)S(1)}, bf16[1024,128]{1,0:T(8,128)(2,1)}, u32[]{:S(2)}, u32[]{:S(2)}) %collective-permute-start.6) | collective-permute-done | bytes 262176 | tf_op jit(solution)/shard_map/ppermute | solution.py:255
  104.3 3.5 %all-to-all-done.2 = bf16[64,24,128]{2,1,0:T(8,128)(2,1)S(1)} async-done(((bf16[64,24,128]{2,1,0:T(8,128)(2,1)}), bf16[64,24,128]{2,1,0:T(8,128)(2,1)S(1)}, u32[]{:S(2)}, u32[]{:S(2)}) %all-to-all-start.2) | async-done | bytes 393248 | tf_op jit(solution)/shard_map/all_to_all | solution.py:40
  112.8 2.8 %copy-done = bf16[6144,512]{1,0:T(8,128)(2,1)S(1)} copy-done((bf16[6144,512]{1,0:T(8,128)(2,1)S(1)}, bf16[6144,512]{1,0:T(8,128)(2,1)}, u32[]{:S(2)}) %copy-start) | copy-done | bytes 6291480
  115.6 7.5 %project.1 = f32[2,192,128]{2,1,0:T(8,128)S(1)} custom-call(s32[3]{0:T(128)S(1)} %pad_add_fusion.info_ref, bf16[16,384,512]{2,1,0:T(8,128)(2,1)S(1)} %bitcast.9, bf16[2048,128]{1,0:T(8,128)(2,1)S(1)} %pad_maximum_fusion.refs_0_, bf16[2048,128]{1,0:T(8,128)(2,1)S(1)} %collective-permute-done.3.up_ref.refs_1_, ...), custom_call_target="tpu_custom_call" | custom-call | flops 805306368 | bytes 8388608 | tf_op jit(solution)/shard_map/project/pallas_call | solution.py:207
  123.1 5.3 %collective-permute-done.10.refs_3_ = bf16[1536,128]{1,0:T(8,128)(2,1)S(1)} collective-permute-done((bf16[1536,128]{1,0:T(8,128)(2,1)S(1)}, bf16[1536,128]{1,0:T(8,128)(2,1)S(1)}, u32[]{:S(2)}, u32[]{:S(2)}) %collective-permute-start.10) | collective-permute-done | bytes 393248 | tf_op jit(solution)/shard_map/ppermute | solution.py:260
  128.5 2.3 %join.1 = bf16[6144,128]{1,0:T(8,128)(2,1)} custom-call(bf16[1536,128]{1,0:T(8,128)(2,1)S(1)} %bitcast.13, bf16[1536,128]{1,0:T(8,128)(2,1)S(1)} %collective-permute-done.8.refs_1_, bf16[1536,128]{1,0:T(8,128)(2,1)} %collective-permute-done.9.refs_2_, bf16[1536,128]{1,0:T(8,128)(2,1)S(1)} %collective-permute-done.10.refs_3_), custom_call_target="tpu_custom_call" | custom-call | bytes 1048576 | tf_op jit(solution)/shard_map/join/pallas_call | solution.py:99
  133.1 2.9 %collective-permute-start.7 = (f32[192,128]{1,0:T(8,128)S(1)}, f32[192,128]{1,0:T(8,128)S(1)}, u32[]{:S(2)}, u32[]{:S(2)}) collective-permute-start(f32[192,128]{1,0:T(8,128)S(1)} %select_bitcast_fusion), channel_id=1, source_target_pairs={{0,16},{16,0},{1,17},{17,1},{2,18},{18,2},{3,19},{19,3},{4,20},{20... | collective-permute-start | bytes 294920 | tf_op jit(solution)/shard_map/ppermute | solution.py:264
  136.1 4.1 %collective-permute-done.7 = f32[192,128]{1,0:T(8,128)S(1)} collective-permute-done((f32[192,128]{1,0:T(8,128)S(1)}, f32[192,128]{1,0:T(8,128)S(1)}, u32[]{:S(2)}, u32[]{:S(2)}) %collective-permute-start.7) | collective-permute-done | bytes 98336 | tf_op jit(solution)/shard_map/ppermute | solution.py:264
  140.2 5.6 %attend.1 = bf16[192,128]{1,0:T(8,128)(2,1)} custom-call(s32[3]{0:T(128)S(1)} %pad_add_fusion.info_ref, f32[192,128]{1,0:T(8,128)S(1)} %bitcast_add_fusion.q_ref, f32[192,128]{1,0:T(8,128)S(1)} %get-tuple-element.38.cos_ref, f32[192,128]{1,0:T(8,128)S(1)} %get-tuple-element.39.sin_ref, bf16[1536,128]{1,0:T(8,128)(2,1)S(1)} %bitcast.14, ...), custom_call_target="tpu_custom_call" | custom-call | flops 603979776 | bytes 3145728 | tf_op jit(solution)/shard_map/attend/pallas_call | solution.py:232
  (37 shorter events, 12.2 us)
Async XLA Ops:
  6.5 1.0 copy-start.1
  7.6 28.5 %copy-start.2 = (bf16[1024,256]{1,0:T(8,128)(2,1)S(1)}, bf16[1024,256]{1,0:T(8,128)(2,1)}, u32[]{:S(2)}) copy-start(bf16[1024,256]{1,0:T(8,128)(2,1)} %w_ref.1) | copy-start | bytes 1572868
  7.6 30.1 %copy-start.3 = (bf16[512,128]{1,0:T(8,128)(2,1)S(1)}, bf16[512,128]{1,0:T(8,128)(2,1)}, u32[]{:S(2)}) copy-start(bf16[512,128]{1,0:T(8,128)(2,1)} %param.4) | copy-start | bytes 393220
  8.4 27.6 %all-to-all-start = ((bf16[32,12,512]{2,1,0:T(8,128)(2,1)}), bf16[32,12,512]{2,1,0:T(8,128)(2,1)S(1)}, u32[]{:S(2)}, u32[]{:S(2)}) async-start(bf16[32,12,512]{2,1,0:T(8,128)(2,1)} %slabs.1), calls=%async_computation | async-start | bytes 1048576 | tf_op jit(solution)/shard_map/all_to_all | solution.py:276
  20.2 92.6 %all-gather.3.cloned.1.call-start = ((), (), s32[]{:S(2)}) async-start(), calls=%async_computation.3 | async-start | bytes 6684672 | tf_op jit(solution)/shard_map/all_gather | solution.py:281
  37.7 14.8 %collective-permute-start = (bf16[512,128]{1,0:T(8,128)(2,1)S(1)}, bf16[512,128]{1,0:T(8,128)(2,1)S(1)}, u32[]{:S(2)}, u32[]{:S(2)}) collective-permute-start(bf16[512,128]{1,0:T(8,128)(2,1)S(1)} %copy-done.3), channel_id=1, source_target_pairs={{0,32},{32,64},{64,96},{96,0},{1,33},{33,65},{65,97},{97,1},{2,34}... | collective-permute-start | bytes 393224 | tf_op jit(solution)/shard_map/ppermute | solution.py:255
  42.2 14.3 %collective-permute-start.1 = (bf16[512,128]{1,0:T(8,128)(2,1)S(1)}, bf16[512,128]{1,0:T(8,128)(2,1)S(1)}, u32[]{:S(2)}, u32[]{:S(2)}) collective-permute-start(bf16[512,128]{1,0:T(8,128)(2,1)S(1)} %copy-done.3), channel_id=1, source_target_pairs={{0,64},{32,96},{64,0},{96,32},{1,65},{33,97},{65,1},{97,33},{2,66}... | collective-permute-start | bytes 393224 | tf_op jit(solution)/shard_map/ppermute | solution.py:255
  47.2 13.4 %collective-permute-start.2 = (bf16[512,128]{1,0:T(8,128)(2,1)S(1)}, bf16[512,128]{1,0:T(8,128)(2,1)S(1)}, u32[]{:S(2)}, u32[]{:S(2)}) collective-permute-start(bf16[512,128]{1,0:T(8,128)(2,1)S(1)} %copy-done.3), channel_id=1, source_target_pairs={{0,96},{32,0},{64,32},{96,64},{1,97},{33,1},{65,33},{97,65},{2,98}... | collective-permute-start | bytes 393224 | tf_op jit(solution)/shard_map/ppermute | solution.py:255
  60.7 20.1 %all-to-all-start.1 = ((f32[32,24,128]{2,1,0:T(8,128)}), f32[32,24,128]{2,1,0:T(8,128)S(1)}, u32[]{:S(2)}, u32[]{:S(2)}) async-start(f32[32,24,128]{2,1,0:T(8,128)} %get-tuple-element.24), calls=%async_computation.1 | async-start | bytes 786432 | tf_op jit(solution)/shard_map/all_to_all | solution.py:283
  65.0 25.5 %collective-permute-start.3 = (bf16[2048,128]{1,0:T(8,128)(2,1)S(1)}, bf16[2048,128]{1,0:T(8,128)(2,1)S(1)}, u32[]{:S(2)}, u32[]{:S(2)}) collective-permute-start(bf16[2048,128]{1,0:T(8,128)(2,1)S(1)} %pad_maximum_fusion.refs_0_), channel_id=1, source_target_pairs={{0,128},{128,256},{256,384},{384,0},{1,129},{129,257},{257,385},{3... | collective-permute-start | bytes 1572872 | tf_op jit(solution)/shard_map/ppermute | solution.py:255
  67.4 23.1 %collective-permute-start.4 = (bf16[2048,128]{1,0:T(8,128)(2,1)S(1)}, bf16[2048,128]{1,0:T(8,128)(2,1)S(1)}, u32[]{:S(2)}, u32[]{:S(2)}) collective-permute-start(bf16[2048,128]{1,0:T(8,128)(2,1)S(1)} %pad_maximum_fusion.refs_0_), channel_id=1, source_target_pairs={{0,384},{128,0},{256,128},{384,256},{1,385},{129,1},{257,129},{385... | collective-permute-start | bytes 1572872 | tf_op jit(solution)/shard_map/ppermute | solution.py:255
  81.8 26.0 %all-to-all-start.2 = ((bf16[64,24,128]{2,1,0:T(8,128)(2,1)}), bf16[64,24,128]{2,1,0:T(8,128)(2,1)S(1)}, u32[]{:S(2)}, u32[]{:S(2)}) async-start(bf16[64,24,128]{2,1,0:T(8,128)(2,1)} %broadcast_in_dim.2), calls=%async_computation.2 | async-start | bytes 786432 | tf_op jit(solution)/shard_map/all_to_all | solution.py:40
  90.6 10.4 %collective-permute-start.5 = (bf16[1024,128]{1,0:T(8,128)(2,1)S(1)}, bf16[1024,128]{1,0:T(8,128)(2,1)}, u32[]{:S(2)}, u32[]{:S(2)}) collective-permute-start(bf16[1024,128]{1,0:T(8,128)(2,1)S(1)} %get-tuple-element.25), channel_id=1, source_target_pairs={{0,128},{128,256},{256,384},{384,0},{1,129},{129,257},{257,385},{3... | collective-permute-start | bytes 786440 | tf_op jit(solution)/shard_map/ppermute | solution.py:255
  93.0 11.3 %collective-permute-start.6 = (bf16[1024,128]{1,0:T(8,128)(2,1)S(1)}, bf16[1024,128]{1,0:T(8,128)(2,1)}, u32[]{:S(2)}, u32[]{:S(2)}) collective-permute-start(bf16[1024,128]{1,0:T(8,128)(2,1)S(1)} %get-tuple-element.26), channel_id=1, source_target_pairs={{0,384},{128,0},{256,128},{384,256},{1,385},{129,1},{257,129},{385... | collective-permute-start | bytes 786440 | tf_op jit(solution)/shard_map/ppermute | solution.py:255
  107.8 20.6 %collective-permute-start.10 = (bf16[1536,128]{1,0:T(8,128)(2,1)S(1)}, bf16[1536,128]{1,0:T(8,128)(2,1)S(1)}, u32[]{:S(2)}, u32[]{:S(2)}) collective-permute-start(bf16[1536,128]{1,0:T(8,128)(2,1)S(1)} %bitcast.10), channel_id=1, source_target_pairs={{0,384},{1,385},{2,386},{3,387},{4,388},{5,389},{6,390},{7,391},{8... | collective-permute-start | bytes 1179656 | tf_op jit(solution)/shard_map/ppermute | solution.py:260
  109.1 19.3 %collective-permute-start.8 = (bf16[1536,128]{1,0:T(8,128)(2,1)S(1)}, bf16[1536,128]{1,0:T(8,128)(2,1)S(1)}, u32[]{:S(2)}, u32[]{:S(2)}) collective-permute-start(bf16[1536,128]{1,0:T(8,128)(2,1)S(1)} %bitcast.11), channel_id=1, source_target_pairs={{0,128},{128,256},{256,384},{1,129},{129,257},{257,385},{2,130},{1... | collective-permute-start | bytes 1179656 | tf_op jit(solution)/shard_map/ppermute | solution.py:260
  110.4 18.1 %collective-permute-start.9 = (bf16[1536,128]{1,0:T(8,128)(2,1)S(1)}, bf16[1536,128]{1,0:T(8,128)(2,1)}, u32[]{:S(2)}, u32[]{:S(2)}) collective-permute-start(bf16[1536,128]{1,0:T(8,128)(2,1)S(1)} %bitcast.12), channel_id=1, source_target_pairs={{0,256},{128,384},{1,257},{129,385},{2,258},{130,386},{3,259},{131... | collective-permute-start | bytes 1179656 | tf_op jit(solution)/shard_map/ppermute | solution.py:260
  112.8 2.8 %copy-start = (bf16[6144,512]{1,0:T(8,128)(2,1)S(1)}, bf16[6144,512]{1,0:T(8,128)(2,1)}, u32[]{:S(2)}) copy-start(bf16[6144,512]{1,0:T(8,128)(2,1)} %all-gather.3.cloned.1.call-done) | copy-start | bytes 18874372
  130.7 9.5 %collective-permute-start.11 = (bf16[6144,128]{1,0:T(8,128)(2,1)}, bf16[6144,128]{1,0:T(8,128)(2,1)S(1)}, u32[]{:S(2)}, u32[]{:S(2)}) collective-permute-start(bf16[6144,128]{1,0:T(8,128)(2,1)} %join.1), channel_id=1, source_target_pairs={{0,1},{1,0},{2,3},{3,2},{4,5},{5,4},{6,7},{7,6},{8,9},{9,8},{10,11... | collective-permute-start | bytes 4718600 | tf_op jit(solution)/shard_map/ppermute | solution.py:264
  133.1 7.1 %collective-permute-start.7 = (f32[192,128]{1,0:T(8,128)S(1)}, f32[192,128]{1,0:T(8,128)S(1)}, u32[]{:S(2)}, u32[]{:S(2)}) collective-permute-start(f32[192,128]{1,0:T(8,128)S(1)} %select_bitcast_fusion), channel_id=1, source_target_pairs={{0,16},{16,0},{1,17},{17,1},{2,18},{18,2},{3,19},{19,3},{4,20},{20... | collective-permute-start | bytes 294920 | tf_op jit(solution)/shard_map/ppermute | solution.py:264
Sparse Core Ops, SparseCore 0:
  37.8 55.2 all-gather.2

commit v6 on v4

--- a/solution.py
+++ b/solution.py
@@ -275,7 +275,6 @@
     (hs,) = small_kernel(slabs_kernel, "slabs", [(32, 12, 512)], (hidden,))
     hs = lax.all_to_all(hs, PAIR, 0, 0, tiled=True)
     h, part = mix(info, hs, kv_weight)
-    h, w, part = tie((h, w, part))
     h = lax.all_gather(h, TP, axis=0, tiled=False)
 
     part = lax.all_to_all(part, PAIR, 0, 0, tiled=True)
@@ -292,7 +291,7 @@
     sums = project(info, h, (w, up, jnp.concatenate(cross, axis=0), down))
     keep = jnp.where(yp == 0, sums[0], sums[1])
     come = swap(jnp.where(yp == 0, sums[1], sums[0]), "yp")
-    away, come = tie((mine[1:], come))
+    away, sums = tie((mine[1:], sums))
     (other,) = small_kernel(join_kernel, "join", [(6144, HD)], (rows, *away))
     other = swap(other, "core")
     cosine, sine = angles_of(base + jnp.arange(192, dtype=jnp.int32))

time: 137 us -> 140 us (1.022)
  waiting for transfers between devices: 32.2 us -> 36.6 us
  blocking collectives: 22 us -> 20 us
    all_to_all x1, waiting for transfers between devices: 0.01 us -> 15.7 us  [body(): hs = lax.all_to_all(hs, PAIR, 0, 0, tiled=True)]
    all_to_all x1, waiting for transfers between devices: 8.4 us -> 0.01 us  [body(): part = lax.all_to_all(part, PAIR, 0, 0, tiled=True)]
    ppermute x3, waiting for transfers between devices: 1.39 us -> 8.43 us  [shift_up(): return lax.ppermute(v, axis, [(i, i + by) for i in range(n - by)])]
    all_gather x1, waiting for transfers between devices: 6.22 us -> 0.02 us  [body(): h = lax.all_gather(h, TP, axis=0, tiled=False)]
    all_to_all x1, waiting for transfers between devices: 3.81 us -> 0.98 us  [broadcast_gather(): lax.all_to_all(jnp.broadcast_to(x[None], (n,) + x.shape), axis, 0, 0, til...]
    all_to_all x1, starting transfers between devices: 8.29 us -> 10.6 us  [broadcast_gather(): lax.all_to_all(jnp.broadcast_to(x[None], (n,) + x.shape), axis, 0, 0, til...]
    all_to_all x1, starting transfers between devices: 7.54 us -> 5.29 us  [body(): part = lax.all_to_all(part, PAIR, 0, 0, tiled=True)]
    all_gather x1, blocking collectives: 22 us -> 20 us  [body(): w = lax.all_gather(query_weight, 'yq', axis=0, tiled=True)]
where the time goes in v6:
time: 140 us; the launch traced here: 139 us
  starting transfers between devices  47.6 us (34%)
  waiting for transfers between devices  36.6 us (26%)
  blocking collectives  20 us (14%)
  Pallas kernels  16.8 us (12%)
  between operations  13.7 us (10%)
  local copies, waits for them, and re-layouts  2.56 us (2%)
  other arithmetic  1.99 us (1%)
    all_gather x1, blocking collectives, body(): w = lax.all_gather(query_weight, 'yq', axis=0, tiled=True)  20 us
    all_to_all x1, waiting for transfers between devices, body(): hs = lax.all_to_all(hs, PAIR, 0, 0, tiled=True)  15.7 us
    all_to_all x1, starting transfers between devices, body(): hs = lax.all_to_all(hs, PAIR, 0, 0, tiled=True)  11.8 us
    ppermute x4, starting transfers between devices, shift(): return lax.ppermute(v, axis, [(i, (i + by) % n) for i in range(n)])  11.7 us
    all_to_all x1, starting transfers between devices, broadcast_gather(): lax.all_to_all(jnp.broadcast_to(x[None], (n,) + x.shape), axis, 0, 0, til...  10.6 us
    ppermute x3, waiting for transfers between devices, shift_up(): return lax.ppermute(v, axis, [(i, i + by) for i in range(n - by)])  8.43 us
    ppermute x4, waiting for transfers between devices, shift(): return lax.ppermute(v, axis, [(i, (i + by) % n) for i in range(n)])  6.85 us
    pallas_call x1, Pallas kernels, project(): pl.pallas_call(project_kernel, in_specs=[pl.BlockSpec(memory_space=pltpu....  6.08 us
  transfers between devices with their start and end apart: 13, of which 8 were waited for; matrix products, arithmetic and copies ran while one was open for 2% of the time, Pallas kernels for 4%

profile of v6, /device:TPU:6, one launch (start us, length us, event | category | flops | bytes accessed | tf_op | source)
XLA Modules:
  0.0 139.2 jit_solution(12723711212164349904)
XLA Ops:
  8.4 11.8 %all-to-all-start = ((bf16[32,12,512]{2,1,0:T(8,128)(2,1)}), bf16[32,12,512]{2,1,0:T(8,128)(2,1)S(1)}, u32[]{:S(2)}, u32[]{:S(2)}) async-start(bf16[32,12,512]{2,1,0:T(8,128)(2,1)} %slabs.1), calls=%async_computation | async-start | bytes 1048576 | tf_op jit(solution)/shard_map/all_to_all | solution.py:276
  20.4 15.7 %all-to-all-done.x_ref = bf16[32,12,512]{2,1,0:T(8,128)(2,1)S(1)} async-done(((bf16[32,12,512]{2,1,0:T(8,128)(2,1)}), bf16[32,12,512]{2,1,0:T(8,128)(2,1)S(1)}, u32[]{:S(2)}, u32[]{:S(2)}) %all-to-all-start) | async-done | bytes 393248 | tf_op jit(solution)/shard_map/all_to_all | solution.py:276
  36.2 1.6 %mix.1 = (bf16[384,512]{1,0:T(8,128)(2,1)}, f32[32,24,128]{2,1,0:T(8,128)}) custom-call(s32[3]{0:T(128)S(1)} %pad_add_fusion.info_ref, bf16[32,12,512]{2,1,0:T(8,128)(2,1)S(1)} %all-to-all-done.x_ref, bf16[1024,256]{1,0:T(8,128)(2,1)S(1)} %copy-done.1), custom_call_target="tpu_custom_call" | custom-call | flops 100663296 | bytes 1048576 | tf_op jit(solution)/shard_map/mix/pallas_call | solution.py:67
  37.8 5.3 %all-to-all-start.1 = ((f32[32,24,128]{2,1,0:T(8,128)}), f32[32,24,128]{2,1,0:T(8,128)S(1)}, u32[]{:S(2)}, u32[]{:S(2)}) async-start(f32[32,24,128]{2,1,0:T(8,128)} %get-tuple-element.16), calls=%async_computation.1 | async-start | bytes 786432 | tf_op jit(solution)/shard_map/all_to_all | solution.py:280
  43.1 20.0 %all_gather.11.refs_0_ = bf16[2048,128]{1,0:T(8,128)(2,1)S(1)} all-gather(bf16[512,128]{1,0:T(8,128)(2,1)S(1)} %copy-done.3), channel_id=1, replica_groups=mesh['x'=4,'yq'=4,'yp'=2,'z'=8,'core'=2] {'yq'}, dimensions={0}, use_global_device_ids=true | all-gather | bytes 655360 | tf_op jit(solution)/shard_map/all_gather | solution.py:273
  63.1 2.4 %collective-permute-start = (bf16[2048,128]{1,0:T(8,128)(2,1)S(1)}, bf16[2048,128]{1,0:T(8,128)(2,1)S(1)}, u32[]{:S(2)}, u32[]{:S(2)}) collective-permute-start(bf16[2048,128]{1,0:T(8,128)(2,1)S(1)} %all_gather.11.refs_0_), channel_id=1, source_target_pairs={{0,128},{128,256},{256,384},{384,0},{1,129},{129,257},{257,385},{3... | collective-permute-start | bytes 1572872 | tf_op jit(solution)/shard_map/ppermute | solution.py:254
  65.5 3.4 %collective-permute-start.1 = (bf16[2048,128]{1,0:T(8,128)(2,1)S(1)}, bf16[2048,128]{1,0:T(8,128)(2,1)S(1)}, u32[]{:S(2)}, u32[]{:S(2)}) collective-permute-start(bf16[2048,128]{1,0:T(8,128)(2,1)S(1)} %all_gather.11.refs_0_), channel_id=1, source_target_pairs={{0,384},{128,0},{256,128},{384,256},{1,385},{129,1},{257,129},{385... | collective-permute-start | bytes 1572872 | tf_op jit(solution)/shard_map/ppermute | solution.py:254
  70.1 10.6 %all-to-all-start.2 = ((bf16[64,24,128]{2,1,0:T(8,128)(2,1)}), bf16[64,24,128]{2,1,0:T(8,128)(2,1)S(1)}, u32[]{:S(2)}, u32[]{:S(2)}) async-start(bf16[64,24,128]{2,1,0:T(8,128)(2,1)} %broadcast_in_dim.2), calls=%async_computation.2 | async-start | bytes 786432 | tf_op jit(solution)/shard_map/all_to_all | solution.py:40
  81.0 3.6 %collective-permute-start.2 = (bf16[1024,128]{1,0:T(8,128)(2,1)S(1)}, bf16[1024,128]{1,0:T(8,128)(2,1)S(1)}, u32[]{:S(2)}, u32[]{:S(2)}) collective-permute-start(bf16[1024,128]{1,0:T(8,128)(2,1)S(1)} %get-tuple-element.17), channel_id=1, source_target_pairs={{0,128},{128,256},{256,384},{384,0},{1,129},{129,257},{257,385},{3... | collective-permute-start | bytes 786440 | tf_op jit(solution)/shard_map/ppermute | solution.py:254
  84.6 2.3 %collective-permute-start.3 = (bf16[1024,128]{1,0:T(8,128)(2,1)S(1)}, bf16[1024,128]{1,0:T(8,128)(2,1)}, u32[]{:S(2)}, u32[]{:S(2)}) collective-permute-start(bf16[1024,128]{1,0:T(8,128)(2,1)S(1)} %get-tuple-element.18), channel_id=1, source_target_pairs={{0,384},{128,0},{256,128},{384,256},{1,385},{129,1},{257,129},{385... | collective-permute-start | bytes 786440 | tf_op jit(solution)/shard_map/ppermute | solution.py:254
  86.8 2.4 %collective-permute-done.2 = bf16[1024,128]{1,0:T(8,128)(2,1)S(1)} collective-permute-done((bf16[1024,128]{1,0:T(8,128)(2,1)S(1)}, bf16[1024,128]{1,0:T(8,128)(2,1)S(1)}, u32[]{:S(2)}, u32[]{:S(2)}) %collective-permute-start.2) | collective-permute-done | bytes 262176 | tf_op jit(solution)/shard_map/ppermute | solution.py:254
  89.9 4.2 %collective-permute-done.3 = bf16[1024,128]{1,0:T(8,128)(2,1)} collective-permute-done((bf16[1024,128]{1,0:T(8,128)(2,1)S(1)}, bf16[1024,128]{1,0:T(8,128)(2,1)}, u32[]{:S(2)}, u32[]{:S(2)}) %collective-permute-start.3) | collective-permute-done | bytes 262176 | tf_op jit(solution)/shard_map/ppermute | solution.py:254
  95.1 1.3 collective-permute-start.5
  96.4 1.3 collective-permute-start.6
  97.7 1.3 collective-permute-start.7
  99.0 1.1 pad_maximum_fusion.refs_2_
  100.1 6.1 %project.1 = f32[2,192,128]{2,1,0:T(8,128)S(1)} custom-call(s32[3]{0:T(128)S(1)} %pad_add_fusion.info_ref, bf16[16,384,512]{2,1,0:T(8,128)(2,1)} %bitcast.14, bf16[2048,128]{1,0:T(8,128)(2,1)S(1)} %all_gather.11.refs_0_, bf16[2048,128]{1,0:T(8,128)(2,1)S(1)} %collective-permute-done.up_ref.refs_1_, bf16[2048,128]{1,0:T(8,128)(2,1)S(1)} %pad_maximum_fusion.refs_2_, ...), custom_call_target="tpu_custom_call" | custom-call | flops 805306368 | bytes 8388608 | tf_op jit(solution)/shard_map/project/pallas_call | solution.py:209
  106.2 1.5 %collective-permute-done.6.refs_2_ = bf16[1536,128]{1,0:T(8,128)(2,1)S(1)} collective-permute-done((bf16[1536,128]{1,0:T(8,128)(2,1)S(1)}, bf16[1536,128]{1,0:T(8,128)(2,1)S(1)}, u32[]{:S(2)}, u32[]{:S(2)}) %collective-permute-start.6) | collective-permute-done | bytes 393248 | tf_op jit(solution)/shard_map/ppermute | solution.py:259
  107.7 6.9 %collective-permute-done.7.refs_3_ = bf16[1536,128]{1,0:T(8,128)(2,1)} collective-permute-done((bf16[1536,128]{1,0:T(8,128)(2,1)S(1)}, bf16[1536,128]{1,0:T(8,128)(2,1)}, u32[]{:S(2)}, u32[]{:S(2)}) %collective-permute-start.7) | collective-permute-done | bytes 393248 | tf_op jit(solution)/shard_map/ppermute | solution.py:259
  114.6 2.3 %join.1 = bf16[6144,128]{1,0:T(8,128)(2,1)} custom-call(bf16[1536,128]{1,0:T(8,128)(2,1)S(1)} %bitcast.12, bf16[1536,128]{1,0:T(8,128)(2,1)S(1)} %collective-permute-done.5.refs_1_, bf16[1536,128]{1,0:T(8,128)(2,1)S(1)} %collective-permute-done.6.refs_2_, bf16[1536,128]{1,0:T(8,128)(2,1)} %collective-permute-done.7.refs_3_), custom_call_target="tpu_custom_call" | custom-call | bytes 1048576 | tf_op jit(solution)/shard_map/join/pallas_call | solution.py:99
  116.9 1.9 %collective-permute-start.8 = (bf16[6144,128]{1,0:T(8,128)(2,1)}, bf16[6144,128]{1,0:T(8,128)(2,1)S(1)}, u32[]{:S(2)}, u32[]{:S(2)}) collective-permute-start(bf16[6144,128]{1,0:T(8,128)(2,1)} %join.1), channel_id=1, source_target_pairs={{0,1},{1,0},{2,3},{3,2},{4,5},{5,4},{6,7},{7,6},{8,9},{9,8},{10,11... | collective-permute-start | bytes 4718600 | tf_op jit(solution)/shard_map/ppermute | solution.py:263
  119.3 2.4 %collective-permute-start.4 = (f32[192,128]{1,0:T(8,128)S(1)}, f32[192,128]{1,0:T(8,128)S(1)}, u32[]{:S(2)}, u32[]{:S(2)}) collective-permute-start(f32[192,128]{1,0:T(8,128)S(1)} %select_bitcast_fusion), channel_id=1, source_target_pairs={{0,16},{16,0},{1,17},{17,1},{2,18},{18,2},{3,19},{19,3},{4,20},{20... | collective-permute-start | bytes 294920 | tf_op jit(solution)/shard_map/ppermute | solution.py:263
  121.8 4.5 %collective-permute-done.4 = f32[192,128]{1,0:T(8,128)S(1)} collective-permute-done((f32[192,128]{1,0:T(8,128)S(1)}, f32[192,128]{1,0:T(8,128)S(1)}, u32[]{:S(2)}, u32[]{:S(2)}) %collective-permute-start.4) | collective-permute-done | bytes 98336 | tf_op jit(solution)/shard_map/ppermute | solution.py:263
  126.4 6.0 %attend.1 = bf16[192,128]{1,0:T(8,128)(2,1)} custom-call(s32[3]{0:T(128)S(1)} %pad_add_fusion.info_ref, f32[192,128]{1,0:T(8,128)S(1)} %bitcast_add_fusion.q_ref, f32[192,128]{1,0:T(8,128)S(1)} %get-tuple-element.30.cos_ref, f32[192,128]{1,0:T(8,128)S(1)} %get-tuple-element.31.sin_ref, bf16[1536,128]{1,0:T(8,128)(2,1)S(1)} %bitcast.13, ...), custom_call_target="tpu_custom_call" | custom-call | flops 603979776 | bytes 3145728 | tf_op jit(solution)/shard_map/attend/pallas_call | solution.py:231
  (31 shorter events, 5.7 us)
Async XLA Ops:
  6.5 1.0 copy-start
  7.6 28.6 %copy-start.1 = (bf16[1024,256]{1,0:T(8,128)(2,1)S(1)}, bf16[1024,256]{1,0:T(8,128)(2,1)}, u32[]{:S(2)}) copy-start(bf16[1024,256]{1,0:T(8,128)(2,1)} %w_ref.1) | copy-start | bytes 1572868
  8.4 34.7 %copy-start.3 = (bf16[512,128]{1,0:T(8,128)(2,1)S(1)}, bf16[512,128]{1,0:T(8,128)(2,1)}, u32[]{:S(2)}) copy-start(bf16[512,128]{1,0:T(8,128)(2,1)} %param.4) | copy-start | bytes 393220
  8.4 27.7 %all-to-all-start = ((bf16[32,12,512]{2,1,0:T(8,128)(2,1)}), bf16[32,12,512]{2,1,0:T(8,128)(2,1)S(1)}, u32[]{:S(2)}, u32[]{:S(2)}) async-start(bf16[32,12,512]{2,1,0:T(8,128)(2,1)} %slabs.1), calls=%async_computation | async-start | bytes 1048576 | tf_op jit(solution)/shard_map/all_to_all | solution.py:276
  20.3 79.8 %all-gather.3.cloned.1.call-start = ((), (), s32[]{:S(2)}) async-start(), calls=%async_computation.3 | async-start | bytes 6684672 | tf_op jit(solution)/shard_map/all_gather | solution.py:278
  37.8 31.2 %all-to-all-start.1 = ((f32[32,24,128]{2,1,0:T(8,128)}), f32[32,24,128]{2,1,0:T(8,128)S(1)}, u32[]{:S(2)}, u32[]{:S(2)}) async-start(f32[32,24,128]{2,1,0:T(8,128)} %get-tuple-element.16), calls=%async_computation.1 | async-start | bytes 786432 | tf_op jit(solution)/shard_map/all_to_all | solution.py:280
  63.1 17.6 %collective-permute-start = (bf16[2048,128]{1,0:T(8,128)(2,1)S(1)}, bf16[2048,128]{1,0:T(8,128)(2,1)S(1)}, u32[]{:S(2)}, u32[]{:S(2)}) collective-permute-start(bf16[2048,128]{1,0:T(8,128)(2,1)S(1)} %all_gather.11.refs_0_), channel_id=1, source_target_pairs={{0,128},{128,256},{256,384},{384,0},{1,129},{129,257},{257,385},{3... | collective-permute-start | bytes 1572872 | tf_op jit(solution)/shard_map/ppermute | solution.py:254
  65.5 15.4 %collective-permute-start.1 = (bf16[2048,128]{1,0:T(8,128)(2,1)S(1)}, bf16[2048,128]{1,0:T(8,128)(2,1)S(1)}, u32[]{:S(2)}, u32[]{:S(2)}) collective-permute-start(bf16[2048,128]{1,0:T(8,128)(2,1)S(1)} %all_gather.11.refs_0_), channel_id=1, source_target_pairs={{0,384},{128,0},{256,128},{384,256},{1,385},{129,1},{257,129},{385... | collective-permute-start | bytes 1572872 | tf_op jit(solution)/shard_map/ppermute | solution.py:254
  70.1 25.0 %all-to-all-start.2 = ((bf16[64,24,128]{2,1,0:T(8,128)(2,1)}), bf16[64,24,128]{2,1,0:T(8,128)(2,1)S(1)}, u32[]{:S(2)}, u32[]{:S(2)}) async-start(bf16[64,24,128]{2,1,0:T(8,128)(2,1)} %broadcast_in_dim.2), calls=%async_computation.2 | async-start | bytes 786432 | tf_op jit(solution)/shard_map/all_to_all | solution.py:40
  81.0 8.3 %collective-permute-start.2 = (bf16[1024,128]{1,0:T(8,128)(2,1)S(1)}, bf16[1024,128]{1,0:T(8,128)(2,1)S(1)}, u32[]{:S(2)}, u32[]{:S(2)}) collective-permute-start(bf16[1024,128]{1,0:T(8,128)(2,1)S(1)} %get-tuple-element.17), channel_id=1, source_target_pairs={{0,128},{128,256},{256,384},{384,0},{1,129},{129,257},{257,385},{3... | collective-permute-start | bytes 786440 | tf_op jit(solution)/shard_map/ppermute | solution.py:254
  84.6 9.6 %collective-permute-start.3 = (bf16[1024,128]{1,0:T(8,128)(2,1)S(1)}, bf16[1024,128]{1,0:T(8,128)(2,1)}, u32[]{:S(2)}, u32[]{:S(2)}) collective-permute-start(bf16[1024,128]{1,0:T(8,128)(2,1)S(1)} %get-tuple-element.18), channel_id=1, source_target_pairs={{0,384},{128,0},{256,128},{384,256},{1,385},{129,1},{257,129},{385... | collective-permute-start | bytes 786440 | tf_op jit(solution)/shard_map/ppermute | solution.py:254
  89.2 0.7 copy-start.2
  95.1 11.1 %collective-permute-start.5 = (bf16[1536,128]{1,0:T(8,128)(2,1)S(1)}, bf16[1536,128]{1,0:T(8,128)(2,1)S(1)}, u32[]{:S(2)}, u32[]{:S(2)}) collective-permute-start(bf16[1536,128]{1,0:T(8,128)(2,1)S(1)} %bitcast.9), channel_id=1, source_target_pairs={{0,128},{128,256},{256,384},{1,129},{129,257},{257,385},{2,130},{1... | collective-permute-start | bytes 1179656 | tf_op jit(solution)/shard_map/ppermute | solution.py:259
  96.4 11.3 %collective-permute-start.6 = (bf16[1536,128]{1,0:T(8,128)(2,1)S(1)}, bf16[1536,128]{1,0:T(8,128)(2,1)S(1)}, u32[]{:S(2)}, u32[]{:S(2)}) collective-permute-start(bf16[1536,128]{1,0:T(8,128)(2,1)S(1)} %bitcast.10), channel_id=1, source_target_pairs={{0,256},{128,384},{1,257},{129,385},{2,258},{130,386},{3,259},{131... | collective-permute-start | bytes 1179656 | tf_op jit(solution)/shard_map/ppermute | solution.py:259
  97.7 16.9 %collective-permute-start.7 = (bf16[1536,128]{1,0:T(8,128)(2,1)S(1)}, bf16[1536,128]{1,0:T(8,128)(2,1)}, u32[]{:S(2)}, u32[]{:S(2)}) collective-permute-start(bf16[1536,128]{1,0:T(8,128)(2,1)S(1)} %bitcast.11), channel_id=1, source_target_pairs={{0,384},{1,385},{2,386},{3,387},{4,388},{5,389},{6,390},{7,391},{8... | collective-permute-start | bytes 1179656 | tf_op jit(solution)/shard_map/ppermute | solution.py:259
  116.9 9.5 %collective-permute-start.8 = (bf16[6144,128]{1,0:T(8,128)(2,1)}, bf16[6144,128]{1,0:T(8,128)(2,1)S(1)}, u32[]{:S(2)}, u32[]{:S(2)}) collective-permute-start(bf16[6144,128]{1,0:T(8,128)(2,1)} %join.1), channel_id=1, source_target_pairs={{0,1},{1,0},{2,3},{3,2},{4,5},{5,4},{6,7},{7,6},{8,9},{9,8},{10,11... | collective-permute-start | bytes 4718600 | tf_op jit(solution)/shard_map/ppermute | solution.py:263
  119.3 7.1 %collective-permute-start.4 = (f32[192,128]{1,0:T(8,128)S(1)}, f32[192,128]{1,0:T(8,128)S(1)}, u32[]{:S(2)}, u32[]{:S(2)}) collective-permute-start(f32[192,128]{1,0:T(8,128)S(1)} %select_bitcast_fusion), channel_id=1, source_target_pairs={{0,16},{16,0},{1,17},{17,1},{2,18},{18,2},{3,19},{19,3},{4,20},{20... | collective-permute-start | bytes 294920 | tf_op jit(solution)/shard_map/ppermute | solution.py:263
Sparse Core Ops, SparseCore 0:
  37.9 56.8 all-gather.2

commit v7 on v4

--- a/solution.py
+++ b/solution.py
@@ -109,17 +109,17 @@
 
 def project_kernel(info_ref, h_ref, *refs):
     w_refs, o_ref, h_buf, w_buf, sems = refs[:4], *refs[4:]
-    x = info_ref[0]
+    x, yq = info_ref[0], info_ref[1] // 2
     copies = []
     for n in range(4):
-        at = lax.rem(x + 4 - n, 4) * 4
-        copies.append(
-            (
-                pltpu.make_async_copy(h_ref.at[pl.ds(at, 4)], h_buf.at[n], sems.at[n, 0]),
-                pltpu.make_async_copy(w_refs[n], w_buf.at[n], sems.at[n, 1]),
+        group = [pltpu.make_async_copy(w_refs[n], w_buf.at[n], sems.at[n, 4])]
+        for back in range(4):
+            block = lax.rem(x + 4 - n, 4) * 4 + lax.rem(yq + 4 - back, 4)
+            group.append(
+                pltpu.make_async_copy(h_ref.at[block], h_buf.at[n, back], sems.at[n, back])
             )
-        )
-        for copy in copies[n]:
+        copies.append(group)
+        for copy in group:
             copy.start()
     total = None
     for n in range(4):
@@ -214,7 +214,7 @@
         scratch_shapes=[
             pltpu.VMEM((4, count // 4, m, part), jnp.bfloat16),
             pltpu.VMEM((4, count // 4 * part, HD), jnp.bfloat16),
-            pltpu.SemaphoreType.DMA((4, 2)),
+            pltpu.SemaphoreType.DMA((4, 5)),
         ],
         compiler_params=pltpu.CompilerParams(vmem_limit_bytes=48 * 2**20),
         cost_estimate=pl.CostEstimate(
@@ -270,13 +270,15 @@
     info = jnp.stack([x, y, core])
     tie = lax.optimization_barrier
 
-    w = lax.all_gather(query_weight, "yq", axis=0, tiled=True)
-
     (hs,) = small_kernel(slabs_kernel, "slabs", [(32, 12, 512)], (hidden,))
+    hs, w = tie((hs, query_weight))
     hs = lax.all_to_all(hs, PAIR, 0, 0, tiled=True)
+
+    w = [w] + [shift(w, "yq", d) for d in (1, 2, 3)]
+    hs, w = tie((hs, w))
     h, part = mix(info, hs, kv_weight)
-    h, w, part = tie((h, w, part))
     h = lax.all_gather(h, TP, axis=0, tiled=False)
+    w = jnp.concatenate(w, axis=0)
 
     part = lax.all_to_all(part, PAIR, 0, 0, tiled=True)
     up, down = shift(w, "x", 1), shift(w, "x", -1)

time: 137 us -> 138 us (level)
  blocking collectives: 22 us -> 0 us
  starting transfers between devices: 48.5 us -> 64.9 us
  waiting for transfers between devices: 32.2 us -> 38.5 us
    all_gather x1 -> x0, blocking collectives: 22 us -> none  [body(): w = lax.all_gather(query_weight, 'yq', axis=0, tiled=True)]
    ppermute x4 -> x7, starting transfers between devices: 11.7 us -> 26.5 us  [shift(): return lax.ppermute(v, axis, [(i, (i + by) % n) for i in range(n)])]
    ppermute x4 -> x7, waiting for transfers between devices: 7.61 us -> 15.5 us  [shift(): return lax.ppermute(v, axis, [(i, (i + by) % n) for i in range(n)])]
    all_to_all x1, starting transfers between devices: 8.29 us -> 10.4 us  [broadcast_gather(): lax.all_to_all(jnp.broadcast_to(x[None], (n,) + x.shape), axis, 0, 0, til...]
  transfers between devices with their start and end apart: 13 -> 16, of which waited for: 8 -> 11; matrix products, arithmetic and copies ran while one was open for 2% -> 2% of each run, Pallas kernels for 4% -> 5%
where the time goes in v7:
time: 138 us; the launch traced here: 136 us
  starting transfers between devices  64.9 us (47%)
  waiting for transfers between devices  38.5 us (28%)
  Pallas kernels  14.5 us (11%)
  between operations  13.7 us (10%)
  local copies, waits for them, and re-layouts  2.98 us (2%)
  other arithmetic  1.91 us (1%)
    ppermute x7, starting transfers between devices, shift(): return lax.ppermute(v, axis, [(i, (i + by) % n) for i in range(n)])  26.5 us
    ppermute x7, waiting for transfers between devices, shift(): return lax.ppermute(v, axis, [(i, (i + by) % n) for i in range(n)])  15.5 us
    all_to_all x1, starting transfers between devices, body(): hs = lax.all_to_all(hs, PAIR, 0, 0, tiled=True)  11.7 us
    all_to_all x1, starting transfers between devices, broadcast_gather(): lax.all_to_all(jnp.broadcast_to(x[None], (n,) + x.shape), axis, 0, 0, til...  10.4 us
    all_to_all x1, waiting for transfers between devices, body(): part = lax.all_to_all(part, PAIR, 0, 0, tiled=True)  7.52 us
    all_to_all x1, starting transfers between devices, body(): part = lax.all_to_all(part, PAIR, 0, 0, tiled=True)  7.08 us
    pallas_call x1, Pallas kernels, project(): pl.pallas_call(project_kernel, in_specs=[pl.BlockSpec(memory_space=pltpu....  6.18 us
    ppermute x2, waiting for transfers between devices, swap(): return lax.ppermute(v, axis, [(0, 1), (1, 0)])  5.85 us
  transfers between devices with their start and end apart: 16, of which 11 were waited for; matrix products, arithmetic and copies ran while one was open for 2% of the time, Pallas kernels for 5%

profile of v7, /device:TPU:6, one launch (start us, length us, event | category | flops | bytes accessed | tf_op | source)
XLA Modules:
  0.0 136.5 jit_solution(9461602462308032066)
XLA Ops:
  8.4 11.7 %all-to-all-start = ((bf16[32,12,512]{2,1,0:T(8,128)(2,1)}), bf16[32,12,512]{2,1,0:T(8,128)(2,1)S(1)}, u32[]{:S(2)}, u32[]{:S(2)}) async-start(bf16[32,12,512]{2,1,0:T(8,128)(2,1)} %slabs.1), calls=%async_computation | async-start | bytes 1048576 | tf_op jit(solution)/shard_map/all_to_all | solution.py:275
  20.2 4.5 %collective-permute-start = (bf16[512,128]{1,0:T(8,128)(2,1)S(1)}, bf16[512,128]{1,0:T(8,128)(2,1)S(1)}, u32[]{:S(2)}, u32[]{:S(2)}) collective-permute-start(bf16[512,128]{1,0:T(8,128)(2,1)S(1)} %copy-done.4), channel_id=1, source_target_pairs={{0,32},{32,64},{64,96},{96,0},{1,33},{33,65},{65,97},{97,1},{2,34}... | collective-permute-start | bytes 393224 | tf_op jit(solution)/shard_map/ppermute | solution.py:254
  24.7 5.0 %collective-permute-start.1 = (bf16[512,128]{1,0:T(8,128)(2,1)S(1)}, bf16[512,128]{1,0:T(8,128)(2,1)S(1)}, u32[]{:S(2)}, u32[]{:S(2)}) collective-permute-start(bf16[512,128]{1,0:T(8,128)(2,1)S(1)} %copy-done.4), channel_id=1, source_target_pairs={{0,64},{32,96},{64,0},{96,32},{1,65},{33,97},{65,1},{97,33},{2,66}... | collective-permute-start | bytes 393224 | tf_op jit(solution)/shard_map/ppermute | solution.py:254
  29.8 5.3 %collective-permute-start.2 = (bf16[512,128]{1,0:T(8,128)(2,1)S(1)}, bf16[512,128]{1,0:T(8,128)(2,1)S(1)}, u32[]{:S(2)}, u32[]{:S(2)}) collective-permute-start(bf16[512,128]{1,0:T(8,128)(2,1)S(1)} %copy-done.4), channel_id=1, source_target_pairs={{0,96},{32,0},{64,32},{96,64},{1,97},{33,1},{65,33},{97,65},{2,98}... | collective-permute-start | bytes 393224 | tf_op jit(solution)/shard_map/ppermute | solution.py:254
  36.2 4.2 %collective-permute-done.1 = bf16[512,128]{1,0:T(8,128)(2,1)S(1)} collective-permute-done((bf16[512,128]{1,0:T(8,128)(2,1)S(1)}, bf16[512,128]{1,0:T(8,128)(2,1)S(1)}, u32[]{:S(2)}, u32[]{:S(2)}) %collective-permute-start.1) | collective-permute-done | bytes 131104 | tf_op jit(solution)/shard_map/ppermute | solution.py:254
  40.4 3.0 %collective-permute-done.2 = bf16[512,128]{1,0:T(8,128)(2,1)S(1)} collective-permute-done((bf16[512,128]{1,0:T(8,128)(2,1)S(1)}, bf16[512,128]{1,0:T(8,128)(2,1)S(1)}, u32[]{:S(2)}, u32[]{:S(2)}) %collective-permute-start.2) | collective-permute-done | bytes 131104 | tf_op jit(solution)/shard_map/ppermute | solution.py:254
  43.5 1.6 %mix.1 = (bf16[384,512]{1,0:T(8,128)(2,1)}, f32[32,24,128]{2,1,0:T(8,128)}) custom-call(s32[3]{0:T(128)S(1)} %pad_add_fusion.info_ref, bf16[32,12,512]{2,1,0:T(8,128)(2,1)S(1)} %all-to-all-done.x_ref, bf16[1024,256]{1,0:T(8,128)(2,1)S(1)} %copy-done.3), custom_call_target="tpu_custom_call" | custom-call | flops 100663296 | bytes 1048576 | tf_op jit(solution)/shard_map/mix/pallas_call | solution.py:67
  45.1 7.1 %all-to-all-start.1 = ((f32[32,24,128]{2,1,0:T(8,128)}), f32[32,24,128]{2,1,0:T(8,128)S(1)}, u32[]{:S(2)}, u32[]{:S(2)}) async-start(f32[32,24,128]{2,1,0:T(8,128)} %get-tuple-element.31), calls=%async_computation.1 | async-start | bytes 786432 | tf_op jit(solution)/shard_map/all_to_all | solution.py:283
  52.3 2.4 %collective-permute-start.3 = (bf16[2048,128]{1,0:T(8,128)(2,1)S(1)}, bf16[2048,128]{1,0:T(8,128)(2,1)S(1)}, u32[]{:S(2)}, u32[]{:S(2)}) collective-permute-start(bf16[2048,128]{1,0:T(8,128)(2,1)S(1)} %constant_dynamic-update-slice_fusion.refs_0_), channel_id=1, source_target_pairs={{0,128},{128,256},{256,384},{384,0},{1,129},{129,257},{257,385},{3... | collective-permute-start | bytes 1572872 | tf_op jit(solution)/shard_map/ppermute | solution.py:254
  54.7 3.5 %collective-permute-start.4 = (bf16[2048,128]{1,0:T(8,128)(2,1)S(1)}, bf16[2048,128]{1,0:T(8,128)(2,1)S(1)}, u32[]{:S(2)}, u32[]{:S(2)}) collective-permute-start(bf16[2048,128]{1,0:T(8,128)(2,1)S(1)} %constant_dynamic-update-slice_fusion.refs_0_), channel_id=1, source_target_pairs={{0,384},{128,0},{256,128},{384,256},{1,385},{129,1},{257,129},{385... | collective-permute-start | bytes 1572872 | tf_op jit(solution)/shard_map/ppermute | solution.py:254
  58.2 7.5 %all-to-all-done.1 = f32[32,24,128]{2,1,0:T(8,128)S(1)} async-done(((f32[32,24,128]{2,1,0:T(8,128)}), f32[32,24,128]{2,1,0:T(8,128)S(1)}, u32[]{:S(2)}, u32[]{:S(2)}) %all-to-all-start.1) | async-done | bytes 393248 | tf_op jit(solution)/shard_map/all_to_all | solution.py:283
  66.8 10.4 %all-to-all-start.2 = ((bf16[64,24,128]{2,1,0:T(8,128)(2,1)}), bf16[64,24,128]{2,1,0:T(8,128)(2,1)S(1)}, u32[]{:S(2)}, u32[]{:S(2)}) async-start(bf16[64,24,128]{2,1,0:T(8,128)(2,1)} %broadcast_in_dim.2), calls=%async_computation.2 | async-start | bytes 786432 | tf_op jit(solution)/shard_map/all_to_all | solution.py:40
  77.2 2.3 %collective-permute-start.5 = (bf16[1024,128]{1,0:T(8,128)(2,1)S(1)}, bf16[1024,128]{1,0:T(8,128)(2,1)S(1)}, u32[]{:S(2)}, u32[]{:S(2)}) collective-permute-start(bf16[1024,128]{1,0:T(8,128)(2,1)S(1)} %get-tuple-element.32), channel_id=1, source_target_pairs={{0,128},{128,256},{256,384},{384,0},{1,129},{129,257},{257,385},{3... | collective-permute-start | bytes 786440 | tf_op jit(solution)/shard_map/ppermute | solution.py:254
  79.6 3.5 %collective-permute-start.6 = (bf16[1024,128]{1,0:T(8,128)(2,1)S(1)}, bf16[1024,128]{1,0:T(8,128)(2,1)}, u32[]{:S(2)}, u32[]{:S(2)}) collective-permute-start(bf16[1024,128]{1,0:T(8,128)(2,1)S(1)} %get-tuple-element.33), channel_id=1, source_target_pairs={{0,384},{128,0},{256,128},{384,256},{1,385},{129,1},{257,129},{385... | collective-permute-start | bytes 786440 | tf_op jit(solution)/shard_map/ppermute | solution.py:254
  83.1 3.7 %collective-permute-done.5 = bf16[1024,128]{1,0:T(8,128)(2,1)S(1)} collective-permute-done((bf16[1024,128]{1,0:T(8,128)(2,1)S(1)}, bf16[1024,128]{1,0:T(8,128)(2,1)S(1)}, u32[]{:S(2)}, u32[]{:S(2)}) %collective-permute-start.5) | collective-permute-done | bytes 262176 | tf_op jit(solution)/shard_map/ppermute | solution.py:254
  86.8 3.4 %collective-permute-done.6 = bf16[1024,128]{1,0:T(8,128)(2,1)} collective-permute-done((bf16[1024,128]{1,0:T(8,128)(2,1)S(1)}, bf16[1024,128]{1,0:T(8,128)(2,1)}, u32[]{:S(2)}, u32[]{:S(2)}) %collective-permute-start.6) | collective-permute-done | bytes 262176 | tf_op jit(solution)/shard_map/ppermute | solution.py:254
  90.2 3.9 %all-to-all-done.2 = bf16[64,24,128]{2,1,0:T(8,128)(2,1)S(1)} async-done(((bf16[64,24,128]{2,1,0:T(8,128)(2,1)}), bf16[64,24,128]{2,1,0:T(8,128)(2,1)S(1)}, u32[]{:S(2)}, u32[]{:S(2)}) %all-to-all-start.2) | async-done | bytes 393248 | tf_op jit(solution)/shard_map/all_to_all | solution.py:40
  99.0 5.3 %all-gather.3.cloned.1.call-done = bf16[6144,512]{1,0:T(8,128)(2,1)} async-done(((bf16[384,512]{1,0:T(8,128)(2,1)}), bf16[6144,512]{1,0:T(8,128)(2,1)}) %all-gather.3.cloned.1.call-update) | async-done | bytes 6291472 | tf_op jit(solution)/shard_map/all_gather | solution.py:280
  105.4 6.2 %project.1 = f32[2,192,128]{2,1,0:T(8,128)S(1)} custom-call(s32[3]{0:T(128)S(1)} %pad_add_fusion.info_ref, bf16[16,384,512]{2,1,0:T(8,128)(2,1)} %bitcast.14, bf16[2048,128]{1,0:T(8,128)(2,1)S(1)} %copy-done.1, bf16[2048,128]{1,0:T(8,128)(2,1)S(1)} %collective-permute-done.3.up_ref.refs_1_, bf16[2048,128]{1,0:T(8,128)(2,1)S(1)} %pad_maximum_fusion.refs_2_, ...), custom_call_target="tpu_custom_call" | custom-call | flops 805306368 | bytes 8388608 | tf_op jit(solution)/shard_map/project/pallas_call | solution.py:209
  111.6 3.4 %collective-permute-start.10 = (f32[192,128]{1,0:T(8,128)S(1)}, f32[192,128]{1,0:T(8,128)S(1)}, u32[]{:S(2)}, u32[]{:S(2)}) collective-permute-start(f32[192,128]{1,0:T(8,128)S(1)} %select_bitcast_fusion), channel_id=1, source_target_pairs={{0,16},{16,0},{1,17},{17,1},{2,18},{18,2},{3,19},{19,3},{4,20},{20... | collective-permute-start | bytes 294920 | tf_op jit(solution)/shard_map/ppermute | solution.py:263
  115.4 3.1 %collective-permute-done.10 = f32[192,128]{1,0:T(8,128)S(1)} collective-permute-done((f32[192,128]{1,0:T(8,128)S(1)}, f32[192,128]{1,0:T(8,128)S(1)}, u32[]{:S(2)}, u32[]{:S(2)}) %collective-permute-start.10) | collective-permute-done | bytes 98336 | tf_op jit(solution)/shard_map/ppermute | solution.py:263
  118.6 1.9 %collective-permute-start.11 = (bf16[6144,128]{1,0:T(8,128)(2,1)S(1)}, bf16[6144,128]{1,0:T(8,128)(2,1)S(1)}, u32[]{:S(2)}, u32[]{:S(2)}) collective-permute-start(bf16[6144,128]{1,0:T(8,128)(2,1)S(1)} %join.1), channel_id=1, source_target_pairs={{0,1},{1,0},{2,3},{3,2},{4,5},{5,4},{6,7},{7,6},{8,9},{9,8},{10,11... | collective-permute-start | bytes 4718600 | tf_op jit(solution)/shard_map/ppermute | solution.py:263
  121.1 2.8 %collective-permute-done.11.refs_4_ = bf16[6144,128]{1,0:T(8,128)(2,1)S(1)} collective-permute-done((bf16[6144,128]{1,0:T(8,128)(2,1)S(1)}, bf16[6144,128]{1,0:T(8,128)(2,1)S(1)}, u32[]{:S(2)}, u32[]{:S(2)}) %collective-permute-start.11) | collective-permute-done | bytes 1572896 | tf_op jit(solution)/shard_map/ppermute | solution.py:263
  123.9 5.7 %attend.1 = bf16[192,128]{1,0:T(8,128)(2,1)} custom-call(s32[3]{0:T(128)S(1)} %pad_add_fusion.info_ref, f32[192,128]{1,0:T(8,128)S(1)} %bitcast_add_fusion.q_ref, f32[192,128]{1,0:T(8,128)S(1)} %get-tuple-element.46.cos_ref, f32[192,128]{1,0:T(8,128)S(1)} %get-tuple-element.47.sin_ref, bf16[1536,128]{1,0:T(8,128)(2,1)S(1)} %bitcast.13, ...), custom_call_target="tpu_custom_call" | custom-call | flops 603979776 | bytes 3145728 | tf_op jit(solution)/shard_map/attend/pallas_call | solution.py:231
  (42 shorter events, 11.3 us)
Async XLA Ops:
  6.5 1.0 copy-start.2
  7.6 12.6 %copy-start.4 = (bf16[512,128]{1,0:T(8,128)(2,1)S(1)}, bf16[512,128]{1,0:T(8,128)(2,1)}, u32[]{:S(2)}) copy-start(bf16[512,128]{1,0:T(8,128)(2,1)} %param.4) | copy-start | bytes 393220
  7.6 35.9 %copy-start.3 = (bf16[1024,256]{1,0:T(8,128)(2,1)S(1)}, bf16[1024,256]{1,0:T(8,128)(2,1)}, u32[]{:S(2)}) copy-start(bf16[1024,256]{1,0:T(8,128)(2,1)} %w_ref.1) | copy-start | bytes 1572868
  8.4 35.0 %all-to-all-start = ((bf16[32,12,512]{2,1,0:T(8,128)(2,1)}), bf16[32,12,512]{2,1,0:T(8,128)(2,1)S(1)}, u32[]{:S(2)}, u32[]{:S(2)}) async-start(bf16[32,12,512]{2,1,0:T(8,128)(2,1)} %slabs.1), calls=%async_computation | async-start | bytes 1048576 | tf_op jit(solution)/shard_map/all_to_all | solution.py:275
  20.2 84.2 %all-gather.3.cloned.1.call-start = ((), (), s32[]{:S(2)}) async-start(), calls=%async_computation.3 | async-start | bytes 6684672 | tf_op jit(solution)/shard_map/all_gather | solution.py:280
  20.2 16.0 %collective-permute-start = (bf16[512,128]{1,0:T(8,128)(2,1)S(1)}, bf16[512,128]{1,0:T(8,128)(2,1)S(1)}, u32[]{:S(2)}, u32[]{:S(2)}) collective-permute-start(bf16[512,128]{1,0:T(8,128)(2,1)S(1)} %copy-done.4), channel_id=1, source_target_pairs={{0,32},{32,64},{64,96},{96,0},{1,33},{33,65},{65,97},{97,1},{2,34}... | collective-permute-start | bytes 393224 | tf_op jit(solution)/shard_map/ppermute | solution.py:254
  24.7 15.7 %collective-permute-start.1 = (bf16[512,128]{1,0:T(8,128)(2,1)S(1)}, bf16[512,128]{1,0:T(8,128)(2,1)S(1)}, u32[]{:S(2)}, u32[]{:S(2)}) collective-permute-start(bf16[512,128]{1,0:T(8,128)(2,1)S(1)} %copy-done.4), channel_id=1, source_target_pairs={{0,64},{32,96},{64,0},{96,32},{1,65},{33,97},{65,1},{97,33},{2,66}... | collective-permute-start | bytes 393224 | tf_op jit(solution)/shard_map/ppermute | solution.py:254
  29.8 13.7 %collective-permute-start.2 = (bf16[512,128]{1,0:T(8,128)(2,1)S(1)}, bf16[512,128]{1,0:T(8,128)(2,1)S(1)}, u32[]{:S(2)}, u32[]{:S(2)}) collective-permute-start(bf16[512,128]{1,0:T(8,128)(2,1)S(1)} %copy-done.4), channel_id=1, source_target_pairs={{0,96},{32,0},{64,32},{96,64},{1,97},{33,1},{65,33},{97,65},{2,98}... | collective-permute-start | bytes 393224 | tf_op jit(solution)/shard_map/ppermute | solution.py:254
  45.1 20.6 %all-to-all-start.1 = ((f32[32,24,128]{2,1,0:T(8,128)}), f32[32,24,128]{2,1,0:T(8,128)S(1)}, u32[]{:S(2)}, u32[]{:S(2)}) async-start(f32[32,24,128]{2,1,0:T(8,128)} %get-tuple-element.31), calls=%async_computation.1 | async-start | bytes 786432 | tf_op jit(solution)/shard_map/all_to_all | solution.py:283
  52.3 44.4 %copy-start = (bf16[2048,128]{1,0:T(8,128)(2,1)}, bf16[2048,128]{1,0:T(8,128)(2,1)S(1)}, u32[]{:S(2)}) copy-start(bf16[2048,128]{1,0:T(8,128)(2,1)S(1)} %constant_dynamic-update-slice_fusion.refs_0_) | copy-start | bytes 1572868
  52.3 24.8 %collective-permute-start.3 = (bf16[2048,128]{1,0:T(8,128)(2,1)S(1)}, bf16[2048,128]{1,0:T(8,128)(2,1)S(1)}, u32[]{:S(2)}, u32[]{:S(2)}) collective-permute-start(bf16[2048,128]{1,0:T(8,128)(2,1)S(1)} %constant_dynamic-update-slice_fusion.refs_0_), channel_id=1, source_target_pairs={{0,128},{128,256},{256,384},{384,0},{1,129},{129,257},{257,385},{3... | collective-permute-start | bytes 1572872 | tf_op jit(solution)/shard_map/ppermute | solution.py:254
  54.7 22.4 %collective-permute-start.4 = (bf16[2048,128]{1,0:T(8,128)(2,1)S(1)}, bf16[2048,128]{1,0:T(8,128)(2,1)S(1)}, u32[]{:S(2)}, u32[]{:S(2)}) collective-permute-start(bf16[2048,128]{1,0:T(8,128)(2,1)S(1)} %constant_dynamic-update-slice_fusion.refs_0_), channel_id=1, source_target_pairs={{0,384},{128,0},{256,128},{384,256},{1,385},{129,1},{257,129},{385... | collective-permute-start | bytes 1572872 | tf_op jit(solution)/shard_map/ppermute | solution.py:254
  66.8 27.4 %all-to-all-start.2 = ((bf16[64,24,128]{2,1,0:T(8,128)(2,1)}), bf16[64,24,128]{2,1,0:T(8,128)(2,1)S(1)}, u32[]{:S(2)}, u32[]{:S(2)}) async-start(bf16[64,24,128]{2,1,0:T(8,128)(2,1)} %broadcast_in_dim.2), calls=%async_computation.2 | async-start | bytes 786432 | tf_op jit(solution)/shard_map/all_to_all | solution.py:40
  77.2 9.6 %collective-permute-start.5 = (bf16[1024,128]{1,0:T(8,128)(2,1)S(1)}, bf16[1024,128]{1,0:T(8,128)(2,1)S(1)}, u32[]{:S(2)}, u32[]{:S(2)}) collective-permute-start(bf16[1024,128]{1,0:T(8,128)(2,1)S(1)} %get-tuple-element.32), channel_id=1, source_target_pairs={{0,128},{128,256},{256,384},{384,0},{1,129},{129,257},{257,385},{3... | collective-permute-start | bytes 786440 | tf_op jit(solution)/shard_map/ppermute | solution.py:254
  79.6 10.7 %collective-permute-start.6 = (bf16[1024,128]{1,0:T(8,128)(2,1)S(1)}, bf16[1024,128]{1,0:T(8,128)(2,1)}, u32[]{:S(2)}, u32[]{:S(2)}) collective-permute-start(bf16[1024,128]{1,0:T(8,128)(2,1)S(1)} %get-tuple-element.33), channel_id=1, source_target_pairs={{0,384},{128,0},{256,128},{384,256},{1,385},{129,1},{257,129},{385... | collective-permute-start | bytes 786440 | tf_op jit(solution)/shard_map/ppermute | solution.py:254
  94.1 20.9 %collective-permute-start.7 = (bf16[1536,128]{1,0:T(8,128)(2,1)S(1)}, bf16[1536,128]{1,0:T(8,128)(2,1)S(1)}, u32[]{:S(2)}, u32[]{:S(2)}) collective-permute-start(bf16[1536,128]{1,0:T(8,128)(2,1)S(1)} %bitcast.9), channel_id=1, source_target_pairs={{0,128},{128,256},{256,384},{1,129},{129,257},{257,385},{2,130},{1... | collective-permute-start | bytes 1179656 | tf_op jit(solution)/shard_map/ppermute | solution.py:259
  95.4 19.6 %collective-permute-start.8 = (bf16[1536,128]{1,0:T(8,128)(2,1)S(1)}, bf16[1536,128]{1,0:T(8,128)(2,1)S(1)}, u32[]{:S(2)}, u32[]{:S(2)}) collective-permute-start(bf16[1536,128]{1,0:T(8,128)(2,1)S(1)} %bitcast.10), channel_id=1, source_target_pairs={{0,256},{128,384},{1,257},{129,385},{2,258},{130,386},{3,259},{131... | collective-permute-start | bytes 1179656 | tf_op jit(solution)/shard_map/ppermute | solution.py:259
  96.7 18.7 %collective-permute-start.9 = (bf16[1536,128]{1,0:T(8,128)(2,1)S(1)}, bf16[1536,128]{1,0:T(8,128)(2,1)S(1)}, u32[]{:S(2)}, u32[]{:S(2)}) collective-permute-start(bf16[1536,128]{1,0:T(8,128)(2,1)S(1)} %bitcast.11), channel_id=1, source_target_pairs={{0,384},{1,385},{2,386},{3,387},{4,388},{5,389},{6,390},{7,391},{8... | collective-permute-start | bytes 1179656 | tf_op jit(solution)/shard_map/ppermute | solution.py:259
  104.4 1.0 copy-start.1
  111.6 6.8 %collective-permute-start.10 = (f32[192,128]{1,0:T(8,128)S(1)}, f32[192,128]{1,0:T(8,128)S(1)}, u32[]{:S(2)}, u32[]{:S(2)}) collective-permute-start(f32[192,128]{1,0:T(8,128)S(1)} %select_bitcast_fusion), channel_id=1, source_target_pairs={{0,16},{16,0},{1,17},{17,1},{2,18},{18,2},{3,19},{19,3},{4,20},{20... | collective-permute-start | bytes 294920 | tf_op jit(solution)/shard_map/ppermute | solution.py:263
  118.6 5.3 %collective-permute-start.11 = (bf16[6144,128]{1,0:T(8,128)(2,1)S(1)}, bf16[6144,128]{1,0:T(8,128)(2,1)S(1)}, u32[]{:S(2)}, u32[]{:S(2)}) collective-permute-start(bf16[6144,128]{1,0:T(8,128)(2,1)S(1)} %join.1), channel_id=1, source_target_pairs={{0,1},{1,0},{2,3},{3,2},{4,5},{5,4},{6,7},{7,6},{8,9},{9,8},{10,11... | collective-permute-start | bytes 4718600 | tf_op jit(solution)/shard_map/ppermute | solution.py:263
Sparse Core Ops, SparseCore 0:
  45.2 59.1 all-gather.2

commit v8 on v7

--- a/solution.py
+++ b/solution.py
@@ -274,11 +274,11 @@
     hs, w = tie((hs, query_weight))
     hs = lax.all_to_all(hs, PAIR, 0, 0, tiled=True)
 
-    w = [w] + [shift(w, "yq", d) for d in (1, 2, 3)]
-    hs, w = tie((hs, w))
+    one, three = shift(w, "yq", 1), shift(w, "yq", 3)
+    hs, w, one, three = tie((hs, w, one, three))
     h, part = mix(info, hs, kv_weight)
     h = lax.all_gather(h, TP, axis=0, tiled=False)
-    w = jnp.concatenate(w, axis=0)
+    w = jnp.concatenate([w, one, shift(w, "yq", 2), three], axis=0)
 
     part = lax.all_to_all(part, PAIR, 0, 0, tiled=True)
     up, down = shift(w, "x", 1), shift(w, "x", -1)

time: 138 us -> 135 us (0.978)
  waiting for transfers between devices: 38.5 us -> 34.6 us
    all_to_all x1, waiting for transfers between devices: 7.52 us -> 0.01 us  [body(): part = lax.all_to_all(part, PAIR, 0, 0, tiled=True)]
    ppermute x7, waiting for transfers between devices: 15.5 us -> 23 us  [shift(): return lax.ppermute(v, axis, [(i, (i + by) % n) for i in range(n)])]
    ppermute x3, waiting for transfers between devices: 0.36 us -> 6.07 us  [shift_up(): return lax.ppermute(v, axis, [(i, i + by) for i in range(n - by)])]
    all_gather x1, waiting for transfers between devices: 5.33 us -> 0.02 us  [body(): h = lax.all_gather(h, TP, axis=0, tiled=False)]
    all_to_all x1, starting transfers between devices: 10.4 us -> 13.6 us  [broadcast_gather(): lax.all_to_all(jnp.broadcast_to(x[None], (n,) + x.shape), axis, 0, 0, til...]
    ppermute x2, waiting for transfers between devices: 5.85 us -> 2.78 us  [swap(): return lax.ppermute(v, axis, [(0, 1), (1, 0)])]
    ppermute x7, starting transfers between devices: 26.5 us -> 24 us  [shift(): return lax.ppermute(v, axis, [(i, (i + by) % n) for i in range(n)])]
  transfers between devices with their start and end apart: 16 -> 16, of which waited for: 11 -> 8; matrix products, arithmetic and copies ran while one was open for 2% -> 2% of each run, Pallas kernels for 5% -> 5%
where the time goes in v8:
time: 135 us; the launch traced here: 133 us
  starting transfers between devices  65.6 us (49%)
  waiting for transfers between devices  34.6 us (26%)
  Pallas kernels  14.5 us (11%)
  between operations  13.8 us (10%)
  local copies, waits for them, and re-layouts  2.97 us (2%)
  other arithmetic  1.91 us (1%)
    ppermute x7, starting transfers between devices, shift(): return lax.ppermute(v, axis, [(i, (i + by) % n) for i in range(n)])  24 us
    ppermute x7, waiting for transfers between devices, shift(): return lax.ppermute(v, axis, [(i, (i + by) % n) for i in range(n)])  23 us
    all_to_all x1, starting transfers between devices, broadcast_gather(): lax.all_to_all(jnp.broadcast_to(x[None], (n,) + x.shape), axis, 0, 0, til...  13.6 us
    all_to_all x1, starting transfers between devices, body(): hs = lax.all_to_all(hs, PAIR, 0, 0, tiled=True)  11.7 us
    all_to_all x1, starting transfers between devices, body(): part = lax.all_to_all(part, PAIR, 0, 0, tiled=True)  7.8 us
    pallas_call x1, Pallas kernels, project(): pl.pallas_call(project_kernel, in_specs=[pl.BlockSpec(memory_space=pltpu....  6.18 us
    ppermute x3, waiting for transfers between devices, shift_up(): return lax.ppermute(v, axis, [(i, i + by) for i in range(n - by)])  6.07 us
    pallas_call x1, Pallas kernels, attend(): pl.pallas_call(attend_kernel, in_specs=[pl.BlockSpec(memory_space=pltpu.S...  5.75 us
  transfers between devices with their start and end apart: 16, of which 8 were waited for; matrix products, arithmetic and copies ran while one was open for 2% of the time, Pallas kernels for 5%

profile of v8, /device:TPU:6, one launch (start us, length us, event | category | flops | bytes accessed | tf_op | source)
XLA Modules:
  0.0 133.4 jit_solution(2757704831811343489)
XLA Ops:
  8.4 11.7 %all-to-all-start = ((bf16[32,12,512]{2,1,0:T(8,128)(2,1)}), bf16[32,12,512]{2,1,0:T(8,128)(2,1)S(1)}, u32[]{:S(2)}, u32[]{:S(2)}) async-start(bf16[32,12,512]{2,1,0:T(8,128)(2,1)} %slabs.1), calls=%async_computation | async-start | bytes 1048576 | tf_op jit(solution)/shard_map/all_to_all | solution.py:275
  20.2 4.5 %collective-permute-start = (bf16[512,128]{1,0:T(8,128)(2,1)S(1)}, bf16[512,128]{1,0:T(8,128)(2,1)S(1)}, u32[]{:S(2)}, u32[]{:S(2)}) collective-permute-start(bf16[512,128]{1,0:T(8,128)(2,1)S(1)} %copy-done.4), channel_id=1, source_target_pairs={{0,32},{32,64},{64,96},{96,0},{1,33},{33,65},{65,97},{97,1},{2,34}... | collective-permute-start | bytes 393224 | tf_op jit(solution)/shard_map/ppermute | solution.py:254
  24.7 3.5 %collective-permute-start.1 = (bf16[512,128]{1,0:T(8,128)(2,1)S(1)}, bf16[512,128]{1,0:T(8,128)(2,1)S(1)}, u32[]{:S(2)}, u32[]{:S(2)}) collective-permute-start(bf16[512,128]{1,0:T(8,128)(2,1)S(1)} %copy-done.4), channel_id=1, source_target_pairs={{0,96},{32,0},{64,32},{96,64},{1,97},{33,1},{65,33},{97,65},{2,98}... | collective-permute-start | bytes 393224 | tf_op jit(solution)/shard_map/ppermute | solution.py:254
  28.3 7.7 %collective-permute-done = bf16[512,128]{1,0:T(8,128)(2,1)S(1)} collective-permute-done((bf16[512,128]{1,0:T(8,128)(2,1)S(1)}, bf16[512,128]{1,0:T(8,128)(2,1)S(1)}, u32[]{:S(2)}, u32[]{:S(2)}) %collective-permute-start) | collective-permute-done | bytes 131104 | tf_op jit(solution)/shard_map/ppermute | solution.py:254
  36.0 1.6 %mix.1 = (bf16[384,512]{1,0:T(8,128)(2,1)}, f32[32,24,128]{2,1,0:T(8,128)}) custom-call(s32[3]{0:T(128)S(1)} %pad_add_fusion.info_ref, bf16[32,12,512]{2,1,0:T(8,128)(2,1)S(1)} %all-to-all-done.x_ref, bf16[1024,256]{1,0:T(8,128)(2,1)S(1)} %copy-done.3), custom_call_target="tpu_custom_call" | custom-call | flops 100663296 | bytes 1048576 | tf_op jit(solution)/shard_map/mix/pallas_call | solution.py:67
  37.6 7.8 %all-to-all-start.1 = ((f32[32,24,128]{2,1,0:T(8,128)}), f32[32,24,128]{2,1,0:T(8,128)S(1)}, u32[]{:S(2)}, u32[]{:S(2)}) async-start(f32[32,24,128]{2,1,0:T(8,128)} %get-tuple-element.29), calls=%async_computation.1 | async-start | bytes 786432 | tf_op jit(solution)/shard_map/all_to_all | solution.py:283
  45.5 4.3 %collective-permute-start.2 = (bf16[512,128]{1,0:T(8,128)(2,1)S(1)}, bf16[512,128]{1,0:T(8,128)(2,1)S(1)}, u32[]{:S(2)}, u32[]{:S(2)}) collective-permute-start(bf16[512,128]{1,0:T(8,128)(2,1)S(1)} %copy-done.4), channel_id=1, source_target_pairs={{0,64},{32,96},{64,0},{96,32},{1,65},{33,97},{65,1},{97,33},{2,66}... | collective-permute-start | bytes 393224 | tf_op jit(solution)/shard_map/ppermute | solution.py:254
  49.9 7.2 %collective-permute-done.2 = bf16[512,128]{1,0:T(8,128)(2,1)S(1)} collective-permute-done((bf16[512,128]{1,0:T(8,128)(2,1)S(1)}, bf16[512,128]{1,0:T(8,128)(2,1)S(1)}, u32[]{:S(2)}, u32[]{:S(2)}) %collective-permute-start.2) | collective-permute-done | bytes 131104 | tf_op jit(solution)/shard_map/ppermute | solution.py:254
  57.1 2.4 %collective-permute-start.3 = (bf16[2048,128]{1,0:T(8,128)(2,1)S(1)}, bf16[2048,128]{1,0:T(8,128)(2,1)S(1)}, u32[]{:S(2)}, u32[]{:S(2)}) collective-permute-start(bf16[2048,128]{1,0:T(8,128)(2,1)S(1)} %constant_dynamic-update-slice_fusion.refs_0_), channel_id=1, source_target_pairs={{0,128},{128,256},{256,384},{384,0},{1,129},{129,257},{257,385},{3... | collective-permute-start | bytes 1572872 | tf_op jit(solution)/shard_map/ppermute | solution.py:254
  59.5 3.5 %collective-permute-start.4 = (bf16[2048,128]{1,0:T(8,128)(2,1)S(1)}, bf16[2048,128]{1,0:T(8,128)(2,1)S(1)}, u32[]{:S(2)}, u32[]{:S(2)}) collective-permute-start(bf16[2048,128]{1,0:T(8,128)(2,1)S(1)} %constant_dynamic-update-slice_fusion.refs_0_), channel_id=1, source_target_pairs={{0,384},{128,0},{256,128},{384,256},{1,385},{129,1},{257,129},{385... | collective-permute-start | bytes 1572872 | tf_op jit(solution)/shard_map/ppermute | solution.py:254
  64.1 13.6 %all-to-all-start.2 = ((bf16[64,24,128]{2,1,0:T(8,128)(2,1)}), bf16[64,24,128]{2,1,0:T(8,128)(2,1)S(1)}, u32[]{:S(2)}, u32[]{:S(2)}) async-start(bf16[64,24,128]{2,1,0:T(8,128)(2,1)} %broadcast_in_dim.2), calls=%async_computation.2 | async-start | bytes 786432 | tf_op jit(solution)/shard_map/all_to_all | solution.py:40
  77.8 3.6 %collective-permute-start.5 = (bf16[1024,128]{1,0:T(8,128)(2,1)S(1)}, bf16[1024,128]{1,0:T(8,128)(2,1)S(1)}, u32[]{:S(2)}, u32[]{:S(2)}) collective-permute-start(bf16[1024,128]{1,0:T(8,128)(2,1)S(1)} %get-tuple-element.30), channel_id=1, source_target_pairs={{0,128},{128,256},{256,384},{384,0},{1,129},{129,257},{257,385},{3... | collective-permute-start | bytes 786440 | tf_op jit(solution)/shard_map/ppermute | solution.py:254
  81.4 2.2 %collective-permute-start.6 = (bf16[1024,128]{1,0:T(8,128)(2,1)S(1)}, bf16[1024,128]{1,0:T(8,128)(2,1)}, u32[]{:S(2)}, u32[]{:S(2)}) collective-permute-start(bf16[1024,128]{1,0:T(8,128)(2,1)S(1)} %get-tuple-element.31), channel_id=1, source_target_pairs={{0,384},{128,0},{256,128},{384,256},{1,385},{129,1},{257,129},{385... | collective-permute-start | bytes 786440 | tf_op jit(solution)/shard_map/ppermute | solution.py:254
  83.6 3.4 %collective-permute-done.5 = bf16[1024,128]{1,0:T(8,128)(2,1)S(1)} collective-permute-done((bf16[1024,128]{1,0:T(8,128)(2,1)S(1)}, bf16[1024,128]{1,0:T(8,128)(2,1)S(1)}, u32[]{:S(2)}, u32[]{:S(2)}) %collective-permute-start.5) | collective-permute-done | bytes 262176 | tf_op jit(solution)/shard_map/ppermute | solution.py:254
  87.1 4.6 %collective-permute-done.6 = bf16[1024,128]{1,0:T(8,128)(2,1)} collective-permute-done((bf16[1024,128]{1,0:T(8,128)(2,1)S(1)}, bf16[1024,128]{1,0:T(8,128)(2,1)}, u32[]{:S(2)}, u32[]{:S(2)}) %collective-permute-start.6) | collective-permute-done | bytes 262176 | tf_op jit(solution)/shard_map/ppermute | solution.py:254
  91.7 2.7 %all-to-all-done.2 = bf16[64,24,128]{2,1,0:T(8,128)(2,1)S(1)} async-done(((bf16[64,24,128]{2,1,0:T(8,128)(2,1)}), bf16[64,24,128]{2,1,0:T(8,128)(2,1)S(1)}, u32[]{:S(2)}, u32[]{:S(2)}) %all-to-all-start.2) | async-done | bytes 393248 | tf_op jit(solution)/shard_map/all_to_all | solution.py:40
  95.7 1.3 collective-permute-start.8
  97.0 1.3 collective-permute-start.9
  100.3 6.2 %project.1 = f32[2,192,128]{2,1,0:T(8,128)S(1)} custom-call(s32[3]{0:T(128)S(1)} %pad_add_fusion.info_ref, bf16[16,384,512]{2,1,0:T(8,128)(2,1)} %bitcast.14, bf16[2048,128]{1,0:T(8,128)(2,1)S(1)} %copy-done.1, bf16[2048,128]{1,0:T(8,128)(2,1)S(1)} %collective-permute-done.3.up_ref.refs_1_, bf16[2048,128]{1,0:T(8,128)(2,1)S(1)} %pad_maximum_fusion.refs_2_, ...), custom_call_target="tpu_custom_call" | custom-call | flops 805306368 | bytes 8388608 | tf_op jit(solution)/shard_map/project/pallas_call | solution.py:209
  106.6 2.7 %collective-permute-start.10 = (f32[192,128]{1,0:T(8,128)S(1)}, f32[192,128]{1,0:T(8,128)S(1)}, u32[]{:S(2)}, u32[]{:S(2)}) collective-permute-start(f32[192,128]{1,0:T(8,128)S(1)} %select_bitcast_fusion), channel_id=1, source_target_pairs={{0,16},{16,0},{1,17},{17,1},{2,18},{18,2},{3,19},{19,3},{4,20},{20... | collective-permute-start | bytes 294920 | tf_op jit(solution)/shard_map/ppermute | solution.py:263
  109.3 6.1 %collective-permute-done.9.refs_3_ = bf16[1536,128]{1,0:T(8,128)(2,1)S(1)} collective-permute-done((bf16[1536,128]{1,0:T(8,128)(2,1)S(1)}, bf16[1536,128]{1,0:T(8,128)(2,1)S(1)}, u32[]{:S(2)}, u32[]{:S(2)}) %collective-permute-start.9) | collective-permute-done | bytes 393248 | tf_op jit(solution)/shard_map/ppermute | solution.py:259
  115.5 1.9 %collective-permute-start.11 = (bf16[6144,128]{1,0:T(8,128)(2,1)S(1)}, bf16[6144,128]{1,0:T(8,128)(2,1)S(1)}, u32[]{:S(2)}, u32[]{:S(2)}) collective-permute-start(bf16[6144,128]{1,0:T(8,128)(2,1)S(1)} %join.1), channel_id=1, source_target_pairs={{0,1},{1,0},{2,3},{3,2},{4,5},{5,4},{6,7},{7,6},{8,9},{9,8},{10,11... | collective-permute-start | bytes 4718600 | tf_op jit(solution)/shard_map/ppermute | solution.py:263
  118.0 2.8 %collective-permute-done.11.refs_4_ = bf16[6144,128]{1,0:T(8,128)(2,1)S(1)} collective-permute-done((bf16[6144,128]{1,0:T(8,128)(2,1)S(1)}, bf16[6144,128]{1,0:T(8,128)(2,1)S(1)}, u32[]{:S(2)}, u32[]{:S(2)}) %collective-permute-start.11) | collective-permute-done | bytes 1572896 | tf_op jit(solution)/shard_map/ppermute | solution.py:263
  120.8 5.7 %attend.1 = bf16[192,128]{1,0:T(8,128)(2,1)} custom-call(s32[3]{0:T(128)S(1)} %pad_add_fusion.info_ref, f32[192,128]{1,0:T(8,128)S(1)} %bitcast_add_fusion.q_ref, f32[192,128]{1,0:T(8,128)S(1)} %get-tuple-element.44.cos_ref, f32[192,128]{1,0:T(8,128)S(1)} %get-tuple-element.45.sin_ref, bf16[1536,128]{1,0:T(8,128)(2,1)S(1)} %bitcast.13, ...), custom_call_target="tpu_custom_call" | custom-call | flops 603979776 | bytes 3145728 | tf_op jit(solution)/shard_map/attend/pallas_call | solution.py:231
  (42 shorter events, 7.3 us)
Async XLA Ops:
  6.5 1.0 copy-start.2
  7.6 12.6 %copy-start.4 = (bf16[512,128]{1,0:T(8,128)(2,1)S(1)}, bf16[512,128]{1,0:T(8,128)(2,1)}, u32[]{:S(2)}) copy-start(bf16[512,128]{1,0:T(8,128)(2,1)} %param.4) | copy-start | bytes 393220
  7.6 28.4 %copy-start.3 = (bf16[1024,256]{1,0:T(8,128)(2,1)S(1)}, bf16[1024,256]{1,0:T(8,128)(2,1)}, u32[]{:S(2)}) copy-start(bf16[1024,256]{1,0:T(8,128)(2,1)} %w_ref.1) | copy-start | bytes 1572868
  8.4 27.6 %all-to-all-start = ((bf16[32,12,512]{2,1,0:T(8,128)(2,1)}), bf16[32,12,512]{2,1,0:T(8,128)(2,1)S(1)}, u32[]{:S(2)}, u32[]{:S(2)}) async-start(bf16[32,12,512]{2,1,0:T(8,128)(2,1)} %slabs.1), calls=%async_computation | async-start | bytes 1048576 | tf_op jit(solution)/shard_map/all_to_all | solution.py:275
  20.2 79.1 %all-gather.3.cloned.1.call-start = ((), (), s32[]{:S(2)}) async-start(), calls=%async_computation.3 | async-start | bytes 6684672 | tf_op jit(solution)/shard_map/all_gather | solution.py:280
  20.2 15.7 %collective-permute-start = (bf16[512,128]{1,0:T(8,128)(2,1)S(1)}, bf16[512,128]{1,0:T(8,128)(2,1)S(1)}, u32[]{:S(2)}, u32[]{:S(2)}) collective-permute-start(bf16[512,128]{1,0:T(8,128)(2,1)S(1)} %copy-done.4), channel_id=1, source_target_pairs={{0,32},{32,64},{64,96},{96,0},{1,33},{33,65},{65,97},{97,1},{2,34}... | collective-permute-start | bytes 393224 | tf_op jit(solution)/shard_map/ppermute | solution.py:254
  24.7 11.2 %collective-permute-start.1 = (bf16[512,128]{1,0:T(8,128)(2,1)S(1)}, bf16[512,128]{1,0:T(8,128)(2,1)S(1)}, u32[]{:S(2)}, u32[]{:S(2)}) collective-permute-start(bf16[512,128]{1,0:T(8,128)(2,1)S(1)} %copy-done.4), channel_id=1, source_target_pairs={{0,96},{32,0},{64,32},{96,64},{1,97},{33,1},{65,33},{97,65},{2,98}... | collective-permute-start | bytes 393224 | tf_op jit(solution)/shard_map/ppermute | solution.py:254
  37.6 25.4 %all-to-all-start.1 = ((f32[32,24,128]{2,1,0:T(8,128)}), f32[32,24,128]{2,1,0:T(8,128)S(1)}, u32[]{:S(2)}, u32[]{:S(2)}) async-start(f32[32,24,128]{2,1,0:T(8,128)} %get-tuple-element.29), calls=%async_computation.1 | async-start | bytes 786432 | tf_op jit(solution)/shard_map/all_to_all | solution.py:283
  45.5 11.6 %collective-permute-start.2 = (bf16[512,128]{1,0:T(8,128)(2,1)S(1)}, bf16[512,128]{1,0:T(8,128)(2,1)S(1)}, u32[]{:S(2)}, u32[]{:S(2)}) collective-permute-start(bf16[512,128]{1,0:T(8,128)(2,1)S(1)} %copy-done.4), channel_id=1, source_target_pairs={{0,64},{32,96},{64,0},{96,32},{1,65},{33,97},{65,1},{97,33},{2,66}... | collective-permute-start | bytes 393224 | tf_op jit(solution)/shard_map/ppermute | solution.py:254
  57.1 39.8 %copy-start = (bf16[2048,128]{1,0:T(8,128)(2,1)}, bf16[2048,128]{1,0:T(8,128)(2,1)S(1)}, u32[]{:S(2)}) copy-start(bf16[2048,128]{1,0:T(8,128)(2,1)S(1)} %constant_dynamic-update-slice_fusion.refs_0_) | copy-start | bytes 1572868
  57.1 20.6 %collective-permute-start.3 = (bf16[2048,128]{1,0:T(8,128)(2,1)S(1)}, bf16[2048,128]{1,0:T(8,128)(2,1)S(1)}, u32[]{:S(2)}, u32[]{:S(2)}) collective-permute-start(bf16[2048,128]{1,0:T(8,128)(2,1)S(1)} %constant_dynamic-update-slice_fusion.refs_0_), channel_id=1, source_target_pairs={{0,128},{128,256},{256,384},{384,0},{1,129},{129,257},{257,385},{3... | collective-permute-start | bytes 1572872 | tf_op jit(solution)/shard_map/ppermute | solution.py:254
  59.5 18.2 %collective-permute-start.4 = (bf16[2048,128]{1,0:T(8,128)(2,1)S(1)}, bf16[2048,128]{1,0:T(8,128)(2,1)S(1)}, u32[]{:S(2)}, u32[]{:S(2)}) collective-permute-start(bf16[2048,128]{1,0:T(8,128)(2,1)S(1)} %constant_dynamic-update-slice_fusion.refs_0_), channel_id=1, source_target_pairs={{0,384},{128,0},{256,128},{384,256},{1,385},{129,1},{257,129},{385... | collective-permute-start | bytes 1572872 | tf_op jit(solution)/shard_map/ppermute | solution.py:254
  64.1 30.3 %all-to-all-start.2 = ((bf16[64,24,128]{2,1,0:T(8,128)(2,1)}), bf16[64,24,128]{2,1,0:T(8,128)(2,1)S(1)}, u32[]{:S(2)}, u32[]{:S(2)}) async-start(bf16[64,24,128]{2,1,0:T(8,128)(2,1)} %broadcast_in_dim.2), calls=%async_computation.2 | async-start | bytes 786432 | tf_op jit(solution)/shard_map/all_to_all | solution.py:40
  77.8 9.3 %collective-permute-start.5 = (bf16[1024,128]{1,0:T(8,128)(2,1)S(1)}, bf16[1024,128]{1,0:T(8,128)(2,1)S(1)}, u32[]{:S(2)}, u32[]{:S(2)}) collective-permute-start(bf16[1024,128]{1,0:T(8,128)(2,1)S(1)} %get-tuple-element.30), channel_id=1, source_target_pairs={{0,128},{128,256},{256,384},{384,0},{1,129},{129,257},{257,385},{3... | collective-permute-start | bytes 786440 | tf_op jit(solution)/shard_map/ppermute | solution.py:254
  81.4 10.3 %collective-permute-start.6 = (bf16[1024,128]{1,0:T(8,128)(2,1)S(1)}, bf16[1024,128]{1,0:T(8,128)(2,1)}, u32[]{:S(2)}, u32[]{:S(2)}) collective-permute-start(bf16[1024,128]{1,0:T(8,128)(2,1)S(1)} %get-tuple-element.31), channel_id=1, source_target_pairs={{0,384},{128,0},{256,128},{384,256},{1,385},{129,1},{257,129},{385... | collective-permute-start | bytes 786440 | tf_op jit(solution)/shard_map/ppermute | solution.py:254
  94.4 14.9 %collective-permute-start.7 = (bf16[1536,128]{1,0:T(8,128)(2,1)S(1)}, bf16[1536,128]{1,0:T(8,128)(2,1)S(1)}, u32[]{:S(2)}, u32[]{:S(2)}) collective-permute-start(bf16[1536,128]{1,0:T(8,128)(2,1)S(1)} %bitcast.9), channel_id=1, source_target_pairs={{0,128},{128,256},{256,384},{1,129},{129,257},{257,385},{2,130},{1... | collective-permute-start | bytes 1179656 | tf_op jit(solution)/shard_map/ppermute | solution.py:259
  95.7 13.6 %collective-permute-start.8 = (bf16[1536,128]{1,0:T(8,128)(2,1)S(1)}, bf16[1536,128]{1,0:T(8,128)(2,1)S(1)}, u32[]{:S(2)}, u32[]{:S(2)}) collective-permute-start(bf16[1536,128]{1,0:T(8,128)(2,1)S(1)} %bitcast.10), channel_id=1, source_target_pairs={{0,256},{128,384},{1,257},{129,385},{2,258},{130,386},{3,259},{131... | collective-permute-start | bytes 1179656 | tf_op jit(solution)/shard_map/ppermute | solution.py:259
  97.0 18.4 %collective-permute-start.9 = (bf16[1536,128]{1,0:T(8,128)(2,1)S(1)}, bf16[1536,128]{1,0:T(8,128)(2,1)S(1)}, u32[]{:S(2)}, u32[]{:S(2)}) collective-permute-start(bf16[1536,128]{1,0:T(8,128)(2,1)S(1)} %bitcast.11), channel_id=1, source_target_pairs={{0,384},{1,385},{2,386},{3,387},{4,388},{5,389},{6,390},{7,391},{8... | collective-permute-start | bytes 1179656 | tf_op jit(solution)/shard_map/ppermute | solution.py:259
  99.3 1.0 copy-start.1
  106.6 8.8 %collective-permute-start.10 = (f32[192,128]{1,0:T(8,128)S(1)}, f32[192,128]{1,0:T(8,128)S(1)}, u32[]{:S(2)}, u32[]{:S(2)}) collective-permute-start(f32[192,128]{1,0:T(8,128)S(1)} %select_bitcast_fusion), channel_id=1, source_target_pairs={{0,16},{16,0},{1,17},{17,1},{2,18},{18,2},{3,19},{19,3},{4,20},{20... | collective-permute-start | bytes 294920 | tf_op jit(solution)/shard_map/ppermute | solution.py:263
  115.5 5.3 %collective-permute-start.11 = (bf16[6144,128]{1,0:T(8,128)(2,1)S(1)}, bf16[6144,128]{1,0:T(8,128)(2,1)S(1)}, u32[]{:S(2)}, u32[]{:S(2)}) collective-permute-start(bf16[6144,128]{1,0:T(8,128)(2,1)S(1)} %join.1), channel_id=1, source_target_pairs={{0,1},{1,0},{2,3},{3,2},{4,5},{5,4},{6,7},{7,6},{8,9},{9,8},{10,11... | collective-permute-start | bytes 4718600 | tf_op jit(solution)/shard_map/ppermute | solution.py:263
Sparse Core Ops, SparseCore 0:
  37.8 59.7 all-gather.2

commit v9 on v8

--- a/solution.py
+++ b/solution.py
@@ -278,7 +278,7 @@
     hs, w, one, three = tie((hs, w, one, three))
     h, part = mix(info, hs, kv_weight)
     h = lax.all_gather(h, TP, axis=0, tiled=False)
-    w = jnp.concatenate([w, one, shift(w, "yq", 2), three], axis=0)
+    w = jnp.concatenate([w, one, shift(one, "yq", 1), three], axis=0)
 
     part = lax.all_to_all(part, PAIR, 0, 0, tiled=True)
     up, down = shift(w, "x", 1), shift(w, "x", -1)

time: 135 us -> 135 us (level)
  starting transfers between devices: 65.6 us -> 63.6 us
    all_to_all x1, starting transfers between devices: 13.6 us -> 11.3 us  [broadcast_gather(): lax.all_to_all(jnp.broadcast_to(x[None], (n,) + x.shape), axis, 0, 0, til...]
  transfers between devices with their start and end apart: 16 -> 16, of which waited for: 8 -> 9; matrix products, arithmetic and copies ran while one was open for 2% -> 2% of each run, Pallas kernels for 5% -> 5%
where the time goes in v9:
time: 135 us; the launch traced here: 132 us
  starting transfers between devices  63.6 us (47%)
  waiting for transfers between devices  35.6 us (26%)
  Pallas kernels  14.5 us (11%)
  between operations  13.8 us (10%)
  local copies, waits for them, and re-layouts  2.97 us (2%)
  other arithmetic  1.91 us (1%)
    ppermute x7, starting transfers between devices, shift(): return lax.ppermute(v, axis, [(i, (i + by) % n) for i in range(n)])  24.8 us
    ppermute x7, waiting for transfers between devices, shift(): return lax.ppermute(v, axis, [(i, (i + by) % n) for i in range(n)])  24 us
    all_to_all x1, starting transfers between devices, body(): hs = lax.all_to_all(hs, PAIR, 0, 0, tiled=True)  11.7 us
    all_to_all x1, starting transfers between devices, broadcast_gather(): lax.all_to_all(jnp.broadcast_to(x[None], (n,) + x.shape), axis, 0, 0, til...  11.3 us
    all_to_all x1, starting transfers between devices, body(): part = lax.all_to_all(part, PAIR, 0, 0, tiled=True)  7.8 us
    pallas_call x1, Pallas kernels, project(): pl.pallas_call(project_kernel, in_specs=[pl.BlockSpec(memory_space=pltpu....  6.18 us
    ppermute x3, waiting for transfers between devices, shift_up(): return lax.ppermute(v, axis, [(i, i + by) for i in range(n - by)])  5.9 us
    pallas_call x1, Pallas kernels, attend(): pl.pallas_call(attend_kernel, in_specs=[pl.BlockSpec(memory_space=pltpu.S...  5.75 us
  transfers between devices with their start and end apart: 16, of which 9 were waited for; matrix products, arithmetic and copies ran while one was open for 2% of the time, Pallas kernels for 5%

profile of v9, /device:TPU:6, one launch (start us, length us, event | category | flops | bytes accessed | tf_op | source)
XLA Modules:
  0.0 132.4 jit_solution(6633864513465490704)
XLA Ops:
  8.4 11.7 %all-to-all-start = ((bf16[32,12,512]{2,1,0:T(8,128)(2,1)}), bf16[32,12,512]{2,1,0:T(8,128)(2,1)S(1)}, u32[]{:S(2)}, u32[]{:S(2)}) async-start(bf16[32,12,512]{2,1,0:T(8,128)(2,1)} %slabs.1), calls=%async_computation | async-start | bytes 1048576 | tf_op jit(solution)/shard_map/all_to_all | solution.py:275
  20.2 4.5 %collective-permute-start = (bf16[512,128]{1,0:T(8,128)(2,1)S(1)}, bf16[512,128]{1,0:T(8,128)(2,1)S(1)}, u32[]{:S(2)}, u32[]{:S(2)}) collective-permute-start(bf16[512,128]{1,0:T(8,128)(2,1)S(1)} %copy-done.4), channel_id=1, source_target_pairs={{0,32},{32,64},{64,96},{96,0},{1,33},{33,65},{65,97},{97,1},{2,34}... | collective-permute-start | bytes 393224 | tf_op jit(solution)/shard_map/ppermute | solution.py:254
  24.7 3.5 %collective-permute-start.1 = (bf16[512,128]{1,0:T(8,128)(2,1)S(1)}, bf16[512,128]{1,0:T(8,128)(2,1)S(1)}, u32[]{:S(2)}, u32[]{:S(2)}) collective-permute-start(bf16[512,128]{1,0:T(8,128)(2,1)S(1)} %copy-done.4), channel_id=1, source_target_pairs={{0,96},{32,0},{64,32},{96,64},{1,97},{33,1},{65,33},{97,65},{2,98}... | collective-permute-start | bytes 393224 | tf_op jit(solution)/shard_map/ppermute | solution.py:254
  28.3 7.7 %collective-permute-done = bf16[512,128]{1,0:T(8,128)(2,1)S(1)} collective-permute-done((bf16[512,128]{1,0:T(8,128)(2,1)S(1)}, bf16[512,128]{1,0:T(8,128)(2,1)S(1)}, u32[]{:S(2)}, u32[]{:S(2)}) %collective-permute-start) | collective-permute-done | bytes 131104 | tf_op jit(solution)/shard_map/ppermute | solution.py:254
  36.0 1.6 %mix.1 = (bf16[384,512]{1,0:T(8,128)(2,1)}, f32[32,24,128]{2,1,0:T(8,128)}) custom-call(s32[3]{0:T(128)S(1)} %pad_add_fusion.info_ref, bf16[32,12,512]{2,1,0:T(8,128)(2,1)S(1)} %all-to-all-done.x_ref, bf16[1024,256]{1,0:T(8,128)(2,1)S(1)} %copy-done.3), custom_call_target="tpu_custom_call" | custom-call | flops 100663296 | bytes 1048576 | tf_op jit(solution)/shard_map/mix/pallas_call | solution.py:67
  37.6 7.8 %all-to-all-start.1 = ((f32[32,24,128]{2,1,0:T(8,128)}), f32[32,24,128]{2,1,0:T(8,128)S(1)}, u32[]{:S(2)}, u32[]{:S(2)}) async-start(f32[32,24,128]{2,1,0:T(8,128)} %get-tuple-element.29), calls=%async_computation.1 | async-start | bytes 786432 | tf_op jit(solution)/shard_map/all_to_all | solution.py:283
  45.5 5.2 %collective-permute-start.2 = (bf16[512,128]{1,0:T(8,128)(2,1)S(1)}, bf16[512,128]{1,0:T(8,128)(2,1)S(1)}, u32[]{:S(2)}, u32[]{:S(2)}) collective-permute-start(bf16[512,128]{1,0:T(8,128)(2,1)S(1)} %collective-permute-done), channel_id=1, source_target_pairs={{0,32},{32,64},{64,96},{96,0},{1,33},{33,65},{65,97},{97,1},{2,34}... | collective-permute-start | bytes 393224 | tf_op jit(solution)/shard_map/ppermute | solution.py:254
  50.7 8.6 %collective-permute-done.2 = bf16[512,128]{1,0:T(8,128)(2,1)S(1)} collective-permute-done((bf16[512,128]{1,0:T(8,128)(2,1)S(1)}, bf16[512,128]{1,0:T(8,128)(2,1)S(1)}, u32[]{:S(2)}, u32[]{:S(2)}) %collective-permute-start.2) | collective-permute-done | bytes 131104 | tf_op jit(solution)/shard_map/ppermute | solution.py:254
  59.4 2.4 %collective-permute-start.3 = (bf16[2048,128]{1,0:T(8,128)(2,1)S(1)}, bf16[2048,128]{1,0:T(8,128)(2,1)S(1)}, u32[]{:S(2)}, u32[]{:S(2)}) collective-permute-start(bf16[2048,128]{1,0:T(8,128)(2,1)S(1)} %constant_dynamic-update-slice_fusion.refs_0_), channel_id=1, source_target_pairs={{0,128},{128,256},{256,384},{384,0},{1,129},{129,257},{257,385},{3... | collective-permute-start | bytes 1572872 | tf_op jit(solution)/shard_map/ppermute | solution.py:254
  61.8 3.5 %collective-permute-start.4 = (bf16[2048,128]{1,0:T(8,128)(2,1)S(1)}, bf16[2048,128]{1,0:T(8,128)(2,1)S(1)}, u32[]{:S(2)}, u32[]{:S(2)}) collective-permute-start(bf16[2048,128]{1,0:T(8,128)(2,1)S(1)} %constant_dynamic-update-slice_fusion.refs_0_), channel_id=1, source_target_pairs={{0,384},{128,0},{256,128},{384,256},{1,385},{129,1},{257,129},{385... | collective-permute-start | bytes 1572872 | tf_op jit(solution)/shard_map/ppermute | solution.py:254
  66.3 11.3 %all-to-all-start.2 = ((bf16[64,24,128]{2,1,0:T(8,128)(2,1)}), bf16[64,24,128]{2,1,0:T(8,128)(2,1)S(1)}, u32[]{:S(2)}, u32[]{:S(2)}) async-start(bf16[64,24,128]{2,1,0:T(8,128)(2,1)} %broadcast_in_dim.2), calls=%async_computation.2 | async-start | bytes 786432 | tf_op jit(solution)/shard_map/all_to_all | solution.py:40
  78.3 3.0 %collective-permute-start.5 = (bf16[1024,128]{1,0:T(8,128)(2,1)S(1)}, bf16[1024,128]{1,0:T(8,128)(2,1)S(1)}, u32[]{:S(2)}, u32[]{:S(2)}) collective-permute-start(bf16[1024,128]{1,0:T(8,128)(2,1)S(1)} %get-tuple-element.30), channel_id=1, source_target_pairs={{0,128},{128,256},{256,384},{384,0},{1,129},{129,257},{257,385},{3... | collective-permute-start | bytes 786440 | tf_op jit(solution)/shard_map/ppermute | solution.py:254
  81.3 2.9 %collective-permute-start.6 = (bf16[1024,128]{1,0:T(8,128)(2,1)S(1)}, bf16[1024,128]{1,0:T(8,128)(2,1)}, u32[]{:S(2)}, u32[]{:S(2)}) collective-permute-start(bf16[1024,128]{1,0:T(8,128)(2,1)S(1)} %get-tuple-element.31), channel_id=1, source_target_pairs={{0,384},{128,0},{256,128},{384,256},{1,385},{129,1},{257,129},{385... | collective-permute-start | bytes 786440 | tf_op jit(solution)/shard_map/ppermute | solution.py:254
  84.2 3.0 %collective-permute-done.5 = bf16[1024,128]{1,0:T(8,128)(2,1)S(1)} collective-permute-done((bf16[1024,128]{1,0:T(8,128)(2,1)S(1)}, bf16[1024,128]{1,0:T(8,128)(2,1)S(1)}, u32[]{:S(2)}, u32[]{:S(2)}) %collective-permute-start.5) | collective-permute-done | bytes 262176 | tf_op jit(solution)/shard_map/ppermute | solution.py:254
  87.2 4.1 %collective-permute-done.6 = bf16[1024,128]{1,0:T(8,128)(2,1)} collective-permute-done((bf16[1024,128]{1,0:T(8,128)(2,1)S(1)}, bf16[1024,128]{1,0:T(8,128)(2,1)}, u32[]{:S(2)}, u32[]{:S(2)}) %collective-permute-start.6) | collective-permute-done | bytes 262176 | tf_op jit(solution)/shard_map/ppermute | solution.py:254
  91.3 2.8 %all-to-all-done.2 = bf16[64,24,128]{2,1,0:T(8,128)(2,1)S(1)} async-done(((bf16[64,24,128]{2,1,0:T(8,128)(2,1)}), bf16[64,24,128]{2,1,0:T(8,128)(2,1)S(1)}, u32[]{:S(2)}, u32[]{:S(2)}) %all-to-all-start.2) | async-done | bytes 393248 | tf_op jit(solution)/shard_map/all_to_all | solution.py:40
  95.4 1.3 collective-permute-start.8
  96.7 1.3 collective-permute-start.9
  100.1 6.2 %project.1 = f32[2,192,128]{2,1,0:T(8,128)S(1)} custom-call(s32[3]{0:T(128)S(1)} %pad_add_fusion.info_ref, bf16[16,384,512]{2,1,0:T(8,128)(2,1)} %bitcast.14, bf16[2048,128]{1,0:T(8,128)(2,1)S(1)} %copy-done.1, bf16[2048,128]{1,0:T(8,128)(2,1)S(1)} %collective-permute-done.3.up_ref.refs_1_, bf16[2048,128]{1,0:T(8,128)(2,1)S(1)} %pad_maximum_fusion.refs_2_, ...), custom_call_target="tpu_custom_call" | custom-call | flops 805306368 | bytes 8388608 | tf_op jit(solution)/shard_map/project/pallas_call | solution.py:209
  106.3 2.2 %collective-permute-start.10 = (f32[192,128]{1,0:T(8,128)S(1)}, f32[192,128]{1,0:T(8,128)S(1)}, u32[]{:S(2)}, u32[]{:S(2)}) collective-permute-start(f32[192,128]{1,0:T(8,128)S(1)} %select_bitcast_fusion), channel_id=1, source_target_pairs={{0,16},{16,0},{1,17},{17,1},{2,18},{18,2},{3,19},{19,3},{4,20},{20... | collective-permute-start | bytes 294920 | tf_op jit(solution)/shard_map/ppermute | solution.py:263
  108.5 5.9 %collective-permute-done.9.refs_3_ = bf16[1536,128]{1,0:T(8,128)(2,1)S(1)} collective-permute-done((bf16[1536,128]{1,0:T(8,128)(2,1)S(1)}, bf16[1536,128]{1,0:T(8,128)(2,1)S(1)}, u32[]{:S(2)}, u32[]{:S(2)}) %collective-permute-start.9) | collective-permute-done | bytes 393248 | tf_op jit(solution)/shard_map/ppermute | solution.py:259
  114.5 1.9 %collective-permute-start.11 = (bf16[6144,128]{1,0:T(8,128)(2,1)S(1)}, bf16[6144,128]{1,0:T(8,128)(2,1)S(1)}, u32[]{:S(2)}, u32[]{:S(2)}) collective-permute-start(bf16[6144,128]{1,0:T(8,128)(2,1)S(1)} %join.1), channel_id=1, source_target_pairs={{0,1},{1,0},{2,3},{3,2},{4,5},{5,4},{6,7},{7,6},{8,9},{9,8},{10,11... | collective-permute-start | bytes 4718600 | tf_op jit(solution)/shard_map/ppermute | solution.py:263
  117.0 2.8 %collective-permute-done.11.refs_4_ = bf16[6144,128]{1,0:T(8,128)(2,1)S(1)} collective-permute-done((bf16[6144,128]{1,0:T(8,128)(2,1)S(1)}, bf16[6144,128]{1,0:T(8,128)(2,1)S(1)}, u32[]{:S(2)}, u32[]{:S(2)}) %collective-permute-start.11) | collective-permute-done | bytes 1572896 | tf_op jit(solution)/shard_map/ppermute | solution.py:263
  119.8 5.7 %attend.1 = bf16[192,128]{1,0:T(8,128)(2,1)} custom-call(s32[3]{0:T(128)S(1)} %pad_add_fusion.info_ref, f32[192,128]{1,0:T(8,128)S(1)} %bitcast_add_fusion.q_ref, f32[192,128]{1,0:T(8,128)S(1)} %get-tuple-element.44.cos_ref, f32[192,128]{1,0:T(8,128)S(1)} %get-tuple-element.45.sin_ref, bf16[1536,128]{1,0:T(8,128)(2,1)S(1)} %bitcast.13, ...), custom_call_target="tpu_custom_call" | custom-call | flops 603979776 | bytes 3145728 | tf_op jit(solution)/shard_map/attend/pallas_call | solution.py:231
  (42 shorter events, 7.9 us)
Async XLA Ops:
  6.5 1.0 copy-start.2
  7.6 12.6 %copy-start.4 = (bf16[512,128]{1,0:T(8,128)(2,1)S(1)}, bf16[512,128]{1,0:T(8,128)(2,1)}, u32[]{:S(2)}) copy-start(bf16[512,128]{1,0:T(8,128)(2,1)} %param.4) | copy-start | bytes 393220
  7.6 28.4 %copy-start.3 = (bf16[1024,256]{1,0:T(8,128)(2,1)S(1)}, bf16[1024,256]{1,0:T(8,128)(2,1)}, u32[]{:S(2)}) copy-start(bf16[1024,256]{1,0:T(8,128)(2,1)} %w_ref.1) | copy-start | bytes 1572868
  8.4 27.6 %all-to-all-start = ((bf16[32,12,512]{2,1,0:T(8,128)(2,1)}), bf16[32,12,512]{2,1,0:T(8,128)(2,1)S(1)}, u32[]{:S(2)}, u32[]{:S(2)}) async-start(bf16[32,12,512]{2,1,0:T(8,128)(2,1)} %slabs.1), calls=%async_computation | async-start | bytes 1048576 | tf_op jit(solution)/shard_map/all_to_all | solution.py:275
  20.2 78.8 %all-gather.3.cloned.1.call-start = ((), (), s32[]{:S(2)}) async-start(), calls=%async_computation.3 | async-start | bytes 6684672 | tf_op jit(solution)/shard_map/all_gather | solution.py:280
  20.2 15.7 %collective-permute-start = (bf16[512,128]{1,0:T(8,128)(2,1)S(1)}, bf16[512,128]{1,0:T(8,128)(2,1)S(1)}, u32[]{:S(2)}, u32[]{:S(2)}) collective-permute-start(bf16[512,128]{1,0:T(8,128)(2,1)S(1)} %copy-done.4), channel_id=1, source_target_pairs={{0,32},{32,64},{64,96},{96,0},{1,33},{33,65},{65,97},{97,1},{2,34}... | collective-permute-start | bytes 393224 | tf_op jit(solution)/shard_map/ppermute | solution.py:254
  24.7 11.2 %collective-permute-start.1 = (bf16[512,128]{1,0:T(8,128)(2,1)S(1)}, bf16[512,128]{1,0:T(8,128)(2,1)S(1)}, u32[]{:S(2)}, u32[]{:S(2)}) collective-permute-start(bf16[512,128]{1,0:T(8,128)(2,1)S(1)} %copy-done.4), channel_id=1, source_target_pairs={{0,96},{32,0},{64,32},{96,64},{1,97},{33,1},{65,33},{97,65},{2,98}... | collective-permute-start | bytes 393224 | tf_op jit(solution)/shard_map/ppermute | solution.py:254
  37.6 27.6 %all-to-all-start.1 = ((f32[32,24,128]{2,1,0:T(8,128)}), f32[32,24,128]{2,1,0:T(8,128)S(1)}, u32[]{:S(2)}, u32[]{:S(2)}) async-start(f32[32,24,128]{2,1,0:T(8,128)} %get-tuple-element.29), calls=%async_computation.1 | async-start | bytes 786432 | tf_op jit(solution)/shard_map/all_to_all | solution.py:283
  45.5 13.8 %collective-permute-start.2 = (bf16[512,128]{1,0:T(8,128)(2,1)S(1)}, bf16[512,128]{1,0:T(8,128)(2,1)S(1)}, u32[]{:S(2)}, u32[]{:S(2)}) collective-permute-start(bf16[512,128]{1,0:T(8,128)(2,1)S(1)} %collective-permute-done), channel_id=1, source_target_pairs={{0,32},{32,64},{64,96},{96,0},{1,33},{33,65},{65,97},{97,1},{2,34}... | collective-permute-start | bytes 393224 | tf_op jit(solution)/shard_map/ppermute | solution.py:254
  59.4 37.3 %copy-start = (bf16[2048,128]{1,0:T(8,128)(2,1)}, bf16[2048,128]{1,0:T(8,128)(2,1)S(1)}, u32[]{:S(2)}) copy-start(bf16[2048,128]{1,0:T(8,128)(2,1)S(1)} %constant_dynamic-update-slice_fusion.refs_0_) | copy-start | bytes 1572868
  59.4 18.2 %collective-permute-start.3 = (bf16[2048,128]{1,0:T(8,128)(2,1)S(1)}, bf16[2048,128]{1,0:T(8,128)(2,1)S(1)}, u32[]{:S(2)}, u32[]{:S(2)}) collective-permute-start(bf16[2048,128]{1,0:T(8,128)(2,1)S(1)} %constant_dynamic-update-slice_fusion.refs_0_), channel_id=1, source_target_pairs={{0,128},{128,256},{256,384},{384,0},{1,129},{129,257},{257,385},{3... | collective-permute-start | bytes 1572872 | tf_op jit(solution)/shard_map/ppermute | solution.py:254
  61.8 16.5 %collective-permute-start.4 = (bf16[2048,128]{1,0:T(8,128)(2,1)S(1)}, bf16[2048,128]{1,0:T(8,128)(2,1)S(1)}, u32[]{:S(2)}, u32[]{:S(2)}) collective-permute-start(bf16[2048,128]{1,0:T(8,128)(2,1)S(1)} %constant_dynamic-update-slice_fusion.refs_0_), channel_id=1, source_target_pairs={{0,384},{128,0},{256,128},{384,256},{1,385},{129,1},{257,129},{385... | collective-permute-start | bytes 1572872 | tf_op jit(solution)/shard_map/ppermute | solution.py:254
  66.3 27.7 %all-to-all-start.2 = ((bf16[64,24,128]{2,1,0:T(8,128)(2,1)}), bf16[64,24,128]{2,1,0:T(8,128)(2,1)S(1)}, u32[]{:S(2)}, u32[]{:S(2)}) async-start(bf16[64,24,128]{2,1,0:T(8,128)(2,1)} %broadcast_in_dim.2), calls=%async_computation.2 | async-start | bytes 786432 | tf_op jit(solution)/shard_map/all_to_all | solution.py:40
  78.3 8.8 %collective-permute-start.5 = (bf16[1024,128]{1,0:T(8,128)(2,1)S(1)}, bf16[1024,128]{1,0:T(8,128)(2,1)S(1)}, u32[]{:S(2)}, u32[]{:S(2)}) collective-permute-start(bf16[1024,128]{1,0:T(8,128)(2,1)S(1)} %get-tuple-element.30), channel_id=1, source_target_pairs={{0,128},{128,256},{256,384},{384,0},{1,129},{129,257},{257,385},{3... | collective-permute-start | bytes 786440 | tf_op jit(solution)/shard_map/ppermute | solution.py:254
  81.3 9.9 %collective-permute-start.6 = (bf16[1024,128]{1,0:T(8,128)(2,1)S(1)}, bf16[1024,128]{1,0:T(8,128)(2,1)}, u32[]{:S(2)}, u32[]{:S(2)}) collective-permute-start(bf16[1024,128]{1,0:T(8,128)(2,1)S(1)} %get-tuple-element.31), channel_id=1, source_target_pairs={{0,384},{128,0},{256,128},{384,256},{1,385},{129,1},{257,129},{385... | collective-permute-start | bytes 786440 | tf_op jit(solution)/shard_map/ppermute | solution.py:254
  94.1 14.4 %collective-permute-start.7 = (bf16[1536,128]{1,0:T(8,128)(2,1)S(1)}, bf16[1536,128]{1,0:T(8,128)(2,1)S(1)}, u32[]{:S(2)}, u32[]{:S(2)}) collective-permute-start(bf16[1536,128]{1,0:T(8,128)(2,1)S(1)} %bitcast.9), channel_id=1, source_target_pairs={{0,128},{128,256},{256,384},{1,129},{129,257},{257,385},{2,130},{1... | collective-permute-start | bytes 1179656 | tf_op jit(solution)/shard_map/ppermute | solution.py:259
  95.4 13.1 %collective-permute-start.8 = (bf16[1536,128]{1,0:T(8,128)(2,1)S(1)}, bf16[1536,128]{1,0:T(8,128)(2,1)S(1)}, u32[]{:S(2)}, u32[]{:S(2)}) collective-permute-start(bf16[1536,128]{1,0:T(8,128)(2,1)S(1)} %bitcast.10), channel_id=1, source_target_pairs={{0,256},{128,384},{1,257},{129,385},{2,258},{130,386},{3,259},{131... | collective-permute-start | bytes 1179656 | tf_op jit(solution)/shard_map/ppermute | solution.py:259
  96.7 17.7 %collective-permute-start.9 = (bf16[1536,128]{1,0:T(8,128)(2,1)S(1)}, bf16[1536,128]{1,0:T(8,128)(2,1)S(1)}, u32[]{:S(2)}, u32[]{:S(2)}) collective-permute-start(bf16[1536,128]{1,0:T(8,128)(2,1)S(1)} %bitcast.11), channel_id=1, source_target_pairs={{0,384},{1,385},{2,386},{3,387},{4,388},{5,389},{6,390},{7,391},{8... | collective-permute-start | bytes 1179656 | tf_op jit(solution)/shard_map/ppermute | solution.py:259
  99.0 1.0 copy-start.1
  106.3 8.1 %collective-permute-start.10 = (f32[192,128]{1,0:T(8,128)S(1)}, f32[192,128]{1,0:T(8,128)S(1)}, u32[]{:S(2)}, u32[]{:S(2)}) collective-permute-start(f32[192,128]{1,0:T(8,128)S(1)} %select_bitcast_fusion), channel_id=1, source_target_pairs={{0,16},{16,0},{1,17},{17,1},{2,18},{18,2},{3,19},{19,3},{4,20},{20... | collective-permute-start | bytes 294920 | tf_op jit(solution)/shard_map/ppermute | solution.py:263
  114.5 5.3 %collective-permute-start.11 = (bf16[6144,128]{1,0:T(8,128)(2,1)S(1)}, bf16[6144,128]{1,0:T(8,128)(2,1)S(1)}, u32[]{:S(2)}, u32[]{:S(2)}) collective-permute-start(bf16[6144,128]{1,0:T(8,128)(2,1)S(1)} %join.1), channel_id=1, source_target_pairs={{0,1},{1,0},{2,3},{3,2},{4,5},{5,4},{6,7},{7,6},{8,9},{9,8},{10,11... | collective-permute-start | bytes 4718600 | tf_op jit(solution)/shard_map/ppermute | solution.py:263
Sparse Core Ops, SparseCore 0:
  37.8 59.7 all-gather.2

commit v10 on v9

--- a/solution.py
+++ b/solution.py
@@ -275,10 +275,11 @@
     hs = lax.all_to_all(hs, PAIR, 0, 0, tiled=True)
 
     one, three = shift(w, "yq", 1), shift(w, "yq", 3)
-    hs, w, one, three = tie((hs, w, one, three))
+    two = shift(one, "yq", 1)
+    hs, w, one, two, three = tie((hs, w, one, two, three))
     h, part = mix(info, hs, kv_weight)
     h = lax.all_gather(h, TP, axis=0, tiled=False)
-    w = jnp.concatenate([w, one, shift(one, "yq", 1), three], axis=0)
+    w = jnp.concatenate([w, one, two, three], axis=0)
 
     part = lax.all_to_all(part, PAIR, 0, 0, tiled=True)
     up, down = shift(w, "x", 1), shift(w, "x", -1)

time: 135 us -> 139 us (1.030); the launches traced: 132 us -> 138 us
  waiting for transfers between devices: 35.6 us -> 47.9 us
  starting transfers between devices: 63.6 us -> 57.1 us
    all_to_all x1, waiting for transfers between devices: 0.01 us -> 8.29 us  [body(): part = lax.all_to_all(part, PAIR, 0, 0, tiled=True)]
    all_gather x1, waiting for transfers between devices: 0.02 us -> 7.35 us  [body(): h = lax.all_gather(h, TP, axis=0, tiled=False)]
    ppermute x3, waiting for transfers between devices: 5.9 us -> 0.01 us  [shift_up(): return lax.ppermute(v, axis, [(i, i + by) for i in range(n - by)])]
    all_to_all x1, starting transfers between devices: 11.3 us -> 7.52 us  [broadcast_gather(): lax.all_to_all(jnp.broadcast_to(x[None], (n,) + x.shape), axis, 0, 0, til...]
    ppermute x2, waiting for transfers between devices: 2.78 us -> 6.14 us  [swap(): return lax.ppermute(v, axis, [(0, 1), (1, 0)])]
    ppermute x7, starting transfers between devices: 24.8 us -> 21.5 us  [shift(): return lax.ppermute(v, axis, [(i, (i + by) % n) for i in range(n)])]
    ppermute x7, waiting for transfers between devices: 24 us -> 22.1 us  [shift(): return lax.ppermute(v, axis, [(i, (i + by) % n) for i in range(n)])]
where the time goes in v10:
time: 139 us; the launch traced here: 138 us
  starting transfers between devices  57.1 us (41%)
  waiting for transfers between devices  47.9 us (34%)
  Pallas kernels  14.5 us (10%)
  between operations  13.7 us (10%)
  local copies, waits for them, and re-layouts  2.98 us (2%)
  other arithmetic  1.91 us (1%)
    ppermute x7, waiting for transfers between devices, shift(): return lax.ppermute(v, axis, [(i, (i + by) % n) for i in range(n)])  22.1 us
    ppermute x7, starting transfers between devices, shift(): return lax.ppermute(v, axis, [(i, (i + by) % n) for i in range(n)])  21.5 us
    all_to_all x1, starting transfers between devices, body(): hs = lax.all_to_all(hs, PAIR, 0, 0, tiled=True)  11.7 us
    all_to_all x1, waiting for transfers between devices, body(): part = lax.all_to_all(part, PAIR, 0, 0, tiled=True)  8.29 us
    all_to_all x1, starting transfers between devices, broadcast_gather(): lax.all_to_all(jnp.broadcast_to(x[None], (n,) + x.shape), axis, 0, 0, til...  7.52 us
    all_gather x1, waiting for transfers between devices, body(): h = lax.all_gather(h, TP, axis=0, tiled=False)  7.35 us
    all_to_all x1, starting transfers between devices, body(): part = lax.all_to_all(part, PAIR, 0, 0, tiled=True)  7.07 us
    pallas_call x1, Pallas kernels, project(): pl.pallas_call(project_kernel, in_specs=[pl.BlockSpec(memory_space=pltpu....  6.18 us
  transfers between devices with their start and end apart: 16, of which 9 were waited for; matrix products, arithmetic and copies ran while one was open for 2% of the time, Pallas kernels for 5%

profile of v10, /device:TPU:6, one launch (start us, length us, event | category | flops | bytes accessed | tf_op | source)
XLA Modules:
  0.0 138.1 jit_solution(12332914477928837479)
XLA Ops:
  8.4 11.7 %all-to-all-start = ((bf16[32,12,512]{2,1,0:T(8,128)(2,1)}), bf16[32,12,512]{2,1,0:T(8,128)(2,1)S(1)}, u32[]{:S(2)}, u32[]{:S(2)}) async-start(bf16[32,12,512]{2,1,0:T(8,128)(2,1)} %slabs.1), calls=%async_computation | async-start | bytes 1048576 | tf_op jit(solution)/shard_map/all_to_all | solution.py:275
  20.2 4.5 %collective-permute-start = (bf16[512,128]{1,0:T(8,128)(2,1)S(1)}, bf16[512,128]{1,0:T(8,128)(2,1)S(1)}, u32[]{:S(2)}, u32[]{:S(2)}) collective-permute-start(bf16[512,128]{1,0:T(8,128)(2,1)S(1)} %copy-done.4), channel_id=1, source_target_pairs={{0,32},{32,64},{64,96},{96,0},{1,33},{33,65},{65,97},{97,1},{2,34}... | collective-permute-start | bytes 393224 | tf_op jit(solution)/shard_map/ppermute | solution.py:254
  24.7 3.5 %collective-permute-start.2 = (bf16[512,128]{1,0:T(8,128)(2,1)S(1)}, bf16[512,128]{1,0:T(8,128)(2,1)S(1)}, u32[]{:S(2)}, u32[]{:S(2)}) collective-permute-start(bf16[512,128]{1,0:T(8,128)(2,1)S(1)} %copy-done.4), channel_id=1, source_target_pairs={{0,96},{32,0},{64,32},{96,64},{1,97},{33,1},{65,33},{97,65},{2,98}... | collective-permute-start | bytes 393224 | tf_op jit(solution)/shard_map/ppermute | solution.py:254
  28.2 7.8 %collective-permute-done = bf16[512,128]{1,0:T(8,128)(2,1)S(1)} collective-permute-done((bf16[512,128]{1,0:T(8,128)(2,1)S(1)}, bf16[512,128]{1,0:T(8,128)(2,1)S(1)}, u32[]{:S(2)}, u32[]{:S(2)}) %collective-permute-start) | collective-permute-done | bytes 131104 | tf_op jit(solution)/shard_map/ppermute | solution.py:254
  36.0 1.9 %collective-permute-start.1 = (bf16[512,128]{1,0:T(8,128)(2,1)S(1)}, bf16[512,128]{1,0:T(8,128)(2,1)S(1)}, u32[]{:S(2)}, u32[]{:S(2)}) collective-permute-start(bf16[512,128]{1,0:T(8,128)(2,1)S(1)} %collective-permute-done), channel_id=1, source_target_pairs={{0,32},{32,64},{64,96},{96,0},{1,33},{33,65},{65,97},{97,1},{2,34}... | collective-permute-start | bytes 393224 | tf_op jit(solution)/shard_map/ppermute | solution.py:254
  38.0 7.2 %collective-permute-done.1 = bf16[512,128]{1,0:T(8,128)(2,1)S(1)} collective-permute-done((bf16[512,128]{1,0:T(8,128)(2,1)S(1)}, bf16[512,128]{1,0:T(8,128)(2,1)S(1)}, u32[]{:S(2)}, u32[]{:S(2)}) %collective-permute-start.1) | collective-permute-done | bytes 131104 | tf_op jit(solution)/shard_map/ppermute | solution.py:254
  45.2 1.6 %mix.1 = (bf16[384,512]{1,0:T(8,128)(2,1)}, f32[32,24,128]{2,1,0:T(8,128)}) custom-call(s32[3]{0:T(128)S(1)} %pad_add_fusion.info_ref, bf16[32,12,512]{2,1,0:T(8,128)(2,1)S(1)} %all-to-all-done.x_ref, bf16[1024,256]{1,0:T(8,128)(2,1)S(1)} %copy-done.3), custom_call_target="tpu_custom_call" | custom-call | flops 100663296 | bytes 1048576 | tf_op jit(solution)/shard_map/mix/pallas_call | solution.py:67
  46.8 7.1 %all-to-all-start.1 = ((f32[32,24,128]{2,1,0:T(8,128)}), f32[32,24,128]{2,1,0:T(8,128)S(1)}, u32[]{:S(2)}, u32[]{:S(2)}) async-start(f32[32,24,128]{2,1,0:T(8,128)} %get-tuple-element.31), calls=%async_computation.1 | async-start | bytes 786432 | tf_op jit(solution)/shard_map/all_to_all | solution.py:284
  54.0 2.4 %collective-permute-start.3 = (bf16[2048,128]{1,0:T(8,128)(2,1)S(1)}, bf16[2048,128]{1,0:T(8,128)(2,1)S(1)}, u32[]{:S(2)}, u32[]{:S(2)}) collective-permute-start(bf16[2048,128]{1,0:T(8,128)(2,1)S(1)} %constant_dynamic-update-slice_fusion.refs_0_), channel_id=1, source_target_pairs={{0,128},{128,256},{256,384},{384,0},{1,129},{129,257},{257,385},{3... | collective-permute-start | bytes 1572872 | tf_op jit(solution)/shard_map/ppermute | solution.py:254
  56.4 3.5 %collective-permute-start.4 = (bf16[2048,128]{1,0:T(8,128)(2,1)S(1)}, bf16[2048,128]{1,0:T(8,128)(2,1)S(1)}, u32[]{:S(2)}, u32[]{:S(2)}) collective-permute-start(bf16[2048,128]{1,0:T(8,128)(2,1)S(1)} %constant_dynamic-update-slice_fusion.refs_0_), channel_id=1, source_target_pairs={{0,384},{128,0},{256,128},{384,256},{1,385},{129,1},{257,129},{385... | collective-permute-start | bytes 1572872 | tf_op jit(solution)/shard_map/ppermute | solution.py:254
  59.9 8.3 %all-to-all-done.1 = f32[32,24,128]{2,1,0:T(8,128)S(1)} async-done(((f32[32,24,128]{2,1,0:T(8,128)}), f32[32,24,128]{2,1,0:T(8,128)S(1)}, u32[]{:S(2)}, u32[]{:S(2)}) %all-to-all-start.1) | async-done | bytes 393248 | tf_op jit(solution)/shard_map/all_to_all | solution.py:284
  69.2 7.5 %all-to-all-start.2 = ((bf16[64,24,128]{2,1,0:T(8,128)(2,1)}), bf16[64,24,128]{2,1,0:T(8,128)(2,1)S(1)}, u32[]{:S(2)}, u32[]{:S(2)}) async-start(bf16[64,24,128]{2,1,0:T(8,128)(2,1)} %broadcast_in_dim.2), calls=%async_computation.2 | async-start | bytes 786432 | tf_op jit(solution)/shard_map/all_to_all | solution.py:40
  76.8 2.3 %collective-permute-start.5 = (bf16[1024,128]{1,0:T(8,128)(2,1)S(1)}, bf16[1024,128]{1,0:T(8,128)(2,1)S(1)}, u32[]{:S(2)}, u32[]{:S(2)}) collective-permute-start(bf16[1024,128]{1,0:T(8,128)(2,1)S(1)} %get-tuple-element.32), channel_id=1, source_target_pairs={{0,128},{128,256},{256,384},{384,0},{1,129},{129,257},{257,385},{3... | collective-permute-start | bytes 786440 | tf_op jit(solution)/shard_map/ppermute | solution.py:254
  79.2 3.5 %collective-permute-start.6 = (bf16[1024,128]{1,0:T(8,128)(2,1)S(1)}, bf16[1024,128]{1,0:T(8,128)(2,1)}, u32[]{:S(2)}, u32[]{:S(2)}) collective-permute-start(bf16[1024,128]{1,0:T(8,128)(2,1)S(1)} %get-tuple-element.33), channel_id=1, source_target_pairs={{0,384},{128,0},{256,128},{384,256},{1,385},{129,1},{257,129},{385... | collective-permute-start | bytes 786440 | tf_op jit(solution)/shard_map/ppermute | solution.py:254
  82.7 3.7 %collective-permute-done.5 = bf16[1024,128]{1,0:T(8,128)(2,1)S(1)} collective-permute-done((bf16[1024,128]{1,0:T(8,128)(2,1)S(1)}, bf16[1024,128]{1,0:T(8,128)(2,1)S(1)}, u32[]{:S(2)}, u32[]{:S(2)}) %collective-permute-start.5) | collective-permute-done | bytes 262176 | tf_op jit(solution)/shard_map/ppermute | solution.py:254
  86.5 3.4 %collective-permute-done.6 = bf16[1024,128]{1,0:T(8,128)(2,1)} collective-permute-done((bf16[1024,128]{1,0:T(8,128)(2,1)S(1)}, bf16[1024,128]{1,0:T(8,128)(2,1)}, u32[]{:S(2)}, u32[]{:S(2)}) %collective-permute-start.6) | collective-permute-done | bytes 262176 | tf_op jit(solution)/shard_map/ppermute | solution.py:254
  89.8 3.9 %all-to-all-done.2 = bf16[64,24,128]{2,1,0:T(8,128)(2,1)S(1)} async-done(((bf16[64,24,128]{2,1,0:T(8,128)(2,1)}), bf16[64,24,128]{2,1,0:T(8,128)(2,1)S(1)}, u32[]{:S(2)}, u32[]{:S(2)}) %all-to-all-start.2) | async-done | bytes 393248 | tf_op jit(solution)/shard_map/all_to_all | solution.py:40
  98.7 7.3 %all-gather.3.cloned.1.call-done = bf16[6144,512]{1,0:T(8,128)(2,1)} async-done(((bf16[384,512]{1,0:T(8,128)(2,1)}), bf16[6144,512]{1,0:T(8,128)(2,1)}) %all-gather.3.cloned.1.call-update) | async-done | bytes 6291472 | tf_op jit(solution)/shard_map/all_gather | solution.py:281
  107.0 6.2 %project.1 = f32[2,192,128]{2,1,0:T(8,128)S(1)} custom-call(s32[3]{0:T(128)S(1)} %pad_add_fusion.info_ref, bf16[16,384,512]{2,1,0:T(8,128)(2,1)} %bitcast.14, bf16[2048,128]{1,0:T(8,128)(2,1)S(1)} %copy-done.1, bf16[2048,128]{1,0:T(8,128)(2,1)S(1)} %collective-permute-done.3.up_ref.refs_1_, bf16[2048,128]{1,0:T(8,128)(2,1)S(1)} %pad_maximum_fusion.refs_2_, ...), custom_call_target="tpu_custom_call" | custom-call | flops 805306368 | bytes 8388608 | tf_op jit(solution)/shard_map/project/pallas_call | solution.py:209
  113.3 3.4 %collective-permute-start.10 = (f32[192,128]{1,0:T(8,128)S(1)}, f32[192,128]{1,0:T(8,128)S(1)}, u32[]{:S(2)}, u32[]{:S(2)}) collective-permute-start(f32[192,128]{1,0:T(8,128)S(1)} %select_bitcast_fusion), channel_id=1, source_target_pairs={{0,16},{16,0},{1,17},{17,1},{2,18},{18,2},{3,19},{19,3},{4,20},{20... | collective-permute-start | bytes 294920 | tf_op jit(solution)/shard_map/ppermute | solution.py:263
  116.7 3.4 %collective-permute-done.10 = f32[192,128]{1,0:T(8,128)S(1)} collective-permute-done((f32[192,128]{1,0:T(8,128)S(1)}, f32[192,128]{1,0:T(8,128)S(1)}, u32[]{:S(2)}, u32[]{:S(2)}) %collective-permute-start.10) | collective-permute-done | bytes 98336 | tf_op jit(solution)/shard_map/ppermute | solution.py:263
  120.2 1.9 %collective-permute-start.11 = (bf16[6144,128]{1,0:T(8,128)(2,1)S(1)}, bf16[6144,128]{1,0:T(8,128)(2,1)S(1)}, u32[]{:S(2)}, u32[]{:S(2)}) collective-permute-start(bf16[6144,128]{1,0:T(8,128)(2,1)S(1)} %join.1), channel_id=1, source_target_pairs={{0,1},{1,0},{2,3},{3,2},{4,5},{5,4},{6,7},{7,6},{8,9},{9,8},{10,11... | collective-permute-start | bytes 4718600 | tf_op jit(solution)/shard_map/ppermute | solution.py:263
  122.7 2.8 %collective-permute-done.11.refs_4_ = bf16[6144,128]{1,0:T(8,128)(2,1)S(1)} collective-permute-done((bf16[6144,128]{1,0:T(8,128)(2,1)S(1)}, bf16[6144,128]{1,0:T(8,128)(2,1)S(1)}, u32[]{:S(2)}, u32[]{:S(2)}) %collective-permute-start.11) | collective-permute-done | bytes 1572896 | tf_op jit(solution)/shard_map/ppermute | solution.py:263
  125.5 5.8 %attend.1 = bf16[192,128]{1,0:T(8,128)(2,1)} custom-call(s32[3]{0:T(128)S(1)} %pad_add_fusion.info_ref, f32[192,128]{1,0:T(8,128)S(1)} %bitcast_add_fusion.q_ref, f32[192,128]{1,0:T(8,128)S(1)} %get-tuple-element.46.cos_ref, f32[192,128]{1,0:T(8,128)S(1)} %get-tuple-element.47.sin_ref, bf16[1536,128]{1,0:T(8,128)(2,1)S(1)} %bitcast.13, ...), custom_call_target="tpu_custom_call" | custom-call | flops 603979776 | bytes 3145728 | tf_op jit(solution)/shard_map/attend/pallas_call | solution.py:231
  (42 shorter events, 9.8 us)
Async XLA Ops:
  6.5 1.0 copy-start.2
  7.6 12.6 %copy-start.4 = (bf16[512,128]{1,0:T(8,128)(2,1)S(1)}, bf16[512,128]{1,0:T(8,128)(2,1)}, u32[]{:S(2)}) copy-start(bf16[512,128]{1,0:T(8,128)(2,1)} %param.4) | copy-start | bytes 393220
  7.6 37.6 %copy-start.3 = (bf16[1024,256]{1,0:T(8,128)(2,1)S(1)}, bf16[1024,256]{1,0:T(8,128)(2,1)}, u32[]{:S(2)}) copy-start(bf16[1024,256]{1,0:T(8,128)(2,1)} %w_ref.1) | copy-start | bytes 1572868
  8.4 36.8 %all-to-all-start = ((bf16[32,12,512]{2,1,0:T(8,128)(2,1)}), bf16[32,12,512]{2,1,0:T(8,128)(2,1)S(1)}, u32[]{:S(2)}, u32[]{:S(2)}) async-start(bf16[32,12,512]{2,1,0:T(8,128)(2,1)} %slabs.1), calls=%async_computation | async-start | bytes 1048576 | tf_op jit(solution)/shard_map/all_to_all | solution.py:275
  20.2 85.9 %all-gather.3.cloned.1.call-start = ((), (), s32[]{:S(2)}) async-start(), calls=%async_computation.3 | async-start | bytes 6684672 | tf_op jit(solution)/shard_map/all_gather | solution.py:281
  20.2 15.7 %collective-permute-start = (bf16[512,128]{1,0:T(8,128)(2,1)S(1)}, bf16[512,128]{1,0:T(8,128)(2,1)S(1)}, u32[]{:S(2)}, u32[]{:S(2)}) collective-permute-start(bf16[512,128]{1,0:T(8,128)(2,1)S(1)} %copy-done.4), channel_id=1, source_target_pairs={{0,32},{32,64},{64,96},{96,0},{1,33},{33,65},{65,97},{97,1},{2,34}... | collective-permute-start | bytes 393224 | tf_op jit(solution)/shard_map/ppermute | solution.py:254
  24.7 13.3 %collective-permute-start.2 = (bf16[512,128]{1,0:T(8,128)(2,1)S(1)}, bf16[512,128]{1,0:T(8,128)(2,1)S(1)}, u32[]{:S(2)}, u32[]{:S(2)}) collective-permute-start(bf16[512,128]{1,0:T(8,128)(2,1)S(1)} %copy-done.4), channel_id=1, source_target_pairs={{0,96},{32,0},{64,32},{96,64},{1,97},{33,1},{65,33},{97,65},{2,98}... | collective-permute-start | bytes 393224 | tf_op jit(solution)/shard_map/ppermute | solution.py:254
  36.0 9.2 %collective-permute-start.1 = (bf16[512,128]{1,0:T(8,128)(2,1)S(1)}, bf16[512,128]{1,0:T(8,128)(2,1)S(1)}, u32[]{:S(2)}, u32[]{:S(2)}) collective-permute-start(bf16[512,128]{1,0:T(8,128)(2,1)S(1)} %collective-permute-done), channel_id=1, source_target_pairs={{0,32},{32,64},{64,96},{96,0},{1,33},{33,65},{65,97},{97,1},{2,34}... | collective-permute-start | bytes 393224 | tf_op jit(solution)/shard_map/ppermute | solution.py:254
  46.8 21.4 %all-to-all-start.1 = ((f32[32,24,128]{2,1,0:T(8,128)}), f32[32,24,128]{2,1,0:T(8,128)S(1)}, u32[]{:S(2)}, u32[]{:S(2)}) async-start(f32[32,24,128]{2,1,0:T(8,128)} %get-tuple-element.31), calls=%async_computation.1 | async-start | bytes 786432 | tf_op jit(solution)/shard_map/all_to_all | solution.py:284
  54.0 42.3 %copy-start = (bf16[2048,128]{1,0:T(8,128)(2,1)}, bf16[2048,128]{1,0:T(8,128)(2,1)S(1)}, u32[]{:S(2)}) copy-start(bf16[2048,128]{1,0:T(8,128)(2,1)S(1)} %constant_dynamic-update-slice_fusion.refs_0_) | copy-start | bytes 1572868
  54.0 22.7 %collective-permute-start.3 = (bf16[2048,128]{1,0:T(8,128)(2,1)S(1)}, bf16[2048,128]{1,0:T(8,128)(2,1)S(1)}, u32[]{:S(2)}, u32[]{:S(2)}) collective-permute-start(bf16[2048,128]{1,0:T(8,128)(2,1)S(1)} %constant_dynamic-update-slice_fusion.refs_0_), channel_id=1, source_target_pairs={{0,128},{128,256},{256,384},{384,0},{1,129},{129,257},{257,385},{3... | collective-permute-start | bytes 1572872 | tf_op jit(solution)/shard_map/ppermute | solution.py:254
  56.4 20.4 %collective-permute-start.4 = (bf16[2048,128]{1,0:T(8,128)(2,1)S(1)}, bf16[2048,128]{1,0:T(8,128)(2,1)S(1)}, u32[]{:S(2)}, u32[]{:S(2)}) collective-permute-start(bf16[2048,128]{1,0:T(8,128)(2,1)S(1)} %constant_dynamic-update-slice_fusion.refs_0_), channel_id=1, source_target_pairs={{0,384},{128,0},{256,128},{384,256},{1,385},{129,1},{257,129},{385... | collective-permute-start | bytes 1572872 | tf_op jit(solution)/shard_map/ppermute | solution.py:254
  69.2 24.5 %all-to-all-start.2 = ((bf16[64,24,128]{2,1,0:T(8,128)(2,1)}), bf16[64,24,128]{2,1,0:T(8,128)(2,1)S(1)}, u32[]{:S(2)}, u32[]{:S(2)}) async-start(bf16[64,24,128]{2,1,0:T(8,128)(2,1)} %broadcast_in_dim.2), calls=%async_computation.2 | async-start | bytes 786432 | tf_op jit(solution)/shard_map/all_to_all | solution.py:40
  76.8 9.6 %collective-permute-start.5 = (bf16[1024,128]{1,0:T(8,128)(2,1)S(1)}, bf16[1024,128]{1,0:T(8,128)(2,1)S(1)}, u32[]{:S(2)}, u32[]{:S(2)}) collective-permute-start(bf16[1024,128]{1,0:T(8,128)(2,1)S(1)} %get-tuple-element.32), channel_id=1, source_target_pairs={{0,128},{128,256},{256,384},{384,0},{1,129},{129,257},{257,385},{3... | collective-permute-start | bytes 786440 | tf_op jit(solution)/shard_map/ppermute | solution.py:254
  79.2 10.6 %collective-permute-start.6 = (bf16[1024,128]{1,0:T(8,128)(2,1)S(1)}, bf16[1024,128]{1,0:T(8,128)(2,1)}, u32[]{:S(2)}, u32[]{:S(2)}) collective-permute-start(bf16[1024,128]{1,0:T(8,128)(2,1)S(1)} %get-tuple-element.33), channel_id=1, source_target_pairs={{0,384},{128,0},{256,128},{384,256},{1,385},{129,1},{257,129},{385... | collective-permute-start | bytes 786440 | tf_op jit(solution)/shard_map/ppermute | solution.py:254
  93.8 23.0 %collective-permute-start.7 = (bf16[1536,128]{1,0:T(8,128)(2,1)S(1)}, bf16[1536,128]{1,0:T(8,128)(2,1)S(1)}, u32[]{:S(2)}, u32[]{:S(2)}) collective-permute-start(bf16[1536,128]{1,0:T(8,128)(2,1)S(1)} %bitcast.9), channel_id=1, source_target_pairs={{0,128},{128,256},{256,384},{1,129},{129,257},{257,385},{2,130},{1... | collective-permute-start | bytes 1179656 | tf_op jit(solution)/shard_map/ppermute | solution.py:259
  95.1 21.7 %collective-permute-start.8 = (bf16[1536,128]{1,0:T(8,128)(2,1)S(1)}, bf16[1536,128]{1,0:T(8,128)(2,1)S(1)}, u32[]{:S(2)}, u32[]{:S(2)}) collective-permute-start(bf16[1536,128]{1,0:T(8,128)(2,1)S(1)} %bitcast.10), channel_id=1, source_target_pairs={{0,256},{128,384},{1,257},{129,385},{2,258},{130,386},{3,259},{131... | collective-permute-start | bytes 1179656 | tf_op jit(solution)/shard_map/ppermute | solution.py:259
  96.4 20.4 %collective-permute-start.9 = (bf16[1536,128]{1,0:T(8,128)(2,1)S(1)}, bf16[1536,128]{1,0:T(8,128)(2,1)S(1)}, u32[]{:S(2)}, u32[]{:S(2)}) collective-permute-start(bf16[1536,128]{1,0:T(8,128)(2,1)S(1)} %bitcast.11), channel_id=1, source_target_pairs={{0,384},{1,385},{2,386},{3,387},{4,388},{5,389},{6,390},{7,391},{8... | collective-permute-start | bytes 1179656 | tf_op jit(solution)/shard_map/ppermute | solution.py:259
  106.0 1.0 copy-start.1
  113.3 6.8 %collective-permute-start.10 = (f32[192,128]{1,0:T(8,128)S(1)}, f32[192,128]{1,0:T(8,128)S(1)}, u32[]{:S(2)}, u32[]{:S(2)}) collective-permute-start(f32[192,128]{1,0:T(8,128)S(1)} %select_bitcast_fusion), channel_id=1, source_target_pairs={{0,16},{16,0},{1,17},{17,1},{2,18},{18,2},{3,19},{19,3},{4,20},{20... | collective-permute-start | bytes 294920 | tf_op jit(solution)/shard_map/ppermute | solution.py:263
  120.2 5.3 %collective-permute-start.11 = (bf16[6144,128]{1,0:T(8,128)(2,1)S(1)}, bf16[6144,128]{1,0:T(8,128)(2,1)S(1)}, u32[]{:S(2)}, u32[]{:S(2)}) collective-permute-start(bf16[6144,128]{1,0:T(8,128)(2,1)S(1)} %join.1), channel_id=1, source_target_pairs={{0,1},{1,0},{2,3},{3,2},{4,5},{5,4},{6,7},{7,6},{8,9},{9,8},{10,11... | collective-permute-start | bytes 4718600 | tf_op jit(solution)/shard_map/ppermute | solution.py:263
Sparse Core Ops, SparseCore 0:
  46.9 59.0 all-gather.2

commit v11 on v9

--- a/solution.py
+++ b/solution.py
@@ -81,10 +81,10 @@
     )(info, x, w)
 
 
-def ends_kernel(up_ref, down_ref, first_ref, last_ref):
-    part = first_ref.shape[0]
-    first_ref[...] = up_ref[:part]
-    last_ref[...] = down_ref[part:]
+def ends_kernel(up_ref, down_ref, down2_ref, first_ref, last_ref):
+    first_ref[...] = up_ref[:1024]
+    last_ref[:512] = down_ref[1024:]
+    last_ref[512:] = down2_ref[...]
 
 
 def join_kernel(*refs):
@@ -108,16 +108,22 @@
 
 
 def project_kernel(info_ref, h_ref, *refs):
-    w_refs, o_ref, h_buf, w_buf, sems = refs[:4], *refs[4:]
+    w_refs, o_ref, h_buf, w_buf, sems = refs[:8], *refs[8:]
     x, yq = info_ref[0], info_ref[1] // 2
     copies = []
     for n in range(4):
-        group = [pltpu.make_async_copy(w_refs[n], w_buf.at[n], sems.at[n, 4])]
-        for back in range(4):
+        size = w_refs[2 * n].shape[0]
+        group = [
+            pltpu.make_async_copy(
+                w_refs[2 * n], w_buf.at[n, pl.ds(0, size)], sems.at[n, 4]
+            ),
+            pltpu.make_async_copy(
+                w_refs[2 * n + 1], w_buf.at[n, pl.ds(size, 2048 - size)], sems.at[n, 5]
+            ),
+        ]
+        for i, back in enumerate((0, 1, 3, 2)):
             block = lax.rem(x + 4 - n, 4) * 4 + lax.rem(yq + 4 - back, 4)
-            group.append(
-                pltpu.make_async_copy(h_ref.at[block], h_buf.at[n, back], sems.at[n, back])
-            )
+            group.append(pltpu.make_async_copy(h_ref.at[block], h_buf.at[n, i], sems.at[n, i]))
         copies.append(group)
         for copy in group:
             copy.start()
@@ -208,13 +214,13 @@
     hbm = pl.BlockSpec(memory_space=pl.ANY)
     return pl.pallas_call(
         project_kernel,
-        in_specs=[pl.BlockSpec(memory_space=pltpu.SMEM)] + [hbm] * 5,
+        in_specs=[pl.BlockSpec(memory_space=pltpu.SMEM)] + [hbm] * 9,
         out_specs=pl.BlockSpec(memory_space=pltpu.VMEM),
         out_shape=jax.ShapeDtypeStruct((2, m // 2, HD), jnp.float32),
         scratch_shapes=[
             pltpu.VMEM((4, count // 4, m, part), jnp.bfloat16),
             pltpu.VMEM((4, count // 4 * part, HD), jnp.bfloat16),
-            pltpu.SemaphoreType.DMA((4, 5)),
+            pltpu.SemaphoreType.DMA((4, 6)),
         ],
         compiler_params=pltpu.CompilerParams(vmem_limit_bytes=48 * 2**20),
         cost_estimate=pl.CostEstimate(
@@ -278,7 +284,8 @@
     hs, w, one, three = tie((hs, w, one, three))
     h, part = mix(info, hs, kv_weight)
     h = lax.all_gather(h, TP, axis=0, tiled=False)
-    w = jnp.concatenate([w, one, shift(one, "yq", 1), three], axis=0)
+    two = shift(one, "yq", 1)
+    w = jnp.concatenate([w, one, three], axis=0)
 
     part = lax.all_to_all(part, PAIR, 0, 0, tiled=True)
     up, down = shift(w, "x", 1), shift(w, "x", -1)
@@ -286,12 +293,13 @@
     cosine, sine = angles_of(base + z * 24 + jnp.arange(24, dtype=jnp.int32))
     rows = jnp.where(core == 0, rotate(rows, cosine, sine), rows).astype(jnp.bfloat16)
     rows = broadcast_gather(rows, ("yq", "yp", "z")).reshape(1536, HD)
-    first, last = small_kernel(ends_kernel, "ends", [(1024, HD)] * 2, (up, down))
+    up2, down2 = shift(two, "x", 1), shift(two, "x", -1)
+    rows, up, down, up2, down2 = tie((rows, up, down, up2, down2))
+    first, last = small_kernel(ends_kernel, "ends", [(1024, HD)] * 2, (up, down, down2))
     cross = [shift(first, "x", 1), shift(last, "x", -1)]
-    rows, cross = tie((rows, cross))
     mine = [rows] + [shift_up(rows, "x", d) for d in (1, 2, 3)]
 
-    sums = project(info, h, (w, up, jnp.concatenate(cross, axis=0), down))
+    sums = project(info, h, (w, two, up, up2, *cross, down, down2))
     keep = jnp.where(yp == 0, sums[0], sums[1])
     come = swap(jnp.where(yp == 0, sums[1], sums[0]), "yp")
     away, come = tie((mine[1:], come))

time: 135 us -> 155 us (1.15); the launches traced: 132 us -> 154 us
  waiting for transfers between devices: 35.6 us -> 53.1 us
  starting transfers between devices: 63.6 us -> 67.9 us
    all_to_all x1, waiting for transfers between devices: 0.01 us -> 14.2 us  [body(): part = lax.all_to_all(part, PAIR, 0, 0, tiled=True)]
    ppermute x7 -> x9, waiting for transfers between devices: 24 us -> 32.9 us  [shift(): return lax.ppermute(v, axis, [(i, (i + by) % n) for i in range(n)])]
    ppermute x3, waiting for transfers between devices: 5.9 us -> 0.01 us  [shift_up(): return lax.ppermute(v, axis, [(i, i + by) for i in range(n - by)])]
    ppermute x7 -> x9, starting transfers between devices: 24.8 us -> 29.8 us  [shift(): return lax.ppermute(v, axis, [(i, (i + by) % n) for i in range(n)])]
    ppermute x2, waiting for transfers between devices: 2.78 us -> 5.85 us  [swap(): return lax.ppermute(v, axis, [(0, 1), (1, 0)])]
    all_to_all x1, waiting for transfers between devices: 2.84 us -> 0.01 us  [broadcast_gather(): lax.all_to_all(jnp.broadcast_to(x[None], (n,) + x.shape), axis, 0, 0, til...]
    all_to_all x1, starting transfers between devices: 11.3 us -> 9.33 us  [broadcast_gather(): lax.all_to_all(jnp.broadcast_to(x[None], (n,) + x.shape), axis, 0, 0, til...]
  transfers between devices with their start and end apart: 16 -> 18, of which waited for: 9 -> 9; matrix products, arithmetic and copies ran while one was open for 2% -> 1% of each run, Pallas kernels for 5% -> 5%
where the time goes in v11:
time: 155 us; the launch traced here: 154 us
  starting transfers between devices  67.9 us (44%)
  waiting for transfers between devices  53.1 us (34%)
  Pallas kernels  15.8 us (10%)
  between operations  13.7 us (9%)
  local copies, waits for them, and re-layouts  2.82 us (2%)
    ppermute x9, waiting for transfers between devices, shift(): return lax.ppermute(v, axis, [(i, (i + by) % n) for i in range(n)])  32.9 us
    ppermute x9, starting transfers between devices, shift(): return lax.ppermute(v, axis, [(i, (i + by) % n) for i in range(n)])  29.8 us
    all_to_all x1, waiting for transfers between devices, body(): part = lax.all_to_all(part, PAIR, 0, 0, tiled=True)  14.2 us
    all_to_all x1, starting transfers between devices, body(): hs = lax.all_to_all(hs, PAIR, 0, 0, tiled=True)  11.7 us
    all_to_all x1, starting transfers between devices, broadcast_gather(): lax.all_to_all(jnp.broadcast_to(x[None], (n,) + x.shape), axis, 0, 0, til...  9.33 us
    all_to_all x1, starting transfers between devices, body(): part = lax.all_to_all(part, PAIR, 0, 0, tiled=True)  7.8 us
    pallas_call x1, Pallas kernels, project(): pl.pallas_call(project_kernel, in_specs=[pl.BlockSpec(memory_space=pltpu....  6.62 us
    ppermute x2, waiting for transfers between devices, swap(): return lax.ppermute(v, axis, [(0, 1), (1, 0)])  5.85 us
  transfers between devices with their start and end apart: 18, of which 9 were waited for; matrix products, arithmetic and copies ran while one was open for 1% of the time, Pallas kernels for 5%

profile of v11, /device:TPU:6, one launch (start us, length us, event | category | flops | bytes accessed | tf_op | source)
XLA Modules:
  0.0 154.2 jit_solution(6838005518731812178)
XLA Ops:
  8.4 11.7 %all-to-all-start = ((bf16[32,12,512]{2,1,0:T(8,128)(2,1)}), bf16[32,12,512]{2,1,0:T(8,128)(2,1)S(1)}, u32[]{:S(2)}, u32[]{:S(2)}) async-start(bf16[32,12,512]{2,1,0:T(8,128)(2,1)} %slabs.1), calls=%async_computation | async-start | bytes 1048576 | tf_op jit(solution)/shard_map/all_to_all | solution.py:281
  20.2 4.5 %collective-permute-start = (bf16[512,128]{1,0:T(8,128)(2,1)S(1)}, bf16[512,128]{1,0:T(8,128)(2,1)S(1)}, u32[]{:S(2)}, u32[]{:S(2)}) collective-permute-start(bf16[512,128]{1,0:T(8,128)(2,1)S(1)} %copy-done.4), channel_id=1, source_target_pairs={{0,32},{32,64},{64,96},{96,0},{1,33},{33,65},{65,97},{97,1},{2,34}... | collective-permute-start | bytes 393224 | tf_op jit(solution)/shard_map/ppermute | solution.py:260
  24.7 3.5 %collective-permute-start.1 = (bf16[512,128]{1,0:T(8,128)(2,1)S(1)}, bf16[512,128]{1,0:T(8,128)(2,1)S(1)}, u32[]{:S(2)}, u32[]{:S(2)}) collective-permute-start(bf16[512,128]{1,0:T(8,128)(2,1)S(1)} %copy-done.4), channel_id=1, source_target_pairs={{0,96},{32,0},{64,32},{96,64},{1,97},{33,1},{65,33},{97,65},{2,98}... | collective-permute-start | bytes 393224 | tf_op jit(solution)/shard_map/ppermute | solution.py:260
  28.3 7.7 %collective-permute-done = bf16[512,128]{1,0:T(8,128)(2,1)S(1)} collective-permute-done((bf16[512,128]{1,0:T(8,128)(2,1)S(1)}, bf16[512,128]{1,0:T(8,128)(2,1)S(1)}, u32[]{:S(2)}, u32[]{:S(2)}) %collective-permute-start) | collective-permute-done | bytes 131104 | tf_op jit(solution)/shard_map/ppermute | solution.py:260
  36.0 1.6 %mix.1 = (bf16[384,512]{1,0:T(8,128)(2,1)}, f32[32,24,128]{2,1,0:T(8,128)}) custom-call(s32[3]{0:T(128)S(1)} %pad_add_fusion.info_ref, bf16[32,12,512]{2,1,0:T(8,128)(2,1)S(1)} %all-to-all-done.x_ref, bf16[1024,256]{1,0:T(8,128)(2,1)S(1)} %copy-done.1), custom_call_target="tpu_custom_call" | custom-call | flops 100663296 | bytes 1048576 | tf_op jit(solution)/shard_map/mix/pallas_call | solution.py:67
  37.7 7.8 %all-to-all-start.1 = ((f32[32,24,128]{2,1,0:T(8,128)}), f32[32,24,128]{2,1,0:T(8,128)S(1)}, u32[]{:S(2)}, u32[]{:S(2)}) async-start(f32[32,24,128]{2,1,0:T(8,128)} %get-tuple-element.31), calls=%async_computation.1 | async-start | bytes 786432 | tf_op jit(solution)/shard_map/all_to_all | solution.py:290
  45.5 14.2 %all-to-all-done.1 = f32[32,24,128]{2,1,0:T(8,128)S(1)} async-done(((f32[32,24,128]{2,1,0:T(8,128)}), f32[32,24,128]{2,1,0:T(8,128)S(1)}, u32[]{:S(2)}, u32[]{:S(2)}) %all-to-all-start.1) | async-done | bytes 393248 | tf_op jit(solution)/shard_map/all_to_all | solution.py:290
  60.8 9.3 %all-to-all-start.2 = ((bf16[64,24,128]{2,1,0:T(8,128)(2,1)}), bf16[64,24,128]{2,1,0:T(8,128)(2,1)S(1)}, u32[]{:S(2)}, u32[]{:S(2)}) async-start(bf16[64,24,128]{2,1,0:T(8,128)(2,1)} %broadcast_in_dim.2), calls=%async_computation.2 | async-start | bytes 786432 | tf_op jit(solution)/shard_map/all_to_all | solution.py:40
  70.2 2.3 %collective-permute-start.3 = (bf16[1536,128]{1,0:T(8,128)(2,1)S(1)}, bf16[1536,128]{1,0:T(8,128)(2,1)S(1)}, u32[]{:S(2)}, u32[]{:S(2)}) collective-permute-start(bf16[1536,128]{1,0:T(8,128)(2,1)S(1)} %constant_dynamic-update-slice_fusion.refs_0_), channel_id=1, source_target_pairs={{0,128},{128,256},{256,384},{384,0},{1,129},{129,257},{257,385},{3... | collective-permute-start | bytes 1179656 | tf_op jit(solution)/shard_map/ppermute | solution.py:260
  72.6 3.5 %collective-permute-start.4 = (bf16[1536,128]{1,0:T(8,128)(2,1)S(1)}, bf16[1536,128]{1,0:T(8,128)(2,1)S(1)}, u32[]{:S(2)}, u32[]{:S(2)}) collective-permute-start(bf16[1536,128]{1,0:T(8,128)(2,1)S(1)} %constant_dynamic-update-slice_fusion.refs_0_), channel_id=1, source_target_pairs={{0,384},{128,0},{256,128},{384,256},{1,385},{129,1},{257,129},{385... | collective-permute-start | bytes 1179656 | tf_op jit(solution)/shard_map/ppermute | solution.py:260
  76.1 4.4 %collective-permute-start.2 = (bf16[512,128]{1,0:T(8,128)(2,1)S(1)}, bf16[512,128]{1,0:T(8,128)(2,1)S(1)}, u32[]{:S(2)}, u32[]{:S(2)}) collective-permute-start(bf16[512,128]{1,0:T(8,128)(2,1)S(1)} %collective-permute-done), channel_id=1, source_target_pairs={{0,32},{32,64},{64,96},{96,0},{1,33},{33,65},{65,97},{97,1},{2,34}... | collective-permute-start | bytes 393224 | tf_op jit(solution)/shard_map/ppermute | solution.py:260
  80.5 6.9 %collective-permute-done.2.refs_1_ = bf16[512,128]{1,0:T(8,128)(2,1)S(1)} collective-permute-done((bf16[512,128]{1,0:T(8,128)(2,1)S(1)}, bf16[512,128]{1,0:T(8,128)(2,1)S(1)}, u32[]{:S(2)}, u32[]{:S(2)}) %collective-permute-start.2) | collective-permute-done | bytes 131104 | tf_op jit(solution)/shard_map/ppermute | solution.py:260
  87.4 3.5 %collective-permute-start.5 = (bf16[512,128]{1,0:T(8,128)(2,1)S(1)}, bf16[512,128]{1,0:T(8,128)(2,1)S(1)}, u32[]{:S(2)}, u32[]{:S(2)}) collective-permute-start(bf16[512,128]{1,0:T(8,128)(2,1)S(1)} %collective-permute-done.2.refs_1_), channel_id=1, source_target_pairs={{0,128},{128,256},{256,384},{384,0},{1,129},{129,257},{257,385},{3... | collective-permute-start | bytes 393224 | tf_op jit(solution)/shard_map/ppermute | solution.py:260
  90.9 2.3 %collective-permute-start.6 = (bf16[512,128]{1,0:T(8,128)(2,1)S(1)}, bf16[512,128]{1,0:T(8,128)(2,1)S(1)}, u32[]{:S(2)}, u32[]{:S(2)}) collective-permute-start(bf16[512,128]{1,0:T(8,128)(2,1)S(1)} %collective-permute-done.2.refs_1_), channel_id=1, source_target_pairs={{0,384},{128,0},{256,128},{384,256},{1,385},{129,1},{257,129},{385... | collective-permute-start | bytes 393224 | tf_op jit(solution)/shard_map/ppermute | solution.py:260
  94.3 4.7 %collective-permute-done.6.down2_ref.refs_7_ = bf16[512,128]{1,0:T(8,128)(2,1)S(1)} collective-permute-done((bf16[512,128]{1,0:T(8,128)(2,1)S(1)}, bf16[512,128]{1,0:T(8,128)(2,1)S(1)}, u32[]{:S(2)}, u32[]{:S(2)}) %collective-permute-start.6) | collective-permute-done | bytes 131104 | tf_op jit(solution)/shard_map/ppermute | solution.py:260
  99.8 1.9 %collective-permute-start.7 = (bf16[1024,128]{1,0:T(8,128)(2,1)}, bf16[1024,128]{1,0:T(8,128)(2,1)S(1)}, u32[]{:S(2)}, u32[]{:S(2)}) collective-permute-start(bf16[1024,128]{1,0:T(8,128)(2,1)} %get-tuple-element.36), channel_id=1, source_target_pairs={{0,128},{128,256},{256,384},{384,0},{1,129},{129,257},{257,385},{3... | collective-permute-start | bytes 786440 | tf_op jit(solution)/shard_map/ppermute | solution.py:260
  101.7 3.9 %collective-permute-start.8 = (bf16[1024,128]{1,0:T(8,128)(2,1)}, bf16[1024,128]{1,0:T(8,128)(2,1)S(1)}, u32[]{:S(2)}, u32[]{:S(2)}) collective-permute-start(bf16[1024,128]{1,0:T(8,128)(2,1)} %get-tuple-element.37), channel_id=1, source_target_pairs={{0,384},{128,0},{256,128},{384,256},{1,385},{129,1},{257,129},{385... | collective-permute-start | bytes 786440 | tf_op jit(solution)/shard_map/ppermute | solution.py:260
  109.6 12.5 %collective-permute-done.8.refs_5_ = bf16[1024,128]{1,0:T(8,128)(2,1)S(1)} collective-permute-done((bf16[1024,128]{1,0:T(8,128)(2,1)}, bf16[1024,128]{1,0:T(8,128)(2,1)S(1)}, u32[]{:S(2)}, u32[]{:S(2)}) %collective-permute-start.8) | collective-permute-done | bytes 262176 | tf_op jit(solution)/shard_map/ppermute | solution.py:260
  123.0 6.6 %project.1 = f32[2,192,128]{2,1,0:T(8,128)S(1)} custom-call(s32[3]{0:T(128)S(1)} %pad_add_fusion.info_ref, bf16[16,384,512]{2,1,0:T(8,128)(2,1)} %bitcast.14, bf16[1536,128]{1,0:T(8,128)(2,1)S(1)} %constant_dynamic-update-slice_fusion.refs_0_, bf16[512,128]{1,0:T(8,128)(2,1)S(1)} %collective-permute-done.2.refs_1_, ...), custom_call_target="tpu_custom_call" | custom-call | flops 805306368 | bytes 8388608 | tf_op jit(solution)/shard_map/project/pallas_call | solution.py:215
  129.7 3.4 %collective-permute-start.12 = (f32[192,128]{1,0:T(8,128)S(1)}, f32[192,128]{1,0:T(8,128)S(1)}, u32[]{:S(2)}, u32[]{:S(2)}) collective-permute-start(f32[192,128]{1,0:T(8,128)S(1)} %select_bitcast_fusion), channel_id=1, source_target_pairs={{0,16},{16,0},{1,17},{17,1},{2,18},{18,2},{3,19},{19,3},{4,20},{20... | collective-permute-start | bytes 294920 | tf_op jit(solution)/shard_map/ppermute | solution.py:269
  133.1 3.1 %collective-permute-done.12 = f32[192,128]{1,0:T(8,128)S(1)} collective-permute-done((f32[192,128]{1,0:T(8,128)S(1)}, f32[192,128]{1,0:T(8,128)S(1)}, u32[]{:S(2)}, u32[]{:S(2)}) %collective-permute-start.12) | collective-permute-done | bytes 98336 | tf_op jit(solution)/shard_map/ppermute | solution.py:269
  136.3 1.9 %collective-permute-start.13 = (bf16[6144,128]{1,0:T(8,128)(2,1)S(1)}, bf16[6144,128]{1,0:T(8,128)(2,1)S(1)}, u32[]{:S(2)}, u32[]{:S(2)}) collective-permute-start(bf16[6144,128]{1,0:T(8,128)(2,1)S(1)} %join.1), channel_id=1, source_target_pairs={{0,1},{1,0},{2,3},{3,2},{4,5},{5,4},{6,7},{7,6},{8,9},{9,8},{10,11... | collective-permute-start | bytes 4718600 | tf_op jit(solution)/shard_map/ppermute | solution.py:269
  138.8 2.8 %collective-permute-done.13.refs_4_ = bf16[6144,128]{1,0:T(8,128)(2,1)S(1)} collective-permute-done((bf16[6144,128]{1,0:T(8,128)(2,1)S(1)}, bf16[6144,128]{1,0:T(8,128)(2,1)S(1)}, u32[]{:S(2)}, u32[]{:S(2)}) %collective-permute-start.13) | collective-permute-done | bytes 1572896 | tf_op jit(solution)/shard_map/ppermute | solution.py:269
  141.6 5.8 %attend.1 = bf16[192,128]{1,0:T(8,128)(2,1)} custom-call(s32[3]{0:T(128)S(1)} %pad_add_fusion.info_ref, f32[192,128]{1,0:T(8,128)S(1)} %bitcast_add_fusion.q_ref, f32[192,128]{1,0:T(8,128)S(1)} %get-tuple-element.48.cos_ref, f32[192,128]{1,0:T(8,128)S(1)} %get-tuple-element.49.sin_ref, bf16[1536,128]{1,0:T(8,128)(2,1)S(1)} %bitcast.13, ...), custom_call_target="tpu_custom_call" | custom-call | flops 603979776 | bytes 3145728 | tf_op jit(solution)/shard_map/attend/pallas_call | solution.py:237
  (44 shorter events, 10.6 us)
Async XLA Ops:
  6.5 1.0 copy-start
  7.6 12.6 %copy-start.4 = (bf16[512,128]{1,0:T(8,128)(2,1)S(1)}, bf16[512,128]{1,0:T(8,128)(2,1)}, u32[]{:S(2)}) copy-start(bf16[512,128]{1,0:T(8,128)(2,1)} %param.4) | copy-start | bytes 393220
  7.6 28.5 %copy-start.1 = (bf16[1024,256]{1,0:T(8,128)(2,1)S(1)}, bf16[1024,256]{1,0:T(8,128)(2,1)}, u32[]{:S(2)}) copy-start(bf16[1024,256]{1,0:T(8,128)(2,1)} %w_ref.1) | copy-start | bytes 1572868
  8.4 27.6 %all-to-all-start = ((bf16[32,12,512]{2,1,0:T(8,128)(2,1)}), bf16[32,12,512]{2,1,0:T(8,128)(2,1)S(1)}, u32[]{:S(2)}, u32[]{:S(2)}) async-start(bf16[32,12,512]{2,1,0:T(8,128)(2,1)} %slabs.1), calls=%async_computation | async-start | bytes 1048576 | tf_op jit(solution)/shard_map/all_to_all | solution.py:281
  20.2 102.0 %all-gather.3.cloned.1.call-start = ((), (), s32[]{:S(2)}) async-start(), calls=%async_computation.3 | async-start | bytes 6684672 | tf_op jit(solution)/shard_map/all_gather | solution.py:286
  20.2 15.7 %collective-permute-start = (bf16[512,128]{1,0:T(8,128)(2,1)S(1)}, bf16[512,128]{1,0:T(8,128)(2,1)S(1)}, u32[]{:S(2)}, u32[]{:S(2)}) collective-permute-start(bf16[512,128]{1,0:T(8,128)(2,1)S(1)} %copy-done.4), channel_id=1, source_target_pairs={{0,32},{32,64},{64,96},{96,0},{1,33},{33,65},{65,97},{97,1},{2,34}... | collective-permute-start | bytes 393224 | tf_op jit(solution)/shard_map/ppermute | solution.py:260
  24.7 11.2 %collective-permute-start.1 = (bf16[512,128]{1,0:T(8,128)(2,1)S(1)}, bf16[512,128]{1,0:T(8,128)(2,1)S(1)}, u32[]{:S(2)}, u32[]{:S(2)}) collective-permute-start(bf16[512,128]{1,0:T(8,128)(2,1)S(1)} %copy-done.4), channel_id=1, source_target_pairs={{0,96},{32,0},{64,32},{96,64},{1,97},{33,1},{65,33},{97,65},{2,98}... | collective-permute-start | bytes 393224 | tf_op jit(solution)/shard_map/ppermute | solution.py:260
  37.7 22.1 %all-to-all-start.1 = ((f32[32,24,128]{2,1,0:T(8,128)}), f32[32,24,128]{2,1,0:T(8,128)S(1)}, u32[]{:S(2)}, u32[]{:S(2)}) async-start(f32[32,24,128]{2,1,0:T(8,128)} %get-tuple-element.31), calls=%async_computation.1 | async-start | bytes 786432 | tf_op jit(solution)/shard_map/all_to_all | solution.py:290
  60.8 38.2 %all-to-all-start.2 = ((bf16[64,24,128]{2,1,0:T(8,128)(2,1)}), bf16[64,24,128]{2,1,0:T(8,128)(2,1)S(1)}, u32[]{:S(2)}, u32[]{:S(2)}) async-start(bf16[64,24,128]{2,1,0:T(8,128)(2,1)} %broadcast_in_dim.2), calls=%async_computation.2 | async-start | bytes 786432 | tf_op jit(solution)/shard_map/all_to_all | solution.py:40
  70.2 28.7 %collective-permute-start.3 = (bf16[1536,128]{1,0:T(8,128)(2,1)S(1)}, bf16[1536,128]{1,0:T(8,128)(2,1)S(1)}, u32[]{:S(2)}, u32[]{:S(2)}) collective-permute-start(bf16[1536,128]{1,0:T(8,128)(2,1)S(1)} %constant_dynamic-update-slice_fusion.refs_0_), channel_id=1, source_target_pairs={{0,128},{128,256},{256,384},{384,0},{1,129},{129,257},{257,385},{3... | collective-permute-start | bytes 1179656 | tf_op jit(solution)/shard_map/ppermute | solution.py:260
  72.6 26.4 %collective-permute-start.4 = (bf16[1536,128]{1,0:T(8,128)(2,1)S(1)}, bf16[1536,128]{1,0:T(8,128)(2,1)S(1)}, u32[]{:S(2)}, u32[]{:S(2)}) collective-permute-start(bf16[1536,128]{1,0:T(8,128)(2,1)S(1)} %constant_dynamic-update-slice_fusion.refs_0_), channel_id=1, source_target_pairs={{0,384},{128,0},{256,128},{384,256},{1,385},{129,1},{257,129},{385... | collective-permute-start | bytes 1179656 | tf_op jit(solution)/shard_map/ppermute | solution.py:260
  76.1 11.3 %collective-permute-start.2 = (bf16[512,128]{1,0:T(8,128)(2,1)S(1)}, bf16[512,128]{1,0:T(8,128)(2,1)S(1)}, u32[]{:S(2)}, u32[]{:S(2)}) collective-permute-start(bf16[512,128]{1,0:T(8,128)(2,1)S(1)} %collective-permute-done), channel_id=1, source_target_pairs={{0,32},{32,64},{64,96},{96,0},{1,33},{33,65},{65,97},{97,1},{2,34}... | collective-permute-start | bytes 393224 | tf_op jit(solution)/shard_map/ppermute | solution.py:260
  87.4 6.8 %collective-permute-start.5 = (bf16[512,128]{1,0:T(8,128)(2,1)S(1)}, bf16[512,128]{1,0:T(8,128)(2,1)S(1)}, u32[]{:S(2)}, u32[]{:S(2)}) collective-permute-start(bf16[512,128]{1,0:T(8,128)(2,1)S(1)} %collective-permute-done.2.refs_1_), channel_id=1, source_target_pairs={{0,128},{128,256},{256,384},{384,0},{1,129},{129,257},{257,385},{3... | collective-permute-start | bytes 393224 | tf_op jit(solution)/shard_map/ppermute | solution.py:260
  90.9 8.1 %collective-permute-start.6 = (bf16[512,128]{1,0:T(8,128)(2,1)S(1)}, bf16[512,128]{1,0:T(8,128)(2,1)S(1)}, u32[]{:S(2)}, u32[]{:S(2)}) collective-permute-start(bf16[512,128]{1,0:T(8,128)(2,1)S(1)} %collective-permute-done.2.refs_1_), channel_id=1, source_target_pairs={{0,384},{128,0},{256,128},{384,256},{1,385},{129,1},{257,129},{385... | collective-permute-start | bytes 393224 | tf_op jit(solution)/shard_map/ppermute | solution.py:260
  94.2 5.6 %copy-start.2 = (bf16[512,128]{1,0:T(8,128)(2,1)}, bf16[512,128]{1,0:T(8,128)(2,1)S(1)}, u32[]{:S(2)}) copy-start(bf16[512,128]{1,0:T(8,128)(2,1)S(1)} %collective-permute-done.5.refs_3_) | copy-start | bytes 393220
  99.8 9.8 %collective-permute-start.7 = (bf16[1024,128]{1,0:T(8,128)(2,1)}, bf16[1024,128]{1,0:T(8,128)(2,1)S(1)}, u32[]{:S(2)}, u32[]{:S(2)}) collective-permute-start(bf16[1024,128]{1,0:T(8,128)(2,1)} %get-tuple-element.36), channel_id=1, source_target_pairs={{0,128},{128,256},{256,384},{384,0},{1,129},{129,257},{257,385},{3... | collective-permute-start | bytes 786440 | tf_op jit(solution)/shard_map/ppermute | solution.py:260
  101.7 20.4 %collective-permute-start.8 = (bf16[1024,128]{1,0:T(8,128)(2,1)}, bf16[1024,128]{1,0:T(8,128)(2,1)S(1)}, u32[]{:S(2)}, u32[]{:S(2)}) collective-permute-start(bf16[1024,128]{1,0:T(8,128)(2,1)} %get-tuple-element.37), channel_id=1, source_target_pairs={{0,384},{128,0},{256,128},{384,256},{1,385},{129,1},{257,129},{385... | collective-permute-start | bytes 786440 | tf_op jit(solution)/shard_map/ppermute | solution.py:260
  105.7 27.4 %collective-permute-start.10 = (bf16[1536,128]{1,0:T(8,128)(2,1)S(1)}, bf16[1536,128]{1,0:T(8,128)(2,1)S(1)}, u32[]{:S(2)}, u32[]{:S(2)}) collective-permute-start(bf16[1536,128]{1,0:T(8,128)(2,1)S(1)} %bitcast.9), channel_id=1, source_target_pairs={{0,256},{128,384},{1,257},{129,385},{2,258},{130,386},{3,259},{131... | collective-permute-start | bytes 1179656 | tf_op jit(solution)/shard_map/ppermute | solution.py:265
  107.0 26.1 %collective-permute-start.11 = (bf16[1536,128]{1,0:T(8,128)(2,1)S(1)}, bf16[1536,128]{1,0:T(8,128)(2,1)S(1)}, u32[]{:S(2)}, u32[]{:S(2)}) collective-permute-start(bf16[1536,128]{1,0:T(8,128)(2,1)S(1)} %bitcast.10), channel_id=1, source_target_pairs={{0,384},{1,385},{2,386},{3,387},{4,388},{5,389},{6,390},{7,391},{8... | collective-permute-start | bytes 1179656 | tf_op jit(solution)/shard_map/ppermute | solution.py:265
  108.3 24.8 %collective-permute-start.9 = (bf16[1536,128]{1,0:T(8,128)(2,1)S(1)}, bf16[1536,128]{1,0:T(8,128)(2,1)S(1)}, u32[]{:S(2)}, u32[]{:S(2)}) collective-permute-start(bf16[1536,128]{1,0:T(8,128)(2,1)S(1)} %bitcast.11), channel_id=1, source_target_pairs={{0,128},{128,256},{256,384},{1,129},{129,257},{257,385},{2,130},{1... | collective-permute-start | bytes 1179656 | tf_op jit(solution)/shard_map/ppermute | solution.py:265
  122.1 0.9 copy-start.3
  129.7 6.5 %collective-permute-start.12 = (f32[192,128]{1,0:T(8,128)S(1)}, f32[192,128]{1,0:T(8,128)S(1)}, u32[]{:S(2)}, u32[]{:S(2)}) collective-permute-start(f32[192,128]{1,0:T(8,128)S(1)} %select_bitcast_fusion), channel_id=1, source_target_pairs={{0,16},{16,0},{1,17},{17,1},{2,18},{18,2},{3,19},{19,3},{4,20},{20... | collective-permute-start | bytes 294920 | tf_op jit(solution)/shard_map/ppermute | solution.py:269
  136.3 5.3 %collective-permute-start.13 = (bf16[6144,128]{1,0:T(8,128)(2,1)S(1)}, bf16[6144,128]{1,0:T(8,128)(2,1)S(1)}, u32[]{:S(2)}, u32[]{:S(2)}) collective-permute-start(bf16[6144,128]{1,0:T(8,128)(2,1)S(1)} %join.1), channel_id=1, source_target_pairs={{0,1},{1,0},{2,3},{3,2},{4,5},{5,4},{6,7},{7,6},{8,9},{9,8},{10,11... | collective-permute-start | bytes 4718600 | tf_op jit(solution)/shard_map/ppermute | solution.py:269
Sparse Core Ops, SparseCore 0:
  37.8 59.7 all-gather.2

commit v12 on v9

--- a/solution.py
+++ b/solution.py
@@ -145,12 +145,17 @@
             pltpu.make_async_copy(other, buf.at[i, 1 - core], sems.at[i, 1]),
         ]
 
-    for i in range(4):
-
-        @pl.when(x >= i)
-        def _(i=i):
-            for copy in copies(i):
-                copy.start()
+    for values in range(2):
+        for i in range(4):
+            for own in range(2):
+
+                @pl.when((x >= i) & (core == own))
+                def _(i=i, which=(own + values) % 2):
+                    copies(i)[which].start()
+
+    def wait(i, values):
+        which = jnp.where(core == 0, values, 1 - values)
+        pltpu.make_async_copy(mine[0], buf.at[i, values], sems.at[i, which]).wait()
 
     sums = q_ref[...]
     q = sums * cos_ref[...] + pltpu.roll(sums, HD // 2, 1) * sin_ref[...]
@@ -167,22 +172,16 @@
             q, k, (((1,), (1,)), ((), ())), preferred_element_type=jnp.float32
         )
 
-    for copy in copies(0):
-        copy.wait()
+    wait(0, 0)
     s = scores(buf[0, 0])
     qp = y * rows + lax.broadcasted_iota(jnp.int32, s.shape, 0)
     kp = lax.broadcasted_iota(jnp.int32, s.shape, 1)
     s = jnp.where(qp >= kp, s, -jnp.inf)
     s_ref[0] = s
     top = lanes(s, jnp.maximum)
-    for i in range(1, 4):
-
-        @pl.when(x >= i)
-        def _(i=i):
-            for copy in copies(i):
-                copy.wait()
 
     def first_pass(i, top):
+        wait(i, 0)
         s = scores(buf[i, 0])
         s_ref[i] = s
         return jnp.maximum(top, lanes(s, jnp.maximum))
@@ -193,6 +192,7 @@
 
     def second_pass(i, state):
         tot, acc = state
+        wait(i, 1)
         e = jnp.exp2((s_ref[i] - top) * scale)
         return tot + lanes(e, jnp.add), acc + jnp.dot(
             e.astype(jnp.bfloat16), buf[i, 1], preferred_element_type=jnp.float32

time: 135 us -> 135 us (level)
  no operation moved by 1% of the time
where the time goes in v12:
time: 135 us; the launch traced here: 133 us
  starting transfers between devices  63.6 us (47%)
  waiting for transfers between devices  35.6 us (26%)
  Pallas kernels  14.6 us (11%)
  between operations  13.8 us (10%)
  local copies, waits for them, and re-layouts  2.97 us (2%)
  other arithmetic  1.91 us (1%)
    ppermute x7, starting transfers between devices, shift(): return lax.ppermute(v, axis, [(i, (i + by) % n) for i in range(n)])  24.8 us
    ppermute x7, waiting for transfers between devices, shift(): return lax.ppermute(v, axis, [(i, (i + by) % n) for i in range(n)])  24 us
    all_to_all x1, starting transfers between devices, body(): hs = lax.all_to_all(hs, PAIR, 0, 0, tiled=True)  11.7 us
    all_to_all x1, starting transfers between devices, broadcast_gather(): lax.all_to_all(jnp.broadcast_to(x[None], (n,) + x.shape), axis, 0, 0, til...  11.3 us
    all_to_all x1, starting transfers between devices, body(): part = lax.all_to_all(part, PAIR, 0, 0, tiled=True)  7.8 us
    pallas_call x1, Pallas kernels, project(): pl.pallas_call(project_kernel, in_specs=[pl.BlockSpec(memory_space=pltpu....  6.18 us
    ppermute x3, waiting for transfers between devices, shift_up(): return lax.ppermute(v, axis, [(i, i + by) for i in range(n - by)])  5.9 us
    pallas_call x1, Pallas kernels, attend(): pl.pallas_call(attend_kernel, in_specs=[pl.BlockSpec(memory_space=pltpu.S...  5.86 us
  transfers between devices with their start and end apart: 16, of which 9 were waited for; matrix products, arithmetic and copies ran while one was open for 2% of the time, Pallas kernels for 5%

profile of v12, /device:TPU:6, one launch (start us, length us, event | category | flops | bytes accessed | tf_op | source)
XLA Modules:
  0.0 132.5 jit_solution(16298778295014679840)
XLA Ops:
  8.4 11.7 %all-to-all-start = ((bf16[32,12,512]{2,1,0:T(8,128)(2,1)}), bf16[32,12,512]{2,1,0:T(8,128)(2,1)S(1)}, u32[]{:S(2)}, u32[]{:S(2)}) async-start(bf16[32,12,512]{2,1,0:T(8,128)(2,1)} %slabs.1), calls=%async_computation | async-start | bytes 1048576 | tf_op jit(solution)/shard_map/all_to_all | solution.py:275
  20.2 4.5 %collective-permute-start = (bf16[512,128]{1,0:T(8,128)(2,1)S(1)}, bf16[512,128]{1,0:T(8,128)(2,1)S(1)}, u32[]{:S(2)}, u32[]{:S(2)}) collective-permute-start(bf16[512,128]{1,0:T(8,128)(2,1)S(1)} %copy-done.4), channel_id=1, source_target_pairs={{0,32},{32,64},{64,96},{96,0},{1,33},{33,65},{65,97},{97,1},{2,34}... | collective-permute-start | bytes 393224 | tf_op jit(solution)/shard_map/ppermute | solution.py:254
  24.7 3.5 %collective-permute-start.1 = (bf16[512,128]{1,0:T(8,128)(2,1)S(1)}, bf16[512,128]{1,0:T(8,128)(2,1)S(1)}, u32[]{:S(2)}, u32[]{:S(2)}) collective-permute-start(bf16[512,128]{1,0:T(8,128)(2,1)S(1)} %copy-done.4), channel_id=1, source_target_pairs={{0,96},{32,0},{64,32},{96,64},{1,97},{33,1},{65,33},{97,65},{2,98}... | collective-permute-start | bytes 393224 | tf_op jit(solution)/shard_map/ppermute | solution.py:254
  28.3 7.7 %collective-permute-done = bf16[512,128]{1,0:T(8,128)(2,1)S(1)} collective-permute-done((bf16[512,128]{1,0:T(8,128)(2,1)S(1)}, bf16[512,128]{1,0:T(8,128)(2,1)S(1)}, u32[]{:S(2)}, u32[]{:S(2)}) %collective-permute-start) | collective-permute-done | bytes 131104 | tf_op jit(solution)/shard_map/ppermute | solution.py:254
  36.0 1.6 %mix.1 = (bf16[384,512]{1,0:T(8,128)(2,1)}, f32[32,24,128]{2,1,0:T(8,128)}) custom-call(s32[3]{0:T(128)S(1)} %pad_add_fusion.info_ref, bf16[32,12,512]{2,1,0:T(8,128)(2,1)S(1)} %all-to-all-done.x_ref, bf16[1024,256]{1,0:T(8,128)(2,1)S(1)} %copy-done.3), custom_call_target="tpu_custom_call" | custom-call | flops 100663296 | bytes 1048576 | tf_op jit(solution)/shard_map/mix/pallas_call | solution.py:67
  37.6 7.8 %all-to-all-start.1 = ((f32[32,24,128]{2,1,0:T(8,128)}), f32[32,24,128]{2,1,0:T(8,128)S(1)}, u32[]{:S(2)}, u32[]{:S(2)}) async-start(f32[32,24,128]{2,1,0:T(8,128)} %get-tuple-element.29), calls=%async_computation.1 | async-start | bytes 786432 | tf_op jit(solution)/shard_map/all_to_all | solution.py:283
  45.5 5.2 %collective-permute-start.2 = (bf16[512,128]{1,0:T(8,128)(2,1)S(1)}, bf16[512,128]{1,0:T(8,128)(2,1)S(1)}, u32[]{:S(2)}, u32[]{:S(2)}) collective-permute-start(bf16[512,128]{1,0:T(8,128)(2,1)S(1)} %collective-permute-done), channel_id=1, source_target_pairs={{0,32},{32,64},{64,96},{96,0},{1,33},{33,65},{65,97},{97,1},{2,34}... | collective-permute-start | bytes 393224 | tf_op jit(solution)/shard_map/ppermute | solution.py:254
  50.7 8.6 %collective-permute-done.2 = bf16[512,128]{1,0:T(8,128)(2,1)S(1)} collective-permute-done((bf16[512,128]{1,0:T(8,128)(2,1)S(1)}, bf16[512,128]{1,0:T(8,128)(2,1)S(1)}, u32[]{:S(2)}, u32[]{:S(2)}) %collective-permute-start.2) | collective-permute-done | bytes 131104 | tf_op jit(solution)/shard_map/ppermute | solution.py:254
  59.4 2.4 %collective-permute-start.3 = (bf16[2048,128]{1,0:T(8,128)(2,1)S(1)}, bf16[2048,128]{1,0:T(8,128)(2,1)S(1)}, u32[]{:S(2)}, u32[]{:S(2)}) collective-permute-start(bf16[2048,128]{1,0:T(8,128)(2,1)S(1)} %constant_dynamic-update-slice_fusion.refs_0_), channel_id=1, source_target_pairs={{0,128},{128,256},{256,384},{384,0},{1,129},{129,257},{257,385},{3... | collective-permute-start | bytes 1572872 | tf_op jit(solution)/shard_map/ppermute | solution.py:254
  61.8 3.5 %collective-permute-start.4 = (bf16[2048,128]{1,0:T(8,128)(2,1)S(1)}, bf16[2048,128]{1,0:T(8,128)(2,1)S(1)}, u32[]{:S(2)}, u32[]{:S(2)}) collective-permute-start(bf16[2048,128]{1,0:T(8,128)(2,1)S(1)} %constant_dynamic-update-slice_fusion.refs_0_), channel_id=1, source_target_pairs={{0,384},{128,0},{256,128},{384,256},{1,385},{129,1},{257,129},{385... | collective-permute-start | bytes 1572872 | tf_op jit(solution)/shard_map/ppermute | solution.py:254
  66.3 11.3 %all-to-all-start.2 = ((bf16[64,24,128]{2,1,0:T(8,128)(2,1)}), bf16[64,24,128]{2,1,0:T(8,128)(2,1)S(1)}, u32[]{:S(2)}, u32[]{:S(2)}) async-start(bf16[64,24,128]{2,1,0:T(8,128)(2,1)} %broadcast_in_dim.2), calls=%async_computation.2 | async-start | bytes 786432 | tf_op jit(solution)/shard_map/all_to_all | solution.py:40
  78.3 3.0 %collective-permute-start.5 = (bf16[1024,128]{1,0:T(8,128)(2,1)S(1)}, bf16[1024,128]{1,0:T(8,128)(2,1)S(1)}, u32[]{:S(2)}, u32[]{:S(2)}) collective-permute-start(bf16[1024,128]{1,0:T(8,128)(2,1)S(1)} %get-tuple-element.30), channel_id=1, source_target_pairs={{0,128},{128,256},{256,384},{384,0},{1,129},{129,257},{257,385},{3... | collective-permute-start | bytes 786440 | tf_op jit(solution)/shard_map/ppermute | solution.py:254
  81.3 2.9 %collective-permute-start.6 = (bf16[1024,128]{1,0:T(8,128)(2,1)S(1)}, bf16[1024,128]{1,0:T(8,128)(2,1)}, u32[]{:S(2)}, u32[]{:S(2)}) collective-permute-start(bf16[1024,128]{1,0:T(8,128)(2,1)S(1)} %get-tuple-element.31), channel_id=1, source_target_pairs={{0,384},{128,0},{256,128},{384,256},{1,385},{129,1},{257,129},{385... | collective-permute-start | bytes 786440 | tf_op jit(solution)/shard_map/ppermute | solution.py:254
  84.2 3.0 %collective-permute-done.5 = bf16[1024,128]{1,0:T(8,128)(2,1)S(1)} collective-permute-done((bf16[1024,128]{1,0:T(8,128)(2,1)S(1)}, bf16[1024,128]{1,0:T(8,128)(2,1)S(1)}, u32[]{:S(2)}, u32[]{:S(2)}) %collective-permute-start.5) | collective-permute-done | bytes 262176 | tf_op jit(solution)/shard_map/ppermute | solution.py:254
  87.2 4.1 %collective-permute-done.6 = bf16[1024,128]{1,0:T(8,128)(2,1)} collective-permute-done((bf16[1024,128]{1,0:T(8,128)(2,1)S(1)}, bf16[1024,128]{1,0:T(8,128)(2,1)}, u32[]{:S(2)}, u32[]{:S(2)}) %collective-permute-start.6) | collective-permute-done | bytes 262176 | tf_op jit(solution)/shard_map/ppermute | solution.py:254
  91.3 2.8 %all-to-all-done.2 = bf16[64,24,128]{2,1,0:T(8,128)(2,1)S(1)} async-done(((bf16[64,24,128]{2,1,0:T(8,128)(2,1)}), bf16[64,24,128]{2,1,0:T(8,128)(2,1)S(1)}, u32[]{:S(2)}, u32[]{:S(2)}) %all-to-all-start.2) | async-done | bytes 393248 | tf_op jit(solution)/shard_map/all_to_all | solution.py:40
  95.4 1.3 collective-permute-start.8
  96.7 1.3 collective-permute-start.9
  100.1 6.2 %project.1 = f32[2,192,128]{2,1,0:T(8,128)S(1)} custom-call(s32[3]{0:T(128)S(1)} %pad_add_fusion.info_ref, bf16[16,384,512]{2,1,0:T(8,128)(2,1)} %bitcast.14, bf16[2048,128]{1,0:T(8,128)(2,1)S(1)} %copy-done.1, bf16[2048,128]{1,0:T(8,128)(2,1)S(1)} %collective-permute-done.3.up_ref.refs_1_, bf16[2048,128]{1,0:T(8,128)(2,1)S(1)} %pad_maximum_fusion.refs_2_, ...), custom_call_target="tpu_custom_call" | custom-call | flops 805306368 | bytes 8388608 | tf_op jit(solution)/shard_map/project/pallas_call | solution.py:209
  106.3 2.2 %collective-permute-start.10 = (f32[192,128]{1,0:T(8,128)S(1)}, f32[192,128]{1,0:T(8,128)S(1)}, u32[]{:S(2)}, u32[]{:S(2)}) collective-permute-start(f32[192,128]{1,0:T(8,128)S(1)} %select_bitcast_fusion), channel_id=1, source_target_pairs={{0,16},{16,0},{1,17},{17,1},{2,18},{18,2},{3,19},{19,3},{4,20},{20... | collective-permute-start | bytes 294920 | tf_op jit(solution)/shard_map/ppermute | solution.py:263
  108.5 5.9 %collective-permute-done.9.refs_3_ = bf16[1536,128]{1,0:T(8,128)(2,1)S(1)} collective-permute-done((bf16[1536,128]{1,0:T(8,128)(2,1)S(1)}, bf16[1536,128]{1,0:T(8,128)(2,1)S(1)}, u32[]{:S(2)}, u32[]{:S(2)}) %collective-permute-start.9) | collective-permute-done | bytes 393248 | tf_op jit(solution)/shard_map/ppermute | solution.py:259
  114.5 1.9 %collective-permute-start.11 = (bf16[6144,128]{1,0:T(8,128)(2,1)S(1)}, bf16[6144,128]{1,0:T(8,128)(2,1)S(1)}, u32[]{:S(2)}, u32[]{:S(2)}) collective-permute-start(bf16[6144,128]{1,0:T(8,128)(2,1)S(1)} %join.1), channel_id=1, source_target_pairs={{0,1},{1,0},{2,3},{3,2},{4,5},{5,4},{6,7},{7,6},{8,9},{9,8},{10,11... | collective-permute-start | bytes 4718600 | tf_op jit(solution)/shard_map/ppermute | solution.py:263
  117.0 2.8 %collective-permute-done.11.refs_4_ = bf16[6144,128]{1,0:T(8,128)(2,1)S(1)} collective-permute-done((bf16[6144,128]{1,0:T(8,128)(2,1)S(1)}, bf16[6144,128]{1,0:T(8,128)(2,1)S(1)}, u32[]{:S(2)}, u32[]{:S(2)}) %collective-permute-start.11) | collective-permute-done | bytes 1572896 | tf_op jit(solution)/shard_map/ppermute | solution.py:263
  119.8 5.9 %attend.1 = bf16[192,128]{1,0:T(8,128)(2,1)} custom-call(s32[3]{0:T(128)S(1)} %pad_add_fusion.info_ref, f32[192,128]{1,0:T(8,128)S(1)} %bitcast_add_fusion.q_ref, f32[192,128]{1,0:T(8,128)S(1)} %get-tuple-element.44.cos_ref, f32[192,128]{1,0:T(8,128)S(1)} %get-tuple-element.45.sin_ref, bf16[1536,128]{1,0:T(8,128)(2,1)S(1)} %bitcast.13, ...), custom_call_target="tpu_custom_call" | custom-call | flops 603979776 | bytes 3145728 | tf_op jit(solution)/shard_map/attend/pallas_call | solution.py:231
  (42 shorter events, 7.9 us)
Async XLA Ops:
  6.5 1.0 copy-start.2
  7.6 12.6 %copy-start.4 = (bf16[512,128]{1,0:T(8,128)(2,1)S(1)}, bf16[512,128]{1,0:T(8,128)(2,1)}, u32[]{:S(2)}) copy-start(bf16[512,128]{1,0:T(8,128)(2,1)} %param.4) | copy-start | bytes 393220
  7.6 28.4 %copy-start.3 = (bf16[1024,256]{1,0:T(8,128)(2,1)S(1)}, bf16[1024,256]{1,0:T(8,128)(2,1)}, u32[]{:S(2)}) copy-start(bf16[1024,256]{1,0:T(8,128)(2,1)} %w_ref.1) | copy-start | bytes 1572868
  8.4 27.6 %all-to-all-start = ((bf16[32,12,512]{2,1,0:T(8,128)(2,1)}), bf16[32,12,512]{2,1,0:T(8,128)(2,1)S(1)}, u32[]{:S(2)}, u32[]{:S(2)}) async-start(bf16[32,12,512]{2,1,0:T(8,128)(2,1)} %slabs.1), calls=%async_computation | async-start | bytes 1048576 | tf_op jit(solution)/shard_map/all_to_all | solution.py:275
  20.2 78.8 %all-gather.3.cloned.1.call-start = ((), (), s32[]{:S(2)}) async-start(), calls=%async_computation.3 | async-start | bytes 6684672 | tf_op jit(solution)/shard_map/all_gather | solution.py:280
  20.2 15.7 %collective-permute-start = (bf16[512,128]{1,0:T(8,128)(2,1)S(1)}, bf16[512,128]{1,0:T(8,128)(2,1)S(1)}, u32[]{:S(2)}, u32[]{:S(2)}) collective-permute-start(bf16[512,128]{1,0:T(8,128)(2,1)S(1)} %copy-done.4), channel_id=1, source_target_pairs={{0,32},{32,64},{64,96},{96,0},{1,33},{33,65},{65,97},{97,1},{2,34}... | collective-permute-start | bytes 393224 | tf_op jit(solution)/shard_map/ppermute | solution.py:254
  24.7 11.2 %collective-permute-start.1 = (bf16[512,128]{1,0:T(8,128)(2,1)S(1)}, bf16[512,128]{1,0:T(8,128)(2,1)S(1)}, u32[]{:S(2)}, u32[]{:S(2)}) collective-permute-start(bf16[512,128]{1,0:T(8,128)(2,1)S(1)} %copy-done.4), channel_id=1, source_target_pairs={{0,96},{32,0},{64,32},{96,64},{1,97},{33,1},{65,33},{97,65},{2,98}... | collective-permute-start | bytes 393224 | tf_op jit(solution)/shard_map/ppermute | solution.py:254
  37.6 27.6 %all-to-all-start.1 = ((f32[32,24,128]{2,1,0:T(8,128)}), f32[32,24,128]{2,1,0:T(8,128)S(1)}, u32[]{:S(2)}, u32[]{:S(2)}) async-start(f32[32,24,128]{2,1,0:T(8,128)} %get-tuple-element.29), calls=%async_computation.1 | async-start | bytes 786432 | tf_op jit(solution)/shard_map/all_to_all | solution.py:283
  45.5 13.8 %collective-permute-start.2 = (bf16[512,128]{1,0:T(8,128)(2,1)S(1)}, bf16[512,128]{1,0:T(8,128)(2,1)S(1)}, u32[]{:S(2)}, u32[]{:S(2)}) collective-permute-start(bf16[512,128]{1,0:T(8,128)(2,1)S(1)} %collective-permute-done), channel_id=1, source_target_pairs={{0,32},{32,64},{64,96},{96,0},{1,33},{33,65},{65,97},{97,1},{2,34}... | collective-permute-start | bytes 393224 | tf_op jit(solution)/shard_map/ppermute | solution.py:254
  59.4 37.3 %copy-start = (bf16[2048,128]{1,0:T(8,128)(2,1)}, bf16[2048,128]{1,0:T(8,128)(2,1)S(1)}, u32[]{:S(2)}) copy-start(bf16[2048,128]{1,0:T(8,128)(2,1)S(1)} %constant_dynamic-update-slice_fusion.refs_0_) | copy-start | bytes 1572868
  59.4 18.2 %collective-permute-start.3 = (bf16[2048,128]{1,0:T(8,128)(2,1)S(1)}, bf16[2048,128]{1,0:T(8,128)(2,1)S(1)}, u32[]{:S(2)}, u32[]{:S(2)}) collective-permute-start(bf16[2048,128]{1,0:T(8,128)(2,1)S(1)} %constant_dynamic-update-slice_fusion.refs_0_), channel_id=1, source_target_pairs={{0,128},{128,256},{256,384},{384,0},{1,129},{129,257},{257,385},{3... | collective-permute-start | bytes 1572872 | tf_op jit(solution)/shard_map/ppermute | solution.py:254
  61.8 16.5 %collective-permute-start.4 = (bf16[2048,128]{1,0:T(8,128)(2,1)S(1)}, bf16[2048,128]{1,0:T(8,128)(2,1)S(1)}, u32[]{:S(2)}, u32[]{:S(2)}) collective-permute-start(bf16[2048,128]{1,0:T(8,128)(2,1)S(1)} %constant_dynamic-update-slice_fusion.refs_0_), channel_id=1, source_target_pairs={{0,384},{128,0},{256,128},{384,256},{1,385},{129,1},{257,129},{385... | collective-permute-start | bytes 1572872 | tf_op jit(solution)/shard_map/ppermute | solution.py:254
  66.3 27.7 %all-to-all-start.2 = ((bf16[64,24,128]{2,1,0:T(8,128)(2,1)}), bf16[64,24,128]{2,1,0:T(8,128)(2,1)S(1)}, u32[]{:S(2)}, u32[]{:S(2)}) async-start(bf16[64,24,128]{2,1,0:T(8,128)(2,1)} %broadcast_in_dim.2), calls=%async_computation.2 | async-start | bytes 786432 | tf_op jit(solution)/shard_map/all_to_all | solution.py:40
  78.3 8.8 %collective-permute-start.5 = (bf16[1024,128]{1,0:T(8,128)(2,1)S(1)}, bf16[1024,128]{1,0:T(8,128)(2,1)S(1)}, u32[]{:S(2)}, u32[]{:S(2)}) collective-permute-start(bf16[1024,128]{1,0:T(8,128)(2,1)S(1)} %get-tuple-element.30), channel_id=1, source_target_pairs={{0,128},{128,256},{256,384},{384,0},{1,129},{129,257},{257,385},{3... | collective-permute-start | bytes 786440 | tf_op jit(solution)/shard_map/ppermute | solution.py:254
  81.3 9.9 %collective-permute-start.6 = (bf16[1024,128]{1,0:T(8,128)(2,1)S(1)}, bf16[1024,128]{1,0:T(8,128)(2,1)}, u32[]{:S(2)}, u32[]{:S(2)}) collective-permute-start(bf16[1024,128]{1,0:T(8,128)(2,1)S(1)} %get-tuple-element.31), channel_id=1, source_target_pairs={{0,384},{128,0},{256,128},{384,256},{1,385},{129,1},{257,129},{385... | collective-permute-start | bytes 786440 | tf_op jit(solution)/shard_map/ppermute | solution.py:254
  94.1 14.4 %collective-permute-start.7 = (bf16[1536,128]{1,0:T(8,128)(2,1)S(1)}, bf16[1536,128]{1,0:T(8,128)(2,1)S(1)}, u32[]{:S(2)}, u32[]{:S(2)}) collective-permute-start(bf16[1536,128]{1,0:T(8,128)(2,1)S(1)} %bitcast.9), channel_id=1, source_target_pairs={{0,128},{128,256},{256,384},{1,129},{129,257},{257,385},{2,130},{1... | collective-permute-start | bytes 1179656 | tf_op jit(solution)/shard_map/ppermute | solution.py:259
  95.4 13.1 %collective-permute-start.8 = (bf16[1536,128]{1,0:T(8,128)(2,1)S(1)}, bf16[1536,128]{1,0:T(8,128)(2,1)S(1)}, u32[]{:S(2)}, u32[]{:S(2)}) collective-permute-start(bf16[1536,128]{1,0:T(8,128)(2,1)S(1)} %bitcast.10), channel_id=1, source_target_pairs={{0,256},{128,384},{1,257},{129,385},{2,258},{130,386},{3,259},{131... | collective-permute-start | bytes 1179656 | tf_op jit(solution)/shard_map/ppermute | solution.py:259
  96.7 17.7 %collective-permute-start.9 = (bf16[1536,128]{1,0:T(8,128)(2,1)S(1)}, bf16[1536,128]{1,0:T(8,128)(2,1)S(1)}, u32[]{:S(2)}, u32[]{:S(2)}) collective-permute-start(bf16[1536,128]{1,0:T(8,128)(2,1)S(1)} %bitcast.11), channel_id=1, source_target_pairs={{0,384},{1,385},{2,386},{3,387},{4,388},{5,389},{6,390},{7,391},{8... | collective-permute-start | bytes 1179656 | tf_op jit(solution)/shard_map/ppermute | solution.py:259
  99.0 1.0 copy-start.1
  106.3 8.1 %collective-permute-start.10 = (f32[192,128]{1,0:T(8,128)S(1)}, f32[192,128]{1,0:T(8,128)S(1)}, u32[]{:S(2)}, u32[]{:S(2)}) collective-permute-start(f32[192,128]{1,0:T(8,128)S(1)} %select_bitcast_fusion), channel_id=1, source_target_pairs={{0,16},{16,0},{1,17},{17,1},{2,18},{18,2},{3,19},{19,3},{4,20},{20... | collective-permute-start | bytes 294920 | tf_op jit(solution)/shard_map/ppermute | solution.py:263
  114.5 5.3 %collective-permute-start.11 = (bf16[6144,128]{1,0:T(8,128)(2,1)S(1)}, bf16[6144,128]{1,0:T(8,128)(2,1)S(1)}, u32[]{:S(2)}, u32[]{:S(2)}) collective-permute-start(bf16[6144,128]{1,0:T(8,128)(2,1)S(1)} %join.1), channel_id=1, source_target_pairs={{0,1},{1,0},{2,3},{3,2},{4,5},{5,4},{6,7},{7,6},{8,9},{9,8},{10,11... | collective-permute-start | bytes 4718600 | tf_op jit(solution)/shard_map/ppermute | solution.py:263
Sparse Core Ops, SparseCore 0:
  37.8 59.7 all-gather.2

commit v13 on v9

--- a/solution.py
+++ b/solution.py
@@ -278,7 +278,9 @@
     hs, w, one, three = tie((hs, w, one, three))
     h, part = mix(info, hs, kv_weight)
     h = lax.all_gather(h, TP, axis=0, tiled=False)
-    w = jnp.concatenate([w, one, shift(one, "yq", 1), three], axis=0)
+    two = shift(one, "yq", 1)
+    part, two = tie((part, two))
+    w = jnp.concatenate([w, one, two, three], axis=0)
 
     part = lax.all_to_all(part, PAIR, 0, 0, tiled=True)
     up, down = shift(w, "x", 1), shift(w, "x", -1)

time: 135 us -> 140 us (1.037)
  waiting for transfers between devices: 35.6 us -> 42 us
    all_to_all x1, waiting for transfers between devices: 0.01 us -> 9.78 us  [body(): part = lax.all_to_all(part, PAIR, 0, 0, tiled=True)]
    ppermute x7, waiting for transfers between devices: 24 us -> 19.3 us  [shift(): return lax.ppermute(v, axis, [(i, (i + by) % n) for i in range(n)])]
    all_to_all x1, starting transfers between devices: 11.3 us -> 7.71 us  [broadcast_gather(): lax.all_to_all(jnp.broadcast_to(x[None], (n,) + x.shape), axis, 0, 0, til...]
where the time goes in v13:
time: 140 us; the launch traced here: 138 us
  starting transfers between devices  63 us (45%)
  waiting for transfers between devices  42 us (30%)
  Pallas kernels  14.5 us (10%)
  between operations  13.8 us (10%)
  local copies, waits for them, and re-layouts  2.97 us (2%)
  other arithmetic  1.91 us (1%)
    ppermute x7, starting transfers between devices, shift(): return lax.ppermute(v, axis, [(i, (i + by) % n) for i in range(n)])  25.4 us
    ppermute x7, waiting for transfers between devices, shift(): return lax.ppermute(v, axis, [(i, (i + by) % n) for i in range(n)])  19.3 us
    all_to_all x1, starting transfers between devices, body(): hs = lax.all_to_all(hs, PAIR, 0, 0, tiled=True)  11.7 us
    all_to_all x1, waiting for transfers between devices, body(): part = lax.all_to_all(part, PAIR, 0, 0, tiled=True)  9.78 us
    all_to_all x1, starting transfers between devices, body(): part = lax.all_to_all(part, PAIR, 0, 0, tiled=True)  9.15 us
    all_to_all x1, starting transfers between devices, broadcast_gather(): lax.all_to_all(jnp.broadcast_to(x[None], (n,) + x.shape), axis, 0, 0, til...  7.71 us
    ppermute x3, waiting for transfers between devices, shift_up(): return lax.ppermute(v, axis, [(i, i + by) for i in range(n - by)])  6.25 us
    pallas_call x1, Pallas kernels, project(): pl.pallas_call(project_kernel, in_specs=[pl.BlockSpec(memory_space=pltpu....  6.18 us
  transfers between devices with their start and end apart: 16, of which 9 were waited for; matrix products, arithmetic and copies ran while one was open for 2% of the time, Pallas kernels for 5%

profile of v13, /device:TPU:6, one launch (start us, length us, event | category | flops | bytes accessed | tf_op | source)
XLA Modules:
  0.0 138.2 jit_solution(11254778807750288440)
XLA Ops:
  8.4 11.7 %all-to-all-start = ((bf16[32,12,512]{2,1,0:T(8,128)(2,1)}), bf16[32,12,512]{2,1,0:T(8,128)(2,1)S(1)}, u32[]{:S(2)}, u32[]{:S(2)}) async-start(bf16[32,12,512]{2,1,0:T(8,128)(2,1)} %slabs.1), calls=%async_computation | async-start | bytes 1048576 | tf_op jit(solution)/shard_map/all_to_all | solution.py:275
  20.2 4.5 %collective-permute-start = (bf16[512,128]{1,0:T(8,128)(2,1)S(1)}, bf16[512,128]{1,0:T(8,128)(2,1)S(1)}, u32[]{:S(2)}, u32[]{:S(2)}) collective-permute-start(bf16[512,128]{1,0:T(8,128)(2,1)S(1)} %copy-done.4), channel_id=1, source_target_pairs={{0,32},{32,64},{64,96},{96,0},{1,33},{33,65},{65,97},{97,1},{2,34}... | collective-permute-start | bytes 393224 | tf_op jit(solution)/shard_map/ppermute | solution.py:254
  24.7 3.5 %collective-permute-start.1 = (bf16[512,128]{1,0:T(8,128)(2,1)S(1)}, bf16[512,128]{1,0:T(8,128)(2,1)S(1)}, u32[]{:S(2)}, u32[]{:S(2)}) collective-permute-start(bf16[512,128]{1,0:T(8,128)(2,1)S(1)} %copy-done.4), channel_id=1, source_target_pairs={{0,96},{32,0},{64,32},{96,64},{1,97},{33,1},{65,33},{97,65},{2,98}... | collective-permute-start | bytes 393224 | tf_op jit(solution)/shard_map/ppermute | solution.py:254
  28.3 7.7 %collective-permute-done = bf16[512,128]{1,0:T(8,128)(2,1)S(1)} collective-permute-done((bf16[512,128]{1,0:T(8,128)(2,1)S(1)}, bf16[512,128]{1,0:T(8,128)(2,1)S(1)}, u32[]{:S(2)}, u32[]{:S(2)}) %collective-permute-start) | collective-permute-done | bytes 131104 | tf_op jit(solution)/shard_map/ppermute | solution.py:254
  36.0 1.6 %mix.1 = (bf16[384,512]{1,0:T(8,128)(2,1)}, f32[32,24,128]{2,1,0:T(8,128)}) custom-call(s32[3]{0:T(128)S(1)} %pad_add_fusion.info_ref, bf16[32,12,512]{2,1,0:T(8,128)(2,1)S(1)} %all-to-all-done.x_ref, bf16[1024,256]{1,0:T(8,128)(2,1)S(1)} %copy-done.3), custom_call_target="tpu_custom_call" | custom-call | flops 100663296 | bytes 1048576 | tf_op jit(solution)/shard_map/mix/pallas_call | solution.py:67
  37.6 5.8 %collective-permute-start.2 = (bf16[512,128]{1,0:T(8,128)(2,1)S(1)}, bf16[512,128]{1,0:T(8,128)(2,1)S(1)}, u32[]{:S(2)}, u32[]{:S(2)}) collective-permute-start(bf16[512,128]{1,0:T(8,128)(2,1)S(1)} %collective-permute-done), channel_id=1, source_target_pairs={{0,32},{32,64},{64,96},{96,0},{1,33},{33,65},{65,97},{97,1},{2,34}... | collective-permute-start | bytes 393224 | tf_op jit(solution)/shard_map/ppermute | solution.py:254
  43.4 4.1 %collective-permute-done.2 = bf16[512,128]{1,0:T(8,128)(2,1)S(1)} collective-permute-done((bf16[512,128]{1,0:T(8,128)(2,1)S(1)}, bf16[512,128]{1,0:T(8,128)(2,1)S(1)}, u32[]{:S(2)}, u32[]{:S(2)}) %collective-permute-start.2) | collective-permute-done | bytes 131104 | tf_op jit(solution)/shard_map/ppermute | solution.py:254
  47.5 9.1 %all-to-all-start.1 = ((f32[32,24,128]{2,1,0:T(8,128)}), f32[32,24,128]{2,1,0:T(8,128)S(1)}, u32[]{:S(2)}, u32[]{:S(2)}) async-start(f32[32,24,128]{2,1,0:T(8,128)} %get-tuple-element.33), calls=%async_computation.1 | async-start | bytes 786432 | tf_op jit(solution)/shard_map/all_to_all | solution.py:285
  56.8 2.4 %collective-permute-start.3 = (bf16[2048,128]{1,0:T(8,128)(2,1)S(1)}, bf16[2048,128]{1,0:T(8,128)(2,1)S(1)}, u32[]{:S(2)}, u32[]{:S(2)}) collective-permute-start(bf16[2048,128]{1,0:T(8,128)(2,1)S(1)} %constant_dynamic-update-slice_fusion.refs_0_), channel_id=1, source_target_pairs={{0,128},{128,256},{256,384},{384,0},{1,129},{129,257},{257,385},{3... | collective-permute-start | bytes 1572872 | tf_op jit(solution)/shard_map/ppermute | solution.py:254
  59.2 3.5 %collective-permute-start.4 = (bf16[2048,128]{1,0:T(8,128)(2,1)S(1)}, bf16[2048,128]{1,0:T(8,128)(2,1)S(1)}, u32[]{:S(2)}, u32[]{:S(2)}) collective-permute-start(bf16[2048,128]{1,0:T(8,128)(2,1)S(1)} %constant_dynamic-update-slice_fusion.refs_0_), channel_id=1, source_target_pairs={{0,384},{128,0},{256,128},{384,256},{1,385},{129,1},{257,129},{385... | collective-permute-start | bytes 1572872 | tf_op jit(solution)/shard_map/ppermute | solution.py:254
  62.7 9.8 %all-to-all-done.1 = f32[32,24,128]{2,1,0:T(8,128)S(1)} async-done(((f32[32,24,128]{2,1,0:T(8,128)}), f32[32,24,128]{2,1,0:T(8,128)S(1)}, u32[]{:S(2)}, u32[]{:S(2)}) %all-to-all-start.1) | async-done | bytes 393248 | tf_op jit(solution)/shard_map/all_to_all | solution.py:285
  73.5 7.7 %all-to-all-start.2 = ((bf16[64,24,128]{2,1,0:T(8,128)(2,1)}), bf16[64,24,128]{2,1,0:T(8,128)(2,1)S(1)}, u32[]{:S(2)}, u32[]{:S(2)}) async-start(bf16[64,24,128]{2,1,0:T(8,128)(2,1)} %broadcast_in_dim.2), calls=%async_computation.2 | async-start | bytes 786432 | tf_op jit(solution)/shard_map/all_to_all | solution.py:40
  81.3 2.4 %collective-permute-start.5 = (bf16[1024,128]{1,0:T(8,128)(2,1)S(1)}, bf16[1024,128]{1,0:T(8,128)(2,1)S(1)}, u32[]{:S(2)}, u32[]{:S(2)}) collective-permute-start(bf16[1024,128]{1,0:T(8,128)(2,1)S(1)} %get-tuple-element.34), channel_id=1, source_target_pairs={{0,128},{128,256},{256,384},{384,0},{1,129},{129,257},{257,385},{3... | collective-permute-start | bytes 786440 | tf_op jit(solution)/shard_map/ppermute | solution.py:254
  83.7 3.5 %collective-permute-start.6 = (bf16[1024,128]{1,0:T(8,128)(2,1)S(1)}, bf16[1024,128]{1,0:T(8,128)(2,1)}, u32[]{:S(2)}, u32[]{:S(2)}) collective-permute-start(bf16[1024,128]{1,0:T(8,128)(2,1)S(1)} %get-tuple-element.35), channel_id=1, source_target_pairs={{0,384},{128,0},{256,128},{384,256},{1,385},{129,1},{257,129},{385... | collective-permute-start | bytes 786440 | tf_op jit(solution)/shard_map/ppermute | solution.py:254
  87.2 4.1 %collective-permute-done.5 = bf16[1024,128]{1,0:T(8,128)(2,1)S(1)} collective-permute-done((bf16[1024,128]{1,0:T(8,128)(2,1)S(1)}, bf16[1024,128]{1,0:T(8,128)(2,1)S(1)}, u32[]{:S(2)}, u32[]{:S(2)}) %collective-permute-start.5) | collective-permute-done | bytes 262176 | tf_op jit(solution)/shard_map/ppermute | solution.py:254
  91.2 3.4 %collective-permute-done.6 = bf16[1024,128]{1,0:T(8,128)(2,1)} collective-permute-done((bf16[1024,128]{1,0:T(8,128)(2,1)S(1)}, bf16[1024,128]{1,0:T(8,128)(2,1)}, u32[]{:S(2)}, u32[]{:S(2)}) %collective-permute-start.6) | collective-permute-done | bytes 262176 | tf_op jit(solution)/shard_map/ppermute | solution.py:254
  94.7 3.8 %all-to-all-done.2 = bf16[64,24,128]{2,1,0:T(8,128)(2,1)S(1)} async-done(((bf16[64,24,128]{2,1,0:T(8,128)(2,1)}), bf16[64,24,128]{2,1,0:T(8,128)(2,1)S(1)}, u32[]{:S(2)}, u32[]{:S(2)}) %all-to-all-start.2) | async-done | bytes 393248 | tf_op jit(solution)/shard_map/all_to_all | solution.py:40
  99.8 1.3 collective-permute-start.8
  104.4 6.2 %project.1 = f32[2,192,128]{2,1,0:T(8,128)S(1)} custom-call(s32[3]{0:T(128)S(1)} %pad_add_fusion.info_ref, bf16[16,384,512]{2,1,0:T(8,128)(2,1)} %bitcast.14, bf16[2048,128]{1,0:T(8,128)(2,1)S(1)} %copy-done.1, bf16[2048,128]{1,0:T(8,128)(2,1)S(1)} %collective-permute-done.3.up_ref.refs_1_, bf16[2048,128]{1,0:T(8,128)(2,1)S(1)} %pad_maximum_fusion.refs_2_, ...), custom_call_target="tpu_custom_call" | custom-call | flops 805306368 | bytes 8388608 | tf_op jit(solution)/shard_map/project/pallas_call | solution.py:209
  110.6 3.2 %collective-permute-start.10 = (f32[192,128]{1,0:T(8,128)S(1)}, f32[192,128]{1,0:T(8,128)S(1)}, u32[]{:S(2)}, u32[]{:S(2)}) collective-permute-start(f32[192,128]{1,0:T(8,128)S(1)} %select_bitcast_fusion), channel_id=1, source_target_pairs={{0,16},{16,0},{1,17},{17,1},{2,18},{18,2},{3,19},{19,3},{4,20},{20... | collective-permute-start | bytes 294920 | tf_op jit(solution)/shard_map/ppermute | solution.py:263
  113.9 6.2 %collective-permute-done.9.refs_3_ = bf16[1536,128]{1,0:T(8,128)(2,1)S(1)} collective-permute-done((bf16[1536,128]{1,0:T(8,128)(2,1)S(1)}, bf16[1536,128]{1,0:T(8,128)(2,1)S(1)}, u32[]{:S(2)}, u32[]{:S(2)}) %collective-permute-start.9) | collective-permute-done | bytes 393248 | tf_op jit(solution)/shard_map/ppermute | solution.py:259
  120.3 1.9 %collective-permute-start.11 = (bf16[6144,128]{1,0:T(8,128)(2,1)S(1)}, bf16[6144,128]{1,0:T(8,128)(2,1)S(1)}, u32[]{:S(2)}, u32[]{:S(2)}) collective-permute-start(bf16[6144,128]{1,0:T(8,128)(2,1)S(1)} %join.1), channel_id=1, source_target_pairs={{0,1},{1,0},{2,3},{3,2},{4,5},{5,4},{6,7},{7,6},{8,9},{9,8},{10,11... | collective-permute-start | bytes 4718600 | tf_op jit(solution)/shard_map/ppermute | solution.py:263
  122.8 2.8 %collective-permute-done.11.refs_4_ = bf16[6144,128]{1,0:T(8,128)(2,1)S(1)} collective-permute-done((bf16[6144,128]{1,0:T(8,128)(2,1)S(1)}, bf16[6144,128]{1,0:T(8,128)(2,1)S(1)}, u32[]{:S(2)}, u32[]{:S(2)}) %collective-permute-start.11) | collective-permute-done | bytes 1572896 | tf_op jit(solution)/shard_map/ppermute | solution.py:263
  125.6 5.8 %attend.1 = bf16[192,128]{1,0:T(8,128)(2,1)} custom-call(s32[3]{0:T(128)S(1)} %pad_add_fusion.info_ref, f32[192,128]{1,0:T(8,128)S(1)} %bitcast_add_fusion.q_ref, f32[192,128]{1,0:T(8,128)S(1)} %get-tuple-element.48.cos_ref, f32[192,128]{1,0:T(8,128)S(1)} %get-tuple-element.49.sin_ref, bf16[1536,128]{1,0:T(8,128)(2,1)S(1)} %bitcast.13, ...), custom_call_target="tpu_custom_call" | custom-call | flops 603979776 | bytes 3145728 | tf_op jit(solution)/shard_map/attend/pallas_call | solution.py:231
  (42 shorter events, 8.6 us)
Async XLA Ops:
  6.5 1.0 copy-start.2
  7.6 12.6 %copy-start.4 = (bf16[512,128]{1,0:T(8,128)(2,1)S(1)}, bf16[512,128]{1,0:T(8,128)(2,1)}, u32[]{:S(2)}) copy-start(bf16[512,128]{1,0:T(8,128)(2,1)} %param.4) | copy-start | bytes 393220
  7.6 28.4 %copy-start.3 = (bf16[1024,256]{1,0:T(8,128)(2,1)S(1)}, bf16[1024,256]{1,0:T(8,128)(2,1)}, u32[]{:S(2)}) copy-start(bf16[1024,256]{1,0:T(8,128)(2,1)} %w_ref.1) | copy-start | bytes 1572868
  8.4 27.6 %all-to-all-start = ((bf16[32,12,512]{2,1,0:T(8,128)(2,1)}), bf16[32,12,512]{2,1,0:T(8,128)(2,1)S(1)}, u32[]{:S(2)}, u32[]{:S(2)}) async-start(bf16[32,12,512]{2,1,0:T(8,128)(2,1)} %slabs.1), calls=%async_computation | async-start | bytes 1048576 | tf_op jit(solution)/shard_map/all_to_all | solution.py:275
  20.2 83.2 %all-gather.3.cloned.1.call-start = ((), (), s32[]{:S(2)}) async-start(), calls=%async_computation.3 | async-start | bytes 6684672 | tf_op jit(solution)/shard_map/all_gather | solution.py:280
  20.2 15.7 %collective-permute-start = (bf16[512,128]{1,0:T(8,128)(2,1)S(1)}, bf16[512,128]{1,0:T(8,128)(2,1)S(1)}, u32[]{:S(2)}, u32[]{:S(2)}) collective-permute-start(bf16[512,128]{1,0:T(8,128)(2,1)S(1)} %copy-done.4), channel_id=1, source_target_pairs={{0,32},{32,64},{64,96},{96,0},{1,33},{33,65},{65,97},{97,1},{2,34}... | collective-permute-start | bytes 393224 | tf_op jit(solution)/shard_map/ppermute | solution.py:254
  24.7 11.2 %collective-permute-start.1 = (bf16[512,128]{1,0:T(8,128)(2,1)S(1)}, bf16[512,128]{1,0:T(8,128)(2,1)S(1)}, u32[]{:S(2)}, u32[]{:S(2)}) collective-permute-start(bf16[512,128]{1,0:T(8,128)(2,1)S(1)} %copy-done.4), channel_id=1, source_target_pairs={{0,96},{32,0},{64,32},{96,64},{1,97},{33,1},{65,33},{97,65},{2,98}... | collective-permute-start | bytes 393224 | tf_op jit(solution)/shard_map/ppermute | solution.py:254
  37.6 9.8 %collective-permute-start.2 = (bf16[512,128]{1,0:T(8,128)(2,1)S(1)}, bf16[512,128]{1,0:T(8,128)(2,1)S(1)}, u32[]{:S(2)}, u32[]{:S(2)}) collective-permute-start(bf16[512,128]{1,0:T(8,128)(2,1)S(1)} %collective-permute-done), channel_id=1, source_target_pairs={{0,32},{32,64},{64,96},{96,0},{1,33},{33,65},{65,97},{97,1},{2,34}... | collective-permute-start | bytes 393224 | tf_op jit(solution)/shard_map/ppermute | solution.py:254
  47.5 25.0 %all-to-all-start.1 = ((f32[32,24,128]{2,1,0:T(8,128)}), f32[32,24,128]{2,1,0:T(8,128)S(1)}, u32[]{:S(2)}, u32[]{:S(2)}) async-start(f32[32,24,128]{2,1,0:T(8,128)} %get-tuple-element.33), calls=%async_computation.1 | async-start | bytes 786432 | tf_op jit(solution)/shard_map/all_to_all | solution.py:285
  56.8 44.3 %copy-start = (bf16[2048,128]{1,0:T(8,128)(2,1)}, bf16[2048,128]{1,0:T(8,128)(2,1)S(1)}, u32[]{:S(2)}) copy-start(bf16[2048,128]{1,0:T(8,128)(2,1)S(1)} %constant_dynamic-update-slice_fusion.refs_0_) | copy-start | bytes 1572868
  56.8 24.4 %collective-permute-start.3 = (bf16[2048,128]{1,0:T(8,128)(2,1)S(1)}, bf16[2048,128]{1,0:T(8,128)(2,1)S(1)}, u32[]{:S(2)}, u32[]{:S(2)}) collective-permute-start(bf16[2048,128]{1,0:T(8,128)(2,1)S(1)} %constant_dynamic-update-slice_fusion.refs_0_), channel_id=1, source_target_pairs={{0,128},{128,256},{256,384},{384,0},{1,129},{129,257},{257,385},{3... | collective-permute-start | bytes 1572872 | tf_op jit(solution)/shard_map/ppermute | solution.py:254
  59.2 22.1 %collective-permute-start.4 = (bf16[2048,128]{1,0:T(8,128)(2,1)S(1)}, bf16[2048,128]{1,0:T(8,128)(2,1)S(1)}, u32[]{:S(2)}, u32[]{:S(2)}) collective-permute-start(bf16[2048,128]{1,0:T(8,128)(2,1)S(1)} %constant_dynamic-update-slice_fusion.refs_0_), channel_id=1, source_target_pairs={{0,384},{128,0},{256,128},{384,256},{1,385},{129,1},{257,129},{385... | collective-permute-start | bytes 1572872 | tf_op jit(solution)/shard_map/ppermute | solution.py:254
  73.5 25.0 %all-to-all-start.2 = ((bf16[64,24,128]{2,1,0:T(8,128)(2,1)}), bf16[64,24,128]{2,1,0:T(8,128)(2,1)S(1)}, u32[]{:S(2)}, u32[]{:S(2)}) async-start(bf16[64,24,128]{2,1,0:T(8,128)(2,1)} %broadcast_in_dim.2), calls=%async_computation.2 | async-start | bytes 786432 | tf_op jit(solution)/shard_map/all_to_all | solution.py:40
  81.3 9.9 %collective-permute-start.5 = (bf16[1024,128]{1,0:T(8,128)(2,1)S(1)}, bf16[1024,128]{1,0:T(8,128)(2,1)S(1)}, u32[]{:S(2)}, u32[]{:S(2)}) collective-permute-start(bf16[1024,128]{1,0:T(8,128)(2,1)S(1)} %get-tuple-element.34), channel_id=1, source_target_pairs={{0,128},{128,256},{256,384},{384,0},{1,129},{129,257},{257,385},{3... | collective-permute-start | bytes 786440 | tf_op jit(solution)/shard_map/ppermute | solution.py:254
  83.7 11.0 %collective-permute-start.6 = (bf16[1024,128]{1,0:T(8,128)(2,1)S(1)}, bf16[1024,128]{1,0:T(8,128)(2,1)}, u32[]{:S(2)}, u32[]{:S(2)}) collective-permute-start(bf16[1024,128]{1,0:T(8,128)(2,1)S(1)} %get-tuple-element.35), channel_id=1, source_target_pairs={{0,384},{128,0},{256,128},{384,256},{1,385},{129,1},{257,129},{385... | collective-permute-start | bytes 786440 | tf_op jit(solution)/shard_map/ppermute | solution.py:254
  98.5 15.4 %collective-permute-start.7 = (bf16[1536,128]{1,0:T(8,128)(2,1)S(1)}, bf16[1536,128]{1,0:T(8,128)(2,1)S(1)}, u32[]{:S(2)}, u32[]{:S(2)}) collective-permute-start(bf16[1536,128]{1,0:T(8,128)(2,1)S(1)} %bitcast.9), channel_id=1, source_target_pairs={{0,128},{128,256},{256,384},{1,129},{129,257},{257,385},{2,130},{1... | collective-permute-start | bytes 1179656 | tf_op jit(solution)/shard_map/ppermute | solution.py:259
  99.8 14.1 %collective-permute-start.8 = (bf16[1536,128]{1,0:T(8,128)(2,1)S(1)}, bf16[1536,128]{1,0:T(8,128)(2,1)S(1)}, u32[]{:S(2)}, u32[]{:S(2)}) collective-permute-start(bf16[1536,128]{1,0:T(8,128)(2,1)S(1)} %bitcast.10), channel_id=1, source_target_pairs={{0,256},{128,384},{1,257},{129,385},{2,258},{130,386},{3,259},{131... | collective-permute-start | bytes 1179656 | tf_op jit(solution)/shard_map/ppermute | solution.py:259
  101.1 19.1 %collective-permute-start.9 = (bf16[1536,128]{1,0:T(8,128)(2,1)S(1)}, bf16[1536,128]{1,0:T(8,128)(2,1)S(1)}, u32[]{:S(2)}, u32[]{:S(2)}) collective-permute-start(bf16[1536,128]{1,0:T(8,128)(2,1)S(1)} %bitcast.11), channel_id=1, source_target_pairs={{0,384},{1,385},{2,386},{3,387},{4,388},{5,389},{6,390},{7,391},{8... | collective-permute-start | bytes 1179656 | tf_op jit(solution)/shard_map/ppermute | solution.py:259
  103.4 1.0 copy-start.1
  110.6 9.5 %collective-permute-start.10 = (f32[192,128]{1,0:T(8,128)S(1)}, f32[192,128]{1,0:T(8,128)S(1)}, u32[]{:S(2)}, u32[]{:S(2)}) collective-permute-start(f32[192,128]{1,0:T(8,128)S(1)} %select_bitcast_fusion), channel_id=1, source_target_pairs={{0,16},{16,0},{1,17},{17,1},{2,18},{18,2},{3,19},{19,3},{4,20},{20... | collective-permute-start | bytes 294920 | tf_op jit(solution)/shard_map/ppermute | solution.py:263
  120.3 5.3 %collective-permute-start.11 = (bf16[6144,128]{1,0:T(8,128)(2,1)S(1)}, bf16[6144,128]{1,0:T(8,128)(2,1)S(1)}, u32[]{:S(2)}, u32[]{:S(2)}) collective-permute-start(bf16[6144,128]{1,0:T(8,128)(2,1)S(1)} %join.1), channel_id=1, source_target_pairs={{0,1},{1,0},{2,3},{3,2},{4,5},{5,4},{6,7},{7,6},{8,9},{9,8},{10,11... | collective-permute-start | bytes 4718600 | tf_op jit(solution)/shard_map/ppermute | solution.py:263
Sparse Core Ops, SparseCore 0:
  37.8 65.4 all-gather.2

commit v14 on v9

--- a/solution.py
+++ b/solution.py
@@ -133,13 +133,13 @@
 
 
 def attend_kernel(info_ref, q_ref, cos_ref, sin_ref, *refs):
-    mine, other_ref, o_ref, buf, s_ref, sems = refs[:4], *refs[4:]
+    mine, near_ref, far_ref, o_ref, buf, s_ref, sems = refs[:4], *refs[4:]
     rows = q_ref.shape[0]
     x, y, core = info_ref[0], info_ref[1], info_ref[2]
     size = mine[0].shape[0]
 
     def copies(i):
-        other = other_ref.at[pl.ds(i * size, size)]
+        other = near_ref if i == 0 else far_ref.at[pl.ds((i - 1) * size, size)]
         return [
             pltpu.make_async_copy(mine[i], buf.at[i, core], sems.at[i, 0]),
             pltpu.make_async_copy(other, buf.at[i, 1 - core], sems.at[i, 1]),
@@ -231,7 +231,7 @@
     return pl.pallas_call(
         attend_kernel,
         in_specs=[pl.BlockSpec(memory_space=pltpu.SMEM), vm, vm, vm]
-        + [pl.BlockSpec(memory_space=pl.ANY)] * 5,
+        + [pl.BlockSpec(memory_space=pl.ANY)] * 6,
         out_specs=vm,
         out_shape=jax.ShapeDtypeStruct(sums.shape, jnp.bfloat16),
         scratch_shapes=[
@@ -246,7 +246,7 @@
             transcendentals=192 * 6144,
         ),
         name="attend",
-    )(info, sums, cosine, sine, *mine, other)
+    )(info, sums, cosine, sine, *mine, *other)
 
 
 def shift(v, axis, by):
@@ -295,8 +295,8 @@
     keep = jnp.where(yp == 0, sums[0], sums[1])
     come = swap(jnp.where(yp == 0, sums[1], sums[0]), "yp")
     away, come = tie((mine[1:], come))
-    (other,) = small_kernel(join_kernel, "join", [(6144, HD)], (rows, *away))
-    other = swap(other, "core")
+    (other,) = small_kernel(join_kernel, "join", [(4608, HD)], tuple(away))
+    other = [swap(rows, "core"), swap(other, "core")]
     cosine, sine = angles_of(base + jnp.arange(192, dtype=jnp.int32))
     cosine = jnp.concatenate([cosine, cosine], axis=1)
     sine = jnp.concatenate([-sine, sine], axis=1)

time: 135 us -> 136 us (level)
  the two profiles are of different devices: /device:TPU:6 before, /device:TPU:1 now
where the time goes in v14:
time: 136 us; the launch traced here: 135 us
  starting transfers between devices  77 us (57%)
  waiting for transfers between devices  27.9 us (21%)
  between operations  13.8 us (10%)
  Pallas kernels  11.4 us (8%)
  local copies, waits for them, and re-layouts  2.96 us (2%)
  other arithmetic  1.91 us (1%)
    ppermute x7, starting transfers between devices, shift(): return lax.ppermute(v, axis, [(i, (i + by) % n) for i in range(n)])  25.3 us
    ppermute x7, waiting for transfers between devices, shift(): return lax.ppermute(v, axis, [(i, (i + by) % n) for i in range(n)])  19.8 us
    all_to_all x1, starting transfers between devices, body(): hs = lax.all_to_all(hs, PAIR, 0, 0, tiled=True)  13 us
    ppermute x3, starting transfers between devices, swap(): return lax.ppermute(v, axis, [(0, 1), (1, 0)])  12.3 us
    all_to_all x1, starting transfers between devices, broadcast_gather(): lax.all_to_all(jnp.broadcast_to(x[None], (n,) + x.shape), axis, 0, 0, til...  10.8 us
    all_to_all x1, starting transfers between devices, body(): part = lax.all_to_all(part, PAIR, 0, 0, tiled=True)  7.97 us
    ppermute x3, starting transfers between devices, shift_up(): return lax.ppermute(v, axis, [(i, i + by) for i in range(n - by)])  7.59 us
    pallas_call x1, Pallas kernels, project(): pl.pallas_call(project_kernel, in_specs=[pl.BlockSpec(memory_space=pltpu....  6.18 us
  transfers between devices with their start and end apart: 17, of which 8 were waited for; matrix products, arithmetic and copies ran while one was open for 2% of the time, Pallas kernels for 5%

profile of v14, /device:TPU:1, one launch (start us, length us, event | category | flops | bytes accessed | tf_op | source)
XLA Modules:
  0.0 134.9 jit_solution(17352977924813717080)
XLA Ops:
  8.4 13.0 %all-to-all-start = ((bf16[32,12,512]{2,1,0:T(8,128)(2,1)}), bf16[32,12,512]{2,1,0:T(8,128)(2,1)S(1)}, u32[]{:S(2)}, u32[]{:S(2)}) async-start(bf16[32,12,512]{2,1,0:T(8,128)(2,1)} %slabs.1), calls=%async_computation | async-start | bytes 1048576 | tf_op jit(solution)/shard_map/all_to_all | solution.py:275
  21.5 4.2 %collective-permute-start = (bf16[512,128]{1,0:T(8,128)(2,1)S(1)}, bf16[512,128]{1,0:T(8,128)(2,1)S(1)}, u32[]{:S(2)}, u32[]{:S(2)}) collective-permute-start(bf16[512,128]{1,0:T(8,128)(2,1)S(1)} %copy-done.5), channel_id=1, source_target_pairs={{0,32},{32,64},{64,96},{96,0},{1,33},{33,65},{65,97},{97,1},{2,34}... | collective-permute-start | bytes 393224 | tf_op jit(solution)/shard_map/ppermute | solution.py:254
  25.7 3.2 %collective-permute-start.1 = (bf16[512,128]{1,0:T(8,128)(2,1)S(1)}, bf16[512,128]{1,0:T(8,128)(2,1)S(1)}, u32[]{:S(2)}, u32[]{:S(2)}) collective-permute-start(bf16[512,128]{1,0:T(8,128)(2,1)S(1)} %copy-done.5), channel_id=1, source_target_pairs={{0,96},{32,0},{64,32},{96,64},{1,97},{33,1},{65,33},{97,65},{2,98}... | collective-permute-start | bytes 393224 | tf_op jit(solution)/shard_map/ppermute | solution.py:254
  29.0 7.8 %collective-permute-done = bf16[512,128]{1,0:T(8,128)(2,1)S(1)} collective-permute-done((bf16[512,128]{1,0:T(8,128)(2,1)S(1)}, bf16[512,128]{1,0:T(8,128)(2,1)S(1)}, u32[]{:S(2)}, u32[]{:S(2)}) %collective-permute-start) | collective-permute-done | bytes 131104 | tf_op jit(solution)/shard_map/ppermute | solution.py:254
  37.1 1.6 %mix.1 = (bf16[384,512]{1,0:T(8,128)(2,1)}, f32[32,24,128]{2,1,0:T(8,128)}) custom-call(s32[3]{0:T(128)S(1)} %pad_add_fusion.info_ref, bf16[32,12,512]{2,1,0:T(8,128)(2,1)S(1)} %all-to-all-done.x_ref, bf16[1024,256]{1,0:T(8,128)(2,1)S(1)} %copy-done.3), custom_call_target="tpu_custom_call" | custom-call | flops 100663296 | bytes 1048576 | tf_op jit(solution)/shard_map/mix/pallas_call | solution.py:67
  38.8 8.0 %all-to-all-start.1 = ((f32[32,24,128]{2,1,0:T(8,128)}), f32[32,24,128]{2,1,0:T(8,128)S(1)}, u32[]{:S(2)}, u32[]{:S(2)}) async-start(f32[32,24,128]{2,1,0:T(8,128)} %get-tuple-element.29), calls=%async_computation.1 | async-start | bytes 786432 | tf_op jit(solution)/shard_map/all_to_all | solution.py:283
  46.8 4.9 %collective-permute-start.2 = (bf16[512,128]{1,0:T(8,128)(2,1)S(1)}, bf16[512,128]{1,0:T(8,128)(2,1)S(1)}, u32[]{:S(2)}, u32[]{:S(2)}) collective-permute-start(bf16[512,128]{1,0:T(8,128)(2,1)S(1)} %collective-permute-done), channel_id=1, source_target_pairs={{0,32},{32,64},{64,96},{96,0},{1,33},{33,65},{65,97},{97,1},{2,34}... | collective-permute-start | bytes 393224 | tf_op jit(solution)/shard_map/ppermute | solution.py:254
  51.7 8.5 %collective-permute-done.2 = bf16[512,128]{1,0:T(8,128)(2,1)S(1)} collective-permute-done((bf16[512,128]{1,0:T(8,128)(2,1)S(1)}, bf16[512,128]{1,0:T(8,128)(2,1)S(1)}, u32[]{:S(2)}, u32[]{:S(2)}) %collective-permute-start.2) | collective-permute-done | bytes 131104 | tf_op jit(solution)/shard_map/ppermute | solution.py:254
  60.2 3.1 %collective-permute-start.3 = (bf16[2048,128]{1,0:T(8,128)(2,1)S(1)}, bf16[2048,128]{1,0:T(8,128)(2,1)S(1)}, u32[]{:S(2)}, u32[]{:S(2)}) collective-permute-start(bf16[2048,128]{1,0:T(8,128)(2,1)S(1)} %constant_dynamic-update-slice_fusion.refs_0_), channel_id=1, source_target_pairs={{0,128},{128,256},{256,384},{384,0},{1,129},{129,257},{257,385},{3... | collective-permute-start | bytes 1572872 | tf_op jit(solution)/shard_map/ppermute | solution.py:254
  63.4 3.4 %collective-permute-start.4 = (bf16[2048,128]{1,0:T(8,128)(2,1)S(1)}, bf16[2048,128]{1,0:T(8,128)(2,1)S(1)}, u32[]{:S(2)}, u32[]{:S(2)}) collective-permute-start(bf16[2048,128]{1,0:T(8,128)(2,1)S(1)} %constant_dynamic-update-slice_fusion.refs_0_), channel_id=1, source_target_pairs={{0,384},{128,0},{256,128},{384,256},{1,385},{129,1},{257,129},{385... | collective-permute-start | bytes 1572872 | tf_op jit(solution)/shard_map/ppermute | solution.py:254
  67.8 10.8 %all-to-all-start.2 = ((bf16[64,24,128]{2,1,0:T(8,128)(2,1)}), bf16[64,24,128]{2,1,0:T(8,128)(2,1)S(1)}, u32[]{:S(2)}, u32[]{:S(2)}) async-start(bf16[64,24,128]{2,1,0:T(8,128)(2,1)} %broadcast_in_dim.2), calls=%async_computation.2 | async-start | bytes 786432 | tf_op jit(solution)/shard_map/all_to_all | solution.py:40
  78.7 2.3 %collective-permute-start.5 = (bf16[1024,128]{1,0:T(8,128)(2,1)S(1)}, bf16[1024,128]{1,0:T(8,128)(2,1)S(1)}, u32[]{:S(2)}, u32[]{:S(2)}) collective-permute-start(bf16[1024,128]{1,0:T(8,128)(2,1)S(1)} %get-tuple-element.30), channel_id=1, source_target_pairs={{0,128},{128,256},{256,384},{384,0},{1,129},{129,257},{257,385},{3... | collective-permute-start | bytes 786440 | tf_op jit(solution)/shard_map/ppermute | solution.py:254
  81.0 4.2 %collective-permute-start.6 = (bf16[1024,128]{1,0:T(8,128)(2,1)S(1)}, bf16[1024,128]{1,0:T(8,128)(2,1)S(1)}, u32[]{:S(2)}, u32[]{:S(2)}) collective-permute-start(bf16[1024,128]{1,0:T(8,128)(2,1)S(1)} %get-tuple-element.31), channel_id=1, source_target_pairs={{0,384},{128,0},{256,128},{384,256},{1,385},{129,1},{257,129},{385... | collective-permute-start | bytes 786440 | tf_op jit(solution)/shard_map/ppermute | solution.py:254
  85.2 2.8 %collective-permute-done.5 = bf16[1024,128]{1,0:T(8,128)(2,1)S(1)} collective-permute-done((bf16[1024,128]{1,0:T(8,128)(2,1)S(1)}, bf16[1024,128]{1,0:T(8,128)(2,1)S(1)}, u32[]{:S(2)}, u32[]{:S(2)}) %collective-permute-start.5) | collective-permute-done | bytes 262176 | tf_op jit(solution)/shard_map/ppermute | solution.py:254
  88.8 3.6 %all-to-all-done.2 = bf16[64,24,128]{2,1,0:T(8,128)(2,1)S(1)} async-done(((bf16[64,24,128]{2,1,0:T(8,128)(2,1)}), bf16[64,24,128]{2,1,0:T(8,128)(2,1)S(1)}, u32[]{:S(2)}, u32[]{:S(2)}) %all-to-all-start.2) | async-done | bytes 393248 | tf_op jit(solution)/shard_map/all_to_all | solution.py:40
  92.5 1.9 %collective-permute-start.7 = (bf16[1536,128]{1,0:T(8,128)(2,1)S(1)}, bf16[1536,128]{1,0:T(8,128)(2,1)S(1)}, u32[]{:S(2)}, u32[]{:S(2)}) collective-permute-start(bf16[1536,128]{1,0:T(8,128)(2,1)S(1)} %bitcast.9), channel_id=1, source_target_pairs={{0,128},{128,256},{256,384},{1,129},{129,257},{257,385},{2,130},{1... | collective-permute-start | bytes 1179656 | tf_op jit(solution)/shard_map/ppermute | solution.py:259
  94.4 4.4 %collective-permute-start.8 = (bf16[1536,128]{1,0:T(8,128)(2,1)S(1)}, bf16[1536,128]{1,0:T(8,128)(2,1)S(1)}, u32[]{:S(2)}, u32[]{:S(2)}) collective-permute-start(bf16[1536,128]{1,0:T(8,128)(2,1)S(1)} %bitcast.10), channel_id=1, source_target_pairs={{0,256},{128,384},{1,257},{129,385},{2,258},{130,386},{3,259},{131... | collective-permute-start | bytes 1179656 | tf_op jit(solution)/shard_map/ppermute | solution.py:259
  98.8 1.3 collective-permute-start.9
  102.1 6.2 %project.1 = f32[2,192,128]{2,1,0:T(8,128)S(1)} custom-call(s32[3]{0:T(128)S(1)} %pad_add_fusion.info_ref, bf16[16,384,512]{2,1,0:T(8,128)(2,1)} %bitcast.14, bf16[2048,128]{1,0:T(8,128)(2,1)S(1)} %copy-done.1, bf16[2048,128]{1,0:T(8,128)(2,1)S(1)} %collective-permute-done.3.up_ref.refs_1_, bf16[2048,128]{1,0:T(8,128)(2,1)S(1)} %pad_maximum_fusion.refs_2_, ...), custom_call_target="tpu_custom_call" | custom-call | flops 805306368 | bytes 8388608 | tf_op jit(solution)/shard_map/project/pallas_call | solution.py:209
  108.4 2.6 %collective-permute-start.10 = (f32[192,128]{1,0:T(8,128)S(1)}, f32[192,128]{1,0:T(8,128)S(1)}, u32[]{:S(2)}, u32[]{:S(2)}) collective-permute-start(f32[192,128]{1,0:T(8,128)S(1)} %select_bitcast_fusion), channel_id=1, source_target_pairs={{0,16},{16,0},{1,17},{17,1},{2,18},{18,2},{3,19},{19,3},{4,20},{20... | collective-permute-start | bytes 294920 | tf_op jit(solution)/shard_map/ppermute | solution.py:263
  111.0 2.9 %collective-permute-done.9.refs_2_.refs_3_ = bf16[1536,128]{1,0:T(8,128)(2,1)S(1)} collective-permute-done((bf16[1536,128]{1,0:T(8,128)(2,1)S(1)}, bf16[1536,128]{1,0:T(8,128)(2,1)S(1)}, u32[]{:S(2)}, u32[]{:S(2)}) %collective-permute-start.9) | collective-permute-done | bytes 393248 | tf_op jit(solution)/shard_map/ppermute | solution.py:259
  114.0 7.8 %collective-permute-start.12 = (bf16[4608,128]{1,0:T(8,128)(2,1)S(1)}, bf16[4608,128]{1,0:T(8,128)(2,1)S(1)}, u32[]{:S(2)}, u32[]{:S(2)}) collective-permute-start(bf16[4608,128]{1,0:T(8,128)(2,1)S(1)} %join.1), channel_id=1, source_target_pairs={{0,1},{1,0},{2,3},{3,2},{4,5},{5,4},{6,7},{7,6},{8,9},{9,8},{10,11... | collective-permute-start | bytes 3538952 | tf_op jit(solution)/shard_map/ppermute | solution.py:263
  121.8 1.9 %collective-permute-start.11 = (bf16[1536,128]{1,0:T(8,128)(2,1)S(1)}, bf16[1536,128]{1,0:T(8,128)(2,1)S(1)}, u32[]{:S(2)}, u32[]{:S(2)}) collective-permute-start(bf16[1536,128]{1,0:T(8,128)(2,1)S(1)} %bitcast.12), channel_id=1, source_target_pairs={{0,1},{1,0},{2,3},{3,2},{4,5},{5,4},{6,7},{7,6},{8,9},{9,8},{10,11... | collective-permute-start | bytes 1179656 | tf_op jit(solution)/shard_map/ppermute | solution.py:263
  125.4 2.6 %attend.1 = bf16[192,128]{1,0:T(8,128)(2,1)} custom-call(s32[3]{0:T(128)S(1)} %pad_add_fusion.info_ref, f32[192,128]{1,0:T(8,128)S(1)} %bitcast_add_fusion.q_ref, f32[192,128]{1,0:T(8,128)S(1)} %get-tuple-element.44.cos_ref, f32[192,128]{1,0:T(8,128)S(1)} %get-tuple-element.45.sin_ref, bf16[1536,128]{1,0:T(8,128)(2,1)S(1)} %bitcast.13, ...), custom_call_target="tpu_custom_call" | custom-call | flops 603979776 | bytes 3145728 | tf_op jit(solution)/shard_map/attend/pallas_call | solution.py:231
  (46 shorter events, 8.2 us)
Async XLA Ops:
  6.5 1.0 copy-start.2
  7.6 13.9 %copy-start.5 = (bf16[512,128]{1,0:T(8,128)(2,1)S(1)}, bf16[512,128]{1,0:T(8,128)(2,1)}, u32[]{:S(2)}) copy-start(bf16[512,128]{1,0:T(8,128)(2,1)} %param.4) | copy-start | bytes 393220
  7.6 29.6 %copy-start.3 = (bf16[1024,256]{1,0:T(8,128)(2,1)S(1)}, bf16[1024,256]{1,0:T(8,128)(2,1)}, u32[]{:S(2)}) copy-start(bf16[1024,256]{1,0:T(8,128)(2,1)} %w_ref.1) | copy-start | bytes 1572868
  8.4 28.7 %all-to-all-start = ((bf16[32,12,512]{2,1,0:T(8,128)(2,1)}), bf16[32,12,512]{2,1,0:T(8,128)(2,1)S(1)}, u32[]{:S(2)}, u32[]{:S(2)}) async-start(bf16[32,12,512]{2,1,0:T(8,128)(2,1)} %slabs.1), calls=%async_computation | async-start | bytes 1048576 | tf_op jit(solution)/shard_map/all_to_all | solution.py:275
  21.4 79.7 %all-gather.3.cloned.1.call-start = ((), (), s32[]{:S(2)}) async-start(), calls=%async_computation.3 | async-start | bytes 6684672 | tf_op jit(solution)/shard_map/all_gather | solution.py:280
  21.5 15.3 %collective-permute-start = (bf16[512,128]{1,0:T(8,128)(2,1)S(1)}, bf16[512,128]{1,0:T(8,128)(2,1)S(1)}, u32[]{:S(2)}, u32[]{:S(2)}) collective-permute-start(bf16[512,128]{1,0:T(8,128)(2,1)S(1)} %copy-done.5), channel_id=1, source_target_pairs={{0,32},{32,64},{64,96},{96,0},{1,33},{33,65},{65,97},{97,1},{2,34}... | collective-permute-start | bytes 393224 | tf_op jit(solution)/shard_map/ppermute | solution.py:254
  25.7 11.1 %collective-permute-start.1 = (bf16[512,128]{1,0:T(8,128)(2,1)S(1)}, bf16[512,128]{1,0:T(8,128)(2,1)S(1)}, u32[]{:S(2)}, u32[]{:S(2)}) collective-permute-start(bf16[512,128]{1,0:T(8,128)(2,1)S(1)} %copy-done.5), channel_id=1, source_target_pairs={{0,96},{32,0},{64,32},{96,64},{1,97},{33,1},{65,33},{97,65},{2,98}... | collective-permute-start | bytes 393224 | tf_op jit(solution)/shard_map/ppermute | solution.py:254
  38.8 28.0 %all-to-all-start.1 = ((f32[32,24,128]{2,1,0:T(8,128)}), f32[32,24,128]{2,1,0:T(8,128)S(1)}, u32[]{:S(2)}, u32[]{:S(2)}) async-start(f32[32,24,128]{2,1,0:T(8,128)} %get-tuple-element.29), calls=%async_computation.1 | async-start | bytes 786432 | tf_op jit(solution)/shard_map/all_to_all | solution.py:283
  46.8 13.4 %collective-permute-start.2 = (bf16[512,128]{1,0:T(8,128)(2,1)S(1)}, bf16[512,128]{1,0:T(8,128)(2,1)S(1)}, u32[]{:S(2)}, u32[]{:S(2)}) collective-permute-start(bf16[512,128]{1,0:T(8,128)(2,1)S(1)} %collective-permute-done), channel_id=1, source_target_pairs={{0,32},{32,64},{64,96},{96,0},{1,33},{33,65},{65,97},{97,1},{2,34}... | collective-permute-start | bytes 393224 | tf_op jit(solution)/shard_map/ppermute | solution.py:254
  60.2 18.5 %copy-start = (bf16[2048,128]{1,0:T(8,128)(2,1)}, bf16[2048,128]{1,0:T(8,128)(2,1)S(1)}, u32[]{:S(2)}) copy-start(bf16[2048,128]{1,0:T(8,128)(2,1)S(1)} %constant_dynamic-update-slice_fusion.refs_0_) | copy-start | bytes 1572868
  60.2 18.4 %collective-permute-start.3 = (bf16[2048,128]{1,0:T(8,128)(2,1)S(1)}, bf16[2048,128]{1,0:T(8,128)(2,1)S(1)}, u32[]{:S(2)}, u32[]{:S(2)}) collective-permute-start(bf16[2048,128]{1,0:T(8,128)(2,1)S(1)} %constant_dynamic-update-slice_fusion.refs_0_), channel_id=1, source_target_pairs={{0,128},{128,256},{256,384},{384,0},{1,129},{129,257},{257,385},{3... | collective-permute-start | bytes 1572872 | tf_op jit(solution)/shard_map/ppermute | solution.py:254
  63.4 15.3 %collective-permute-start.4 = (bf16[2048,128]{1,0:T(8,128)(2,1)S(1)}, bf16[2048,128]{1,0:T(8,128)(2,1)S(1)}, u32[]{:S(2)}, u32[]{:S(2)}) collective-permute-start(bf16[2048,128]{1,0:T(8,128)(2,1)S(1)} %constant_dynamic-update-slice_fusion.refs_0_), channel_id=1, source_target_pairs={{0,384},{128,0},{256,128},{384,256},{1,385},{129,1},{257,129},{385... | collective-permute-start | bytes 1572872 | tf_op jit(solution)/shard_map/ppermute | solution.py:254
  67.8 24.6 %all-to-all-start.2 = ((bf16[64,24,128]{2,1,0:T(8,128)(2,1)}), bf16[64,24,128]{2,1,0:T(8,128)(2,1)S(1)}, u32[]{:S(2)}, u32[]{:S(2)}) async-start(bf16[64,24,128]{2,1,0:T(8,128)(2,1)} %broadcast_in_dim.2), calls=%async_computation.2 | async-start | bytes 786432 | tf_op jit(solution)/shard_map/all_to_all | solution.py:40
  78.7 9.3 %collective-permute-start.5 = (bf16[1024,128]{1,0:T(8,128)(2,1)S(1)}, bf16[1024,128]{1,0:T(8,128)(2,1)S(1)}, u32[]{:S(2)}, u32[]{:S(2)}) collective-permute-start(bf16[1024,128]{1,0:T(8,128)(2,1)S(1)} %get-tuple-element.30), channel_id=1, source_target_pairs={{0,128},{128,256},{256,384},{384,0},{1,129},{129,257},{257,385},{3... | collective-permute-start | bytes 786440 | tf_op jit(solution)/shard_map/ppermute | solution.py:254
  81.0 7.8 %collective-permute-start.6 = (bf16[1024,128]{1,0:T(8,128)(2,1)S(1)}, bf16[1024,128]{1,0:T(8,128)(2,1)S(1)}, u32[]{:S(2)}, u32[]{:S(2)}) collective-permute-start(bf16[1024,128]{1,0:T(8,128)(2,1)S(1)} %get-tuple-element.31), channel_id=1, source_target_pairs={{0,384},{128,0},{256,128},{384,256},{1,385},{129,1},{257,129},{385... | collective-permute-start | bytes 786440 | tf_op jit(solution)/shard_map/ppermute | solution.py:254
  88.8 3.6 %copy-start.4 = (bf16[1024,128]{1,0:T(8,128)(2,1)}, bf16[1024,128]{1,0:T(8,128)(2,1)S(1)}, u32[]{:S(2)}) copy-start(bf16[1024,128]{1,0:T(8,128)(2,1)S(1)} %collective-permute-done.6) | copy-start | bytes 786436
  92.5 18.5 %collective-permute-start.7 = (bf16[1536,128]{1,0:T(8,128)(2,1)S(1)}, bf16[1536,128]{1,0:T(8,128)(2,1)S(1)}, u32[]{:S(2)}, u32[]{:S(2)}) collective-permute-start(bf16[1536,128]{1,0:T(8,128)(2,1)S(1)} %bitcast.9), channel_id=1, source_target_pairs={{0,128},{128,256},{256,384},{1,129},{129,257},{257,385},{2,130},{1... | collective-permute-start | bytes 1179656 | tf_op jit(solution)/shard_map/ppermute | solution.py:259
  94.4 16.6 %collective-permute-start.8 = (bf16[1536,128]{1,0:T(8,128)(2,1)S(1)}, bf16[1536,128]{1,0:T(8,128)(2,1)S(1)}, u32[]{:S(2)}, u32[]{:S(2)}) collective-permute-start(bf16[1536,128]{1,0:T(8,128)(2,1)S(1)} %bitcast.10), channel_id=1, source_target_pairs={{0,256},{128,384},{1,257},{129,385},{2,258},{130,386},{3,259},{131... | collective-permute-start | bytes 1179656 | tf_op jit(solution)/shard_map/ppermute | solution.py:259
  98.8 15.1 %collective-permute-start.9 = (bf16[1536,128]{1,0:T(8,128)(2,1)S(1)}, bf16[1536,128]{1,0:T(8,128)(2,1)S(1)}, u32[]{:S(2)}, u32[]{:S(2)}) collective-permute-start(bf16[1536,128]{1,0:T(8,128)(2,1)S(1)} %bitcast.11), channel_id=1, source_target_pairs={{0,384},{1,385},{2,386},{3,387},{4,388},{5,389},{6,390},{7,391},{8... | collective-permute-start | bytes 1179656 | tf_op jit(solution)/shard_map/ppermute | solution.py:259
  101.1 1.0 copy-start.1
  108.4 5.5 %collective-permute-start.10 = (f32[192,128]{1,0:T(8,128)S(1)}, f32[192,128]{1,0:T(8,128)S(1)}, u32[]{:S(2)}, u32[]{:S(2)}) collective-permute-start(f32[192,128]{1,0:T(8,128)S(1)} %select_bitcast_fusion), channel_id=1, source_target_pairs={{0,16},{16,0},{1,17},{17,1},{2,18},{18,2},{3,19},{19,3},{4,20},{20... | collective-permute-start | bytes 294920 | tf_op jit(solution)/shard_map/ppermute | solution.py:263
  114.0 11.5 %collective-permute-start.12 = (bf16[4608,128]{1,0:T(8,128)(2,1)S(1)}, bf16[4608,128]{1,0:T(8,128)(2,1)S(1)}, u32[]{:S(2)}, u32[]{:S(2)}) collective-permute-start(bf16[4608,128]{1,0:T(8,128)(2,1)S(1)} %join.1), channel_id=1, source_target_pairs={{0,1},{1,0},{2,3},{3,2},{4,5},{5,4},{6,7},{7,6},{8,9},{9,8},{10,11... | collective-permute-start | bytes 3538952 | tf_op jit(solution)/shard_map/ppermute | solution.py:263
  121.8 3.6 %collective-permute-start.11 = (bf16[1536,128]{1,0:T(8,128)(2,1)S(1)}, bf16[1536,128]{1,0:T(8,128)(2,1)S(1)}, u32[]{:S(2)}, u32[]{:S(2)}) collective-permute-start(bf16[1536,128]{1,0:T(8,128)(2,1)S(1)} %bitcast.12), channel_id=1, source_target_pairs={{0,1},{1,0},{2,3},{3,2},{4,5},{5,4},{6,7},{7,6},{8,9},{9,8},{10,11... | collective-permute-start | bytes 1179656 | tf_op jit(solution)/shard_map/ppermute | solution.py:263
Sparse Core Ops, SparseCore 0:
  38.9 59.9 all-gather.2
